TPU v7x, 32 devices: a whole 2x2x4 slice. The times are simulated.
32 devices in a mesh: dom: 8 (over y, x, core), blk: 4 (over z).
Axes of the slice: x: 2, y: 2, z: 4, core: 2. Of those that a mesh axis runs over, the one named last changes fastest.
Arguments:
- adjoint_start: float32 [192, 3, 320], P('dom', None, 'blk'), may hold values from -6 to 6
- right_sides: float32 [192, 3, 320], P('dom', None, 'blk'), may hold values from -6 to 6
- jac_blocks: bfloat16 [192, 7, 320, 320], P('dom', None, 'blk'), may hold values from -0.125 to 0.125
- block_inverse: bfloat16 [192, 320, 320], P('dom', 'blk'), may hold values from -0.15625 to 0.15625
- neighbours: int32 [192, 6], P('dom'), may hold values from 0 to 191, as said below
- pseudo_shift: float32 [192], P('dom'), may hold values from 0.25 to 2
- shape_partials: bfloat16 [192, 320, 192], P('dom', 'blk'), may hold values from -0.3125 to 0.3125
- node_ids: int32 [192, 64], P('dom'), may hold values from 0 to 6143, as said below
Outputs:
- adjoint: float32 [192, 3, 320], P('dom', None, 'blk')
- shape_gradient: float32 [9, 6144], P(None, ('dom', 'blk'))
Inputs may be any that keep to these rules, and one draw needn't show every extreme that they name: `neighbours`: partition k holds elements k * 24 to (k + 1) * 24 - 1; every neighbour of an element lies in its own partition or in the partition just before or after it. `node_ids`: partition k owns mesh nodes k * 768 to (k + 1) * 768 - 1; every node of an element is owned by the element's partition or by the partition just before or after it.
All inputs are finite; a program needn't handle non-finite values.
Results may differ from a plain program's by a relative error of at most 0.0038.
Values may be sent and summed in bfloat16 or wider, within the bound.
No kernel may reach another device: no remote copies, remote signals or barrier semaphores. Data moves between devices by JAX's collectives and lax.ppermute only.
A program may use at most 64 MiB of HBM per device.

v0:
```python
import jax
import jax.numpy as jnp
from jax import lax
from jax.sharding import PartitionSpec as P

RHS = 3
SWEEPS = 2
NODE_DEV = 768


def padded(block, sides, width):
    for axis, dim in sides:
        count = lax.axis_size(axis)
        forward = [(i, i + 1) for i in range(count - 1)]
        backward = [(target, source) for source, target in forward]
        low = lax.ppermute(
            lax.slice_in_dim(block, block.shape[dim] - width, None, axis=dim), axis, forward
        )
        high = lax.ppermute(lax.slice_in_dim(block, 0, width, axis=dim), axis, backward)
        block = jnp.concatenate([low, block, high], axis=dim)
    return block


def passed_along(block, axis, distance):
    devices = range(lax.axis_size(axis))
    route = [(i - distance, i) for i in devices if i - distance in devices]
    return lax.ppermute(block, axis, route)


def local(
    adjoint_start,
    right_sides,
    jac_blocks,
    block_inverse,
    neighbours,
    pseudo_shift,
    shape_partials,
    node_ids,
):
    local_count = neighbours.shape[0]
    part_index = lax.axis_index("dom")
    first_slot = (part_index - 1) * local_count
    self_slots = jnp.arange(local_count, dtype=jnp.int32)[:, None] + local_count
    slots = jnp.concatenate([self_slots, neighbours - first_slot], axis=1)
    adjoint = adjoint_start
    for sweep in range(SWEEPS):
        adj_half = adjoint.astype(jnp.bfloat16)
        columns = lax.all_gather(adj_half, "blk", axis=2, tiled=True)
        extended = padded(columns, (("dom", 0),), local_count)
        picked = extended[slots]
        product = jnp.einsum(
            "ekrc,ekjc->ejr", jac_blocks, picked, preferred_element_type=jnp.float32
        )
        image = pseudo_shift[:, None, None] * adjoint + product
        resid_half = (right_sides - image).astype(jnp.bfloat16)
        resid_full = lax.all_gather(resid_half, "blk", axis=2, tiled=True)
        adjoint = adjoint + jnp.einsum(
            "erc,ejc->ejr", block_inverse, resid_full, preferred_element_type=jnp.float32
        )
    final_half = adjoint.astype(jnp.bfloat16)
    weighted = -jnp.einsum(
        "ejr,erq->ejq", final_half, shape_partials, preferred_element_type=jnp.float32
    )
    node_width = node_ids.shape[1]
    weighted = weighted.reshape(local_count, RHS, node_width, 3)
    values = jnp.transpose(weighted, (0, 2, 1, 3)).reshape(local_count * node_width, RHS * 3)
    node_slots = (node_ids - (part_index - 1) * NODE_DEV).reshape(-1)
    partial_sums = jax.ops.segment_sum(values, node_slots, 3 * NODE_DEV).T
    lower_part = partial_sums[:, :NODE_DEV]
    middle_part = partial_sums[:, NODE_DEV : 2 * NODE_DEV]
    upper_part = partial_sums[:, 2 * NODE_DEV :]
    from_above = passed_along(lower_part, "dom", -1)
    from_below = passed_along(upper_part, "dom", 1)
    owned = middle_part + from_above + from_below
    shape_gradient = lax.psum_scatter(owned, "blk", scatter_dimension=1, tiled=True)
    return (adjoint, shape_gradient)


def solution(mesh):
    in_specs = (
        P("dom", None, "blk"),
        P("dom", None, "blk"),
        P("dom", None, "blk", None),
        P("dom", "blk", None),
        P("dom", None),
        P("dom"),
        P("dom", "blk", None),
        P("dom", None),
    )
    out_specs = (P("dom", None, "blk"), P(None, ("dom", "blk")))
    return jax.shard_map(local, mesh=mesh, in_specs=in_specs, out_specs=out_specs, check_vma=False)
```

profile of v0, /device:TPU:0, one launch (start us, length us, event | category | flops | bytes accessed | tf_op | source)
XLA Modules:
  0.0 157.9 jit_solution(5136134073712509707)
XLA Ops:
  7.3 0.9 convert_element_type.15
  8.2 15.8 %all_gather.12 = bf16[24,3,320]{0,1,2:T(4,128)(2,1)S(1)} all-gather(bf16[24,3,80]{0,1,2:T(4,128)(2,1)S(1)} %copy.93), channel_id=1, replica_groups=mesh['dom'=8,'blk'=4] {'blk'}, dimensions={2}, use_global_device_ids=true | all-gather | bytes 57600 | tf_op jit(solution)/shard_map/all_gather | solution.py:48
  24.1 0.2 copy.94
  24.3 1.3 collective-permute-start.1
  25.6 3.0 %collective-permute-start = (bf16[24,3,320]{2,1,0:T(4,128)(2,1)S(1)}, bf16[24,3,320]{2,1,0:T(4,128)(2,1)S(1)}, u32[]{:S(2)}, u32[]{:S(2)}) collective-permute-start(bf16[24,3,320]{2,1,0:T(4,128)(2,1)S(1)} %copy.94), channel_id=1, source_target_pairs={{0,4},{4,8},{8,12},{12,16},{16,20},{20,24},{24,28},{1,5},{5,9},{9,... | collective-permute-start | bytes 138248 | tf_op jit(solution)/shard_map/ppermute | solution.py:16
  28.7 0.7 subtract_bitcast_fusion
  29.6 0.2 pad_maximum_fusion
  29.8 1.1 gather_fusion
  31.0 6.8 %fusion.4 = bf16[24,3,80]{2,1,0:T(4,128)(2,1)S(1)} fusion(bf16[24,7,3,320]{3,2,1,0:T(4,128)(2,1)S(1)} %bitcast.48, bf16[24,7,80,320]{3,2,1,0:T(8,128)(2,1)} %param.10, f32[24,3,80]{2,0,1:T(8,128)S(1)} %copy-done.3, f32[24,3,80]{2,0,1:T(8,128)S(1)} %copy-done.2, f32[24]{0:T(128)S(1)} %copy-done.5), kind=kOutput, calls=%fused_computation.12 | convolution fusion | flops 25827840 | bytes 8981856 | tf_op jit(solution)/shard_map/ekrc,ekjc->ejr/dot_general | solution.py:51
  38.0 15.3 %all_gather.13 = bf16[24,3,320]{0,1,2:T(4,128)(2,1)S(1)} all-gather(bf16[24,3,80]{0,1,2:T(4,128)(2,1)S(1)} %copy.102), channel_id=1, replica_groups=mesh['dom'=8,'blk'=4] {'blk'}, dimensions={2}, use_global_device_ids=true | all-gather | bytes 57600 | tf_op jit(solution)/shard_map/all_gather | solution.py:56
  53.2 0.2 copy.103
  53.5 0.6 fusion.11
  54.2 14.3 %all_gather.14 = bf16[24,3,320]{0,1,2:T(4,128)(2,1)S(1)} all-gather(bf16[24,3,80]{0,1,2:T(4,128)(2,1)S(1)} %copy.105), channel_id=1, replica_groups=mesh['dom'=8,'blk'=4] {'blk'}, dimensions={2}, use_global_device_ids=true | all-gather | bytes 57600 | tf_op jit(solution)/shard_map/all_gather | solution.py:48
  68.5 0.2 copy.106
  68.8 1.3 collective-permute-start.3
  70.1 3.0 %collective-permute-start.2 = (bf16[24,3,320]{2,1,0:T(4,128)(2,1)S(1)}, bf16[24,3,320]{2,1,0:T(4,128)(2,1)S(1)}, u32[]{:S(2)}, u32[]{:S(2)}) collective-permute-start(bf16[24,3,320]{2,1,0:T(4,128)(2,1)S(1)} %copy.106), channel_id=1, source_target_pairs={{0,4},{4,8},{8,12},{12,16},{16,20},{20,24},{24,28},{1,5},{5,9},{9,... | collective-permute-start | bytes 138248 | tf_op jit(solution)/shard_map/ppermute | solution.py:16
  73.2 0.8 collective-permute-done.2
  74.2 1.1 gather_fusion.1
  75.3 6.8 %fusion.5 = bf16[24,3,80]{2,1,0:T(4,128)(2,1)S(1)} fusion(bf16[24,7,3,320]{3,2,1,0:T(4,128)(2,1)S(1)} %bitcast.47, bf16[24,7,80,320]{3,2,1,0:T(8,128)(2,1)} %param.10, f32[24,3,80]{2,0,1:T(8,128)S(1)} %copy-done.3, f32[24,3,80]{2,1,0:T(4,128)S(1)} %get-tuple-element.17, f32[24]{0:T(128)S(1)} %copy-done.5), kind=kOutput, calls=%fused_computation.13 | convolution fusion | flops 25827840 | bytes 8981856 | tf_op jit(solution)/shard_map/ekrc,ekjc->ejr/dot_general | solution.py:51
  82.3 15.2 %all_gather.15 = bf16[24,3,320]{0,1,2:T(4,128)(2,1)S(1)} all-gather(bf16[24,3,80]{0,1,2:T(4,128)(2,1)S(1)} %copy.112), channel_id=1, replica_groups=mesh['dom'=8,'blk'=4] {'blk'}, dimensions={2}, use_global_device_ids=true | all-gather | bytes 57600 | tf_op jit(solution)/shard_map/all_gather | solution.py:56
  97.5 0.2 copy.113
  97.7 0.6 convolution_add_fusion
  98.3 0.3 convolution_negate_fusion
  99.1 0.3 copy.116
  99.4 9.0 %scatter_custom_fusion = f32[2304,9]{1,0:T(8,128)S(1)} fusion(s32[1536]{0:T(1024)S(1)} %reshape.107, f32[1536,9]{1,0:T(8,128)S(1)} %copy.116, f32[]{:T(128)} %constant.18.clone.1), kind=kCustom, calls=%fused_computation.14 | custom fusion | flops 13824 | bytes 82948 | tf_op jit(solution)/shard_map/scatter-add | solution.py:68
  108.5 1.3 collective-permute-start.4
  109.8 3.2 %collective-permute-start.5 = (f32[9,768]{0,1:T(8,128)S(1)}, f32[9,768]{0,1:T(8,128)S(1)}, u32[]{:S(2)}, u32[]{:S(2)}) collective-permute-start(f32[9,768]{0,1:T(8,128)S(1)} %get-tuple-element.15), channel_id=1, source_target_pairs={{0,4},{4,8},{8,12},{12,16},{16,20},{20,24},{24,28},{1,5},{5,9},{9,... | collective-permute-start | bytes 82952 | tf_op jit(solution)/shard_map/ppermute | solution.py:27
  113.0 1.3 collective-permute-done.5
  114.3 0.8 fusion.8
  115.2 0.6 copy.117
  115.8 33.7 %reduce-scatter.2.cloned.1.call-done = f32[9,192]{0,1:T(8,128)} async-done(((f32[9,768]{0,1:T(8,128)}), f32[9,192]{0,1:T(8,128)}) %reduce-scatter.2.cloned.1.call-update) | async-done | bytes 6928 | tf_op jit(solution)/shard_map/reduce_scatter | solution.py:75
  149.5 1.6 copy.118
  (35 shorter events, 1.7 us)
Async XLA Ops:
  7.2 46.3 %copy-start = (bf16[24,80,320]{2,1,0:T(8,128)(2,1)S(1)}, bf16[24,80,320]{2,1,0:T(8,128)(2,1)}, u32[]{:S(2)}) copy-start(bf16[24,80,320]{2,1,0:T(8,128)(2,1)} %param.11) | copy-start | bytes 3686404
  7.2 23.8 %copy-start.2 = (f32[24,3,80]{2,0,1:T(8,128)S(1)}, f32[24,3,80]{2,0,1:T(8,128)}, u32[]{:S(2)}) copy-start(f32[24,3,80]{2,0,1:T(8,128)} %param.8) | copy-start | bytes 69124
  7.2 23.8 %copy-start.5 = (f32[24]{0:T(128)S(1)}, f32[24]{0:T(128)}, u32[]{:S(2)}) copy-start(f32[24]{0:T(128)} %param.13) | copy-start | bytes 292
  7.2 23.8 %copy-start.3 = (f32[24,3,80]{2,0,1:T(8,128)S(1)}, f32[24,3,80]{2,0,1:T(8,128)}, u32[]{:S(2)}) copy-start(f32[24,3,80]{2,0,1:T(8,128)} %param.9) | copy-start | bytes 69124
  7.2 142.3 %reduce-scatter.2.cloned.1.call-start = ((), (), s32[]{:S(2)}) async-start(), calls=%async_computation.1 | async-start | bytes 491520 | tf_op jit(solution)/shard_map/reduce_scatter | solution.py:75
  24.3 5.3 %collective-permute-start.1 = (bf16[24,3,320]{2,1,0:T(4,128)(2,1)S(1)}, bf16[24,3,320]{2,1,0:T(4,128)(2,1)S(1)}, u32[]{:S(2)}, u32[]{:S(2)}) collective-permute-start(bf16[24,3,320]{2,1,0:T(4,128)(2,1)S(1)} %copy.94), channel_id=1, source_target_pairs={{4,0},{8,4},{12,8},{16,12},{20,16},{24,20},{28,24},{5,1},{9,5},{13... | collective-permute-start | bytes 138248 | tf_op jit(solution)/shard_map/ppermute | solution.py:19
  25.6 4.0 %collective-permute-start = (bf16[24,3,320]{2,1,0:T(4,128)(2,1)S(1)}, bf16[24,3,320]{2,1,0:T(4,128)(2,1)S(1)}, u32[]{:S(2)}, u32[]{:S(2)}) collective-permute-start(bf16[24,3,320]{2,1,0:T(4,128)(2,1)S(1)} %copy.94), channel_id=1, source_target_pairs={{0,4},{4,8},{8,12},{12,16},{16,20},{20,24},{24,28},{1,5},{5,9},{9,... | collective-permute-start | bytes 138248 | tf_op jit(solution)/shard_map/ppermute | solution.py:16
  53.2 19.9 %copy-start.4 = (s32[24,64]{1,0:T(8,128)S(1)}, s32[24,64]{1,0:T(8,128)}, u32[]{:S(2)}) copy-start(s32[24,64]{1,0:T(8,128)} %param.15) | copy-start | bytes 18436
  68.8 4.4 %collective-permute-start.3 = (bf16[24,3,320]{2,1,0:T(4,128)(2,1)S(1)}, bf16[24,3,320]{2,1,0:T(4,128)(2,1)S(1)}, u32[]{:S(2)}, u32[]{:S(2)}) collective-permute-start(bf16[24,3,320]{2,1,0:T(4,128)(2,1)S(1)} %copy.106), channel_id=1, source_target_pairs={{4,0},{8,4},{12,8},{16,12},{20,16},{24,20},{28,24},{5,1},{9,5},{13... | collective-permute-start | bytes 138248 | tf_op jit(solution)/shard_map/ppermute | solution.py:19
  70.1 3.9 %collective-permute-start.2 = (bf16[24,3,320]{2,1,0:T(4,128)(2,1)S(1)}, bf16[24,3,320]{2,1,0:T(4,128)(2,1)S(1)}, u32[]{:S(2)}, u32[]{:S(2)}) collective-permute-start(bf16[24,3,320]{2,1,0:T(4,128)(2,1)S(1)} %copy.106), channel_id=1, source_target_pairs={{0,4},{4,8},{8,12},{12,16},{16,20},{20,24},{24,28},{1,5},{5,9},{9,... | collective-permute-start | bytes 138248 | tf_op jit(solution)/shard_map/ppermute | solution.py:16
  82.1 16.2 %copy-start.1 = (bf16[24,80,192]{2,1,0:T(8,128)(2,1)S(1)}, bf16[24,80,192]{2,1,0:T(8,128)(2,1)}, u32[]{:S(2)}) copy-start(bf16[24,80,192]{2,1,0:T(8,128)(2,1)} %param.14) | copy-start | bytes 2211844
  108.5 4.5 %collective-permute-start.4 = (f32[9,768]{0,1:T(8,128)S(1)}, f32[9,768]{0,1:T(8,128)S(1)}, u32[]{:S(2)}, u32[]{:S(2)}) collective-permute-start(f32[9,768]{0,1:T(8,128)S(1)} %get-tuple-element.14), channel_id=1, source_target_pairs={{4,0},{8,4},{12,8},{16,12},{20,16},{24,20},{28,24},{5,1},{9,5},{13... | collective-permute-start | bytes 82952 | tf_op jit(solution)/shard_map/ppermute | solution.py:27
  109.8 4.5 %collective-permute-start.5 = (f32[9,768]{0,1:T(8,128)S(1)}, f32[9,768]{0,1:T(8,128)S(1)}, u32[]{:S(2)}, u32[]{:S(2)}) collective-permute-start(f32[9,768]{0,1:T(8,128)S(1)} %get-tuple-element.15), channel_id=1, source_target_pairs={{0,4},{4,8},{8,12},{12,16},{16,20},{20,24},{24,28},{1,5},{5,9},{9,... | collective-permute-start | bytes 82952 | tf_op jit(solution)/shard_map/ppermute | solution.py:27
Sparse Core Ops, SparseCore 0:
  115.3 34.1 reduce-scatter.1
where the time goes:
time: 158 us
  blocking collectives  60.6 us (38%)
  waiting for transfers between devices  35.8 us (23%)
  matrix products  15.2 us (10%)
  between operations  14.3 us (9%)
  starting transfers between devices  13.2 us (8%)
  other arithmetic  11.8 us (7%)
  local copies, waits for them, and re-layouts  7.05 us (4%)
    reduce_scatter x1, waiting for transfers between devices, local(): lax.psum_scatter(owned, 'blk', scatter_dimension=1, tiled=True)  33.7 us
    all_gather x2, blocking collectives, local(): resid_full = lax.all_gather(resid_half, 'blk', axis=2, tiled=True)  30.5 us
    all_gather x2, blocking collectives, local(): columns = lax.all_gather(adj_half, 'blk', axis=2, tiled=True)  30.1 us
    dot_general x2, matrix products, local(): jnp.einsum('ekrc,ekjc->ejr', jac_blocks, picked, preferred_element_type=j...  13.7 us
    scatter-add x1, other arithmetic, local(): partial_sums = jax.ops.segment_sum(values, node_slots, 3 * NODE_DEV).T  9.03 us
    ppermute x2, starting transfers between devices, padded(): lax.ppermute(lax.slice_in_dim(block, block.shape[dim] - width, None, axis...  6.07 us
    ppermute x2, starting transfers between devices, passed_along(): return lax.ppermute(block, axis, route)  4.51 us
  transfers between devices with their start and end apart: 7, of which 3 were waited for; matrix products, arithmetic and copies ran while one was open for 1% of the time, Pallas kernels for 0%

commit v1 on v0

v1 whole, which is shorter than its diff:
```python
import functools

import jax
import jax.numpy as jnp
from jax import lax
from jax.experimental import pallas as pl
from jax.experimental.pallas import tpu as pltpu
from jax.sharding import PartitionSpec as P

SWEEPS = 2
NODE_DEV = 768
HALF = jnp.bfloat16
FULL = jnp.float32
LANES = 128
PICK = 8
NT = (((1,), (1,)), ((), ()))
VMEM = pl.BlockSpec(memory_space=pltpu.VMEM)
SMEM = pl.BlockSpec(memory_space=pltpu.SMEM)
ANY = pl.BlockSpec(memory_space=pl.ANY)
MIB = 1024 * 1024


def round_up(size, unit):
    return -(-size // unit) * unit


def iota(shape, dim):
    return lax.broadcasted_iota(jnp.int32, shape, dim)


def hit(condition):
    return jnp.where(condition, 1.0, 0.0)


def call(kernel, name, args, specs, outs, scratch=(), limit=16, flops=0, moved=0):
    return pl.pallas_call(
        kernel,
        in_specs=specs,
        out_specs=[VMEM] * len(outs),
        out_shape=outs,
        scratch_shapes=list(scratch),
        compiler_params=pltpu.CompilerParams(vmem_limit_bytes=limit * MIB),
        cost_estimate=pl.CostEstimate(flops=flops, bytes_accessed=moved, transcendentals=0),
        name=name,
    )(*args)


def over_blk(block):
    count = lax.axis_size("blk")
    return [lax.ppermute(block, "blk", [(i, i ^ k) for i in range(count)]) for k in range(1, count)]


def to_mate(block):
    return lax.ppermute(block, "dom", [(i, i ^ 1) for i in range(lax.axis_size("dom"))])


def to_far(block):
    count = lax.axis_size("dom")
    return lax.ppermute(block, "dom", [(i, (((i + 1) ^ 1) - 1) % count) for i in range(count)])


def round_kernel(adj_ref, half_ref):
    adj = adj_ref[...]
    rows = half_ref.shape[0] - adj.shape[0]
    padded = jnp.concatenate([adj, jnp.zeros((rows, adj.shape[1]), FULL)], axis=0)
    half_ref[...] = padded.astype(HALF)


def prepare_kernel(
    jac_ref, inv_ref, shape_ref, nb_ref, shift_ref, ids_ref,
    jac_out, inv_out, shape_out, pick_out, shift_out, low_out, target_out, spread_out,
    jac_buf, inv_buf, shape_buf, sems,
):
    elements, slots, width, full = jac_ref.shape
    stride = round_up(full, LANES)
    coords = shape_ref.shape[2]
    copies = [pltpu.make_async_copy(jac_ref.at[e], jac_buf.at[e], sems.at[e]) for e in range(elements)]
    copies.append(pltpu.make_async_copy(inv_ref, inv_buf, sems.at[elements]))
    copies.append(pltpu.make_async_copy(shape_ref, shape_buf, sems.at[elements + 1]))
    for copy in copies:
        copy.start()

    dom = lax.axis_index("dom")
    blk = lax.axis_index("blk")
    odd = lax.rem(dom, 2)

    def window(ids, count):
        place = ids - dom * count
        below = jnp.where(place < 0, 1, 0)
        above = jnp.where(place >= count, 1, 0)
        mate = odd * below + (1 - odd) * above
        return 2 * (below + above) - mate, place + (below - above) * count

    rows_part = round_up(3 * elements, 16)
    shape = (PICK, pick_out.shape[1])
    row, lane = iota(shape, 0), iota(shape, 1)
    offset = jnp.where(row < 3, lane - elements * row, -1)

    def pick_rows(e, k):
        if k == 0:
            return hit(offset == e)
        part, inside = window(nb_ref[k - 1, e], elements)
        return hit(offset == part * rows_part + inside)

    @pl.loop(0, elements // 2)
    def _(pair):
        for k in range(slots):
            block = jnp.concatenate([pick_rows(2 * pair, k), pick_rows(2 * pair + 1, k)], axis=0)
            start = pl.multiple_of(k * elements * PICK + pair * 2 * PICK, 16)
            pick_out[pl.ds(start, 2 * PICK), :] = block.astype(HALF)

    shift_out[...] = jnp.zeros(shift_out.shape, FULL)
    for e in range(elements):
        shift_out[pl.ds(e, 3, stride=elements), :] = jnp.full((3, shift_out.shape[1]), shift_ref[e], FULL)

    ids = ids_ref[...]
    blks = lax.axis_size("blk")
    span = NODE_DEV // blks
    part, inside = window(ids, NODE_DEV)
    owner = jnp.zeros_like(inside)
    for cut in range(1, blks):
        owner = owner + jnp.where(inside >= cut * span, 1, 0)
    low = inside - owner * span
    target_out[...] = part * blks + (owner ^ blk)
    shape = (span, LANES)
    for group in range(ids.shape[0]):
        same = iota(shape, 0) == low[group : group + 1, :]
        low_out[:, group * LANES : (group + 1) * LANES] = hit(same).astype(HALF)

    deep = spread_out.shape[0] // 2
    shape = spread_out.shape
    row, lane = iota(shape, 0), iota(shape, 1)
    axis = jnp.where(lane >= LANES, 1, 0) + jnp.where(lane >= 2 * LANES, 1, 0)
    side = lane - axis * LANES
    second = jnp.where(side >= LANES // 2, 1, 0)
    source = second * deep + 3 * (side - second * (LANES // 2)) + axis
    spread_out[...] = hit(row == source).astype(HALF)

    pad = jnp.zeros((width, stride - full), HALF)
    for e in range(elements):
        copies[e].wait()
        for k in range(slots):
            jac_out[e * width : (e + 1) * width, k * stride : k * stride + full] = jac_buf[e, k]
            if stride > full:
                jac_out[e * width : (e + 1) * width, k * stride + full : (k + 1) * stride] = pad
    copies[elements].wait()
    copies[elements + 1].wait()
    for e in range(elements):
        inv_out[e * width : (e + 1) * width, :full] = inv_buf[e]
        if stride > full:
            inv_out[e * width : (e + 1) * width, full:] = pad
        shape_out[e, :, :coords] = shape_buf[e]
        shape_out[e, :, coords:] = jnp.zeros((width, shape_out.shape[2] - coords), HALF)


def put_columns(blocks, stride):
    blk = lax.axis_index("blk")
    width = blocks[0].shape[1]
    shape = (width, stride)
    ahead = iota(shape, 1) - iota(shape, 0)
    total = 0.0
    for k, block in enumerate(blocks):
        place = hit(ahead == (blk ^ k) * width).astype(HALF)
        total = total + jnp.dot(block, place, preferred_element_type=FULL)
    return total.astype(HALF)


def columns_kernel(*refs):
    *blocks, out_ref = refs
    out_ref[...] = put_columns([ref[...] for ref in blocks], out_ref.shape[1])


def residual_kernel(own_ref, mate_ref, far_ref, pick_ref, jac_ref, shift_ref, adj_ref, rhs_ref, out_ref, image):
    rows, width = adj_ref.shape
    elements = rows // 3
    stride = own_ref.shape[1]
    slots = jac_ref.shape[1] // stride
    stacked = [own_ref[...], mate_ref[...], far_ref[...]]
    short = pick_ref.shape[1] - 3 * own_ref.shape[0]
    if short:
        stacked.append(jnp.zeros((short, stride), HALF))
    stacked = jnp.concatenate(stacked, axis=0)
    picked = jnp.dot(pick_ref[...], stacked, preferred_element_type=FULL).astype(HALF)
    image[...] = jnp.zeros(image.shape, FULL)
    for pair in range(elements // 2):
        starts = [k * elements * PICK + pair * 2 * PICK for k in range(slots)]
        left = jnp.concatenate([picked[start : start + 2 * PICK] for start in starts], axis=1)
        for side in range(2):
            e = 2 * pair + side
            blocks = jac_ref[e * width : (e + 1) * width, :]
            product = lax.dot_general(left, blocks, NT, preferred_element_type=FULL)
            first = side * PICK
            image[pl.ds(e, 3, stride=elements), :width] = product[first : first + 3]
    total = shift_ref[:rows, :width] * adj_ref[...] + image[:rows, :width]
    resid = rhs_ref[...] - total
    resid = jnp.concatenate([resid, jnp.zeros((out_ref.shape[0] - rows, width), FULL)], axis=0)
    out_ref[...] = resid.astype(HALF)


def element_of_row(shape, elements, copies=3):
    row = iota(shape, 0)
    for step in range(1, copies + 1):
        row = row - jnp.where(iota(shape, 0) >= step * elements, elements, 0)
    return row


def updated(resid_refs, inv_ref, adj_ref):
    rows, width = adj_ref.shape
    elements = rows // 3
    resid = put_columns([ref[...] for ref in resid_refs], inv_ref.shape[1])
    shape = (resid.shape[0], width)
    owner = element_of_row(shape, elements)
    update = jnp.zeros(shape, FULL)
    for e in range(elements):
        blocks = inv_ref[e * width : (e + 1) * width, :]
        product = lax.dot_general(resid, blocks, NT, preferred_element_type=FULL)
        update = jnp.where(owner == e, product, update)
    adj = jnp.concatenate([adj_ref[...], jnp.zeros((shape[0] - rows, width), FULL)], axis=0)
    return jnp.where(iota(shape, 0) < rows, adj + update, 0.0)


def update_kernel(*refs):
    *resid_refs, inv_ref, adj_ref, adj_out, half_out = refs
    adj = updated(resid_refs, inv_ref, adj_ref)
    adj_out[...] = adj[: adj_out.shape[0]]
    half_out[...] = adj.astype(HALF)


def split(value):
    top = value.astype(HALF)
    return top, (value - top.astype(FULL)).astype(HALF)


def gradient_kernel(*refs):
    blks = lax.axis_size("blk")
    resid_refs = refs[:blks]
    inv_ref, adj_ref, shape_ref, spread_ref, low_ref, target_ref, adj_out = refs[blks : blks + 7]
    piece_outs = refs[blks + 7 : 2 * blks + 7]
    sorted_ref, left_ref, sums_ref = refs[2 * blks + 7 :]
    adj = updated(resid_refs, inv_ref, adj_ref)
    adj_out[...] = adj[: adj_out.shape[0]]
    half = adj.astype(HALF)
    elements = adj_out.shape[0] // 3
    pairs = elements // 2
    tall = round_up(3 * pairs, 16)
    shape = (tall, half.shape[0])
    row, lane = iota(shape, 0), iota(shape, 1)
    group = jnp.where(row >= pairs, 1, 0) + jnp.where(row >= 2 * pairs, 1, 0)
    source = 2 * (row - group * pairs) + group * elements
    source = jnp.where(row < 3 * pairs, source, -2)
    weighted = []
    shape = (tall, shape_ref.shape[2])
    owner = element_of_row(shape, pairs)
    for side in range(2):
        chosen = jnp.dot(hit(lane == source + side).astype(HALF), half, preferred_element_type=FULL).astype(HALF)
        total = jnp.zeros(shape, FULL)
        for pair in range(pairs):
            product = jnp.dot(chosen, shape_ref[2 * pair + side], preferred_element_type=FULL)
            total = jnp.where(owner == pair, product, total)
        weighted.append(total)
    weighted = jnp.concatenate(weighted, axis=1)
    value = 0.0
    for piece in split(weighted):
        value = value + jnp.dot(piece, spread_ref[...], preferred_element_type=FULL)
    top, rest = split(value)
    sorted_ref[:tall] = top.astype(FULL)
    sorted_ref[tall:] = rest.astype(FULL)
    deep = 16
    for pair in range(pairs):
        lanes = slice(pair * LANES, (pair + 1) * LANES)
        mine = iota((deep, LANES), 0) == target_ref[pair : pair + 1, :]
        for part in range(2):
            for j in range(3):
                for c in range(3):
                    at = part * tall + j * pairs + pair
                    values = sorted_ref[at : at + 1, c * LANES : (c + 1) * LANES]
                    start = (part * 9 + j * 3 + c) * deep
                    left_ref[start : start + deep, lanes] = jnp.where(mine, values, 0.0).astype(HALF)
    sums = lax.dot_general(left_ref[...], low_ref[...], NT, preferred_element_type=FULL)
    span = low_ref.shape[0]
    sums = -(sums[: 9 * deep] + sums[9 * deep :])
    tiles = [(tile, tile * LANES, min(span, (tile + 1) * LANES)) for tile in range(sums_ref.shape[0])]
    for tile, start, stop in tiles:
        sums_ref[tile, :, : stop - start] = sums[:, start:stop]
    for k, out_ref in enumerate(piece_outs):
        out_ref[...] = jnp.zeros(out_ref.shape, out_ref.dtype)
        for part in range(3):
            for tile, start, stop in tiles:
                found = sums_ref[tile, pl.ds(part * blks + k, 9, stride=deep), :]
                out_ref[part * 16 : part * 16 + 9, start:stop] = found[:, : stop - start]


def combine_kernel(*refs):
    *piece_refs, own_out, mate_out, far_out = refs
    total = piece_refs[0][...]
    for ref in piece_refs[1:]:
        total = total + ref[...]
    own_out[...] = total[:16]
    mate_out[...] = total[16:32]
    far_out[...] = total[32:48]


def local(
    adjoint_start,
    right_sides,
    jac_blocks,
    block_inverse,
    neighbours,
    pseudo_shift,
    shape_partials,
    node_ids,
):
    elements, sides, width = adjoint_start.shape
    slots, full = jac_blocks.shape[1], jac_blocks.shape[3]
    enodes = node_ids.shape[1]
    coords = shape_partials.shape[2]
    rows = sides * elements
    tall = round_up(rows, 16)
    stride = round_up(full, LANES)
    blks = lax.axis_size("blk")
    span = NODE_DEV // blks
    stacked = round_up(3 * tall, LANES)
    entries = elements * enodes
    sorted_coords = round_up(coords, LANES)

    adj = jnp.transpose(adjoint_start, (1, 0, 2)).reshape(rows, width)
    rhs = jnp.transpose(right_sides, (1, 0, 2)).reshape(rows, width)
    half_shape = jax.ShapeDtypeStruct((tall, width), HALF)
    (half,) = call(round_kernel, "round", [adj], [VMEM], [half_shape])

    jac, inv, shapes, pick, shift, low, target, spread = call(
        prepare_kernel,
        "prepare",
        [jac_blocks, block_inverse, shape_partials, neighbours.T, pseudo_shift, node_ids.reshape(-1, LANES)],
        [ANY, ANY, ANY, SMEM, SMEM, VMEM],
        [
            pltpu.VMEM((elements * width, slots * stride), HALF),
            pltpu.VMEM((elements * width, stride), HALF),
            pltpu.VMEM((elements, width, sorted_coords), HALF),
            pltpu.VMEM((slots * elements * PICK, stacked), HALF),
            pltpu.VMEM((tall, LANES), FULL),
            pltpu.VMEM((span, entries), HALF),
            pltpu.VMEM((entries // LANES, LANES), jnp.int32),
            pltpu.VMEM((2 * sorted_coords, 3 * LANES), HALF),
        ],
        scratch=[
            pltpu.VMEM(jac_blocks.shape, HALF),
            pltpu.VMEM(block_inverse.shape, HALF),
            pltpu.VMEM(shape_partials.shape, HALF),
            pltpu.SemaphoreType.DMA((elements + 2,)),
        ],
        limit=20,
        flops=0,
        moved=24 * MIB,
    )

    for sweep in range(SWEEPS):
        blocks = [half] + over_blk(half)
        wide = jax.ShapeDtypeStruct((tall, stride), HALF)
        (own,) = call(columns_kernel, "columns", blocks, [VMEM] * blks, [wide])
        mate, far = to_mate(own), to_far(own)
        (resid,) = call(
            residual_kernel,
            "residual",
            [own, mate, far, pick, jac, shift, adj, rhs],
            [VMEM] * 8,
            [half_shape],
            scratch=[pltpu.VMEM((tall, LANES), FULL)],
        )
        resids = [resid] + over_blk(resid)
        adj_shape = jax.ShapeDtypeStruct((rows, width), FULL)
        if sweep < SWEEPS - 1:
            adj, half = call(
                update_kernel, "update", resids + [inv, adj], [VMEM] * (blks + 2), [adj_shape, half_shape]
            )
    piece = jax.ShapeDtypeStruct((3 * 16, span), FULL)
    adj, *pieces = call(
        gradient_kernel,
        "gradient",
        resids + [inv, adj, shapes, spread, low, target],
        [VMEM] * (blks + 6),
        [adj_shape] + [piece] * blks,
        scratch=[
            pltpu.VMEM((2 * round_up(rows // 2, 16), 3 * LANES), FULL),
            pltpu.VMEM((2 * 9 * 16, entries), HALF),
            pltpu.VMEM((-(-span // LANES), 9 * 16, LANES), FULL),
        ],
    )
    count = lax.axis_size("blk")
    received = [
        lax.ppermute(pieces[k], "blk", [(i, i ^ k) for i in range(count)]) for k in range(1, count)
    ]
    third = jax.ShapeDtypeStruct((16, span), FULL)
    own, mate, far = call(combine_kernel, "combine", [pieces[0]] + received, [VMEM] * blks, [third] * 3)
    gradient = (own + to_mate(mate) + to_far(far))[:9]
    adjoint = jnp.transpose(adj.reshape(sides, elements, width), (1, 0, 2))
    return (adjoint, gradient)


def solution(mesh):
    in_specs = (
        P("dom", None, "blk"),
        P("dom", None, "blk"),
        P("dom", None, "blk", None),
        P("dom", "blk", None),
        P("dom", None),
        P("dom"),
        P("dom", "blk", None),
        P("dom", None),
    )
    out_specs = (P("dom", None, "blk"), P(None, ("dom", "blk")))
    return jax.shard_map(local, mesh=mesh, in_specs=in_specs, out_specs=out_specs, check_vma=False)
```

time: 158 us -> 80.7 us (0.51)
  blocking collectives: 60.6 us -> 0 us
  Pallas kernels: 0 us -> 20.2 us
  matrix products: 15.2 us -> 0 us
  starting transfers between devices: 13.2 us -> 28.2 us
  waiting for transfers between devices: 35.8 us -> 21.2 us
  between operations: 14.3 us -> 0.76 us
  other arithmetic: 11.8 us -> 0.61 us
  local copies, waits for them, and re-layouts: 7.05 us -> 9.39 us
    all_gather x4 -> x0, blocking collectives: 60.6 us -> none  [the longest x2 30.5 us: local(): resid_full = lax.all_gather(resid_half, 'blk', axis=2, tiled=True)]
    reduce_scatter x1 -> x0, waiting for transfers between devices: 33.7 us -> none  [local(): lax.psum_scatter(owned, 'blk', scatter_dimension=1, tiled=True)]
    pallas_call x0 -> x9, Pallas kernels: none -> 20.2 us  [call(): pl.pallas_call(kernel, in_specs=specs, out_specs=[VMEM] * len(outs), out_...]
    ppermute x6 -> x21, waiting for transfers between devices: 2.1 us -> 21.2 us  [the longest x12 10.9 us: over_blk(): lax.ppermute(block, 'blk', [(i, i ^ k) for i in range(count)])]
    dot_general x5 -> x0, matrix products: 15.2 us -> none  [the longest x2 13.7 us: local(): jnp.einsum('ekrc,ekjc->ejr', jac_blocks, picked, preferred_element_type=j...]
    ppermute x6 -> x21, starting transfers between devices: 13.2 us -> 28.2 us  [the longest x12 19.2 us: over_blk(): lax.ppermute(block, 'blk', [(i, i ^ k) for i in range(count)])]
    scatter-add x1 -> x0, other arithmetic: 9.03 us -> none  [local(): partial_sums = jax.ops.segment_sum(values, node_slots, 3 * NODE_DEV).T]
    unnamed x14 -> x16, local copies, waits for them, and re-layouts: 2.23 us -> 8.62 us
  transfers between devices with their start and end apart: 7 -> 21, of which waited for: 3 -> 15; matrix products, arithmetic and copies ran while one was open for 1% -> 1% of each run, Pallas kernels for 0% -> 13%
where the time goes in v1:
time: 80.7 us; the launch traced here: 80.3 us
  starting transfers between devices  28.2 us (35%)
  waiting for transfers between devices  21.2 us (26%)
  Pallas kernels  20.2 us (25%)
  local copies, waits for them, and re-layouts  9.39 us (12%)
    pallas_call x9, Pallas kernels, call(): pl.pallas_call(kernel, in_specs=specs, out_specs=[VMEM] * len(outs), out_...  20.2 us
    ppermute x12, starting transfers between devices, over_blk(): lax.ppermute(block, 'blk', [(i, i ^ k) for i in range(count)])  19.2 us
    ppermute x12, waiting for transfers between devices, over_blk(): lax.ppermute(block, 'blk', [(i, i ^ k) for i in range(count)])  10.9 us
    unnamed x16, local copies, waits for them, and re-layouts  8.62 us
    ppermute x3, waiting for transfers between devices, to_far(): lax.ppermute(block, 'dom', [(i, ((i + 1 ^ 1) - 1) % count) for i in range...  5.86 us
    ppermute x3, waiting for transfers between devices, local(): lax.ppermute(pieces[k], 'blk', [(i, i ^ k) for i in range(count)])  4.43 us
    ppermute x3, starting transfers between devices, local(): lax.ppermute(pieces[k], 'blk', [(i, i ^ k) for i in range(count)])  4.39 us
    ppermute x3, starting transfers between devices, to_mate(): lax.ppermute(block, 'dom', [(i, i ^ 1) for i in range(lax.axis_size('dom'...  2.81 us
  transfers between devices with their start and end apart: 21, of which 15 were waited for; matrix products, arithmetic and copies ran while one was open for 1% of the time, Pallas kernels for 13%

profile of v1, /device:TPU:0, one launch (start us, length us, event | category | flops | bytes accessed | tf_op | source)
XLA Modules:
  0.0 80.3 jit_solution(6125681566575180233)
XLA Ops:
  1.4 5.1 %collective-permute-start.2 = (bf16[80,80]{1,0:T(8,128)(2,1)S(1)}, bf16[80,80]{1,0:T(8,128)(2,1)S(1)}, u32[]{:S(2)}, u32[]{:S(2)}) collective-permute-start(bf16[80,80]{1,0:T(8,128)(2,1)S(1)} %round.1.refs_0_), channel_id=1, source_target_pairs={{0,3},{1,2},{2,1},{3,0},{4,7},{5,6},{6,5},{7,4},{8,11},{9,10},{10,... | collective-permute-start | bytes 38408 | tf_op jit(solution)/shard_map/ppermute | solution.py:50
  7.2 1.1 %collective-permute-done.2.refs_3_ = bf16[80,80]{1,0:T(8,128)(2,1)S(1)} collective-permute-done((bf16[80,80]{1,0:T(8,128)(2,1)S(1)}, bf16[80,80]{1,0:T(8,128)(2,1)S(1)}, u32[]{:S(2)}, u32[]{:S(2)}) %collective-permute-start.2) | collective-permute-done | bytes 12832 | tf_op jit(solution)/shard_map/ppermute | solution.py:50
  8.3 2.9 %collective-permute-done.1.refs_2_ = bf16[80,80]{1,0:T(8,128)(2,1)S(1)} collective-permute-done((bf16[80,80]{1,0:T(8,128)(2,1)S(1)}, bf16[80,80]{1,0:T(8,128)(2,1)S(1)}, u32[]{:S(2)}, u32[]{:S(2)}) %collective-permute-start.1) | collective-permute-done | bytes 12832 | tf_op jit(solution)/shard_map/ppermute | solution.py:50
  12.0 1.1 %collective-permute-start.3 = (bf16[80,384]{1,0:T(8,128)(2,1)S(1)}, bf16[80,384]{1,0:T(8,128)(2,1)S(1)}, u32[]{:S(2)}, u32[]{:S(2)}) collective-permute-start(bf16[80,384]{1,0:T(8,128)(2,1)S(1)} %columns.2.own_ref), channel_id=1, source_target_pairs={{0,4},{4,0},{8,12},{12,8},{16,20},{20,16},{24,28},{28,24},{1,5},{5... | collective-permute-start | bytes 184328 | tf_op jit(solution)/shard_map/ppermute | solution.py:54
  13.9 3.9 %copy-done = bf16[24,7,80,320]{3,2,1,0:T(8,128)(2,1)S(1)} copy-done((bf16[24,7,80,320]{3,2,1,0:T(8,128)(2,1)S(1)}, bf16[24,7,80,320]{3,2,1,0:T(8,128)(2,1)}, u32[]{:S(2)}) %copy-start) | copy-done | bytes 8601624
  17.8 1.4 %copy-done.1 = bf16[24,80,320]{2,1,0:T(8,128)(2,1)S(1)} copy-done((bf16[24,80,320]{2,1,0:T(8,128)(2,1)S(1)}, bf16[24,80,320]{2,1,0:T(8,128)(2,1)}, u32[]{:S(2)}) %copy-start.1) | copy-done | bytes 1228824
  19.2 1.2 %copy-done.2 = bf16[24,80,192]{2,1,0:T(8,128)(2,1)S(1)} copy-done((bf16[24,80,192]{2,1,0:T(8,128)(2,1)S(1)}, bf16[24,80,192]{2,1,0:T(8,128)(2,1)}, u32[]{:S(2)}) %copy-start.2) | copy-done | bytes 737304
  21.8 10.0 %prepare.1 = (bf16[1920,2688]{1,0:T(8,128)(2,1)S(1)}, bf16[1920,384]{1,0:T(8,128)(2,1)S(1)}, bf16[24,80,256]{2,1,0:T(8,128)(2,1)S(1)}, bf16[1344,256]{1,0:T(8,12...) custom-call(bf16[24,7,80,320]{3,2,1,0:T(8,128)(2,1)S(1)} %copy-done,, ...), custom_call_target="tpu_custom_call" | custom-call | bytes 25165824 | tf_op jit(solution)/shard_map/prepare/pallas_call | solution.py:36
  31.8 3.2 %residual.2.refs_0_ = bf16[80,80]{1,0:T(8,128)(2,1)S(1)} custom-call(bf16[80,384]{1,0:T(8,128)(2,1)S(1)} %columns.2.own_ref, bf16[80,384]{1,0:T(8,128)(2,1)S(1)} %collective-permute-done.3.mate_ref, bf16[80,384]{1,0:T(8,128)(2,1)S(1)} %collective-permute-done.4.far_ref, bf16[1344,256]{1,0:T(8,128)(2,1)S(1)} %get-tuple-element.20.pick_ref, ...), custom_call_target="tpu_custom_call" | custom-call | tf_op jit(solution)/shard_map/residual/pallas_call | solution.py:36
  35.0 1.6 %collective-permute-start.7 = (bf16[80,80]{1,0:T(8,128)(2,1)S(1)}, bf16[80,80]{1,0:T(8,128)(2,1)S(1)}, u32[]{:S(2)}, u32[]{:S(2)}) collective-permute-start(bf16[80,80]{1,0:T(8,128)(2,1)S(1)} %residual.2.refs_0_), channel_id=1, source_target_pairs={{0,3},{1,2},{2,1},{3,0},{4,7},{5,6},{6,5},{7,4},{8,11},{9,10},{10,... | collective-permute-start | bytes 38408 | tf_op jit(solution)/shard_map/ppermute | solution.py:50
  37.2 2.3 %collective-permute-start.5 = (bf16[80,80]{1,0:T(8,128)(2,1)S(1)}, bf16[80,80]{1,0:T(8,128)(2,1)S(1)}, u32[]{:S(2)}, u32[]{:S(2)}) collective-permute-start(bf16[80,80]{1,0:T(8,128)(2,1)S(1)} %residual.2.refs_0_), channel_id=1, source_target_pairs={{0,1},{1,0},{2,3},{3,2},{4,5},{5,4},{6,7},{7,6},{8,9},{9,8},{10,11... | collective-permute-start | bytes 38408 | tf_op jit(solution)/shard_map/ppermute | solution.py:50
  39.5 1.3 %collective-permute-done.7.refs_3_ = bf16[80,80]{1,0:T(8,128)(2,1)S(1)} collective-permute-done((bf16[80,80]{1,0:T(8,128)(2,1)S(1)}, bf16[80,80]{1,0:T(8,128)(2,1)S(1)}, u32[]{:S(2)}, u32[]{:S(2)}) %collective-permute-start.7) | collective-permute-done | bytes 12832 | tf_op jit(solution)/shard_map/ppermute | solution.py:50
  42.4 2.4 %collective-permute-start.10 = (bf16[80,80]{1,0:T(8,128)(2,1)S(1)}, bf16[80,80]{1,0:T(8,128)(2,1)S(1)}, u32[]{:S(2)}, u32[]{:S(2)}) collective-permute-start(bf16[80,80]{1,0:T(8,128)(2,1)S(1)} %get-tuple-element.24.refs_0_), channel_id=1, source_target_pairs={{0,3},{1,2},{2,1},{3,0},{4,7},{5,6},{6,5},{7,4},{8,11},{9,10},{10,... | collective-permute-start | bytes 38408 | tf_op jit(solution)/shard_map/ppermute | solution.py:50
  44.8 0.9 %collective-permute-start.9 = (bf16[80,80]{1,0:T(8,128)(2,1)S(1)}, bf16[80,80]{1,0:T(8,128)(2,1)S(1)}, u32[]{:S(2)}, u32[]{:S(2)}) collective-permute-start(bf16[80,80]{1,0:T(8,128)(2,1)S(1)} %get-tuple-element.24.refs_0_), channel_id=1, source_target_pairs={{0,2},{1,3},{2,0},{3,1},{4,6},{5,7},{6,4},{7,5},{8,10},{9,11},{10,... | collective-permute-start | bytes 38408 | tf_op jit(solution)/shard_map/ppermute | solution.py:50
  45.7 1.1 %collective-permute-start.8 = (bf16[80,80]{1,0:T(8,128)(2,1)S(1)}, bf16[80,80]{1,0:T(8,128)(2,1)S(1)}, u32[]{:S(2)}, u32[]{:S(2)}) collective-permute-start(bf16[80,80]{1,0:T(8,128)(2,1)S(1)} %get-tuple-element.24.refs_0_), channel_id=1, source_target_pairs={{0,1},{1,0},{2,3},{3,2},{4,5},{5,4},{6,7},{7,6},{8,9},{9,8},{10,11... | collective-permute-start | bytes 38408 | tf_op jit(solution)/shard_map/ppermute | solution.py:50
  46.8 1.4 %collective-permute-done.10.refs_3_ = bf16[80,80]{1,0:T(8,128)(2,1)S(1)} collective-permute-done((bf16[80,80]{1,0:T(8,128)(2,1)S(1)}, bf16[80,80]{1,0:T(8,128)(2,1)S(1)}, u32[]{:S(2)}, u32[]{:S(2)}) %collective-permute-start.10) | collective-permute-done | bytes 12832 | tf_op jit(solution)/shard_map/ppermute | solution.py:50
  48.2 1.3 %collective-permute-done.9.refs_2_ = bf16[80,80]{1,0:T(8,128)(2,1)S(1)} collective-permute-done((bf16[80,80]{1,0:T(8,128)(2,1)S(1)}, bf16[80,80]{1,0:T(8,128)(2,1)S(1)}, u32[]{:S(2)}, u32[]{:S(2)}) %collective-permute-start.9) | collective-permute-done | bytes 12832 | tf_op jit(solution)/shard_map/ppermute | solution.py:50
  50.0 1.6 %collective-permute-start.11 = (bf16[80,384]{1,0:T(8,128)(2,1)S(1)}, bf16[80,384]{1,0:T(8,128)(2,1)S(1)}, u32[]{:S(2)}, u32[]{:S(2)}) collective-permute-start(bf16[80,384]{1,0:T(8,128)(2,1)S(1)} %columns.3.own_ref), channel_id=1, source_target_pairs={{0,4},{4,0},{8,12},{12,8},{16,20},{20,16},{24,28},{28,24},{1,5},{5... | collective-permute-start | bytes 184328 | tf_op jit(solution)/shard_map/ppermute | solution.py:54
  51.6 2.9 %collective-permute-done.12.far_ref = bf16[80,384]{1,0:T(8,128)(2,1)S(1)} collective-permute-done((bf16[80,384]{1,0:T(8,128)(2,1)S(1)}, bf16[80,384]{1,0:T(8,128)(2,1)S(1)}, u32[]{:S(2)}, u32[]{:S(2)}) %collective-permute-start.12) | collective-permute-done | bytes 61472 | tf_op jit(solution)/shard_map/ppermute | solution.py:59
  54.6 3.2 %residual.3.refs_0_ = bf16[80,80]{1,0:T(8,128)(2,1)S(1)} custom-call(bf16[80,384]{1,0:T(8,128)(2,1)S(1)} %columns.3.own_ref, bf16[80,384]{1,0:T(8,128)(2,1)S(1)} %collective-permute-done.11.mate_ref, bf16[80,384]{1,0:T(8,128)(2,1)S(1)} %collective-permute-done.12.far_ref, bf16[1344,256]{1,0:T(8,128)(2,1)S(1)} %get-tuple-element.20.pick_ref, ...), custom_call_target="tpu_custom_call" | custom-call | tf_op jit(solution)/shard_map/residual/pallas_call | solution.py:36
  57.8 1.6 %collective-permute-start.15 = (bf16[80,80]{1,0:T(8,128)(2,1)S(1)}, bf16[80,80]{1,0:T(8,128)(2,1)S(1)}, u32[]{:S(2)}, u32[]{:S(2)}) collective-permute-start(bf16[80,80]{1,0:T(8,128)(2,1)S(1)} %residual.3.refs_0_), channel_id=1, source_target_pairs={{0,3},{1,2},{2,1},{3,0},{4,7},{5,6},{6,5},{7,4},{8,11},{9,10},{10,... | collective-permute-start | bytes 38408 | tf_op jit(solution)/shard_map/ppermute | solution.py:50
  59.4 0.9 %collective-permute-start.14 = (bf16[80,80]{1,0:T(8,128)(2,1)S(1)}, bf16[80,80]{1,0:T(8,128)(2,1)S(1)}, u32[]{:S(2)}, u32[]{:S(2)}) collective-permute-start(bf16[80,80]{1,0:T(8,128)(2,1)S(1)} %residual.3.refs_0_), channel_id=1, source_target_pairs={{0,2},{1,3},{2,0},{3,1},{4,6},{5,7},{6,4},{7,5},{8,10},{9,11},{10,... | collective-permute-start | bytes 38408 | tf_op jit(solution)/shard_map/ppermute | solution.py:50
  60.3 2.0 %collective-permute-start.13 = (bf16[80,80]{1,0:T(8,128)(2,1)S(1)}, bf16[80,80]{1,0:T(8,128)(2,1)S(1)}, u32[]{:S(2)}, u32[]{:S(2)}) collective-permute-start(bf16[80,80]{1,0:T(8,128)(2,1)S(1)} %residual.3.refs_0_), channel_id=1, source_target_pairs={{0,1},{1,0},{2,3},{3,2},{4,5},{5,4},{6,7},{7,6},{8,9},{9,8},{10,11... | collective-permute-start | bytes 38408 | tf_op jit(solution)/shard_map/ppermute | solution.py:50
  62.3 1.2 %collective-permute-done.15.refs_3_ = bf16[80,80]{1,0:T(8,128)(2,1)S(1)} collective-permute-done((bf16[80,80]{1,0:T(8,128)(2,1)S(1)}, bf16[80,80]{1,0:T(8,128)(2,1)S(1)}, u32[]{:S(2)}, u32[]{:S(2)}) %collective-permute-start.15) | collective-permute-done | bytes 12832 | tf_op jit(solution)/shard_map/ppermute | solution.py:50
  64.3 2.4 %gradient.1 = (f32[72,80]{1,0:T(8,128)}, f32[48,192]{1,0:T(8,128)S(1)}, f32[48,192]{1,0:T(8,128)S(1)}, f32[48,192]{1,0:T(8,128)S(1)}, f32[48,192]{1,0:T(8,128)S(1)}) custom-call(bf16[80,80]{1,0:T(8,128)(2,1)S(1)} %residual.3.refs_0_, bf16[80,80]{1,0:T(8,128)(2,1)S(1)} %collective-permute-done.13.refs_1_, bf16[80,80]{1,0:T(8,128)(2,1)S(1)} %collective-permute-done.14.refs_2_, ...), custom_call_target="tpu_custom_call" | custom-call | tf_op jit(solution)/shard_map/gradient/pallas_call | solution.py:36
  66.7 1.8 %collective-permute-start.16 = (f32[48,192]{1,0:T(8,128)S(1)}, f32[48,192]{1,0:T(8,128)S(1)}, u32[]{:S(2)}, u32[]{:S(2)}) collective-permute-start(f32[48,192]{1,0:T(8,128)S(1)} %get-tuple-element.32), channel_id=1, source_target_pairs={{0,1},{1,0},{2,3},{3,2},{4,5},{5,4},{6,7},{7,6},{8,9},{9,8},{10,11... | collective-permute-start | bytes 110600 | tf_op jit(solution)/shard_map/ppermute | solution.py:391
  68.5 1.1 %collective-permute-start.17 = (f32[48,192]{1,0:T(8,128)S(1)}, f32[48,192]{1,0:T(8,128)S(1)}, u32[]{:S(2)}, u32[]{:S(2)}) collective-permute-start(f32[48,192]{1,0:T(8,128)S(1)} %get-tuple-element.33), channel_id=1, source_target_pairs={{0,2},{1,3},{2,0},{3,1},{4,6},{5,7},{6,4},{7,5},{8,10},{9,11},{10,... | collective-permute-start | bytes 110600 | tf_op jit(solution)/shard_map/ppermute | solution.py:391
  69.6 1.5 %collective-permute-start.18 = (f32[48,192]{1,0:T(8,128)S(1)}, f32[48,192]{1,0:T(8,128)S(1)}, u32[]{:S(2)}, u32[]{:S(2)}) collective-permute-start(f32[48,192]{1,0:T(8,128)S(1)} %get-tuple-element.34), channel_id=1, source_target_pairs={{0,3},{1,2},{2,1},{3,0},{4,7},{5,6},{6,5},{7,4},{8,11},{9,10},{10,... | collective-permute-start | bytes 110600 | tf_op jit(solution)/shard_map/ppermute | solution.py:391
  71.1 2.6 %collective-permute-done.17.refs_2_ = f32[48,192]{1,0:T(8,128)S(1)} collective-permute-done((f32[48,192]{1,0:T(8,128)S(1)}, f32[48,192]{1,0:T(8,128)S(1)}, u32[]{:S(2)}, u32[]{:S(2)}) %collective-permute-start.17) | collective-permute-done | bytes 36896 | tf_op jit(solution)/shard_map/ppermute | solution.py:391
  73.7 1.8 %collective-permute-done.18.refs_3_ = f32[48,192]{1,0:T(8,128)S(1)} collective-permute-done((f32[48,192]{1,0:T(8,128)S(1)}, f32[48,192]{1,0:T(8,128)S(1)}, u32[]{:S(2)}, u32[]{:S(2)}) %collective-permute-start.18) | collective-permute-done | bytes 36896 | tf_op jit(solution)/shard_map/ppermute | solution.py:391
  75.6 1.2 %collective-permute-start.20 = (f32[16,192]{1,0:T(8,128)S(1)}, f32[16,192]{1,0:T(8,128)S(1)}, u32[]{:S(2)}, u32[]{:S(2)}) collective-permute-start(f32[16,192]{1,0:T(8,128)S(1)} %get-tuple-element.37), channel_id=1, source_target_pairs={{0,28},{4,8},{8,4},{12,16},{16,12},{20,24},{24,20},{28,0},{1,29},{... | collective-permute-start | bytes 36872 | tf_op jit(solution)/shard_map/ppermute | solution.py:59
  76.8 2.9 %collective-permute-done.20 = f32[16,192]{1,0:T(8,128)S(1)} collective-permute-done((f32[16,192]{1,0:T(8,128)S(1)}, f32[16,192]{1,0:T(8,128)S(1)}, u32[]{:S(2)}, u32[]{:S(2)}) %collective-permute-start.20) | collective-permute-done | bytes 12320 | tf_op jit(solution)/shard_map/ppermute | solution.py:59
  (37 shorter events, 8.4 us)
Async XLA Ops:
  0.6 0.8 copy-start.3
  1.4 30.4 %copy-start.4 = (f32[24,3,80]{2,0,1:T(8,128)S(1)}, f32[24,3,80]{2,0,1:T(8,128)}, u32[]{:S(2)}) copy-start(f32[24,3,80]{2,0,1:T(8,128)} %param.8) | copy-start | bytes 69124
  1.4 30.4 %copy-start.5 = (f32[24,3,80]{2,0,1:T(8,128)S(1)}, f32[24,3,80]{2,0,1:T(8,128)}, u32[]{:S(2)}) copy-start(f32[24,3,80]{2,0,1:T(8,128)} %param.9) | copy-start | bytes 69124
  1.4 6.9 %collective-permute-start.2 = (bf16[80,80]{1,0:T(8,128)(2,1)S(1)}, bf16[80,80]{1,0:T(8,128)(2,1)S(1)}, u32[]{:S(2)}, u32[]{:S(2)}) collective-permute-start(bf16[80,80]{1,0:T(8,128)(2,1)S(1)} %round.1.refs_0_), channel_id=1, source_target_pairs={{0,3},{1,2},{2,1},{3,0},{4,7},{5,6},{6,5},{7,4},{8,11},{9,10},{10,... | collective-permute-start | bytes 38408 | tf_op jit(solution)/shard_map/ppermute | solution.py:50
  6.5 4.7 %collective-permute-start.1 = (bf16[80,80]{1,0:T(8,128)(2,1)S(1)}, bf16[80,80]{1,0:T(8,128)(2,1)S(1)}, u32[]{:S(2)}, u32[]{:S(2)}) collective-permute-start(bf16[80,80]{1,0:T(8,128)(2,1)S(1)} %round.1.refs_0_), channel_id=1, source_target_pairs={{0,2},{1,3},{2,0},{3,1},{4,6},{5,7},{6,4},{7,5},{8,10},{9,11},{10,... | collective-permute-start | bytes 38408 | tf_op jit(solution)/shard_map/ppermute | solution.py:50
  6.5 4.7 %collective-permute-start = (bf16[80,80]{1,0:T(8,128)(2,1)S(1)}, bf16[80,80]{1,0:T(8,128)(2,1)S(1)}, u32[]{:S(2)}, u32[]{:S(2)}) collective-permute-start(bf16[80,80]{1,0:T(8,128)(2,1)S(1)} %round.1.refs_0_), channel_id=1, source_target_pairs={{0,1},{1,0},{2,3},{3,2},{4,5},{5,4},{6,7},{7,6},{8,9},{9,8},{10,11... | collective-permute-start | bytes 38408 | tf_op jit(solution)/shard_map/ppermute | solution.py:50
  11.5 20.4 %collective-permute-start.4 = (bf16[80,384]{1,0:T(8,128)(2,1)S(1)}, bf16[80,384]{1,0:T(8,128)(2,1)S(1)}, u32[]{:S(2)}, u32[]{:S(2)}) collective-permute-start(bf16[80,384]{1,0:T(8,128)(2,1)S(1)} %columns.2.own_ref), channel_id=1, source_target_pairs={{0,28},{4,8},{8,4},{12,16},{16,12},{20,24},{24,20},{28,0},{1,29},{... | collective-permute-start | bytes 184328 | tf_op jit(solution)/shard_map/ppermute | solution.py:59
  12.0 19.8 %collective-permute-start.3 = (bf16[80,384]{1,0:T(8,128)(2,1)S(1)}, bf16[80,384]{1,0:T(8,128)(2,1)S(1)}, u32[]{:S(2)}, u32[]{:S(2)}) collective-permute-start(bf16[80,384]{1,0:T(8,128)(2,1)S(1)} %columns.2.own_ref), channel_id=1, source_target_pairs={{0,4},{4,0},{8,12},{12,8},{16,20},{20,16},{24,28},{28,24},{1,5},{5... | collective-permute-start | bytes 184328 | tf_op jit(solution)/shard_map/ppermute | solution.py:54
  13.9 3.9 %copy-start = (bf16[24,7,80,320]{3,2,1,0:T(8,128)(2,1)S(1)}, bf16[24,7,80,320]{3,2,1,0:T(8,128)(2,1)}, u32[]{:S(2)}) copy-start(bf16[24,7,80,320]{3,2,1,0:T(8,128)(2,1)} %jac_ref.1) | copy-start | bytes 25804804
  17.8 1.4 %copy-start.1 = (bf16[24,80,320]{2,1,0:T(8,128)(2,1)S(1)}, bf16[24,80,320]{2,1,0:T(8,128)(2,1)}, u32[]{:S(2)}) copy-start(bf16[24,80,320]{2,1,0:T(8,128)(2,1)} %inv_ref.1) | copy-start | bytes 3686404
  19.2 1.2 %copy-start.2 = (bf16[24,80,192]{2,1,0:T(8,128)(2,1)S(1)}, bf16[24,80,192]{2,1,0:T(8,128)(2,1)}, u32[]{:S(2)}) copy-start(bf16[24,80,192]{2,1,0:T(8,128)(2,1)} %shape_ref.1) | copy-start | bytes 2211844
  20.4 0.7 copy-start.6
  21.1 0.7 copy-start.7
  35.0 5.8 %collective-permute-start.7 = (bf16[80,80]{1,0:T(8,128)(2,1)S(1)}, bf16[80,80]{1,0:T(8,128)(2,1)S(1)}, u32[]{:S(2)}, u32[]{:S(2)}) collective-permute-start(bf16[80,80]{1,0:T(8,128)(2,1)S(1)} %residual.2.refs_0_), channel_id=1, source_target_pairs={{0,3},{1,2},{2,1},{3,0},{4,7},{5,6},{6,5},{7,4},{8,11},{9,10},{10,... | collective-permute-start | bytes 38408 | tf_op jit(solution)/shard_map/ppermute | solution.py:50
  36.6 4.7 %collective-permute-start.6 = (bf16[80,80]{1,0:T(8,128)(2,1)S(1)}, bf16[80,80]{1,0:T(8,128)(2,1)S(1)}, u32[]{:S(2)}, u32[]{:S(2)}) collective-permute-start(bf16[80,80]{1,0:T(8,128)(2,1)S(1)} %residual.2.refs_0_), channel_id=1, source_target_pairs={{0,2},{1,3},{2,0},{3,1},{4,6},{5,7},{6,4},{7,5},{8,10},{9,11},{10,... | collective-permute-start | bytes 38408 | tf_op jit(solution)/shard_map/ppermute | solution.py:50
  37.2 4.3 %collective-permute-start.5 = (bf16[80,80]{1,0:T(8,128)(2,1)S(1)}, bf16[80,80]{1,0:T(8,128)(2,1)S(1)}, u32[]{:S(2)}, u32[]{:S(2)}) collective-permute-start(bf16[80,80]{1,0:T(8,128)(2,1)S(1)} %residual.2.refs_0_), channel_id=1, source_target_pairs={{0,1},{1,0},{2,3},{3,2},{4,5},{5,4},{6,7},{7,6},{8,9},{9,8},{10,11... | collective-permute-start | bytes 38408 | tf_op jit(solution)/shard_map/ppermute | solution.py:50
  42.4 5.8 %collective-permute-start.10 = (bf16[80,80]{1,0:T(8,128)(2,1)S(1)}, bf16[80,80]{1,0:T(8,128)(2,1)S(1)}, u32[]{:S(2)}, u32[]{:S(2)}) collective-permute-start(bf16[80,80]{1,0:T(8,128)(2,1)S(1)} %get-tuple-element.24.refs_0_), channel_id=1, source_target_pairs={{0,3},{1,2},{2,1},{3,0},{4,7},{5,6},{6,5},{7,4},{8,11},{9,10},{10,... | collective-permute-start | bytes 38408 | tf_op jit(solution)/shard_map/ppermute | solution.py:50
  44.8 4.7 %collective-permute-start.9 = (bf16[80,80]{1,0:T(8,128)(2,1)S(1)}, bf16[80,80]{1,0:T(8,128)(2,1)S(1)}, u32[]{:S(2)}, u32[]{:S(2)}) collective-permute-start(bf16[80,80]{1,0:T(8,128)(2,1)S(1)} %get-tuple-element.24.refs_0_), channel_id=1, source_target_pairs={{0,2},{1,3},{2,0},{3,1},{4,6},{5,7},{6,4},{7,5},{8,10},{9,11},{10,... | collective-permute-start | bytes 38408 | tf_op jit(solution)/shard_map/ppermute | solution.py:50
  45.7 4.0 %collective-permute-start.8 = (bf16[80,80]{1,0:T(8,128)(2,1)S(1)}, bf16[80,80]{1,0:T(8,128)(2,1)S(1)}, u32[]{:S(2)}, u32[]{:S(2)}) collective-permute-start(bf16[80,80]{1,0:T(8,128)(2,1)S(1)} %get-tuple-element.24.refs_0_), channel_id=1, source_target_pairs={{0,1},{1,0},{2,3},{3,2},{4,5},{5,4},{6,7},{7,6},{8,9},{9,8},{10,11... | collective-permute-start | bytes 38408 | tf_op jit(solution)/shard_map/ppermute | solution.py:50
  50.0 4.6 %collective-permute-start.12 = (bf16[80,384]{1,0:T(8,128)(2,1)S(1)}, bf16[80,384]{1,0:T(8,128)(2,1)S(1)}, u32[]{:S(2)}, u32[]{:S(2)}) collective-permute-start(bf16[80,384]{1,0:T(8,128)(2,1)S(1)} %columns.3.own_ref), channel_id=1, source_target_pairs={{0,28},{4,8},{8,4},{12,16},{16,12},{20,24},{24,20},{28,0},{1,29},{... | collective-permute-start | bytes 184328 | tf_op jit(solution)/shard_map/ppermute | solution.py:59
  50.0 4.5 %collective-permute-start.11 = (bf16[80,384]{1,0:T(8,128)(2,1)S(1)}, bf16[80,384]{1,0:T(8,128)(2,1)S(1)}, u32[]{:S(2)}, u32[]{:S(2)}) collective-permute-start(bf16[80,384]{1,0:T(8,128)(2,1)S(1)} %columns.3.own_ref), channel_id=1, source_target_pairs={{0,4},{4,0},{8,12},{12,8},{16,20},{20,16},{24,28},{28,24},{1,5},{5... | collective-permute-start | bytes 184328 | tf_op jit(solution)/shard_map/ppermute | solution.py:54
  57.8 5.7 %collective-permute-start.15 = (bf16[80,80]{1,0:T(8,128)(2,1)S(1)}, bf16[80,80]{1,0:T(8,128)(2,1)S(1)}, u32[]{:S(2)}, u32[]{:S(2)}) collective-permute-start(bf16[80,80]{1,0:T(8,128)(2,1)S(1)} %residual.3.refs_0_), channel_id=1, source_target_pairs={{0,3},{1,2},{2,1},{3,0},{4,7},{5,6},{6,5},{7,4},{8,11},{9,10},{10,... | collective-permute-start | bytes 38408 | tf_op jit(solution)/shard_map/ppermute | solution.py:50
  59.4 4.7 %collective-permute-start.14 = (bf16[80,80]{1,0:T(8,128)(2,1)S(1)}, bf16[80,80]{1,0:T(8,128)(2,1)S(1)}, u32[]{:S(2)}, u32[]{:S(2)}) collective-permute-start(bf16[80,80]{1,0:T(8,128)(2,1)S(1)} %residual.3.refs_0_), channel_id=1, source_target_pairs={{0,2},{1,3},{2,0},{3,1},{4,6},{5,7},{6,4},{7,5},{8,10},{9,11},{10,... | collective-permute-start | bytes 38408 | tf_op jit(solution)/shard_map/ppermute | solution.py:50
  60.3 4.0 %collective-permute-start.13 = (bf16[80,80]{1,0:T(8,128)(2,1)S(1)}, bf16[80,80]{1,0:T(8,128)(2,1)S(1)}, u32[]{:S(2)}, u32[]{:S(2)}) collective-permute-start(bf16[80,80]{1,0:T(8,128)(2,1)S(1)} %residual.3.refs_0_), channel_id=1, source_target_pairs={{0,1},{1,0},{2,3},{3,2},{4,5},{5,4},{6,7},{7,6},{8,9},{9,8},{10,11... | collective-permute-start | bytes 38408 | tf_op jit(solution)/shard_map/ppermute | solution.py:50
  66.7 4.4 %collective-permute-start.16 = (f32[48,192]{1,0:T(8,128)S(1)}, f32[48,192]{1,0:T(8,128)S(1)}, u32[]{:S(2)}, u32[]{:S(2)}) collective-permute-start(f32[48,192]{1,0:T(8,128)S(1)} %get-tuple-element.32), channel_id=1, source_target_pairs={{0,1},{1,0},{2,3},{3,2},{4,5},{5,4},{6,7},{7,6},{8,9},{9,8},{10,11... | collective-permute-start | bytes 110600 | tf_op jit(solution)/shard_map/ppermute | solution.py:391
  68.5 5.2 %collective-permute-start.17 = (f32[48,192]{1,0:T(8,128)S(1)}, f32[48,192]{1,0:T(8,128)S(1)}, u32[]{:S(2)}, u32[]{:S(2)}) collective-permute-start(f32[48,192]{1,0:T(8,128)S(1)} %get-tuple-element.33), channel_id=1, source_target_pairs={{0,2},{1,3},{2,0},{3,1},{4,6},{5,7},{6,4},{7,5},{8,10},{9,11},{10,... | collective-permute-start | bytes 110600 | tf_op jit(solution)/shard_map/ppermute | solution.py:391
  69.6 5.9 %collective-permute-start.18 = (f32[48,192]{1,0:T(8,128)S(1)}, f32[48,192]{1,0:T(8,128)S(1)}, u32[]{:S(2)}, u32[]{:S(2)}) collective-permute-start(f32[48,192]{1,0:T(8,128)S(1)} %get-tuple-element.34), channel_id=1, source_target_pairs={{0,3},{1,2},{2,1},{3,0},{4,7},{5,6},{6,5},{7,4},{8,11},{9,10},{10,... | collective-permute-start | bytes 110600 | tf_op jit(solution)/shard_map/ppermute | solution.py:391
  75.5 1.3 %collective-permute-start.19 = (f32[16,192]{1,0:T(8,128)S(1)}, f32[16,192]{1,0:T(8,128)S(1)}, u32[]{:S(2)}, u32[]{:S(2)}) collective-permute-start(f32[16,192]{1,0:T(8,128)S(1)} %get-tuple-element.36), channel_id=1, source_target_pairs={{0,4},{4,0},{8,12},{12,8},{16,20},{20,16},{24,28},{28,24},{1,5},{5... | collective-permute-start | bytes 36872 | tf_op jit(solution)/shard_map/ppermute | solution.py:54
  75.6 4.1 %collective-permute-start.20 = (f32[16,192]{1,0:T(8,128)S(1)}, f32[16,192]{1,0:T(8,128)S(1)}, u32[]{:S(2)}, u32[]{:S(2)}) collective-permute-start(f32[16,192]{1,0:T(8,128)S(1)} %get-tuple-element.37), channel_id=1, source_target_pairs={{0,28},{4,8},{8,4},{12,16},{16,12},{20,24},{24,20},{28,0},{1,29},{... | collective-permute-start | bytes 36872 | tf_op jit(solution)/shard_map/ppermute | solution.py:59

commit v2 on v1

v2 whole, which is shorter than its diff:
```python
import functools

import jax
import jax.numpy as jnp
from jax import lax
from jax.experimental import pallas as pl
from jax.experimental.pallas import tpu as pltpu
from jax.sharding import PartitionSpec as P

SWEEPS = 2
NODE_DEV = 768
HALF = jnp.bfloat16
FULL = jnp.float32
LANES = 128
PICK = 8
NT = (((1,), (1,)), ((), ()))
VMEM = pl.BlockSpec(memory_space=pltpu.VMEM)
HBM = pl.BlockSpec(memory_space=pltpu.HBM)
EARLY, MIDDLE = 4, 12
MIB = 1024 * 1024


def round_up(size, unit):
    return -(-size // unit) * unit


def iota(shape, dim):
    return lax.broadcasted_iota(jnp.int32, shape, dim)


def hit(condition):
    return jnp.where(condition, 1.0, 0.0)


def in_hbm(array):
    return pltpu.with_memory_space_constraint(array, pltpu.HBM)


def call(kernel, name, args, specs, outs, scratch=(), limit=16, flops=0, moved=0):
    return pl.pallas_call(
        kernel,
        in_specs=specs,
        out_specs=[VMEM] * len(outs),
        out_shape=outs,
        scratch_shapes=list(scratch),
        compiler_params=pltpu.CompilerParams(vmem_limit_bytes=limit * MIB),
        cost_estimate=pl.CostEstimate(flops=flops, bytes_accessed=moved, transcendentals=0),
        name=name,
    )(*args)


def far_first():
    return list(reversed(range(1, lax.axis_size("blk"))))


def far_last():
    farthest, *others = far_first()
    return [*others, farthest]


def over_blk(block, order):
    count = lax.axis_size("blk")
    return [lax.ppermute(block, "blk", [(i, i ^ k) for i in range(count)]) for k in order]


def to_mate(block):
    return lax.ppermute(block, "dom", [(i, i ^ 1) for i in range(lax.axis_size("dom"))])


def to_far(block):
    count = lax.axis_size("dom")
    return lax.ppermute(block, "dom", [(i, (((i + 1) ^ 1) - 1) % count) for i in range(count)])


def rounded(block, rows):
    short = rows - block.shape[0]
    if short:
        block = jnp.concatenate([block, jnp.zeros((short, block.shape[1]), block.dtype)], axis=0)
    return block.astype(HALF)


def window(ids, count):
    dom = lax.axis_index("dom")
    odd = lax.rem(dom, 2)
    place = ids - dom * count
    below = jnp.where(place < 0, 1, 0)
    above = jnp.where(place >= count, 1, 0)
    mate = odd * below + (1 - odd) * above
    return 2 * (below + above) - mate, place + (below - above) * count


def started(pairs, sems):
    copies = [pltpu.make_async_copy(source, target, sems.at[i]) for i, (source, target) in enumerate(pairs)]
    for copy in copies:
        copy.start()
    return copies


def slots_kernel(
    nb_hbm, shift_hbm, jac_hbm, adj_hbm, rhs_hbm,
    pick_out, shift_out, jac_out, adj_out, rhs_out, nb_ref, shift_ref, sems,
):
    pairs = [(nb_hbm, nb_ref), (shift_hbm, shift_ref), (adj_hbm, adj_out), (rhs_hbm, rhs_out)]
    kept = jac_out.shape[0]
    copies = started(pairs + [(jac_hbm.at[pl.ds(0, kept)], jac_out)], sems)
    copies[0].wait()
    faces, elements = nb_ref.shape
    rows_part = round_up(3 * elements, 16)
    part, inside = window(nb_ref[...], elements)
    bases = jnp.concatenate([iota((1, elements), 1), part * rows_part + inside], axis=0).astype(FULL)
    deep = elements * PICK
    shape = (deep, elements)
    behind = iota(shape, 0) - PICK * iota(shape, 1)
    owner = hit(jnp.logical_and(behind >= 0, behind < PICK)).astype(HALF)
    columns = lax.dot_general(owner, bases.astype(HALF), NT, preferred_element_type=FULL)
    shape = (elements, PICK, pick_out.shape[1])
    row, lane = iota(shape, 1).reshape(deep, -1), iota(shape, 2).reshape(deep, -1)
    offset = jnp.where(row < 3, lane - elements * row, -1).astype(FULL)
    for k in range(faces + 1):
        pick_out[k * deep : (k + 1) * deep, :] = hit(offset == columns[:, k : k + 1]).astype(HALF)
    shift_out[...] = jnp.zeros(shift_out.shape, FULL)
    copies[1].wait()
    for e in range(elements):
        shift_out[pl.ds(e, 3, stride=elements), :] = jnp.full((3, shift_out.shape[1]), shift_ref[e], FULL)
    for copy in copies[2:]:
        copy.wait()


def read_kernel(first, source, out_ref, sems):
    for copy in started([(source.at[pl.ds(first, out_ref.shape[0])], out_ref)], sems):
        copy.wait()


def nodes_kernel(ids_hbm, shape_hbm, low_out, target_out, spread_out, shape_out, ids_ref, sems):
    copies = started([(ids_hbm, ids_ref), (shape_hbm, shape_out)], sems)
    copies[0].wait()
    blk = lax.axis_index("blk")
    blks = lax.axis_size("blk")
    span = NODE_DEV // blks
    ids = ids_ref[...]
    pairs = ids.shape[0] // 2
    ids = [jnp.concatenate([ids[2 * p : 2 * p + 1], ids[2 * p + 1 : 2 * p + 2]], axis=1) for p in range(pairs)]
    part, inside = window(jnp.concatenate(ids, axis=0), NODE_DEV)
    owner = jnp.zeros_like(inside)
    for cut in range(1, blks):
        owner = owner + jnp.where(inside >= cut * span, 1, 0)
    low = inside - owner * span
    target_out[...] = part * blks + (owner ^ blk)
    shape = (span, LANES)
    for group in range(pairs):
        same = iota(shape, 0) == low[group : group + 1, :]
        low_out[:, group * LANES : (group + 1) * LANES] = hit(same).astype(HALF)

    deep = spread_out.shape[0] // 2
    shape = spread_out.shape
    row, lane = iota(shape, 0), iota(shape, 1)
    axis = jnp.where(lane >= LANES, 1, 0) + jnp.where(lane >= 2 * LANES, 1, 0)
    side = lane - axis * LANES
    second = jnp.where(side >= LANES // 2, 1, 0)
    source = second * deep + 3 * (side - second * (LANES // 2)) + axis
    spread_out[...] = hit(row == source).astype(HALF)
    for copy in copies[1:]:
        copy.wait()


def widened(block, lanes):
    short = lanes - block.shape[1]
    if short == 0:
        return block
    return jnp.concatenate([block, jnp.zeros((block.shape[0], short), block.dtype)], axis=1)


def put_columns(blocks, order, stride):
    blk = lax.axis_index("blk")
    width = blocks[0].shape[1]
    shape = (width, stride)
    ahead = iota(shape, 1) - iota(shape, 0)
    total = 0.0
    for k, block in zip([0, *order], blocks):
        place = hit(ahead == (blk ^ k) * width).astype(HALF)
        total = total + jnp.dot(block, place, preferred_element_type=FULL)
    return total.astype(HALF)


def columns_kernel(order, *refs):
    *blocks, out_ref = refs
    rows, stride = out_ref.shape
    out_ref[...] = put_columns([rounded(ref[...], rows) for ref in blocks], order, stride)


def first_residual_kernel(
    own_ref, mate_ref, far_ref, pick_ref, shift_ref, adj_ref, rhs_ref, early_ref, middle_ref, jac_hbm, inv_hbm,
    out_ref, late_out, inv_out, image, sems,
):
    late = late_out.shape[0]
    copies = started([(jac_hbm.at[pl.ds(jac_hbm.shape[0] - late, late)], late_out), (inv_hbm, inv_out)], sems)
    residual(
        own_ref, mate_ref, far_ref, pick_ref, shift_ref, adj_ref, rhs_ref, [early_ref, middle_ref, late_out], out_ref,
        image, copies[0].wait,
    )
    copies[1].wait()


def residual_kernel(
    own_ref, mate_ref, far_ref, pick_ref, shift_ref, adj_ref, rhs_ref, early_ref, middle_ref, late_ref, out_ref, image
):
    residual(
        own_ref, mate_ref, far_ref, pick_ref, shift_ref, adj_ref, rhs_ref, [early_ref, middle_ref, late_ref], out_ref,
        image, lambda: None,
    )


def residual(
    own_ref, mate_ref, far_ref, pick_ref, shift_ref, adj_ref, rhs_ref, jac_refs, out_ref, image, wait_late
):
    jac = [ref.at[e] for ref in jac_refs for e in range(ref.shape[0])]
    rows, width = adj_ref.shape
    elements = rows // 3
    stride = own_ref.shape[1]
    slots = jac[0].shape[0]
    stacked = [own_ref[...], mate_ref[...], far_ref[...]]
    short = pick_ref.shape[1] - 3 * own_ref.shape[0]
    if short:
        stacked.append(jnp.zeros((short, stride), HALF))
    stacked = jnp.concatenate(stacked, axis=0)
    picked = jnp.dot(pick_ref[...], stacked, preferred_element_type=FULL).astype(HALF)
    image[...] = jnp.zeros(image.shape, FULL)
    for pair in range(elements // 2):
        starts = [k * elements * PICK + pair * 2 * PICK for k in range(slots)]
        left = jnp.concatenate([picked[start : start + 2 * PICK] for start in starts], axis=1)
        for side in range(2):
            e = 2 * pair + side
            if e == elements - jac_refs[-1].shape[0]:
                wait_late()
            blocks = jnp.concatenate([widened(jac[e][k], stride) for k in range(slots)], axis=1)
            product = lax.dot_general(left, blocks, NT, preferred_element_type=FULL)
            first = side * PICK
            image[pl.ds(e, 3, stride=elements), :width] = product[first : first + 3]
    total = shift_ref[:rows, :width] * adj_ref[...] + image[:rows, :width]
    resid = rhs_ref[...] - total
    resid = jnp.concatenate([resid, jnp.zeros((out_ref.shape[0] - rows, width), FULL)], axis=0)
    out_ref[...] = resid.astype(HALF)


def element_of_row(shape, elements, copies=3):
    row = iota(shape, 0)
    for step in range(1, copies + 1):
        row = row - jnp.where(iota(shape, 0) >= step * elements, elements, 0)
    return row


def updated(resid_refs, inv_ref, adj_ref, update):
    rows, width = adj_ref.shape
    elements = rows // 3
    stride = round_up(inv_ref.shape[2], LANES)
    resid = put_columns([ref[...] for ref in resid_refs], far_first(), stride)
    shape = (elements, PICK, resid.shape[0])
    deep = elements * PICK
    element, row, lane = [iota(shape, dim).reshape(deep, -1) for dim in range(3)]
    pick = hit(jnp.where(row < 3, row * elements + element, -1) == lane).astype(HALF)
    resid = jnp.dot(pick, resid, preferred_element_type=FULL).astype(HALF)
    update[...] = jnp.zeros(update.shape, FULL)
    for pair in range(elements // 2):
        left = resid[pair * 2 * PICK : (pair + 1) * 2 * PICK]
        for side in range(2):
            e = 2 * pair + side
            product = lax.dot_general(left, widened(inv_ref[e], stride), NT, preferred_element_type=FULL)
            first = side * PICK
            update[pl.ds(e, 3, stride=elements), :width] = product[first : first + 3]
    short = jnp.zeros((update.shape[0] - rows, width), FULL)
    return jnp.concatenate([adj_ref[...] + update[:rows, :width], short], axis=0)


def update_kernel(*refs):
    *resid_refs, inv_ref, adj_ref, adj_out, half_out, update = refs
    adj = updated(resid_refs, inv_ref, adj_ref, update)
    adj_out[...] = adj[: adj_out.shape[0]]
    half_out[...] = adj.astype(HALF)


def split(value):
    top = value.astype(HALF)
    return top, (value - top.astype(FULL)).astype(HALF)


def gradient_kernel(*refs):
    blks = lax.axis_size("blk")
    resid_refs = refs[:blks]
    inv_ref, adj_ref, shape_ref, spread_ref, low_ref, target_ref, adj_out = refs[blks : blks + 7]
    piece_outs = refs[blks + 7 : 2 * blks + 7]
    sorted_ref, left_ref, sums_ref, update = refs[2 * blks + 7 :]
    adj = updated(resid_refs, inv_ref, adj_ref, update)
    adj_out[...] = adj[: adj_out.shape[0]]
    half = adj.astype(HALF)
    elements = adj_out.shape[0] // 3
    pairs = elements // 2
    tall = round_up(3 * pairs, 16)
    shape = (tall, half.shape[0])
    row, lane = iota(shape, 0), iota(shape, 1)
    group = jnp.where(row >= pairs, 1, 0) + jnp.where(row >= 2 * pairs, 1, 0)
    source = 2 * (row - group * pairs) + group * elements
    source = jnp.where(row < 3 * pairs, source, -2)
    weighted = []
    coords = shape_ref.shape[2]
    shape = (tall, coords)
    owner = element_of_row(shape, pairs)
    for side in range(2):
        chosen = jnp.dot(hit(lane == source + side).astype(HALF), half, preferred_element_type=FULL).astype(HALF)
        total = jnp.zeros(shape, FULL)
        for pair in range(pairs):
            product = jnp.dot(chosen, shape_ref[2 * pair + side], preferred_element_type=FULL)
            total = jnp.where(owner == pair, product, total)
        weighted.append(widened(total, spread_ref.shape[0] // 2))
    weighted = jnp.concatenate(weighted, axis=1)
    value = 0.0
    for piece in split(weighted):
        value = value + jnp.dot(piece, spread_ref[...], preferred_element_type=FULL)
    top, rest = split(value)
    sorted_ref[:tall] = top.astype(FULL)
    sorted_ref[tall:] = rest.astype(FULL)
    deep = 16
    for pair in range(pairs):
        lanes = slice(pair * LANES, (pair + 1) * LANES)
        mine = iota((deep, LANES), 0) == target_ref[pair : pair + 1, :]
        for part in range(2):
            for j in range(3):
                for c in range(3):
                    at = part * tall + j * pairs + pair
                    values = sorted_ref[at : at + 1, c * LANES : (c + 1) * LANES]
                    start = (part * 9 + j * 3 + c) * deep
                    left_ref[start : start + deep, lanes] = jnp.where(mine, values, 0.0).astype(HALF)
    sums = lax.dot_general(left_ref[...], low_ref[...], NT, preferred_element_type=FULL)
    span = low_ref.shape[0]
    sums = -(sums[: 9 * deep] + sums[9 * deep :])
    tiles = [(tile, tile * LANES, min(span, (tile + 1) * LANES)) for tile in range(sums_ref.shape[0])]
    for tile, start, stop in tiles:
        sums_ref[tile, :, : stop - start] = sums[:, start:stop]
    for k, out_ref in enumerate(piece_outs):
        for part in range(3):
            for tile, start, stop in tiles:
                found = sums_ref[tile, pl.ds(part * blks + k, 9, stride=deep), :][:, : stop - start]
                found = jnp.concatenate([found, jnp.zeros((7, stop - start), FULL)], axis=0)
                out_ref[part * 16 : (part + 1) * 16, start:stop] = found.astype(out_ref.dtype)


def combine_kernel(*refs):
    *piece_refs, own_out, mate_out, far_out = refs
    total = piece_refs[0][...]
    for ref in piece_refs[1:]:
        total = total + ref[...].astype(FULL)
    own_out[...] = total[:16]
    mate_out[...] = total[16:32]
    far_out[...] = total[32:48]


def local(
    adjoint_start,
    right_sides,
    jac_blocks,
    block_inverse,
    neighbours,
    pseudo_shift,
    shape_partials,
    node_ids,
):
    elements, sides, width = adjoint_start.shape
    slots, full = jac_blocks.shape[1], jac_blocks.shape[3]
    enodes = node_ids.shape[1]
    coords = shape_partials.shape[2]
    rows = sides * elements
    tall = round_up(rows, 16)
    stride = round_up(full, LANES)
    blks = lax.axis_size("blk")
    span = NODE_DEV // blks
    stacked = round_up(3 * tall, LANES)
    entries = elements * enodes
    sorted_coords = round_up(coords, LANES)

    adj_hbm = jnp.transpose(adjoint_start, (1, 0, 2)).reshape(rows, width)
    rhs = jnp.transpose(right_sides, (1, 0, 2)).reshape(rows, width)
    half_shape = jax.ShapeDtypeStruct((tall, width), HALF)
    jac_hbm = in_hbm(jac_blocks)

    early, middle = min(EARLY, elements - 2), min(MIDDLE, elements - 1 - EARLY)
    adj_shape = jax.ShapeDtypeStruct((rows, width), FULL)
    pick, shift, early_jac, adj, rhs = call(
        slots_kernel,
        "slots",
        [in_hbm(neighbours.T), in_hbm(pseudo_shift), jac_hbm, in_hbm(adj_hbm), in_hbm(rhs)],
        [HBM] * 5,
        [
            jax.ShapeDtypeStruct((slots * elements * PICK, stacked), HALF),
            jax.ShapeDtypeStruct((tall, LANES), FULL),
            pltpu.VMEM((early, *jac_blocks.shape[1:]), HALF),
            pltpu.VMEM((rows, width), FULL),
            pltpu.VMEM((rows, width), FULL),
        ],
        scratch=[
            pltpu.VMEM((slots - 1, elements), jnp.int32),
            pltpu.SMEM((elements,), FULL),
            pltpu.SemaphoreType.DMA((5,)),
        ],
        moved=3 * MIB,
    )
    middle_shape = pltpu.VMEM((middle, *jac_blocks.shape[1:]), HALF)
    late_shape = pltpu.VMEM((elements - early - middle, *jac_blocks.shape[1:]), HALF)
    inv_shape = pltpu.VMEM(block_inverse.shape, HALF)
    (middle_jac,) = call(
        functools.partial(read_kernel, early),
        "blocks",
        [jac_hbm],
        [HBM],
        [middle_shape],
        [pltpu.SemaphoreType.DMA((1,))],
        moved=6 * MIB,
    )
    low, target, spread, shapes = call(
        nodes_kernel,
        "nodes",
        [in_hbm(node_ids), in_hbm(shape_partials)],
        [HBM, HBM],
        [
            jax.ShapeDtypeStruct((span, entries), HALF),
            jax.ShapeDtypeStruct((entries // LANES, LANES), jnp.int32),
            jax.ShapeDtypeStruct((2 * sorted_coords, 3 * LANES), HALF),
            pltpu.VMEM(shape_partials.shape, HALF),
        ],
        scratch=[pltpu.VMEM(node_ids.shape, jnp.int32), pltpu.SemaphoreType.DMA((2,))],
        moved=3 * MIB,
    )

    for sweep in range(SWEEPS):
        order = far_last() if sweep else far_first()
        blocks = [half] + over_blk(half, order) if sweep else [adj] + over_blk(adj_hbm, order)
        wide = jax.ShapeDtypeStruct((tall, stride), HALF)
        (own,) = call(functools.partial(columns_kernel, order), "columns", blocks, [VMEM] * blks, [wide], moved=1 * MIB)
        far, mate = to_far(own), to_mate(own)
        inputs = [own, mate, far, pick, shift, adj, rhs, early_jac, middle_jac]
        image = pltpu.VMEM((tall, LANES), FULL)
        if sweep == 0:
            resid, late_jac, inv = call(
                first_residual_kernel,
                "first_residual",
                inputs + [jac_hbm, in_hbm(block_inverse)],
                [VMEM] * 9 + [HBM] * 2,
                [half_shape, late_shape, inv_shape],
                scratch=[image, pltpu.SemaphoreType.DMA((2,))],
                moved=16 * MIB,
            )
        else:
            (resid,) = call(
                residual_kernel, "residual", inputs + [late_jac], [VMEM] * 10, [half_shape], [image], moved=16 * MIB
            )
        resids = [resid] + over_blk(resid, far_first())
        if sweep < SWEEPS - 1:
            adj, half = call(
                update_kernel,
                "update",
                resids + [inv, adj],
                [VMEM] * (blks + 2),
                [adj_shape, half_shape],
                scratch=[pltpu.VMEM((tall, LANES), FULL)],
                moved=8 * MIB,
            )
    pieces = [jax.ShapeDtypeStruct((3 * 16, span), HALF if k else FULL) for k in range(blks)]
    adj, *pieces = call(
        gradient_kernel,
        "gradient",
        resids + [inv, adj, shapes, spread, low, target],
        [VMEM] * (blks + 6),
        [adj_shape] + pieces,
        scratch=[
            pltpu.VMEM((2 * round_up(rows // 2, 16), 3 * LANES), FULL),
            pltpu.VMEM((2 * 9 * 16, entries), HALF),
            pltpu.VMEM((-(-span // LANES), 9 * 16, LANES), FULL),
            pltpu.VMEM((tall, LANES), FULL),
        ],
    )
    count = lax.axis_size("blk")
    received = [
        lax.ppermute(pieces[k], "blk", [(i, i ^ k) for i in range(count)]) for k in far_first()
    ]
    third = jax.ShapeDtypeStruct((16, span), FULL)
    own, mate, far = call(combine_kernel, "combine", [pieces[0]] + received, [VMEM] * blks, [third] * 3)
    gradient = (own + to_mate(mate) + to_far(far))[:9]
    adjoint = jnp.transpose(adj.reshape(sides, elements, width), (1, 0, 2))
    return (adjoint, gradient)


def solution(mesh):
    in_specs = (
        P("dom", None, "blk"),
        P("dom", None, "blk"),
        P("dom", None, "blk", None),
        P("dom", "blk", None),
        P("dom", None),
        P("dom"),
        P("dom", "blk", None),
        P("dom", None),
    )
    out_specs = (P("dom", None, "blk"), P(None, ("dom", "blk")))
    return jax.shard_map(local, mesh=mesh, in_specs=in_specs, out_specs=out_specs, check_vma=False)
```

time: 80.7 us -> 64.1 us (0.79)
  local copies, waits for them, and re-layouts: 9.39 us -> 0 us
  Pallas kernels: 20.2 us -> 15.9 us
  waiting for transfers between devices: 21.2 us -> 18.3 us
    unnamed x16 -> x0, local copies, waits for them, and re-layouts: 8.62 us -> none
    pallas_call x9 -> x10, Pallas kernels: 20.2 us -> 15.9 us  [call(): pl.pallas_call(kernel, in_specs=specs, out_specs=[VMEM] * len(outs), out_...]
    ppermute x3, starting transfers between devices: 1.79 us -> 4.55 us  [to_far(): lax.ppermute(block, 'dom', [(i, ((i + 1 ^ 1) - 1) % count) for i in range...]
    ppermute x3, starting transfers between devices: 2.81 us -> 0.21 us  [to_mate(): lax.ppermute(block, 'dom', [(i, i ^ 1) for i in range(lax.axis_size('dom'...]
    ppermute x12, waiting for transfers between devices: 10.9 us -> 8.41 us  [over_blk(): lax.ppermute(block, 'blk', [(i, i ^ k) for i in range(count)])]
    ppermute x3, waiting for transfers between devices: 4.43 us -> 2.97 us  [local(): lax.ppermute(pieces[k], 'blk', [(i, i ^ k) for i in range(count)])]
  transfers between devices with their start and end apart: 21 -> 21, of which waited for: 15 -> 15; matrix products, arithmetic and copies ran while one was open for 1% -> 0% of each run, Pallas kernels for 13% -> 8%
where the time goes in v2:
time: 64.1 us; the launch traced here: 63.9 us
  starting transfers between devices  28.3 us (44%)
  waiting for transfers between devices  18.3 us (29%)
  Pallas kernels  15.9 us (25%)
  between operations  0.76 us (1%)
    ppermute x12, starting transfers between devices, over_blk(): lax.ppermute(block, 'blk', [(i, i ^ k) for i in range(count)])  19.1 us
    pallas_call x10, Pallas kernels, call(): pl.pallas_call(kernel, in_specs=specs, out_specs=[VMEM] * len(outs), out_...  15.9 us
    ppermute x12, waiting for transfers between devices, over_blk(): lax.ppermute(block, 'blk', [(i, i ^ k) for i in range(count)])  8.41 us
    ppermute x3, waiting for transfers between devices, to_far(): lax.ppermute(block, 'dom', [(i, ((i + 1 ^ 1) - 1) % count) for i in range...  6.31 us
    ppermute x3, starting transfers between devices, to_far(): lax.ppermute(block, 'dom', [(i, ((i + 1 ^ 1) - 1) % count) for i in range...  4.55 us
    ppermute x3, starting transfers between devices, local(): lax.ppermute(pieces[k], 'blk', [(i, i ^ k) for i in range(count)])  4.39 us
    ppermute x3, waiting for transfers between devices, local(): lax.ppermute(pieces[k], 'blk', [(i, i ^ k) for i in range(count)])  2.97 us
  transfers between devices with their start and end apart: 21, of which 15 were waited for; matrix products, arithmetic and copies ran while one was open for 0% of the time, Pallas kernels for 8%

profile of v2, /device:TPU:0, one launch (start us, length us, event | category | flops | bytes accessed | tf_op | source)
XLA Modules:
  0.0 63.9 jit_solution(707153384517274859)
XLA Ops:
  0.6 5.1 %collective-permute-start = (f32[72,80]{1,0:T(8,128)}, f32[72,80]{1,0:T(8,128)S(1)}, u32[]{:S(2)}, u32[]{:S(2)}) collective-permute-start(f32[72,80]{1,0:T(8,128)} %bitcast.11), channel_id=1, source_target_pairs={{0,3},{1,2},{2,1},{3,0},{4,7},{5,6},{6,5},{7,4},{8,11},{9,10},{10,... | collective-permute-start | bytes 69128 | tf_op jit(solution)/shard_map/ppermute | solution.py:63
  5.7 0.6 %collective-permute-start.2 = (f32[72,80]{1,0:T(8,128)}, f32[72,80]{1,0:T(8,128)S(1)}, u32[]{:S(2)}, u32[]{:S(2)}) collective-permute-start(f32[72,80]{1,0:T(8,128)} %bitcast.13), channel_id=1, source_target_pairs={{0,1},{1,0},{2,3},{3,2},{4,5},{5,4},{6,7},{7,6},{8,9},{9,8},{10,11... | collective-permute-start | bytes 69128 | tf_op jit(solution)/shard_map/ppermute | solution.py:63
  6.4 1.6 %slots.1 = (bf16[1344,256]{1,0:T(8,128)(2,1)S(1)}, f32[80,128]{1,0:T(8,128)S(1)}, bf16[4,7,80,320]{3,2,1,0:T(8,128)(2,1)S(1)}, f32[72,80]{1,0:T(8,128)S(1)}, f32[72,80]{1,0:T(8,128)S(1)}) custom-call(s32[6,24]{1,0:T(8,128)} %bitcast.15, f32[24]{0:T(128)} %shift_hbm.1, bf16[24,7,80,320]{3,2,1,0:T(8,128)(2,1)} %jac_hbm.3, f32[72,80]{1,0:T(8,128)} %bitcast.14, ...), custom_call_target="tpu_custom_call" | custom-call | bytes 3145728 | tf_op jit(solution)/shard_map/slots/pallas_call | solution.py:40
  8.0 2.8 %collective-permute-done.1.refs_2_ = f32[72,80]{1,0:T(8,128)S(1)} collective-permute-done((f32[72,80]{1,0:T(8,128)}, f32[72,80]{1,0:T(8,128)S(1)}, u32[]{:S(2)}, u32[]{:S(2)}) %collective-permute-start.1) | collective-permute-done | bytes 23072 | tf_op jit(solution)/shard_map/ppermute | solution.py:63
  11.1 2.5 %collective-permute-start.4 = (bf16[80,384]{1,0:T(8,128)(2,1)S(1)}, bf16[80,384]{1,0:T(8,128)(2,1)S(1)}, u32[]{:S(2)}, u32[]{:S(2)}) collective-permute-start(bf16[80,384]{1,0:T(8,128)(2,1)S(1)} %columns.2.own_ref), channel_id=1, source_target_pairs={{0,28},{4,8},{8,4},{12,16},{16,12},{20,24},{24,20},{28,0},{1,29},{... | collective-permute-start | bytes 184328 | tf_op jit(solution)/shard_map/ppermute | solution.py:72
  13.7 2.5 %blocks.1.middle_ref = bf16[12,7,80,320]{3,2,1,0:T(8,128)(2,1)S(1)} custom-call(bf16[24,7,80,320]{3,2,1,0:T(8,128)(2,1)} %jac_hbm.3), custom_call_target="tpu_custom_call" | custom-call | bytes 6291456 | tf_op jit(solution)/shard_map/blocks/pallas_call | solution.py:40
  16.2 3.5 %first_residual.1 = (bf16[80,80]{1,0:T(8,128)(2,1)S(1)}, bf16[8,7,80,320]{3,2,1,0:T(8,128)(2,1)S(1)}, bf16[24,80,320]{2,1,0:T(8,128)(2,1)S(1)}) custom-call(bf16[80,384]{1,0:T(8,128)(2,1)S(1)} %columns.2.own_ref, bf16[80,384]{1,0:T(8,128)(2,1)S(1)} %collective-permute-done.3.mate_ref, bf16[80,384]{1,0:T(8,128)(2,1)S(1)} %collective-permute-done.4.far_ref, ...), custom_call_target="tpu_custom_call" | custom-call | bytes 16777216 | tf_op jit(solution)/shard_map/first_residual/pallas_call | solution.py:40
  19.6 1.6 %collective-permute-start.5 = (bf16[80,80]{1,0:T(8,128)(2,1)S(1)}, bf16[80,80]{1,0:T(8,128)(2,1)S(1)}, u32[]{:S(2)}, u32[]{:S(2)}) collective-permute-start(bf16[80,80]{1,0:T(8,128)(2,1)S(1)} %get-tuple-element.29.refs_0_), channel_id=1, source_target_pairs={{0,3},{1,2},{2,1},{3,0},{4,7},{5,6},{6,5},{7,4},{8,11},{9,10},{10,... | collective-permute-start | bytes 38408 | tf_op jit(solution)/shard_map/ppermute | solution.py:63
  21.2 0.6 collective-permute-start.6
  21.8 2.3 %collective-permute-start.7 = (bf16[80,80]{1,0:T(8,128)(2,1)S(1)}, bf16[80,80]{1,0:T(8,128)(2,1)S(1)}, u32[]{:S(2)}, u32[]{:S(2)}) collective-permute-start(bf16[80,80]{1,0:T(8,128)(2,1)S(1)} %get-tuple-element.29.refs_0_), channel_id=1, source_target_pairs={{0,1},{1,0},{2,3},{3,2},{4,5},{5,4},{6,7},{7,6},{8,9},{9,8},{10,11... | collective-permute-start | bytes 38408 | tf_op jit(solution)/shard_map/ppermute | solution.py:63
  24.1 1.2 %collective-permute-done.5.refs_1_ = bf16[80,80]{1,0:T(8,128)(2,1)S(1)} collective-permute-done((bf16[80,80]{1,0:T(8,128)(2,1)S(1)}, bf16[80,80]{1,0:T(8,128)(2,1)S(1)}, u32[]{:S(2)}, u32[]{:S(2)}) %collective-permute-start.5) | collective-permute-done | bytes 12832 | tf_op jit(solution)/shard_map/ppermute | solution.py:63
  25.3 0.7 %collective-permute-done.6.refs_2_ = bf16[80,80]{1,0:T(8,128)(2,1)S(1)} collective-permute-done((bf16[80,80]{1,0:T(8,128)(2,1)S(1)}, bf16[80,80]{1,0:T(8,128)(2,1)S(1)}, u32[]{:S(2)}, u32[]{:S(2)}) %collective-permute-start.6) | collective-permute-done | bytes 12832 | tf_op jit(solution)/shard_map/ppermute | solution.py:63
  26.1 1.0 %update.1 = (f32[72,80]{1,0:T(8,128)S(1)}, bf16[80,80]{1,0:T(8,128)(2,1)S(1)}) custom-call(bf16[80,80]{1,0:T(8,128)(2,1)S(1)} %get-tuple-element.29.refs_0_, bf16[80,80]{1,0:T(8,128)(2,1)S(1)} %collective-permute-done.5.refs_1_, bf16[80,80]{1,0:T(8,128)(2,1)S(1)} %collective-permute-done.6.refs_2_, bf16[80,80]{1,0:T(8,128)(2,1)S(1)} %collective-permute-done.7.refs_3_, ...), custom_call_target="tpu_custom_call" | custom-call | bytes 8388608 | tf_op jit(solution)/shard_map/update/pallas_call | solution.py:40
  27.0 2.4 %collective-permute-start.10 = (bf16[80,80]{1,0:T(8,128)(2,1)S(1)}, bf16[80,80]{1,0:T(8,128)(2,1)S(1)}, u32[]{:S(2)}, u32[]{:S(2)}) collective-permute-start(bf16[80,80]{1,0:T(8,128)(2,1)S(1)} %get-tuple-element.31.refs_0_), channel_id=1, source_target_pairs={{0,3},{1,2},{2,1},{3,0},{4,7},{5,6},{6,5},{7,4},{8,11},{9,10},{10,... | collective-permute-start | bytes 38408 | tf_op jit(solution)/shard_map/ppermute | solution.py:63
  29.4 0.9 %collective-permute-start.8 = (bf16[80,80]{1,0:T(8,128)(2,1)S(1)}, bf16[80,80]{1,0:T(8,128)(2,1)S(1)}, u32[]{:S(2)}, u32[]{:S(2)}) collective-permute-start(bf16[80,80]{1,0:T(8,128)(2,1)S(1)} %get-tuple-element.31.refs_0_), channel_id=1, source_target_pairs={{0,2},{1,3},{2,0},{3,1},{4,6},{5,7},{6,4},{7,5},{8,10},{9,11},{10,... | collective-permute-start | bytes 38408 | tf_op jit(solution)/shard_map/ppermute | solution.py:63
  30.3 1.1 %collective-permute-start.9 = (bf16[80,80]{1,0:T(8,128)(2,1)S(1)}, bf16[80,80]{1,0:T(8,128)(2,1)S(1)}, u32[]{:S(2)}, u32[]{:S(2)}) collective-permute-start(bf16[80,80]{1,0:T(8,128)(2,1)S(1)} %get-tuple-element.31.refs_0_), channel_id=1, source_target_pairs={{0,1},{1,0},{2,3},{3,2},{4,5},{5,4},{6,7},{7,6},{8,9},{9,8},{10,11... | collective-permute-start | bytes 38408 | tf_op jit(solution)/shard_map/ppermute | solution.py:63
  31.5 1.3 %collective-permute-done.10.refs_3_ = bf16[80,80]{1,0:T(8,128)(2,1)S(1)} collective-permute-done((bf16[80,80]{1,0:T(8,128)(2,1)S(1)}, bf16[80,80]{1,0:T(8,128)(2,1)S(1)}, u32[]{:S(2)}, u32[]{:S(2)}) %collective-permute-start.10) | collective-permute-done | bytes 12832 | tf_op jit(solution)/shard_map/ppermute | solution.py:63
  32.7 1.4 %collective-permute-done.8.refs_1_ = bf16[80,80]{1,0:T(8,128)(2,1)S(1)} collective-permute-done((bf16[80,80]{1,0:T(8,128)(2,1)S(1)}, bf16[80,80]{1,0:T(8,128)(2,1)S(1)}, u32[]{:S(2)}, u32[]{:S(2)}) %collective-permute-start.8) | collective-permute-done | bytes 12832 | tf_op jit(solution)/shard_map/ppermute | solution.py:63
  34.7 1.4 %collective-permute-start.12 = (bf16[80,384]{1,0:T(8,128)(2,1)S(1)}, bf16[80,384]{1,0:T(8,128)(2,1)S(1)}, u32[]{:S(2)}, u32[]{:S(2)}) collective-permute-start(bf16[80,384]{1,0:T(8,128)(2,1)S(1)} %columns.3.own_ref), channel_id=1, source_target_pairs={{0,28},{4,8},{8,4},{12,16},{16,12},{20,24},{24,20},{28,0},{1,29},{... | collective-permute-start | bytes 184328 | tf_op jit(solution)/shard_map/ppermute | solution.py:72
  36.1 3.4 %collective-permute-done.12.far_ref = bf16[80,384]{1,0:T(8,128)(2,1)S(1)} collective-permute-done((bf16[80,384]{1,0:T(8,128)(2,1)S(1)}, bf16[80,384]{1,0:T(8,128)(2,1)S(1)}, u32[]{:S(2)}, u32[]{:S(2)}) %collective-permute-start.12) | collective-permute-done | bytes 61472 | tf_op jit(solution)/shard_map/ppermute | solution.py:72
  39.5 3.2 %residual.1.refs_0_ = bf16[80,80]{1,0:T(8,128)(2,1)S(1)} custom-call(bf16[80,384]{1,0:T(8,128)(2,1)S(1)} %columns.3.own_ref, bf16[80,384]{1,0:T(8,128)(2,1)S(1)} %collective-permute-done.11.mate_ref, bf16[80,384]{1,0:T(8,128)(2,1)S(1)} %collective-permute-done.12.far_ref, bf16[1344,256]{1,0:T(8,128)(2,1)S(1)} %get-tuple-element.25.pick_ref, ...), custom_call_target="tpu_custom_call" | custom-call | bytes 16777216 | tf_op jit(solution)/shard_map/residual/pallas_call | solution.py:40
  42.7 1.6 %collective-permute-start.13 = (bf16[80,80]{1,0:T(8,128)(2,1)S(1)}, bf16[80,80]{1,0:T(8,128)(2,1)S(1)}, u32[]{:S(2)}, u32[]{:S(2)}) collective-permute-start(bf16[80,80]{1,0:T(8,128)(2,1)S(1)} %residual.1.refs_0_), channel_id=1, source_target_pairs={{0,3},{1,2},{2,1},{3,0},{4,7},{5,6},{6,5},{7,4},{8,11},{9,10},{10,... | collective-permute-start | bytes 38408 | tf_op jit(solution)/shard_map/ppermute | solution.py:63
  44.2 0.9 %collective-permute-start.14 = (bf16[80,80]{1,0:T(8,128)(2,1)S(1)}, bf16[80,80]{1,0:T(8,128)(2,1)S(1)}, u32[]{:S(2)}, u32[]{:S(2)}) collective-permute-start(bf16[80,80]{1,0:T(8,128)(2,1)S(1)} %residual.1.refs_0_), channel_id=1, source_target_pairs={{0,2},{1,3},{2,0},{3,1},{4,6},{5,7},{6,4},{7,5},{8,10},{9,11},{10,... | collective-permute-start | bytes 38408 | tf_op jit(solution)/shard_map/ppermute | solution.py:63
  45.1 2.0 %collective-permute-start.15 = (bf16[80,80]{1,0:T(8,128)(2,1)S(1)}, bf16[80,80]{1,0:T(8,128)(2,1)S(1)}, u32[]{:S(2)}, u32[]{:S(2)}) collective-permute-start(bf16[80,80]{1,0:T(8,128)(2,1)S(1)} %residual.1.refs_0_), channel_id=1, source_target_pairs={{0,1},{1,0},{2,3},{3,2},{4,5},{5,4},{6,7},{7,6},{8,9},{9,8},{10,11... | collective-permute-start | bytes 38408 | tf_op jit(solution)/shard_map/ppermute | solution.py:63
  47.2 1.2 %nodes.1 = (bf16[192,1536]{1,0:T(8,128)(2,1)S(1)}, s32[12,128]{1,0:T(8,128)S(1)}, bf16[512,384]{1,0:T(8,128)(2,1)S(1)}, bf16[24,80,192]{2,1,0:T(8,128)(2,1)S(1)}) custom-call(s32[24,64]{1,0:T(8,128)} %ids_hbm.1, bf16[24,80,192]{2,1,0:T(8,128)(2,1)} %shape_hbm.1), custom_call_target="tpu_custom_call" | custom-call | bytes 3145728 | tf_op jit(solution)/shard_map/nodes/pallas_call | solution.py:40
  49.1 2.6 %gradient.1 = (f32[72,80]{1,0:T(8,128)}, f32[48,192]{1,0:T(8,128)S(1)}, bf16[48,192]{1,0:T(8,128)(2,1)S(1)}, bf16[48,192]{1,0:T(8,128)(2,1)S(1)}, bf16[48,192]{1,0:T(8,128)(2,1)S(1)}) custom-call(bf16[80,80]{1,0:T(8,128)(2,1)S(1)} %residual.1.refs_0_, bf16[80,80]{1,0:T(8,128)(2,1)S(1)} %collective-permute-done.13.refs_1_, ...), custom_call_target="tpu_custom_call" | custom-call | tf_op jit(solution)/shard_map/gradient/pallas_call | solution.py:40
  51.7 2.4 %collective-permute-start.16 = (bf16[48,192]{1,0:T(8,128)(2,1)S(1)}, bf16[48,192]{1,0:T(8,128)(2,1)S(1)}, u32[]{:S(2)}, u32[]{:S(2)}) collective-permute-start(bf16[48,192]{1,0:T(8,128)(2,1)S(1)} %get-tuple-element.40), channel_id=1, source_target_pairs={{0,3},{1,2},{2,1},{3,0},{4,7},{5,6},{6,5},{7,4},{8,11},{9,10},{10,... | collective-permute-start | bytes 55304 | tf_op jit(solution)/shard_map/ppermute | solution.py:481
  54.1 0.9 %collective-permute-start.17 = (bf16[48,192]{1,0:T(8,128)(2,1)S(1)}, bf16[48,192]{1,0:T(8,128)(2,1)S(1)}, u32[]{:S(2)}, u32[]{:S(2)}) collective-permute-start(bf16[48,192]{1,0:T(8,128)(2,1)S(1)} %get-tuple-element.41), channel_id=1, source_target_pairs={{0,2},{1,3},{2,0},{3,1},{4,6},{5,7},{6,4},{7,5},{8,10},{9,11},{10,... | collective-permute-start | bytes 55304 | tf_op jit(solution)/shard_map/ppermute | solution.py:481
  55.0 1.1 %collective-permute-start.18 = (bf16[48,192]{1,0:T(8,128)(2,1)S(1)}, bf16[48,192]{1,0:T(8,128)(2,1)S(1)}, u32[]{:S(2)}, u32[]{:S(2)}) collective-permute-start(bf16[48,192]{1,0:T(8,128)(2,1)S(1)} %get-tuple-element.42), channel_id=1, source_target_pairs={{0,1},{1,0},{2,3},{3,2},{4,5},{5,4},{6,7},{7,6},{8,9},{9,8},{10,11... | collective-permute-start | bytes 55304 | tf_op jit(solution)/shard_map/ppermute | solution.py:481
  56.1 1.5 %collective-permute-done.16.refs_1_ = bf16[48,192]{1,0:T(8,128)(2,1)S(1)} collective-permute-done((bf16[48,192]{1,0:T(8,128)(2,1)S(1)}, bf16[48,192]{1,0:T(8,128)(2,1)S(1)}, u32[]{:S(2)}, u32[]{:S(2)}) %collective-permute-start.16) | collective-permute-done | bytes 18464 | tf_op jit(solution)/shard_map/ppermute | solution.py:481
  57.5 1.3 %collective-permute-done.17.refs_2_ = bf16[48,192]{1,0:T(8,128)(2,1)S(1)} collective-permute-done((bf16[48,192]{1,0:T(8,128)(2,1)S(1)}, bf16[48,192]{1,0:T(8,128)(2,1)S(1)}, u32[]{:S(2)}, u32[]{:S(2)}) %collective-permute-start.17) | collective-permute-done | bytes 18464 | tf_op jit(solution)/shard_map/ppermute | solution.py:481
  60.3 3.0 %collective-permute-done.20 = f32[16,192]{1,0:T(8,128)S(1)} collective-permute-done((f32[16,192]{1,0:T(8,128)S(1)}, f32[16,192]{1,0:T(8,128)S(1)}, u32[]{:S(2)}, u32[]{:S(2)}) %collective-permute-start.20) | collective-permute-done | bytes 12320 | tf_op jit(solution)/shard_map/ppermute | solution.py:72
  (21 shorter events, 3.7 us)
Async XLA Ops:
  0.6 7.3 %collective-permute-start = (f32[72,80]{1,0:T(8,128)}, f32[72,80]{1,0:T(8,128)S(1)}, u32[]{:S(2)}, u32[]{:S(2)}) collective-permute-start(f32[72,80]{1,0:T(8,128)} %bitcast.11), channel_id=1, source_target_pairs={{0,3},{1,2},{2,1},{3,0},{4,7},{5,6},{6,5},{7,4},{8,11},{9,10},{10,... | collective-permute-start | bytes 69128 | tf_op jit(solution)/shard_map/ppermute | solution.py:63
  5.7 5.1 %collective-permute-start.1 = (f32[72,80]{1,0:T(8,128)}, f32[72,80]{1,0:T(8,128)S(1)}, u32[]{:S(2)}, u32[]{:S(2)}) collective-permute-start(f32[72,80]{1,0:T(8,128)} %bitcast.12), channel_id=1, source_target_pairs={{0,2},{1,3},{2,0},{3,1},{4,6},{5,7},{6,4},{7,5},{8,10},{9,11},{10,... | collective-permute-start | bytes 69128 | tf_op jit(solution)/shard_map/ppermute | solution.py:63
  5.7 5.1 %collective-permute-start.2 = (f32[72,80]{1,0:T(8,128)}, f32[72,80]{1,0:T(8,128)S(1)}, u32[]{:S(2)}, u32[]{:S(2)}) collective-permute-start(f32[72,80]{1,0:T(8,128)} %bitcast.13), channel_id=1, source_target_pairs={{0,1},{1,0},{2,3},{3,2},{4,5},{5,4},{6,7},{7,6},{8,9},{9,8},{10,11... | collective-permute-start | bytes 69128 | tf_op jit(solution)/shard_map/ppermute | solution.py:63
  11.1 5.1 %collective-permute-start.3 = (bf16[80,384]{1,0:T(8,128)(2,1)S(1)}, bf16[80,384]{1,0:T(8,128)(2,1)S(1)}, u32[]{:S(2)}, u32[]{:S(2)}) collective-permute-start(bf16[80,384]{1,0:T(8,128)(2,1)S(1)} %columns.2.own_ref), channel_id=1, source_target_pairs={{0,4},{4,0},{8,12},{12,8},{16,20},{20,16},{24,28},{28,24},{1,5},{5... | collective-permute-start | bytes 184328 | tf_op jit(solution)/shard_map/ppermute | solution.py:67
  11.1 5.0 %collective-permute-start.4 = (bf16[80,384]{1,0:T(8,128)(2,1)S(1)}, bf16[80,384]{1,0:T(8,128)(2,1)S(1)}, u32[]{:S(2)}, u32[]{:S(2)}) collective-permute-start(bf16[80,384]{1,0:T(8,128)(2,1)S(1)} %columns.2.own_ref), channel_id=1, source_target_pairs={{0,28},{4,8},{8,4},{12,16},{16,12},{20,24},{24,20},{28,0},{1,29},{... | collective-permute-start | bytes 184328 | tf_op jit(solution)/shard_map/ppermute | solution.py:72
  19.6 5.7 %collective-permute-start.5 = (bf16[80,80]{1,0:T(8,128)(2,1)S(1)}, bf16[80,80]{1,0:T(8,128)(2,1)S(1)}, u32[]{:S(2)}, u32[]{:S(2)}) collective-permute-start(bf16[80,80]{1,0:T(8,128)(2,1)S(1)} %get-tuple-element.29.refs_0_), channel_id=1, source_target_pairs={{0,3},{1,2},{2,1},{3,0},{4,7},{5,6},{6,5},{7,4},{8,11},{9,10},{10,... | collective-permute-start | bytes 38408 | tf_op jit(solution)/shard_map/ppermute | solution.py:63
  21.2 4.8 %collective-permute-start.6 = (bf16[80,80]{1,0:T(8,128)(2,1)S(1)}, bf16[80,80]{1,0:T(8,128)(2,1)S(1)}, u32[]{:S(2)}, u32[]{:S(2)}) collective-permute-start(bf16[80,80]{1,0:T(8,128)(2,1)S(1)} %get-tuple-element.29.refs_0_), channel_id=1, source_target_pairs={{0,2},{1,3},{2,0},{3,1},{4,6},{5,7},{6,4},{7,5},{8,10},{9,11},{10,... | collective-permute-start | bytes 38408 | tf_op jit(solution)/shard_map/ppermute | solution.py:63
  21.8 4.3 %collective-permute-start.7 = (bf16[80,80]{1,0:T(8,128)(2,1)S(1)}, bf16[80,80]{1,0:T(8,128)(2,1)S(1)}, u32[]{:S(2)}, u32[]{:S(2)}) collective-permute-start(bf16[80,80]{1,0:T(8,128)(2,1)S(1)} %get-tuple-element.29.refs_0_), channel_id=1, source_target_pairs={{0,1},{1,0},{2,3},{3,2},{4,5},{5,4},{6,7},{7,6},{8,9},{9,8},{10,11... | collective-permute-start | bytes 38408 | tf_op jit(solution)/shard_map/ppermute | solution.py:63
  27.0 5.7 %collective-permute-start.10 = (bf16[80,80]{1,0:T(8,128)(2,1)S(1)}, bf16[80,80]{1,0:T(8,128)(2,1)S(1)}, u32[]{:S(2)}, u32[]{:S(2)}) collective-permute-start(bf16[80,80]{1,0:T(8,128)(2,1)S(1)} %get-tuple-element.31.refs_0_), channel_id=1, source_target_pairs={{0,3},{1,2},{2,1},{3,0},{4,7},{5,6},{6,5},{7,4},{8,11},{9,10},{10,... | collective-permute-start | bytes 38408 | tf_op jit(solution)/shard_map/ppermute | solution.py:63
  29.4 4.7 %collective-permute-start.8 = (bf16[80,80]{1,0:T(8,128)(2,1)S(1)}, bf16[80,80]{1,0:T(8,128)(2,1)S(1)}, u32[]{:S(2)}, u32[]{:S(2)}) collective-permute-start(bf16[80,80]{1,0:T(8,128)(2,1)S(1)} %get-tuple-element.31.refs_0_), channel_id=1, source_target_pairs={{0,2},{1,3},{2,0},{3,1},{4,6},{5,7},{6,4},{7,5},{8,10},{9,11},{10,... | collective-permute-start | bytes 38408 | tf_op jit(solution)/shard_map/ppermute | solution.py:63
  30.3 4.0 %collective-permute-start.9 = (bf16[80,80]{1,0:T(8,128)(2,1)S(1)}, bf16[80,80]{1,0:T(8,128)(2,1)S(1)}, u32[]{:S(2)}, u32[]{:S(2)}) collective-permute-start(bf16[80,80]{1,0:T(8,128)(2,1)S(1)} %get-tuple-element.31.refs_0_), channel_id=1, source_target_pairs={{0,1},{1,0},{2,3},{3,2},{4,5},{5,4},{6,7},{7,6},{8,9},{9,8},{10,11... | collective-permute-start | bytes 38408 | tf_op jit(solution)/shard_map/ppermute | solution.py:63
  34.6 1.5 %collective-permute-start.11 = (bf16[80,384]{1,0:T(8,128)(2,1)S(1)}, bf16[80,384]{1,0:T(8,128)(2,1)S(1)}, u32[]{:S(2)}, u32[]{:S(2)}) collective-permute-start(bf16[80,384]{1,0:T(8,128)(2,1)S(1)} %columns.3.own_ref), channel_id=1, source_target_pairs={{0,4},{4,0},{8,12},{12,8},{16,20},{20,16},{24,28},{28,24},{1,5},{5... | collective-permute-start | bytes 184328 | tf_op jit(solution)/shard_map/ppermute | solution.py:67
  34.7 4.8 %collective-permute-start.12 = (bf16[80,384]{1,0:T(8,128)(2,1)S(1)}, bf16[80,384]{1,0:T(8,128)(2,1)S(1)}, u32[]{:S(2)}, u32[]{:S(2)}) collective-permute-start(bf16[80,384]{1,0:T(8,128)(2,1)S(1)} %columns.3.own_ref), channel_id=1, source_target_pairs={{0,28},{4,8},{8,4},{12,16},{16,12},{20,24},{24,20},{28,0},{1,29},{... | collective-permute-start | bytes 184328 | tf_op jit(solution)/shard_map/ppermute | solution.py:72
  42.7 5.8 %collective-permute-start.13 = (bf16[80,80]{1,0:T(8,128)(2,1)S(1)}, bf16[80,80]{1,0:T(8,128)(2,1)S(1)}, u32[]{:S(2)}, u32[]{:S(2)}) collective-permute-start(bf16[80,80]{1,0:T(8,128)(2,1)S(1)} %residual.1.refs_0_), channel_id=1, source_target_pairs={{0,3},{1,2},{2,1},{3,0},{4,7},{5,6},{6,5},{7,4},{8,11},{9,10},{10,... | collective-permute-start | bytes 38408 | tf_op jit(solution)/shard_map/ppermute | solution.py:63
  44.2 4.7 %collective-permute-start.14 = (bf16[80,80]{1,0:T(8,128)(2,1)S(1)}, bf16[80,80]{1,0:T(8,128)(2,1)S(1)}, u32[]{:S(2)}, u32[]{:S(2)}) collective-permute-start(bf16[80,80]{1,0:T(8,128)(2,1)S(1)} %residual.1.refs_0_), channel_id=1, source_target_pairs={{0,2},{1,3},{2,0},{3,1},{4,6},{5,7},{6,4},{7,5},{8,10},{9,11},{10,... | collective-permute-start | bytes 38408 | tf_op jit(solution)/shard_map/ppermute | solution.py:63
  45.1 4.0 %collective-permute-start.15 = (bf16[80,80]{1,0:T(8,128)(2,1)S(1)}, bf16[80,80]{1,0:T(8,128)(2,1)S(1)}, u32[]{:S(2)}, u32[]{:S(2)}) collective-permute-start(bf16[80,80]{1,0:T(8,128)(2,1)S(1)} %residual.1.refs_0_), channel_id=1, source_target_pairs={{0,1},{1,0},{2,3},{3,2},{4,5},{5,4},{6,7},{7,6},{8,9},{9,8},{10,11... | collective-permute-start | bytes 38408 | tf_op jit(solution)/shard_map/ppermute | solution.py:63
  51.7 5.9 %collective-permute-start.16 = (bf16[48,192]{1,0:T(8,128)(2,1)S(1)}, bf16[48,192]{1,0:T(8,128)(2,1)S(1)}, u32[]{:S(2)}, u32[]{:S(2)}) collective-permute-start(bf16[48,192]{1,0:T(8,128)(2,1)S(1)} %get-tuple-element.40), channel_id=1, source_target_pairs={{0,3},{1,2},{2,1},{3,0},{4,7},{5,6},{6,5},{7,4},{8,11},{9,10},{10,... | collective-permute-start | bytes 55304 | tf_op jit(solution)/shard_map/ppermute | solution.py:481
  54.1 4.7 %collective-permute-start.17 = (bf16[48,192]{1,0:T(8,128)(2,1)S(1)}, bf16[48,192]{1,0:T(8,128)(2,1)S(1)}, u32[]{:S(2)}, u32[]{:S(2)}) collective-permute-start(bf16[48,192]{1,0:T(8,128)(2,1)S(1)} %get-tuple-element.41), channel_id=1, source_target_pairs={{0,2},{1,3},{2,0},{3,1},{4,6},{5,7},{6,4},{7,5},{8,10},{9,11},{10,... | collective-permute-start | bytes 55304 | tf_op jit(solution)/shard_map/ppermute | solution.py:481
  55.0 4.1 %collective-permute-start.18 = (bf16[48,192]{1,0:T(8,128)(2,1)S(1)}, bf16[48,192]{1,0:T(8,128)(2,1)S(1)}, u32[]{:S(2)}, u32[]{:S(2)}) collective-permute-start(bf16[48,192]{1,0:T(8,128)(2,1)S(1)} %get-tuple-element.42), channel_id=1, source_target_pairs={{0,1},{1,0},{2,3},{3,2},{4,5},{5,4},{6,7},{7,6},{8,9},{9,8},{10,11... | collective-permute-start | bytes 55304 | tf_op jit(solution)/shard_map/ppermute | solution.py:481
  59.1 1.2 %collective-permute-start.19 = (f32[16,192]{1,0:T(8,128)S(1)}, f32[16,192]{1,0:T(8,128)S(1)}, u32[]{:S(2)}, u32[]{:S(2)}) collective-permute-start(f32[16,192]{1,0:T(8,128)S(1)} %get-tuple-element.44), channel_id=1, source_target_pairs={{0,4},{4,0},{8,12},{12,8},{16,20},{20,16},{24,28},{28,24},{1,5},{5... | collective-permute-start | bytes 36872 | tf_op jit(solution)/shard_map/ppermute | solution.py:67
  59.1 4.1 %collective-permute-start.20 = (f32[16,192]{1,0:T(8,128)S(1)}, f32[16,192]{1,0:T(8,128)S(1)}, u32[]{:S(2)}, u32[]{:S(2)}) collective-permute-start(f32[16,192]{1,0:T(8,128)S(1)} %get-tuple-element.45), channel_id=1, source_target_pairs={{0,28},{4,8},{8,4},{12,16},{16,12},{20,24},{24,20},{28,0},{1,29},{... | collective-permute-start | bytes 36872 | tf_op jit(solution)/shard_map/ppermute | solution.py:72

commit v3 on v2

v3 whole, which is shorter than its diff:
```python
import functools

import jax
import jax.numpy as jnp
from jax import lax
from jax.experimental import pallas as pl
from jax.experimental.pallas import tpu as pltpu
from jax.sharding import PartitionSpec as P

SWEEPS = 2
NODE_DEV = 768
HALF = jnp.bfloat16
FULL = jnp.float32
LANES = 128
PICK = 8
NT = (((1,), (1,)), ((), ()))
VMEM = pl.BlockSpec(memory_space=pltpu.VMEM)
SMEM = pl.BlockSpec(memory_space=pltpu.SMEM)
HBM = pl.BlockSpec(memory_space=pltpu.HBM)
GROUP = 30
MIB = 1024 * 1024


def round_up(size, unit):
    return -(-size // unit) * unit


def iota(shape, dim):
    return lax.broadcasted_iota(jnp.int32, shape, dim)


def hit(condition):
    return jnp.where(condition, 1.0, 0.0)


def in_hbm(array):
    return pltpu.with_memory_space_constraint(array, pltpu.HBM)


def call(kernel, name, args, specs, outs, scratch=(), limit=16, flops=0, moved=0, aliases=None):
    return pl.pallas_call(
        kernel,
        in_specs=specs,
        out_specs=[SMEM if getattr(out, "memory_space", None) is pltpu.SMEM else VMEM for out in outs],
        input_output_aliases=aliases or {},
        out_shape=outs,
        scratch_shapes=list(scratch),
        compiler_params=pltpu.CompilerParams(vmem_limit_bytes=limit * MIB),
        cost_estimate=pl.CostEstimate(flops=flops, bytes_accessed=moved, transcendentals=0),
        name=name,
    )(*args)


def distances():
    return list(range(1, lax.axis_size("blk")))


def over_blk(block, order):
    count = lax.axis_size("blk")
    return [lax.ppermute(block, "blk", [(i, i ^ k) for i in range(count)]) for k in order]


def to_mate(block):
    return lax.ppermute(block, "dom", [(i, i ^ 1) for i in range(lax.axis_size("dom"))])


def to_far(block):
    count = lax.axis_size("dom")
    return lax.ppermute(block, "dom", [(i, (((i + 1) ^ 1) - 1) % count) for i in range(count)])


def rounded(block, rows):
    short = rows - block.shape[0]
    if short:
        block = jnp.concatenate([block, jnp.zeros((short, block.shape[1]), block.dtype)], axis=0)
    return block.astype(HALF)


def window(ids, count):
    dom = lax.axis_index("dom")
    odd = lax.rem(dom, 2)
    place = ids - dom * count
    below = jnp.where(place < 0, 1, 0)
    above = jnp.where(place >= count, 1, 0)
    mate = odd * below + (1 - odd) * above
    return 2 * (below + above) - mate, place + (below - above) * count


def started(pairs, sems):
    copies = [pltpu.make_async_copy(source, target, sems.at[i]) for i, (source, target) in enumerate(pairs)]
    for copy in copies:
        copy.start()
    return copies


def slots_kernel(
    nb_hbm, shift_hbm, adj_hbm, rhs_hbm, _,
    pick_out, shift_out, list_out, count_out, adj_out, rhs_out, nb_ref, scalar_nb_ref, shift_ref, sems,
):
    pairs = [(nb_hbm, nb_ref), (shift_hbm, shift_ref), (adj_hbm, adj_out), (rhs_hbm, rhs_out)]
    copies = started(pairs + [(nb_hbm, scalar_nb_ref)], sems)
    copies[0].wait()
    copies[1].wait()
    copies[4].wait()
    list_far(scalar_nb_ref, list_out, count_out)
    faces, elements = nb_ref.shape
    rows_part = round_up(3 * elements, 16)
    part, inside = window(nb_ref[...], elements)
    bases = jnp.concatenate([iota((1, elements), 1), part * rows_part + inside], axis=0).astype(FULL)
    deep = elements * PICK
    shape = (deep, elements)
    behind = iota(shape, 0) - PICK * iota(shape, 1)
    owner = hit(jnp.logical_and(behind >= 0, behind < PICK)).astype(HALF)
    columns = lax.dot_general(owner, bases.astype(HALF), NT, preferred_element_type=FULL)
    shape = (elements, PICK, pick_out.shape[1])
    row, lane = iota(shape, 1).reshape(deep, -1), iota(shape, 2).reshape(deep, -1)
    offset = jnp.where(row < 3, lane - elements * row, -1).astype(FULL)
    for k in range(faces + 1):
        pick_out[k * deep : (k + 1) * deep, :] = hit(offset == columns[:, k : k + 1]).astype(HALF)
    shift_out[...] = jnp.zeros(shift_out.shape, FULL)
    for e in range(elements):
        shift_out[pl.ds(e, 3, stride=elements), :] = jnp.full((3, shift_out.shape[1]), shift_ref[e], FULL)
    for copy in (copies[2], copies[3]):
        copy.wait()


def list_far(nb_ref, list_out, count_out):
    faces, elements = nb_ref.shape

    count = jnp.int32(0)
    for e in range(elements):
        for k in range(1, faces + 1):
            part, inside = window(nb_ref[k - 1, e], elements)
            list_out[count] = (e * (faces + 1) + k) * 32 + inside
            count = count + lax.shift_right_logical(part, 1)
    for step in range(GROUP):
        list_out[count + step] = elements
    count_out[0] = lax.div(count + GROUP - 1, GROUP)


def nodes_kernel(ids_ref, shape_ref, low_out, target_out, shape_out):
    blk = lax.axis_index("blk")
    blks = lax.axis_size("blk")
    span = NODE_DEV // blks
    ids = ids_ref[...]
    pairs = ids.shape[0] // 2
    ids = [jnp.concatenate([ids[2 * p : 2 * p + 1], ids[2 * p + 1 : 2 * p + 2]], axis=1) for p in range(pairs)]
    part, inside = window(jnp.concatenate(ids, axis=0), NODE_DEV)
    owner = jnp.zeros_like(inside)
    for cut in range(1, blks):
        owner = owner + jnp.where(inside >= cut * span, 1, 0)
    low = inside - owner * span
    target_out[...] = part * blks + (owner ^ blk)
    shape = (span, LANES)
    for group in range(pairs):
        same = iota(shape, 0) == low[group : group + 1, :]
        low_out[:, group * LANES : (group + 1) * LANES] = hit(same).astype(HALF)

    elements, width, coords = shape_ref.shape
    shape = (coords, shape_out.shape[2])
    row, lane = iota(shape, 0), iota(shape, 1)
    axis = jnp.where(lane >= LANES, 1, 0) + jnp.where(lane >= 2 * LANES, 1, 0)
    side = lane - axis * LANES
    for odd in range(2):
        place = side - odd * (LANES // 2)
        inside = jnp.logical_and(place >= 0, place < LANES // 2)
        sort = hit(jnp.logical_and(inside, row == 3 * place + axis)).astype(HALF)
        for e in range(odd, elements, 2):
            shape_out[e] = jnp.dot(shape_ref[e], sort, preferred_element_type=FULL).astype(HALF)


def widened(block, lanes):
    short = lanes - block.shape[1]
    if short == 0:
        return block
    return jnp.concatenate([block, jnp.zeros((block.shape[0], short), block.dtype)], axis=1)


def put_columns(blocks, order, stride):
    blk = lax.axis_index("blk")
    width = blocks[0].shape[1]
    blocks = [widened(block.astype(FULL), LANES) for block in blocks]
    lane = iota(blocks[0].shape, 1)
    tiles = [0.0] * (stride // LANES)
    for owner in range(len(blocks)):
        found = blocks[0]
        for k, block in zip(order, blocks[1:]):
            found = jnp.where((blk ^ owner) == k, block, found)
        tile, offset = divmod(owner * width, LANES)
        if offset:
            found = pltpu.roll(found, offset, 1)
        if offset + width <= LANES:
            tiles[tile] = tiles[tile] + found
        else:
            tiles[tile] = tiles[tile] + jnp.where(lane >= offset, found, 0.0)
            tiles[tile + 1] = tiles[tile + 1] + jnp.where(lane < offset, found, 0.0)
    return jnp.concatenate(tiles, axis=1).astype(HALF)


def columns_kernel(order, *refs):
    *blocks, out_ref = refs
    rows, stride = out_ref.shape
    out_ref[...] = put_columns([rounded(ref[...], rows) for ref in blocks], order, stride)


def near_kernel(own_ref, mate_ref, pick_ref, shift_ref, adj_ref, rhs_ref, jac_ref, _, out_ref, image):
    products([own_ref[...], mate_ref[...]], pick_ref, jac_ref, image)
    out_ref[...] = without(shift_ref, adj_ref, rhs_ref, image)


def without(shift_ref, adj_ref, rhs_ref, image):
    rows, width = adj_ref.shape
    return rhs_ref[...] - (shift_ref[:rows, :width] * adj_ref[...] + image[:rows, :width])


def products(parts, pick_ref, jac_ref, image):
    elements, slots, width, _ = jac_ref.shape
    rows_part, stride = parts[0].shape
    short = pick_ref.shape[1] - len(parts) * rows_part
    if short:
        parts = parts + [jnp.zeros((short, stride), HALF)]
    stacked = jnp.concatenate(parts, axis=0)
    picked = jnp.dot(pick_ref[...], stacked, preferred_element_type=FULL).astype(HALF)
    image[...] = jnp.zeros(image.shape, FULL)
    for pair in range(elements // 2):
        starts = [k * elements * PICK + pair * 2 * PICK for k in range(slots)]
        left = jnp.concatenate([picked[start : start + 2 * PICK] for start in starts], axis=1)
        for side in range(2):
            e = 2 * pair + side
            blocks = jnp.concatenate([widened(jac_ref[e, k], stride) for k in range(slots)], axis=1)
            product = lax.dot_general(left, blocks, NT, preferred_element_type=FULL)
            first = side * PICK
            image[pl.ds(e, 3, stride=elements), :width] = product[first : first + 3]


def far_kernel(near_ref, far_ref, jac_ref, list_ref, count_ref, _shapes, _ids, out_ref, spread, sums, image):
    elements, slots, width, _ = jac_ref.shape
    rows, stride = far_ref.shape
    deep = spread.shape[1]
    shape = (elements, deep, rows)
    element, row, lane = [iota(shape, dim).reshape(elements * deep, rows) for dim in range(3)]
    pick = hit(jnp.where(row < 3, row * elements + element, -1) == lane).astype(HALF)
    taken = jnp.dot(pick, far_ref[...], preferred_element_type=FULL).astype(HALF)
    spread[:elements] = taken.reshape(elements, deep, stride)
    spread[elements:] = jnp.zeros((spread.shape[0] - elements, deep, stride), HALF)
    sums[...] = jnp.zeros(sums.shape, FULL)

    @pl.loop(0, count_ref[0])
    def _(step):
        for i in range(GROUP):
            word = list_ref[step * GROUP + i]
            block = lax.shift_right_logical(word, 5)
            place = lax.bitwise_and(word, 31)
            e = lax.div(block, slots)
            blocks = widened(jac_ref[e, block - e * slots], stride)
            product = lax.dot_general(spread[place], blocks, NT, preferred_element_type=FULL)
            sums[e, :, :width] += product[:PICK]

    for e in range(elements):
        image[pl.ds(e, 3, stride=elements), :] = sums[e, :3, :]
    real = near_ref.shape[0]
    out_ref[...] = rounded(near_ref[...] - image[:real, :width], out_ref.shape[0])


def element_of_row(shape, elements, copies=3):
    row = iota(shape, 0)
    for step in range(1, copies + 1):
        row = row - jnp.where(iota(shape, 0) >= step * elements, elements, 0)
    return row


def updated(resid_refs, inv_ref, adj_ref, update):
    rows, width = adj_ref.shape
    elements = rows // 3
    stride = round_up(inv_ref.shape[2], LANES)
    resid = put_columns([ref[...] for ref in resid_refs], distances(), stride)
    shape = (elements, PICK, resid.shape[0])
    deep = elements * PICK
    element, row, lane = [iota(shape, dim).reshape(deep, -1) for dim in range(3)]
    pick = hit(jnp.where(row < 3, row * elements + element, -1) == lane).astype(HALF)
    resid = jnp.dot(pick, resid, preferred_element_type=FULL).astype(HALF)
    update[...] = jnp.zeros(update.shape, FULL)
    for pair in range(elements // 2):
        left = resid[pair * 2 * PICK : (pair + 1) * 2 * PICK]
        for side in range(2):
            e = 2 * pair + side
            product = lax.dot_general(left, widened(inv_ref[e], stride), NT, preferred_element_type=FULL)
            first = side * PICK
            update[pl.ds(e, 3, stride=elements), :width] = product[first : first + 3]
    short = jnp.zeros((update.shape[0] - rows, width), FULL)
    return jnp.concatenate([adj_ref[...] + update[:rows, :width], short], axis=0)


def update_kernel(*refs):
    *resid_refs, inv_ref, adj_ref, adj_out, half_out, update = refs
    adj = updated(resid_refs, inv_ref, adj_ref, update)
    adj_out[...] = adj[: adj_out.shape[0]]
    half_out[...] = adj.astype(HALF)


def split(value):
    top = value.astype(HALF)
    return top, (value - top.astype(FULL)).astype(HALF)


def gradient_kernel(*refs):
    blks = lax.axis_size("blk")
    resid_refs = refs[:blks]
    inv_ref, adj_ref, shape_ref, low_ref, target_ref, adj_out = refs[blks : blks + 6]
    piece_outs = refs[blks + 6 : 2 * blks + 6]
    sorted_ref, left_ref, sums_ref, update = refs[2 * blks + 6 :]
    adj = updated(resid_refs, inv_ref, adj_ref, update)
    adj_out[...] = adj[: adj_out.shape[0]]
    half = adj.astype(HALF)
    elements = adj_out.shape[0] // 3
    pairs = elements // 2
    tall, width = half.shape
    coords = shape_ref.shape[2]
    depth = 3 if elements % 3 == 0 and 3 * width <= 256 else 1
    shape = (width, depth * width)
    row, lane = iota(shape, 0), iota(shape, 1)
    repeat = jnp.zeros(shape, FULL)
    for step in range(depth):
        repeat = repeat + hit(lane == row + step * width)
    left = jnp.dot(half, repeat.astype(HALF), preferred_element_type=FULL)
    shape = left.shape
    owner = element_of_row(shape, elements)
    group = jnp.zeros(shape, jnp.int32)
    for step in range(1, elements // depth):
        group = group + jnp.where(owner >= step * depth, 1, 0)
    first = (owner - group * depth) * width
    behind = iota(shape, 1) - first
    left = jnp.where(jnp.logical_and(behind >= 0, behind < width), left, 0.0).astype(HALF)
    shape = (tall, coords)
    owner = element_of_row(shape, elements)
    total = jnp.zeros(shape, FULL)
    for start in range(0, elements, depth):
        partials = jnp.concatenate([shape_ref[start + step] for step in range(depth)], axis=0)
        product = jnp.dot(left, partials, preferred_element_type=FULL)
        total = jnp.where(owner >= start, product, total)
    top, rest = split(total)
    sorted_ref[:tall] = top.astype(FULL)
    sorted_ref[tall:] = rest.astype(FULL)
    deep = 16
    for pair in range(pairs):
        lanes = slice(pair * LANES, (pair + 1) * LANES)
        mine = iota((deep, LANES), 0) == target_ref[pair : pair + 1, :]
        for part in range(2):
            for j in range(3):
                for c in range(3):
                    at = part * tall + j * elements + 2 * pair
                    lanes_of_axis = slice(c * LANES, (c + 1) * LANES)
                    values = sorted_ref[at : at + 1, lanes_of_axis] + sorted_ref[at + 1 : at + 2, lanes_of_axis]
                    start = (part * 9 + j * 3 + c) * deep
                    left_ref[start : start + deep, lanes] = jnp.where(mine, values, 0.0).astype(HALF)
    sums = lax.dot_general(left_ref[...], low_ref[...], NT, preferred_element_type=FULL)
    span = low_ref.shape[0]
    sums = -(sums[: 9 * deep] + sums[9 * deep :])
    tiles = [(tile, tile * LANES, min(span, (tile + 1) * LANES)) for tile in range(sums_ref.shape[0])]
    for tile, start, stop in tiles:
        sums_ref[tile, :, : stop - start] = sums[:, start:stop]
    for k, out_ref in enumerate(piece_outs):
        for tile, start, stop in tiles:
            found = [sums_ref[tile, pl.ds(part * blks + k, 9, stride=deep), :][:, : stop - start] for part in range(3)]
            found = jnp.concatenate(found + [jnp.zeros((5, stop - start), FULL)], axis=0)
            out_ref[:, start:stop] = found.astype(out_ref.dtype)


def combine_kernel(*refs):
    *piece_refs, own_out, mate_out, far_out = refs
    total = piece_refs[0][...]
    for ref in piece_refs[1:]:
        total = total + ref[...].astype(FULL)
    own_out[...] = total[:9]
    mate_out[...] = total[9:18]
    far_out[...] = total[18:27]


def local(
    adjoint_start,
    right_sides,
    jac_blocks,
    block_inverse,
    neighbours,
    pseudo_shift,
    shape_partials,
    node_ids,
):
    elements, sides, width = adjoint_start.shape
    slots, full = jac_blocks.shape[1], jac_blocks.shape[3]
    enodes = node_ids.shape[1]
    rows = sides * elements
    tall = round_up(rows, 16)
    stride = round_up(full, LANES)
    blks = lax.axis_size("blk")
    span = NODE_DEV // blks
    stacked = round_up(3 * tall, LANES)
    entries = elements * enodes

    adj_hbm = jnp.transpose(adjoint_start, (1, 0, 2)).reshape(rows, width)
    rhs = jnp.transpose(right_sides, (1, 0, 2)).reshape(rows, width)
    half_shape = jax.ShapeDtypeStruct((tall, width), HALF)

    adj_shape = jax.ShapeDtypeStruct((rows, width), FULL)
    pick, shift, far_list, far_count, adj, rhs = call(
        slots_kernel,
        "slots",
        [in_hbm(neighbours.T), in_hbm(pseudo_shift), in_hbm(adj_hbm), in_hbm(rhs), in_hbm(jac_blocks)],
        [HBM] * 5,
        [
            jax.ShapeDtypeStruct((slots * elements * PICK, stacked), HALF),
            jax.ShapeDtypeStruct((tall, LANES), FULL),
            pltpu.SMEM((round_up(elements * (slots - 1) + GROUP, LANES),), jnp.int32),
            pltpu.SMEM((1,), jnp.int32),
            pltpu.VMEM((rows, width), FULL),
            pltpu.VMEM((rows, width), FULL),
        ],
        scratch=[
            pltpu.VMEM((slots - 1, elements), jnp.int32),
            pltpu.SMEM((slots - 1, elements), jnp.int32),
            pltpu.SMEM((elements,), FULL),
            pltpu.SemaphoreType.DMA((6,)),
        ],
        moved=16 * MIB,
    )
    low, target, shapes = call(
        nodes_kernel,
        "nodes",
        [node_ids, shape_partials],
        [VMEM, VMEM],
        [
            jax.ShapeDtypeStruct((span, entries), HALF),
            jax.ShapeDtypeStruct((entries // LANES, LANES), jnp.int32),
            jax.ShapeDtypeStruct((elements, width, 3 * LANES), HALF),
        ],
        moved=3 * MIB,
    )

    for sweep in range(SWEEPS):
        order = distances()
        blocks = [half] + over_blk(half, order) if sweep else [adj] + over_blk(adj_hbm, order)
        wide = jax.ShapeDtypeStruct((tall, stride), HALF)
        (own,) = call(functools.partial(columns_kernel, order), "columns", blocks, [VMEM] * blks, [wide], moved=1 * MIB)
        far, mate = to_far(own), to_mate(own)
        image = pltpu.VMEM((tall, LANES), FULL)
        near_inputs = [own, mate, pick, shift, adj, rhs]
        far_scratch = [
            pltpu.VMEM((elements + 8, 16, stride), HALF),
            pltpu.VMEM((elements, PICK, LANES), FULL),
            image,
        ]
        (near,) = call(
            near_kernel,
            "near",
            near_inputs + [jac_blocks, in_hbm(block_inverse)],
            [VMEM] * 7 + [HBM],
            [adj_shape],
            [image],
            moved=12 * MIB,
        )
        (resid,) = call(
            far_kernel,
            "far",
            [near, far, jac_blocks, far_list, far_count, in_hbm(shape_partials), in_hbm(node_ids)],
            [VMEM] * 3 + [SMEM] * 2 + [HBM] * 2,
            [half_shape],
            far_scratch,
            moved=4 * MIB,
        )
        resids = [resid] + over_blk(resid, distances())
        if sweep < SWEEPS - 1:
            adj, half = call(
                update_kernel,
                "update",
                resids + [block_inverse, adj],
                [VMEM] * (blks + 2),
                [adj_shape, half_shape],
                scratch=[pltpu.VMEM((tall, LANES), FULL)],
                moved=8 * MIB,
            )
    pieces = [jax.ShapeDtypeStruct((32, span), HALF if k else FULL) for k in range(blks)]
    adj, *pieces = call(
        gradient_kernel,
        "gradient",
        resids + [block_inverse, adj, shapes, low, target],
        [VMEM] * (blks + 5),
        [adj_shape] + pieces,
        scratch=[
            pltpu.VMEM((2 * tall, 3 * LANES), FULL),
            pltpu.VMEM((2 * 9 * 16, entries), HALF),
            pltpu.VMEM((-(-span // LANES), 9 * 16, LANES), FULL),
            pltpu.VMEM((tall, LANES), FULL),
        ],
    )
    count = lax.axis_size("blk")
    received = [
        lax.ppermute(pieces[k], "blk", [(i, i ^ k) for i in range(count)]) for k in reversed(distances())
    ]
    third = jax.ShapeDtypeStruct((9, span), FULL)
    own, mate, far = call(combine_kernel, "combine", [pieces[0]] + received, [VMEM] * blks, [third] * 3)
    gradient = own + to_mate(mate) + to_far(far)
    adjoint = jnp.transpose(adj.reshape(sides, elements, width), (1, 0, 2))
    return (adjoint, gradient)


def solution(mesh):
    in_specs = (
        P("dom", None, "blk"),
        P("dom", None, "blk"),
        P("dom", None, "blk", None),
        P("dom", "blk", None),
        P("dom", None),
        P("dom"),
        P("dom", "blk", None),
        P("dom", None),
    )
    out_specs = (P("dom", None, "blk"), P(None, ("dom", "blk")))
    return jax.shard_map(local, mesh=mesh, in_specs=in_specs, out_specs=out_specs, check_vma=False)
```

time: 64.1 us -> 59.2 us (0.924)
  waiting for transfers between devices: 18.3 us -> 12.8 us
  starting transfers between devices: 28.3 us -> 31.8 us
  Pallas kernels: 15.9 us -> 12.8 us
    ppermute x3, waiting for transfers between devices: 6.31 us -> 1.45 us  [to_far(): lax.ppermute(block, 'dom', [(i, ((i + 1 ^ 1) - 1) % count) for i in range...]
    ppermute x3, starting transfers between devices: 4.55 us -> 8.17 us  [to_far(): lax.ppermute(block, 'dom', [(i, ((i + 1 ^ 1) - 1) % count) for i in range...]
    pallas_call x10 -> x11, Pallas kernels: 15.9 us -> 12.8 us  [call(): pl.pallas_call(kernel, in_specs=specs, out_specs=[SMEM if getattr(out, 'm...]
  transfers between devices with their start and end apart: 21 -> 21, of which waited for: 15 -> 12; matrix products, arithmetic and copies ran while one was open for 0% -> 0% of each run, Pallas kernels for 8% -> 15%
where the time goes in v3:
time: 59.2 us; the launch traced here: 59.1 us
  starting transfers between devices  31.8 us (54%)
  Pallas kernels  12.8 us (22%)
  waiting for transfers between devices  12.8 us (22%)
  between operations  0.88 us (1%)
  other arithmetic  0.61 us (1%)
    ppermute x12, starting transfers between devices, over_blk(): lax.ppermute(block, 'blk', [(i, i ^ k) for i in range(count)])  19.1 us
    pallas_call x11, Pallas kernels, call(): pl.pallas_call(kernel, in_specs=specs, out_specs=[SMEM if getattr(out, 'm...  12.8 us
    ppermute x12, waiting for transfers between devices, over_blk(): lax.ppermute(block, 'blk', [(i, i ^ k) for i in range(count)])  8.76 us
    ppermute x3, starting transfers between devices, to_far(): lax.ppermute(block, 'dom', [(i, ((i + 1 ^ 1) - 1) % count) for i in range...  8.17 us
    ppermute x3, starting transfers between devices, local(): lax.ppermute(pieces[k], 'blk', [(i, i ^ k) for i in range(count)])  4.39 us
    ppermute x3, waiting for transfers between devices, local(): lax.ppermute(pieces[k], 'blk', [(i, i ^ k) for i in range(count)])  2.57 us
    ppermute x3, waiting for transfers between devices, to_far(): lax.ppermute(block, 'dom', [(i, ((i + 1 ^ 1) - 1) % count) for i in range...  1.45 us
  transfers between devices with their start and end apart: 21, of which 12 were waited for; matrix products, arithmetic and copies ran while one was open for 0% of the time, Pallas kernels for 15%

profile of v3, /device:TPU:0, one launch (start us, length us, event | category | flops | bytes accessed | tf_op | source)
XLA Modules:
  0.0 59.1 jit_solution(2823654545244518897)
XLA Ops:
  0.6 5.1 %collective-permute-start.2 = (f32[72,80]{1,0:T(8,128)}, f32[72,80]{1,0:T(8,128)S(1)}, u32[]{:S(2)}, u32[]{:S(2)}) collective-permute-start(f32[72,80]{1,0:T(8,128)} %bitcast.11), channel_id=1, source_target_pairs={{0,3},{1,2},{2,1},{3,0},{4,7},{5,6},{6,5},{7,4},{8,11},{9,10},{10,... | collective-permute-start | bytes 69128 | tf_op jit(solution)/shard_map/ppermute | solution.py:60
  5.7 0.6 %collective-permute-start = (f32[72,80]{1,0:T(8,128)}, f32[72,80]{1,0:T(8,128)S(1)}, u32[]{:S(2)}, u32[]{:S(2)}) collective-permute-start(f32[72,80]{1,0:T(8,128)} %bitcast.13), channel_id=1, source_target_pairs={{0,1},{1,0},{2,3},{3,2},{4,5},{5,4},{6,7},{7,6},{8,9},{9,8},{10,11... | collective-permute-start | bytes 69128 | tf_op jit(solution)/shard_map/ppermute | solution.py:60
  6.4 1.8 %slots.1 = (bf16[1344,256]{1,0:T(8,128)(2,1)S(1)}, f32[80,128]{1,0:T(8,128)S(1)}, s32[256]{0:T(256)S(4)}, s32[1]{0:T(128)S(4)}, f32[72,80]{1,0:T(8,128)S(1)}, /*index=5*/f32[72,80]{1,0:T(8,128)S(1)}) custom-call(s32[6,24]{1,0:T(8,128)} %bitcast.15, f32[24]{0:T(128)} %shift_hbm.1, f32[72,80]{1,0:T(8,128)} %bitcast.14, f32[72,80]{1,0:T(8,128)} %bitcast.10, ...), custom_call_target="tpu_custom_call" | custom-call | bytes 16777216 | tf_op jit(solution)/shard_map/slots/pallas_call | solution.py:41
  8.2 2.6 %collective-permute-done.1.refs_2_ = f32[72,80]{1,0:T(8,128)S(1)} collective-permute-done((f32[72,80]{1,0:T(8,128)}, f32[72,80]{1,0:T(8,128)S(1)}, u32[]{:S(2)}, u32[]{:S(2)}) %collective-permute-start.1) | collective-permute-done | bytes 23072 | tf_op jit(solution)/shard_map/ppermute | solution.py:60
  11.0 2.5 %collective-permute-start.4 = (bf16[80,384]{1,0:T(8,128)(2,1)S(1)}, bf16[80,384]{1,0:T(8,128)(2,1)S(1)}, u32[]{:S(2)}, u32[]{:S(2)}) collective-permute-start(bf16[80,384]{1,0:T(8,128)(2,1)S(1)} %columns.2.own_ref), channel_id=1, source_target_pairs={{0,28},{4,8},{8,4},{12,16},{16,12},{20,24},{24,20},{28,0},{1,29},{... | collective-permute-start | bytes 184328 | tf_op jit(solution)/shard_map/ppermute | solution.py:69
  13.6 3.2 %near.2.near_ref = f32[72,80]{1,0:T(8,128)S(1)} custom-call(bf16[80,384]{1,0:T(8,128)(2,1)S(1)} %columns.2.own_ref, bf16[80,384]{1,0:T(8,128)(2,1)S(1)} %collective-permute-done.3.mate_ref, bf16[1344,256]{1,0:T(8,128)(2,1)S(1)} %get-tuple-element.22.pick_ref, f32[80,128]{1,0:T(8,128)S(1)} %get-tuple-element.23.shift_ref, ...), custom_call_target="tpu_custom_call" | custom-call | bytes 12582912 | tf_op jit(solution)/shard_map/near/pallas_call | solution.py:41
  17.1 1.6 %collective-permute-start.7 = (bf16[80,80]{1,0:T(8,128)(2,1)S(1)}, bf16[80,80]{1,0:T(8,128)(2,1)S(1)}, u32[]{:S(2)}, u32[]{:S(2)}) collective-permute-start(bf16[80,80]{1,0:T(8,128)(2,1)S(1)} %far.2.refs_0_), channel_id=1, source_target_pairs={{0,3},{1,2},{2,1},{3,0},{4,7},{5,6},{6,5},{7,4},{8,11},{9,10},{10,... | collective-permute-start | bytes 38408 | tf_op jit(solution)/shard_map/ppermute | solution.py:60
  19.3 2.3 %collective-permute-start.5 = (bf16[80,80]{1,0:T(8,128)(2,1)S(1)}, bf16[80,80]{1,0:T(8,128)(2,1)S(1)}, u32[]{:S(2)}, u32[]{:S(2)}) collective-permute-start(bf16[80,80]{1,0:T(8,128)(2,1)S(1)} %far.2.refs_0_), channel_id=1, source_target_pairs={{0,1},{1,0},{2,3},{3,2},{4,5},{5,4},{6,7},{7,6},{8,9},{9,8},{10,11... | collective-permute-start | bytes 38408 | tf_op jit(solution)/shard_map/ppermute | solution.py:60
  21.6 1.2 %collective-permute-done.7.refs_3_ = bf16[80,80]{1,0:T(8,128)(2,1)S(1)} collective-permute-done((bf16[80,80]{1,0:T(8,128)(2,1)S(1)}, bf16[80,80]{1,0:T(8,128)(2,1)S(1)}, u32[]{:S(2)}, u32[]{:S(2)}) %collective-permute-start.7) | collective-permute-done | bytes 12832 | tf_op jit(solution)/shard_map/ppermute | solution.py:60
  22.8 0.8 %collective-permute-done.6.refs_2_ = bf16[80,80]{1,0:T(8,128)(2,1)S(1)} collective-permute-done((bf16[80,80]{1,0:T(8,128)(2,1)S(1)}, bf16[80,80]{1,0:T(8,128)(2,1)S(1)}, u32[]{:S(2)}, u32[]{:S(2)}) %collective-permute-start.6) | collective-permute-done | bytes 12832 | tf_op jit(solution)/shard_map/ppermute | solution.py:60
  23.6 0.8 %update.1 = (f32[72,80]{1,0:T(8,128)S(1)}, bf16[80,80]{1,0:T(8,128)(2,1)S(1)}) custom-call(bf16[80,80]{1,0:T(8,128)(2,1)S(1)} %far.2.refs_0_, bf16[80,80]{1,0:T(8,128)(2,1)S(1)} %collective-permute-done.5.refs_1_, bf16[80,80]{1,0:T(8,128)(2,1)S(1)} %collective-permute-done.6.refs_2_, bf16[80,80]{1,0:T(8,128)(2,1)S(1)} %collective-permute-done.7.refs_3_, ...), custom_call_target="tpu_custom_call" | custom-call | bytes 8388608 | tf_op jit(solution)/shard_map/update/pallas_call | solution.py:41
  24.5 2.3 %collective-permute-start.10 = (bf16[80,80]{1,0:T(8,128)(2,1)S(1)}, bf16[80,80]{1,0:T(8,128)(2,1)S(1)}, u32[]{:S(2)}, u32[]{:S(2)}) collective-permute-start(bf16[80,80]{1,0:T(8,128)(2,1)S(1)} %get-tuple-element.27.refs_0_), channel_id=1, source_target_pairs={{0,3},{1,2},{2,1},{3,0},{4,7},{5,6},{6,5},{7,4},{8,11},{9,10},{10,... | collective-permute-start | bytes 38408 | tf_op jit(solution)/shard_map/ppermute | solution.py:60
  26.8 0.9 %collective-permute-start.9 = (bf16[80,80]{1,0:T(8,128)(2,1)S(1)}, bf16[80,80]{1,0:T(8,128)(2,1)S(1)}, u32[]{:S(2)}, u32[]{:S(2)}) collective-permute-start(bf16[80,80]{1,0:T(8,128)(2,1)S(1)} %get-tuple-element.27.refs_0_), channel_id=1, source_target_pairs={{0,2},{1,3},{2,0},{3,1},{4,6},{5,7},{6,4},{7,5},{8,10},{9,11},{10,... | collective-permute-start | bytes 38408 | tf_op jit(solution)/shard_map/ppermute | solution.py:60
  27.7 1.2 %collective-permute-start.8 = (bf16[80,80]{1,0:T(8,128)(2,1)S(1)}, bf16[80,80]{1,0:T(8,128)(2,1)S(1)}, u32[]{:S(2)}, u32[]{:S(2)}) collective-permute-start(bf16[80,80]{1,0:T(8,128)(2,1)S(1)} %get-tuple-element.27.refs_0_), channel_id=1, source_target_pairs={{0,1},{1,0},{2,3},{3,2},{4,5},{5,4},{6,7},{7,6},{8,9},{9,8},{10,11... | collective-permute-start | bytes 38408 | tf_op jit(solution)/shard_map/ppermute | solution.py:60
  28.9 1.2 %collective-permute-done.10.refs_3_ = bf16[80,80]{1,0:T(8,128)(2,1)S(1)} collective-permute-done((bf16[80,80]{1,0:T(8,128)(2,1)S(1)}, bf16[80,80]{1,0:T(8,128)(2,1)S(1)}, u32[]{:S(2)}, u32[]{:S(2)}) %collective-permute-start.10) | collective-permute-done | bytes 12832 | tf_op jit(solution)/shard_map/ppermute | solution.py:60
  30.1 1.4 %collective-permute-done.9.refs_2_ = bf16[80,80]{1,0:T(8,128)(2,1)S(1)} collective-permute-done((bf16[80,80]{1,0:T(8,128)(2,1)S(1)}, bf16[80,80]{1,0:T(8,128)(2,1)S(1)}, u32[]{:S(2)}, u32[]{:S(2)}) %collective-permute-start.9) | collective-permute-done | bytes 12832 | tf_op jit(solution)/shard_map/ppermute | solution.py:60
  31.9 2.8 %collective-permute-start.12 = (bf16[80,384]{1,0:T(8,128)(2,1)S(1)}, bf16[80,384]{1,0:T(8,128)(2,1)S(1)}, u32[]{:S(2)}, u32[]{:S(2)}) collective-permute-start(bf16[80,384]{1,0:T(8,128)(2,1)S(1)} %columns.3.own_ref), channel_id=1, source_target_pairs={{0,28},{4,8},{8,4},{12,16},{16,12},{20,24},{24,20},{28,0},{1,29},{... | collective-permute-start | bytes 184328 | tf_op jit(solution)/shard_map/ppermute | solution.py:69
  34.7 3.2 %near.3.near_ref = f32[72,80]{1,0:T(8,128)S(1)} custom-call(bf16[80,384]{1,0:T(8,128)(2,1)S(1)} %columns.3.own_ref, bf16[80,384]{1,0:T(8,128)(2,1)S(1)} %collective-permute-done.11.mate_ref, bf16[1344,256]{1,0:T(8,128)(2,1)S(1)} %get-tuple-element.22.pick_ref, f32[80,128]{1,0:T(8,128)S(1)} %get-tuple-element.23.shift_ref, ...), custom_call_target="tpu_custom_call" | custom-call | bytes 12582912 | tf_op jit(solution)/shard_map/near/pallas_call | solution.py:41
  38.2 1.7 %collective-permute-start.15 = (bf16[80,80]{1,0:T(8,128)(2,1)S(1)}, bf16[80,80]{1,0:T(8,128)(2,1)S(1)}, u32[]{:S(2)}, u32[]{:S(2)}) collective-permute-start(bf16[80,80]{1,0:T(8,128)(2,1)S(1)} %far.3.refs_0_), channel_id=1, source_target_pairs={{0,3},{1,2},{2,1},{3,0},{4,7},{5,6},{6,5},{7,4},{8,11},{9,10},{10,... | collective-permute-start | bytes 38408 | tf_op jit(solution)/shard_map/ppermute | solution.py:60
  40.0 0.9 %collective-permute-start.14 = (bf16[80,80]{1,0:T(8,128)(2,1)S(1)}, bf16[80,80]{1,0:T(8,128)(2,1)S(1)}, u32[]{:S(2)}, u32[]{:S(2)}) collective-permute-start(bf16[80,80]{1,0:T(8,128)(2,1)S(1)} %far.3.refs_0_), channel_id=1, source_target_pairs={{0,2},{1,3},{2,0},{3,1},{4,6},{5,7},{6,4},{7,5},{8,10},{9,11},{10,... | collective-permute-start | bytes 38408 | tf_op jit(solution)/shard_map/ppermute | solution.py:60
  40.9 1.8 %collective-permute-start.13 = (bf16[80,80]{1,0:T(8,128)(2,1)S(1)}, bf16[80,80]{1,0:T(8,128)(2,1)S(1)}, u32[]{:S(2)}, u32[]{:S(2)}) collective-permute-start(bf16[80,80]{1,0:T(8,128)(2,1)S(1)} %far.3.refs_0_), channel_id=1, source_target_pairs={{0,1},{1,0},{2,3},{3,2},{4,5},{5,4},{6,7},{7,6},{8,9},{9,8},{10,11... | collective-permute-start | bytes 38408 | tf_op jit(solution)/shard_map/ppermute | solution.py:60
  42.7 0.9 %nodes.1 = (bf16[192,1536]{1,0:T(8,128)(2,1)S(1)}, s32[12,128]{1,0:T(8,128)S(1)}, bf16[24,80,384]{2,1,0:T(8,128)(2,1)S(1)}) custom-call(s32[24,64]{1,0:T(8,128)S(1)} %copy-done.4, bf16[24,80,192]{2,1,0:T(8,128)(2,1)S(1)} %copy-done.3), custom_call_target="tpu_custom_call" | custom-call | bytes 3145728 | tf_op jit(solution)/shard_map/nodes/pallas_call | solution.py:41
  43.9 1.0 %collective-permute-done.14.refs_2_ = bf16[80,80]{1,0:T(8,128)(2,1)S(1)} collective-permute-done((bf16[80,80]{1,0:T(8,128)(2,1)S(1)}, bf16[80,80]{1,0:T(8,128)(2,1)S(1)}, u32[]{:S(2)}, u32[]{:S(2)}) %collective-permute-start.14) | collective-permute-done | bytes 12832 | tf_op jit(solution)/shard_map/ppermute | solution.py:60
  44.9 2.2 %gradient.1 = (f32[72,80]{1,0:T(8,128)}, f32[32,192]{1,0:T(8,128)S(1)}, bf16[32,192]{1,0:T(8,128)(2,1)S(1)}, bf16[32,192]{1,0:T(8,128)(2,1)S(1)}, bf16[32,192]{1,0:T(8,128)(2,1)S(1)}) custom-call(bf16[80,80]{1,0:T(8,128)(2,1)S(1)} %far.3.refs_0_, bf16[80,80]{1,0:T(8,128)(2,1)S(1)} %collective-permute-done.13.refs_1_, ...), custom_call_target="tpu_custom_call" | custom-call | tf_op jit(solution)/shard_map/gradient/pallas_call | solution.py:41
  47.1 2.1 %collective-permute-start.16 = (bf16[32,192]{1,0:T(8,128)(2,1)S(1)}, bf16[32,192]{1,0:T(8,128)(2,1)S(1)}, u32[]{:S(2)}, u32[]{:S(2)}) collective-permute-start(bf16[32,192]{1,0:T(8,128)(2,1)S(1)} %get-tuple-element.34), channel_id=1, source_target_pairs={{0,3},{1,2},{2,1},{3,0},{4,7},{5,6},{6,5},{7,4},{8,11},{9,10},{10,... | collective-permute-start | bytes 36872 | tf_op jit(solution)/shard_map/ppermute | solution.py:497
  49.3 0.9 %collective-permute-start.17 = (bf16[32,192]{1,0:T(8,128)(2,1)S(1)}, bf16[32,192]{1,0:T(8,128)(2,1)S(1)}, u32[]{:S(2)}, u32[]{:S(2)}) collective-permute-start(bf16[32,192]{1,0:T(8,128)(2,1)S(1)} %get-tuple-element.35), channel_id=1, source_target_pairs={{0,2},{1,3},{2,0},{3,1},{4,6},{5,7},{6,4},{7,5},{8,10},{9,11},{10,... | collective-permute-start | bytes 36872 | tf_op jit(solution)/shard_map/ppermute | solution.py:497
  50.2 1.3 %collective-permute-start.18 = (bf16[32,192]{1,0:T(8,128)(2,1)S(1)}, bf16[32,192]{1,0:T(8,128)(2,1)S(1)}, u32[]{:S(2)}, u32[]{:S(2)}) collective-permute-start(bf16[32,192]{1,0:T(8,128)(2,1)S(1)} %get-tuple-element.36), channel_id=1, source_target_pairs={{0,1},{1,0},{2,3},{3,2},{4,5},{5,4},{6,7},{7,6},{8,9},{9,8},{10,11... | collective-permute-start | bytes 36872 | tf_op jit(solution)/shard_map/ppermute | solution.py:497
  51.5 1.1 %collective-permute-done.16.refs_1_ = bf16[32,192]{1,0:T(8,128)(2,1)S(1)} collective-permute-done((bf16[32,192]{1,0:T(8,128)(2,1)S(1)}, bf16[32,192]{1,0:T(8,128)(2,1)S(1)}, u32[]{:S(2)}, u32[]{:S(2)}) %collective-permute-start.16) | collective-permute-done | bytes 12320 | tf_op jit(solution)/shard_map/ppermute | solution.py:497
  52.7 1.3 %collective-permute-done.17.refs_2_ = bf16[32,192]{1,0:T(8,128)(2,1)S(1)} collective-permute-done((bf16[32,192]{1,0:T(8,128)(2,1)S(1)}, bf16[32,192]{1,0:T(8,128)(2,1)S(1)}, u32[]{:S(2)}, u32[]{:S(2)}) %collective-permute-start.17) | collective-permute-done | bytes 12320 | tf_op jit(solution)/shard_map/ppermute | solution.py:497
  54.2 2.8 %collective-permute-start.20 = (f32[9,192]{1,0:T(8,128)S(1)}, f32[9,192]{1,0:T(8,128)S(1)}, u32[]{:S(2)}, u32[]{:S(2)}) collective-permute-start(f32[9,192]{1,0:T(8,128)S(1)} %get-tuple-element.39), channel_id=1, source_target_pairs={{0,28},{4,8},{8,4},{12,16},{16,12},{20,24},{24,20},{28,0},{1,29},{... | collective-permute-start | bytes 20744 | tf_op jit(solution)/shard_map/ppermute | solution.py:69
  57.0 1.4 %collective-permute-done.20 = f32[9,192]{1,0:T(8,128)S(1)} collective-permute-done((f32[9,192]{1,0:T(8,128)S(1)}, f32[9,192]{1,0:T(8,128)S(1)}, u32[]{:S(2)}, u32[]{:S(2)}) %collective-permute-start.20) | collective-permute-done | bytes 6944 | tf_op jit(solution)/shard_map/ppermute | solution.py:69
  58.4 0.6 %add_add_fusion = f32[9,192]{1,0:T(8,128)} fusion(f32[9,192]{1,0:T(8,128)S(1)} %collective-permute-done.20, f32[9,192]{1,0:T(8,128)S(1)} %get-tuple-element.37, f32[9,192]{1,0:T(8,128)S(1)} %collective-permute-done.19), kind=kLoop, calls=%fused_computation | loop fusion | flops 3456 | bytes 27648 | tf_op jit(solution)/shard_map/add | solution.py:501
  (32 shorter events, 2.4 us)
Async XLA Ops:
  0.6 7.6 %collective-permute-start.2 = (f32[72,80]{1,0:T(8,128)}, f32[72,80]{1,0:T(8,128)S(1)}, u32[]{:S(2)}, u32[]{:S(2)}) collective-permute-start(f32[72,80]{1,0:T(8,128)} %bitcast.11), channel_id=1, source_target_pairs={{0,3},{1,2},{2,1},{3,0},{4,7},{5,6},{6,5},{7,4},{8,11},{9,10},{10,... | collective-permute-start | bytes 69128 | tf_op jit(solution)/shard_map/ppermute | solution.py:60
  5.7 5.1 %collective-permute-start.1 = (f32[72,80]{1,0:T(8,128)}, f32[72,80]{1,0:T(8,128)S(1)}, u32[]{:S(2)}, u32[]{:S(2)}) collective-permute-start(f32[72,80]{1,0:T(8,128)} %bitcast.12), channel_id=1, source_target_pairs={{0,2},{1,3},{2,0},{3,1},{4,6},{5,7},{6,4},{7,5},{8,10},{9,11},{10,... | collective-permute-start | bytes 69128 | tf_op jit(solution)/shard_map/ppermute | solution.py:60
  5.7 5.1 %collective-permute-start = (f32[72,80]{1,0:T(8,128)}, f32[72,80]{1,0:T(8,128)S(1)}, u32[]{:S(2)}, u32[]{:S(2)}) collective-permute-start(f32[72,80]{1,0:T(8,128)} %bitcast.13), channel_id=1, source_target_pairs={{0,1},{1,0},{2,3},{3,2},{4,5},{5,4},{6,7},{7,6},{8,9},{9,8},{10,11... | collective-permute-start | bytes 69128 | tf_op jit(solution)/shard_map/ppermute | solution.py:60
  6.4 7.2 %copy-start = (bf16[24,7,80,320]{3,2,1,0:T(8,128)(2,1)S(1)}, bf16[24,7,80,320]{3,2,1,0:T(8,128)(2,1)}, u32[]{:S(2)}) copy-start(bf16[24,7,80,320]{3,2,1,0:T(8,128)(2,1)} %jac_ref.7) | copy-start | bytes 25804804
  10.9 2.6 %collective-permute-start.3 = (bf16[80,384]{1,0:T(8,128)(2,1)S(1)}, bf16[80,384]{1,0:T(8,128)(2,1)S(1)}, u32[]{:S(2)}, u32[]{:S(2)}) collective-permute-start(bf16[80,384]{1,0:T(8,128)(2,1)S(1)} %columns.2.own_ref), channel_id=1, source_target_pairs={{0,4},{4,0},{8,12},{12,8},{16,20},{20,16},{24,28},{28,24},{1,5},{5... | collective-permute-start | bytes 184328 | tf_op jit(solution)/shard_map/ppermute | solution.py:64
  11.0 5.7 %collective-permute-start.4 = (bf16[80,384]{1,0:T(8,128)(2,1)S(1)}, bf16[80,384]{1,0:T(8,128)(2,1)S(1)}, u32[]{:S(2)}, u32[]{:S(2)}) collective-permute-start(bf16[80,384]{1,0:T(8,128)(2,1)S(1)} %columns.2.own_ref), channel_id=1, source_target_pairs={{0,28},{4,8},{8,4},{12,16},{16,12},{20,24},{24,20},{28,0},{1,29},{... | collective-permute-start | bytes 184328 | tf_op jit(solution)/shard_map/ppermute | solution.py:69
  16.8 6.9 %copy-start.1 = (bf16[24,80,320]{2,1,0:T(8,128)(2,1)S(1)}, bf16[24,80,320]{2,1,0:T(8,128)(2,1)}, u32[]{:S(2)}) copy-start(bf16[24,80,320]{2,1,0:T(8,128)(2,1)} %refs_4_.3) | copy-start | bytes 3686404
  17.1 5.7 %collective-permute-start.7 = (bf16[80,80]{1,0:T(8,128)(2,1)S(1)}, bf16[80,80]{1,0:T(8,128)(2,1)S(1)}, u32[]{:S(2)}, u32[]{:S(2)}) collective-permute-start(bf16[80,80]{1,0:T(8,128)(2,1)S(1)} %far.2.refs_0_), channel_id=1, source_target_pairs={{0,3},{1,2},{2,1},{3,0},{4,7},{5,6},{6,5},{7,4},{8,11},{9,10},{10,... | collective-permute-start | bytes 38408 | tf_op jit(solution)/shard_map/ppermute | solution.py:60
  18.7 4.9 %collective-permute-start.6 = (bf16[80,80]{1,0:T(8,128)(2,1)S(1)}, bf16[80,80]{1,0:T(8,128)(2,1)S(1)}, u32[]{:S(2)}, u32[]{:S(2)}) collective-permute-start(bf16[80,80]{1,0:T(8,128)(2,1)S(1)} %far.2.refs_0_), channel_id=1, source_target_pairs={{0,2},{1,3},{2,0},{3,1},{4,6},{5,7},{6,4},{7,5},{8,10},{9,11},{10,... | collective-permute-start | bytes 38408 | tf_op jit(solution)/shard_map/ppermute | solution.py:60
  19.3 4.4 %collective-permute-start.5 = (bf16[80,80]{1,0:T(8,128)(2,1)S(1)}, bf16[80,80]{1,0:T(8,128)(2,1)S(1)}, u32[]{:S(2)}, u32[]{:S(2)}) collective-permute-start(bf16[80,80]{1,0:T(8,128)(2,1)S(1)} %far.2.refs_0_), channel_id=1, source_target_pairs={{0,1},{1,0},{2,3},{3,2},{4,5},{5,4},{6,7},{7,6},{8,9},{9,8},{10,11... | collective-permute-start | bytes 38408 | tf_op jit(solution)/shard_map/ppermute | solution.py:60
  24.5 5.6 %collective-permute-start.10 = (bf16[80,80]{1,0:T(8,128)(2,1)S(1)}, bf16[80,80]{1,0:T(8,128)(2,1)S(1)}, u32[]{:S(2)}, u32[]{:S(2)}) collective-permute-start(bf16[80,80]{1,0:T(8,128)(2,1)S(1)} %get-tuple-element.27.refs_0_), channel_id=1, source_target_pairs={{0,3},{1,2},{2,1},{3,0},{4,7},{5,6},{6,5},{7,4},{8,11},{9,10},{10,... | collective-permute-start | bytes 38408 | tf_op jit(solution)/shard_map/ppermute | solution.py:60
  26.8 4.7 %collective-permute-start.9 = (bf16[80,80]{1,0:T(8,128)(2,1)S(1)}, bf16[80,80]{1,0:T(8,128)(2,1)S(1)}, u32[]{:S(2)}, u32[]{:S(2)}) collective-permute-start(bf16[80,80]{1,0:T(8,128)(2,1)S(1)} %get-tuple-element.27.refs_0_), channel_id=1, source_target_pairs={{0,2},{1,3},{2,0},{3,1},{4,6},{5,7},{6,4},{7,5},{8,10},{9,11},{10,... | collective-permute-start | bytes 38408 | tf_op jit(solution)/shard_map/ppermute | solution.py:60
  27.7 4.0 %collective-permute-start.8 = (bf16[80,80]{1,0:T(8,128)(2,1)S(1)}, bf16[80,80]{1,0:T(8,128)(2,1)S(1)}, u32[]{:S(2)}, u32[]{:S(2)}) collective-permute-start(bf16[80,80]{1,0:T(8,128)(2,1)S(1)} %get-tuple-element.27.refs_0_), channel_id=1, source_target_pairs={{0,1},{1,0},{2,3},{3,2},{4,5},{5,4},{6,7},{7,6},{8,9},{9,8},{10,11... | collective-permute-start | bytes 38408 | tf_op jit(solution)/shard_map/ppermute | solution.py:60
  31.8 2.9 %collective-permute-start.11 = (bf16[80,384]{1,0:T(8,128)(2,1)S(1)}, bf16[80,384]{1,0:T(8,128)(2,1)S(1)}, u32[]{:S(2)}, u32[]{:S(2)}) collective-permute-start(bf16[80,384]{1,0:T(8,128)(2,1)S(1)} %columns.3.own_ref), channel_id=1, source_target_pairs={{0,4},{4,0},{8,12},{12,8},{16,20},{20,16},{24,28},{28,24},{1,5},{5... | collective-permute-start | bytes 184328 | tf_op jit(solution)/shard_map/ppermute | solution.py:64
  31.9 6.1 %collective-permute-start.12 = (bf16[80,384]{1,0:T(8,128)(2,1)S(1)}, bf16[80,384]{1,0:T(8,128)(2,1)S(1)}, u32[]{:S(2)}, u32[]{:S(2)}) collective-permute-start(bf16[80,384]{1,0:T(8,128)(2,1)S(1)} %columns.3.own_ref), channel_id=1, source_target_pairs={{0,28},{4,8},{8,4},{12,16},{16,12},{20,24},{24,20},{28,0},{1,29},{... | collective-permute-start | bytes 184328 | tf_op jit(solution)/shard_map/ppermute | solution.py:69
  37.9 4.8 %copy-start.3 = (bf16[24,80,192]{2,1,0:T(8,128)(2,1)S(1)}, bf16[24,80,192]{2,1,0:T(8,128)(2,1)}, u32[]{:S(2)}) copy-start(bf16[24,80,192]{2,1,0:T(8,128)(2,1)} %shape_ref.1) | copy-start | bytes 2211844
  37.9 4.8 %copy-start.4 = (s32[24,64]{1,0:T(8,128)S(1)}, s32[24,64]{1,0:T(8,128)}, u32[]{:S(2)}) copy-start(s32[24,64]{1,0:T(8,128)} %ids_ref.1) | copy-start | bytes 18436
  38.0 6.9 %copy-start.2 = (bf16[24,80,320]{2,1,0:T(8,128)(2,1)S(1)}, bf16[24,80,320]{2,1,0:T(8,128)(2,1)}, u32[]{:S(2)}) copy-start(bf16[24,80,320]{2,1,0:T(8,128)(2,1)} %refs_4_.3) | copy-start | bytes 3686404
  38.2 5.7 %collective-permute-start.15 = (bf16[80,80]{1,0:T(8,128)(2,1)S(1)}, bf16[80,80]{1,0:T(8,128)(2,1)S(1)}, u32[]{:S(2)}, u32[]{:S(2)}) collective-permute-start(bf16[80,80]{1,0:T(8,128)(2,1)S(1)} %far.3.refs_0_), channel_id=1, source_target_pairs={{0,3},{1,2},{2,1},{3,0},{4,7},{5,6},{6,5},{7,4},{8,11},{9,10},{10,... | collective-permute-start | bytes 38408 | tf_op jit(solution)/shard_map/ppermute | solution.py:60
  40.0 4.9 %collective-permute-start.14 = (bf16[80,80]{1,0:T(8,128)(2,1)S(1)}, bf16[80,80]{1,0:T(8,128)(2,1)S(1)}, u32[]{:S(2)}, u32[]{:S(2)}) collective-permute-start(bf16[80,80]{1,0:T(8,128)(2,1)S(1)} %far.3.refs_0_), channel_id=1, source_target_pairs={{0,2},{1,3},{2,0},{3,1},{4,6},{5,7},{6,4},{7,5},{8,10},{9,11},{10,... | collective-permute-start | bytes 38408 | tf_op jit(solution)/shard_map/ppermute | solution.py:60
  40.9 4.0 %collective-permute-start.13 = (bf16[80,80]{1,0:T(8,128)(2,1)S(1)}, bf16[80,80]{1,0:T(8,128)(2,1)S(1)}, u32[]{:S(2)}, u32[]{:S(2)}) collective-permute-start(bf16[80,80]{1,0:T(8,128)(2,1)S(1)} %far.3.refs_0_), channel_id=1, source_target_pairs={{0,1},{1,0},{2,3},{3,2},{4,5},{5,4},{6,7},{7,6},{8,9},{9,8},{10,11... | collective-permute-start | bytes 38408 | tf_op jit(solution)/shard_map/ppermute | solution.py:60
  47.1 5.5 %collective-permute-start.16 = (bf16[32,192]{1,0:T(8,128)(2,1)S(1)}, bf16[32,192]{1,0:T(8,128)(2,1)S(1)}, u32[]{:S(2)}, u32[]{:S(2)}) collective-permute-start(bf16[32,192]{1,0:T(8,128)(2,1)S(1)} %get-tuple-element.34), channel_id=1, source_target_pairs={{0,3},{1,2},{2,1},{3,0},{4,7},{5,6},{6,5},{7,4},{8,11},{9,10},{10,... | collective-permute-start | bytes 36872 | tf_op jit(solution)/shard_map/ppermute | solution.py:497
  49.3 4.7 %collective-permute-start.17 = (bf16[32,192]{1,0:T(8,128)(2,1)S(1)}, bf16[32,192]{1,0:T(8,128)(2,1)S(1)}, u32[]{:S(2)}, u32[]{:S(2)}) collective-permute-start(bf16[32,192]{1,0:T(8,128)(2,1)S(1)} %get-tuple-element.35), channel_id=1, source_target_pairs={{0,2},{1,3},{2,0},{3,1},{4,6},{5,7},{6,4},{7,5},{8,10},{9,11},{10,... | collective-permute-start | bytes 36872 | tf_op jit(solution)/shard_map/ppermute | solution.py:497
  50.2 3.9 %collective-permute-start.18 = (bf16[32,192]{1,0:T(8,128)(2,1)S(1)}, bf16[32,192]{1,0:T(8,128)(2,1)S(1)}, u32[]{:S(2)}, u32[]{:S(2)}) collective-permute-start(bf16[32,192]{1,0:T(8,128)(2,1)S(1)} %get-tuple-element.36), channel_id=1, source_target_pairs={{0,1},{1,0},{2,3},{3,2},{4,5},{5,4},{6,7},{7,6},{8,9},{9,8},{10,11... | collective-permute-start | bytes 36872 | tf_op jit(solution)/shard_map/ppermute | solution.py:497
  54.1 2.9 %collective-permute-start.19 = (f32[9,192]{1,0:T(8,128)S(1)}, f32[9,192]{1,0:T(8,128)S(1)}, u32[]{:S(2)}, u32[]{:S(2)}) collective-permute-start(f32[9,192]{1,0:T(8,128)S(1)} %get-tuple-element.38), channel_id=1, source_target_pairs={{0,4},{4,0},{8,12},{12,8},{16,20},{20,16},{24,28},{28,24},{1,5},{5... | collective-permute-start | bytes 20744 | tf_op jit(solution)/shard_map/ppermute | solution.py:64
  54.2 4.3 %collective-permute-start.20 = (f32[9,192]{1,0:T(8,128)S(1)}, f32[9,192]{1,0:T(8,128)S(1)}, u32[]{:S(2)}, u32[]{:S(2)}) collective-permute-start(f32[9,192]{1,0:T(8,128)S(1)} %get-tuple-element.39), channel_id=1, source_target_pairs={{0,28},{4,8},{8,4},{12,16},{16,12},{20,24},{24,20},{28,0},{1,29},{... | collective-permute-start | bytes 20744 | tf_op jit(solution)/shard_map/ppermute | solution.py:69

commit v4 on v3

--- a/solution.py
+++ b/solution.py
@@ -17,7 +17,7 @@
 VMEM = pl.BlockSpec(memory_space=pltpu.VMEM)
 SMEM = pl.BlockSpec(memory_space=pltpu.SMEM)
 HBM = pl.BlockSpec(memory_space=pltpu.HBM)
-GROUP = 30
+GROUP = 60
 MIB = 1024 * 1024
 
 
@@ -156,17 +156,13 @@
         same = iota(shape, 0) == low[group : group + 1, :]
         low_out[:, group * LANES : (group + 1) * LANES] = hit(same).astype(HALF)
 
-    elements, width, coords = shape_ref.shape
-    shape = (coords, shape_out.shape[2])
-    row, lane = iota(shape, 0), iota(shape, 1)
-    axis = jnp.where(lane >= LANES, 1, 0) + jnp.where(lane >= 2 * LANES, 1, 0)
-    side = lane - axis * LANES
-    for odd in range(2):
-        place = side - odd * (LANES // 2)
-        inside = jnp.logical_and(place >= 0, place < LANES // 2)
-        sort = hit(jnp.logical_and(inside, row == 3 * place + axis)).astype(HALF)
-        for e in range(odd, elements, 2):
-            shape_out[e] = jnp.dot(shape_ref[e], sort, preferred_element_type=FULL).astype(HALF)
+    elements, _, coords = shape_ref.shape
+    nodes = coords // 3
+    row, lane = iota((coords, coords), 0), iota((coords, coords), 1)
+    axis = jnp.where(lane >= nodes, 1, 0) + jnp.where(lane >= 2 * nodes, 1, 0)
+    sort = hit(row == 3 * (lane - axis * nodes) + axis).astype(HALF)
+    for e in range(elements):
+        shape_out[e] = jnp.dot(shape_ref[e], sort, preferred_element_type=FULL).astype(HALF)
 
 
 def widened(block, lanes):
@@ -176,35 +172,76 @@
     return jnp.concatenate([block, jnp.zeros((block.shape[0], short), block.dtype)], axis=1)
 
 
+def laid(blocks, width, stride):
+    lane = iota(blocks[0].shape, 1)
+    tiles = [0.0] * (stride // LANES)
+    for place, block in enumerate(blocks):
+        tile, offset = divmod(place * width, LANES)
+        if offset:
+            block = pltpu.roll(block, offset, 1)
+        if offset + width <= LANES:
+            tiles[tile] = tiles[tile] + block
+        else:
+            tiles[tile] = tiles[tile] + jnp.where(lane >= offset, block, 0.0)
+            tiles[tile + 1] = tiles[tile + 1] + jnp.where(lane < offset, block, 0.0)
+    return tiles
+
+
 def put_columns(blocks, order, stride):
     blk = lax.axis_index("blk")
     width = blocks[0].shape[1]
     blocks = [widened(block.astype(FULL), LANES) for block in blocks]
-    lane = iota(blocks[0].shape, 1)
-    tiles = [0.0] * (stride // LANES)
+    placed = []
     for owner in range(len(blocks)):
         found = blocks[0]
         for k, block in zip(order, blocks[1:]):
             found = jnp.where((blk ^ owner) == k, block, found)
-        tile, offset = divmod(owner * width, LANES)
-        if offset:
-            found = pltpu.roll(found, offset, 1)
-        if offset + width <= LANES:
-            tiles[tile] = tiles[tile] + found
-        else:
-            tiles[tile] = tiles[tile] + jnp.where(lane >= offset, found, 0.0)
-            tiles[tile + 1] = tiles[tile + 1] + jnp.where(lane < offset, found, 0.0)
-    return jnp.concatenate(tiles, axis=1).astype(HALF)
-
-
-def columns_kernel(order, *refs):
+        placed.append(found)
+    return laid(placed, width, stride)
+
+
+def cut_of(rows, full):
+    tail = full % LANES
+    if tail == 0:
+        return 0
+    return round_up(rows // 2, 8) if tail <= LANES // 2 else rows
+
+
+def packed_rows(rows, full):
+    return round_up(full // LANES * rows + cut_of(rows, full), 16)
+
+
+def columns_kernel(order, rows, full, *refs):
     *blocks, out_ref = refs
-    rows, stride = out_ref.shape
-    out_ref[...] = put_columns([rounded(ref[...], rows) for ref in blocks], order, stride)
+    tiles = put_columns([ref[...] for ref in blocks], order, round_up(full, LANES))
+    cut = cut_of(rows, full)
+    parts = [tile[:rows] for tile in tiles[: full // LANES]]
+    if cut:
+        last = tiles[-1][:cut]
+        if cut < rows:
+            lower = pltpu.roll(tiles[-1][cut:rows], LANES // 2, 1)
+            last = last + jnp.concatenate([lower, jnp.zeros((2 * cut - rows, LANES), FULL)], axis=0)
+        parts.append(last)
+    out_ref[...] = rounded(jnp.concatenate(parts, axis=0), out_ref.shape[0])
+
+
+def unpacked(ref, rows, full):
+    block = ref[...].astype(FULL)
+    whole, cut = full // LANES, cut_of(rows, full)
+    tiles = [block[i * rows : (i + 1) * rows] for i in range(whole)]
+    if cut:
+        last = block[whole * rows : whole * rows + cut]
+        if cut < rows:
+            low = iota(last.shape, 1) < LANES // 2
+            lower = pltpu.roll(jnp.where(low, 0.0, last), LANES // 2, 1)
+            last = jnp.concatenate([jnp.where(low, last, 0.0), lower[: rows - cut]], axis=0)
+        tiles.append(last)
+    return rounded(jnp.concatenate(tiles, axis=1), round_up(rows, 16))
 
 
 def near_kernel(own_ref, mate_ref, pick_ref, shift_ref, adj_ref, rhs_ref, jac_ref, _, out_ref, image):
-    products([own_ref[...], mate_ref[...]], pick_ref, jac_ref, image)
+    rows, full = adj_ref.shape[0], jac_ref.shape[3]
+    products([unpacked(own_ref, rows, full), unpacked(mate_ref, rows, full)], pick_ref, jac_ref, image)
     out_ref[...] = without(shift_ref, adj_ref, rhs_ref, image)
 
 
@@ -233,28 +270,50 @@
             image[pl.ds(e, 3, stride=elements), :width] = product[first : first + 3]
 
 
+def pair_products(lefts, blocks):
+    full = blocks[0].shape[1]
+    deep = full // (2 * LANES) * (2 * LANES)
+    lower = iota((2 * PICK, LANES), 0) >= PICK
+    mine = [jnp.logical_not(lower), lower]
+    rest = [jnp.where(mine[i], lefts[i][:, deep : deep + LANES], 0.0).astype(HALF) for i in range(2)]
+    blocks_rest = [widened(block[:, deep:], LANES) for block in blocks]
+    shared = lax.dot_general(
+        jnp.concatenate(rest, axis=1), jnp.concatenate(blocks_rest, axis=1), NT, preferred_element_type=FULL
+    )
+    products = []
+    for i, (left, block) in enumerate(zip(lefts, blocks)):
+        product = lax.dot_general(left[:, :deep], block[:, :deep], NT, preferred_element_type=FULL)
+        half = slice(i * PICK, (i + 1) * PICK)
+        products.append(product[half] + shared[half])
+    return products
+
+
 def far_kernel(near_ref, far_ref, jac_ref, list_ref, count_ref, _shapes, _ids, out_ref, spread, sums, image):
     elements, slots, width, _ = jac_ref.shape
-    rows, stride = far_ref.shape
+    far = unpacked(far_ref, near_ref.shape[0], jac_ref.shape[3])
+    rows, stride = far.shape
     deep = spread.shape[1]
     shape = (elements, deep, rows)
     element, row, lane = [iota(shape, dim).reshape(elements * deep, rows) for dim in range(3)]
+    row = row - jnp.where(row >= PICK, PICK, 0)
     pick = hit(jnp.where(row < 3, row * elements + element, -1) == lane).astype(HALF)
-    taken = jnp.dot(pick, far_ref[...], preferred_element_type=FULL).astype(HALF)
+    taken = jnp.dot(pick, far, preferred_element_type=FULL).astype(HALF)
     spread[:elements] = taken.reshape(elements, deep, stride)
     spread[elements:] = jnp.zeros((spread.shape[0] - elements, deep, stride), HALF)
     sums[...] = jnp.zeros(sums.shape, FULL)
 
     @pl.loop(0, count_ref[0])
     def _(step):
-        for i in range(GROUP):
-            word = list_ref[step * GROUP + i]
-            block = lax.shift_right_logical(word, 5)
-            place = lax.bitwise_and(word, 31)
-            e = lax.div(block, slots)
-            blocks = widened(jac_ref[e, block - e * slots], stride)
-            product = lax.dot_general(spread[place], blocks, NT, preferred_element_type=FULL)
-            sums[e, :, :width] += product[:PICK]
+        for i in range(0, GROUP, 2):
+            owners, lefts, blocks = [], [], []
+            for side in range(2):
+                word = list_ref[step * GROUP + i + side]
+                block = lax.shift_right_logical(word, 5)
+                owners.append(lax.div(block, slots))
+                lefts.append(spread[lax.bitwise_and(word, 31)])
+                blocks.append(jac_ref[owners[side], block - owners[side] * slots])
+            for e, product in zip(owners, pair_products(lefts, blocks)):
+                sums[e, :, :width] += product
 
     for e in range(elements):
         image[pl.ds(e, 3, stride=elements), :] = sums[e, :3, :]
@@ -274,6 +333,7 @@
     elements = rows // 3
     stride = round_up(inv_ref.shape[2], LANES)
     resid = put_columns([ref[...] for ref in resid_refs], distances(), stride)
+    resid = jnp.concatenate(resid, axis=1).astype(HALF)
     shape = (elements, PICK, resid.shape[0])
     deep = elements * PICK
     element, row, lane = [iota(shape, dim).reshape(deep, -1) for dim in range(3)]
@@ -282,11 +342,8 @@
     update[...] = jnp.zeros(update.shape, FULL)
     for pair in range(elements // 2):
         left = resid[pair * 2 * PICK : (pair + 1) * 2 * PICK]
-        for side in range(2):
-            e = 2 * pair + side
-            product = lax.dot_general(left, widened(inv_ref[e], stride), NT, preferred_element_type=FULL)
-            first = side * PICK
-            update[pl.ds(e, 3, stride=elements), :width] = product[first : first + 3]
+        for side, product in enumerate(pair_products([left, left], [inv_ref[2 * pair], inv_ref[2 * pair + 1]])):
+            update[pl.ds(2 * pair + side, 3, stride=elements), :width] = product[:3]
     short = jnp.zeros((update.shape[0] - rows, width), FULL)
     return jnp.concatenate([adj_ref[...] + update[:rows, :width], short], axis=0)
 
@@ -307,8 +364,8 @@
     blks = lax.axis_size("blk")
     resid_refs = refs[:blks]
     inv_ref, adj_ref, shape_ref, low_ref, target_ref, adj_out = refs[blks : blks + 6]
-    piece_outs = refs[blks + 6 : 2 * blks + 6]
-    sorted_ref, left_ref, sums_ref, update = refs[2 * blks + 6 :]
+    part_outs = refs[blks + 6 : blks + 9]
+    sorted_ref, left_ref, sums_ref, update = refs[blks + 9 :]
     adj = updated(resid_refs, inv_ref, adj_ref, update)
     adj_out[...] = adj[: adj_out.shape[0]]
     half = adj.astype(HALF)
@@ -317,12 +374,8 @@
     tall, width = half.shape
     coords = shape_ref.shape[2]
     depth = 3 if elements % 3 == 0 and 3 * width <= 256 else 1
-    shape = (width, depth * width)
-    row, lane = iota(shape, 0), iota(shape, 1)
-    repeat = jnp.zeros(shape, FULL)
-    for step in range(depth):
-        repeat = repeat + hit(lane == row + step * width)
-    left = jnp.dot(half, repeat.astype(HALF), preferred_element_type=FULL)
+    block = widened(half.astype(FULL), LANES)
+    left = jnp.concatenate(laid([block] * depth, width, round_up(depth * width, LANES)), axis=1)[:, : depth * width]
     shape = left.shape
     owner = element_of_row(shape, elements)
     group = jnp.zeros(shape, jnp.int32)
@@ -338,7 +391,16 @@
         partials = jnp.concatenate([shape_ref[start + step] for step in range(depth)], axis=0)
         product = jnp.dot(left, partials, preferred_element_type=FULL)
         total = jnp.where(owner >= start, product, total)
-    top, rest = split(total)
+    low = iota((tall, LANES), 1) < LANES // 2
+    odd = lax.bitwise_and(owner[:, :LANES], 1) == 1
+    values = [total[:, :LANES], widened(total[:, LANES:], LANES)]
+    turned = [pltpu.roll(value, LANES // 2, 1) for value in values]
+    value = [
+        jnp.where(odd, jnp.where(low, 0.0, turned[0]), jnp.where(low, values[0], 0.0)),
+        jnp.where(odd, jnp.where(low, 0.0, values[0]), jnp.where(low, turned[0], 0.0)),
+        jnp.where(odd, turned[1], values[1]),
+    ]
+    top, rest = split(jnp.concatenate(value, axis=1))
     sorted_ref[:tall] = top.astype(FULL)
     sorted_ref[tall:] = rest.astype(FULL)
     deep = 16
@@ -359,21 +421,18 @@
     tiles = [(tile, tile * LANES, min(span, (tile + 1) * LANES)) for tile in range(sums_ref.shape[0])]
     for tile, start, stop in tiles:
         sums_ref[tile, :, : stop - start] = sums[:, start:stop]
+    for part, out_ref in enumerate(part_outs):
+        for tile, start, stop in tiles:
+            found = [sums_ref[tile, pl.ds(part * blks + k, 9, stride=deep), :][:, : stop - start] for k in range(blks)]
+            found = jnp.concatenate(found + [jnp.zeros((out_ref.shape[0] - 9 * blks, stop - start), FULL)], axis=0)
+            out_ref[:, start:stop] = found.astype(out_ref.dtype)
+
+
+def combine_kernel(own_ref, mate_ref, far_ref, *piece_outs):
+    total = own_ref[...] + mate_ref[...].astype(FULL) + far_ref[...].astype(FULL)
     for k, out_ref in enumerate(piece_outs):
-        for tile, start, stop in tiles:
-            found = [sums_ref[tile, pl.ds(part * blks + k, 9, stride=deep), :][:, : stop - start] for part in range(3)]
-            found = jnp.concatenate(found + [jnp.zeros((5, stop - start), FULL)], axis=0)
-            out_ref[:, start:stop] = found.astype(out_ref.dtype)
-
-
-def combine_kernel(*refs):
-    *piece_refs, own_out, mate_out, far_out = refs
-    total = piece_refs[0][...]
-    for ref in piece_refs[1:]:
-        total = total + ref[...].astype(FULL)
-    own_out[...] = total[:9]
-    mate_out[...] = total[9:18]
-    far_out[...] = total[18:27]
+        piece = total[9 * k : 9 * (k + 1)]
+        out_ref[...] = rounded(piece, 16) if k else piece
 
 
 def local(
@@ -431,7 +490,7 @@
         [
             jax.ShapeDtypeStruct((span, entries), HALF),
             jax.ShapeDtypeStruct((entries // LANES, LANES), jnp.int32),
-            jax.ShapeDtypeStruct((elements, width, 3 * LANES), HALF),
+            jax.ShapeDtypeStruct(shape_partials.shape, HALF),
         ],
         moved=3 * MIB,
     )
@@ -439,8 +498,8 @@
     for sweep in range(SWEEPS):
         order = distances()
         blocks = [half] + over_blk(half, order) if sweep else [adj] + over_blk(adj_hbm, order)
-        wide = jax.ShapeDtypeStruct((tall, stride), HALF)
-        (own,) = call(functools.partial(columns_kernel, order), "columns", blocks, [VMEM] * blks, [wide], moved=1 * MIB)
+        wide = jax.ShapeDtypeStruct((packed_rows(rows, full), LANES), HALF)
+        (own,) = call(functools.partial(columns_kernel, order, rows, full), "columns", blocks, [VMEM] * blks, [wide], moved=1 * MIB)
         far, mate = to_far(own), to_mate(own)
         image = pltpu.VMEM((tall, LANES), FULL)
         near_inputs = [own, mate, pick, shift, adj, rhs]
@@ -478,13 +537,13 @@
                 scratch=[pltpu.VMEM((tall, LANES), FULL)],
                 moved=8 * MIB,
             )
-    pieces = [jax.ShapeDtypeStruct((32, span), HALF if k else FULL) for k in range(blks)]
-    adj, *pieces = call(
+    deep = round_up(9 * blks, 16)
+    adj, own, mate, far = call(
         gradient_kernel,
         "gradient",
         resids + [block_inverse, adj, shapes, low, target],
         [VMEM] * (blks + 5),
-        [adj_shape] + pieces,
+        [adj_shape] + [jax.ShapeDtypeStruct((deep, span), kind) for kind in (FULL, HALF, HALF)],
         scratch=[
             pltpu.VMEM((2 * tall, 3 * LANES), FULL),
             pltpu.VMEM((2 * 9 * 16, entries), HALF),
@@ -492,13 +551,15 @@
             pltpu.VMEM((tall, LANES), FULL),
         ],
     )
+    far, mate = to_far(far), to_mate(mate)
+    shapes = [jax.ShapeDtypeStruct((16, span), HALF)] * (blks - 1)
+    pieces = call(
+        combine_kernel, "combine", [own, mate, far], [VMEM] * 3, [jax.ShapeDtypeStruct((9, span), FULL)] + shapes
+    )
+    gradient = pieces[0]
     count = lax.axis_size("blk")
-    received = [
-        lax.ppermute(pieces[k], "blk", [(i, i ^ k) for i in range(count)]) for k in reversed(distances())
-    ]
-    third = jax.ShapeDtypeStruct((9, span), FULL)
-    own, mate, far = call(combine_kernel, "combine", [pieces[0]] + received, [VMEM] * blks, [third] * 3)
-    gradient = own + to_mate(mate) + to_far(far)
+    for k in reversed(distances()):
+        gradient = gradient + lax.ppermute(pieces[k], "blk", [(i, i ^ k) for i in range(count)])[:9].astype(FULL)
     adjoint = jnp.transpose(adj.reshape(sides, elements, width), (1, 0, 2))
     return (adjoint, gradient)
 

time: 59.2 us -> 58.2 us (0.983)
  starting transfers between devices: 31.8 us -> 30.4 us
  waiting for transfers between devices: 12.8 us -> 14.1 us
    ppermute x3, starting transfers between devices: 8.17 us -> 6.66 us  [to_far(): lax.ppermute(block, 'dom', [(i, ((i + 1 ^ 1) - 1) % count) for i in range...]
    ppermute x3, waiting for transfers between devices: 1.45 us -> 2.44 us  [to_far(): lax.ppermute(block, 'dom', [(i, ((i + 1 ^ 1) - 1) % count) for i in range...]
where the time goes in v4:
time: 58.2 us
  starting transfers between devices  30.4 us (52%)
  waiting for transfers between devices  14.1 us (24%)
  Pallas kernels  12.3 us (21%)
  between operations  0.75 us (1%)
  other arithmetic  0.61 us (1%)
    ppermute x12, starting transfers between devices, over_blk(): lax.ppermute(block, 'blk', [(i, i ^ k) for i in range(count)])  19.1 us
    pallas_call x11, Pallas kernels, call(): pl.pallas_call(kernel, in_specs=specs, out_specs=[SMEM if getattr(out, 'm...  12.3 us
    ppermute x12, waiting for transfers between devices, over_blk(): lax.ppermute(block, 'blk', [(i, i ^ k) for i in range(count)])  9.33 us
    ppermute x3, starting transfers between devices, to_far(): lax.ppermute(block, 'dom', [(i, ((i + 1 ^ 1) - 1) % count) for i in range...  6.66 us
    ppermute x3, starting transfers between devices, local(): lax.ppermute(pieces[k], 'blk', [(i, i ^ k) for i in range(count)])[:9]  4.45 us
    ppermute x3, waiting for transfers between devices, to_far(): lax.ppermute(block, 'dom', [(i, ((i + 1 ^ 1) - 1) % count) for i in range...  2.44 us
    ppermute x3, waiting for transfers between devices, local(): lax.ppermute(pieces[k], 'blk', [(i, i ^ k) for i in range(count)])[:9]  2.34 us
  transfers between devices with their start and end apart: 21, of which 12 were waited for; matrix products, arithmetic and copies ran while one was open for 0% of the time, Pallas kernels for 15%

profile of v4, /device:TPU:0, one launch (start us, length us, event | category | flops | bytes accessed | tf_op | source)
XLA Modules:
  0.0 58.2 jit_solution(17711590585874727962)
XLA Ops:
  0.6 5.1 %collective-permute-start.2 = (f32[72,80]{1,0:T(8,128)}, f32[72,80]{1,0:T(8,128)S(1)}, u32[]{:S(2)}, u32[]{:S(2)}) collective-permute-start(f32[72,80]{1,0:T(8,128)} %bitcast.11), channel_id=1, source_target_pairs={{0,3},{1,2},{2,1},{3,0},{4,7},{5,6},{6,5},{7,4},{8,11},{9,10},{10,... | collective-permute-start | bytes 69128 | tf_op jit(solution)/shard_map/ppermute | solution.py:60
  5.8 0.6 %collective-permute-start = (f32[72,80]{1,0:T(8,128)}, f32[72,80]{1,0:T(8,128)S(1)}, u32[]{:S(2)}, u32[]{:S(2)}) collective-permute-start(f32[72,80]{1,0:T(8,128)} %bitcast.13), channel_id=1, source_target_pairs={{0,1},{1,0},{2,3},{3,2},{4,5},{5,4},{6,7},{7,6},{8,9},{9,8},{10,11... | collective-permute-start | bytes 69128 | tf_op jit(solution)/shard_map/ppermute | solution.py:60
  6.4 1.8 %slots.1 = (bf16[1344,256]{1,0:T(8,128)(2,1)S(1)}, f32[80,128]{1,0:T(8,128)S(1)}, s32[256]{0:T(256)S(4)}, s32[1]{0:T(128)S(4)}, f32[72,80]{1,0:T(8,128)S(1)}, /*index=5*/f32[72,80]{1,0:T(8,128)S(1)}) custom-call(s32[6,24]{1,0:T(8,128)} %bitcast.15, f32[24]{0:T(128)} %shift_hbm.1, f32[72,80]{1,0:T(8,128)} %bitcast.14, f32[72,80]{1,0:T(8,128)} %bitcast.10, ...), custom_call_target="tpu_custom_call" | custom-call | bytes 16777216 | tf_op jit(solution)/shard_map/slots/pallas_call | solution.py:41
  8.2 2.6 %collective-permute-done.1.refs_2_ = f32[72,80]{1,0:T(8,128)S(1)} collective-permute-done((f32[72,80]{1,0:T(8,128)}, f32[72,80]{1,0:T(8,128)S(1)}, u32[]{:S(2)}, u32[]{:S(2)}) %collective-permute-start.1) | collective-permute-done | bytes 23072 | tf_op jit(solution)/shard_map/ppermute | solution.py:60
  11.0 2.5 %collective-permute-start.4 = (bf16[192,128]{1,0:T(8,128)(2,1)S(1)}, bf16[192,128]{1,0:T(8,128)(2,1)S(1)}, u32[]{:S(2)}, u32[]{:S(2)}) collective-permute-start(bf16[192,128]{1,0:T(8,128)(2,1)S(1)} %columns.2.own_ref), channel_id=1, source_target_pairs={{0,28},{4,8},{8,4},{12,16},{16,12},{20,24},{24,20},{28,0},{1,29},{... | collective-permute-start | bytes 147464 | tf_op jit(solution)/shard_map/ppermute | solution.py:69
  13.6 3.3 %near.2.near_ref = f32[72,80]{1,0:T(8,128)S(1)} custom-call(bf16[192,128]{1,0:T(8,128)(2,1)S(1)} %columns.2.own_ref, bf16[192,128]{1,0:T(8,128)(2,1)S(1)} %collective-permute-done.3.mate_ref, bf16[1344,256]{1,0:T(8,128)(2,1)S(1)} %get-tuple-element.22.pick_ref, f32[80,128]{1,0:T(8,128)S(1)} %get-tuple-element.23.shift_ref, ...), custom_call_target="tpu_custom_call" | custom-call | bytes 12582912 | tf_op jit(solution)/shard_map/near/pallas_call | solution.py:41
  17.2 1.6 %collective-permute-start.7 = (bf16[80,80]{1,0:T(8,128)(2,1)S(1)}, bf16[80,80]{1,0:T(8,128)(2,1)S(1)}, u32[]{:S(2)}, u32[]{:S(2)}) collective-permute-start(bf16[80,80]{1,0:T(8,128)(2,1)S(1)} %far.2.refs_0_), channel_id=1, source_target_pairs={{0,3},{1,2},{2,1},{3,0},{4,7},{5,6},{6,5},{7,4},{8,11},{9,10},{10,... | collective-permute-start | bytes 38408 | tf_op jit(solution)/shard_map/ppermute | solution.py:60
  18.8 0.6 %collective-permute-start.6 = (bf16[80,80]{1,0:T(8,128)(2,1)S(1)}, bf16[80,80]{1,0:T(8,128)(2,1)S(1)}, u32[]{:S(2)}, u32[]{:S(2)}) collective-permute-start(bf16[80,80]{1,0:T(8,128)(2,1)S(1)} %far.2.refs_0_), channel_id=1, source_target_pairs={{0,2},{1,3},{2,0},{3,1},{4,6},{5,7},{6,4},{7,5},{8,10},{9,11},{10,... | collective-permute-start | bytes 38408 | tf_op jit(solution)/shard_map/ppermute | solution.py:60
  19.4 2.3 %collective-permute-start.5 = (bf16[80,80]{1,0:T(8,128)(2,1)S(1)}, bf16[80,80]{1,0:T(8,128)(2,1)S(1)}, u32[]{:S(2)}, u32[]{:S(2)}) collective-permute-start(bf16[80,80]{1,0:T(8,128)(2,1)S(1)} %far.2.refs_0_), channel_id=1, source_target_pairs={{0,1},{1,0},{2,3},{3,2},{4,5},{5,4},{6,7},{7,6},{8,9},{9,8},{10,11... | collective-permute-start | bytes 38408 | tf_op jit(solution)/shard_map/ppermute | solution.py:60
  21.7 1.3 %collective-permute-done.7.refs_3_ = bf16[80,80]{1,0:T(8,128)(2,1)S(1)} collective-permute-done((bf16[80,80]{1,0:T(8,128)(2,1)S(1)}, bf16[80,80]{1,0:T(8,128)(2,1)S(1)}, u32[]{:S(2)}, u32[]{:S(2)}) %collective-permute-start.7) | collective-permute-done | bytes 12832 | tf_op jit(solution)/shard_map/ppermute | solution.py:60
  23.7 0.7 %update.1 = (f32[72,80]{1,0:T(8,128)S(1)}, bf16[80,80]{1,0:T(8,128)(2,1)S(1)}) custom-call(bf16[80,80]{1,0:T(8,128)(2,1)S(1)} %far.2.refs_0_, bf16[80,80]{1,0:T(8,128)(2,1)S(1)} %collective-permute-done.5.refs_1_, bf16[80,80]{1,0:T(8,128)(2,1)S(1)} %collective-permute-done.6.refs_2_, bf16[80,80]{1,0:T(8,128)(2,1)S(1)} %collective-permute-done.7.refs_3_, ...), custom_call_target="tpu_custom_call" | custom-call | bytes 8388608 | tf_op jit(solution)/shard_map/update/pallas_call | solution.py:41
  24.3 2.4 %collective-permute-start.10 = (bf16[80,80]{1,0:T(8,128)(2,1)S(1)}, bf16[80,80]{1,0:T(8,128)(2,1)S(1)}, u32[]{:S(2)}, u32[]{:S(2)}) collective-permute-start(bf16[80,80]{1,0:T(8,128)(2,1)S(1)} %get-tuple-element.27.refs_0_), channel_id=1, source_target_pairs={{0,3},{1,2},{2,1},{3,0},{4,7},{5,6},{6,5},{7,4},{8,11},{9,10},{10,... | collective-permute-start | bytes 38408 | tf_op jit(solution)/shard_map/ppermute | solution.py:60
  26.8 0.9 %collective-permute-start.9 = (bf16[80,80]{1,0:T(8,128)(2,1)S(1)}, bf16[80,80]{1,0:T(8,128)(2,1)S(1)}, u32[]{:S(2)}, u32[]{:S(2)}) collective-permute-start(bf16[80,80]{1,0:T(8,128)(2,1)S(1)} %get-tuple-element.27.refs_0_), channel_id=1, source_target_pairs={{0,2},{1,3},{2,0},{3,1},{4,6},{5,7},{6,4},{7,5},{8,10},{9,11},{10,... | collective-permute-start | bytes 38408 | tf_op jit(solution)/shard_map/ppermute | solution.py:60
  27.7 1.1 %collective-permute-start.8 = (bf16[80,80]{1,0:T(8,128)(2,1)S(1)}, bf16[80,80]{1,0:T(8,128)(2,1)S(1)}, u32[]{:S(2)}, u32[]{:S(2)}) collective-permute-start(bf16[80,80]{1,0:T(8,128)(2,1)S(1)} %get-tuple-element.27.refs_0_), channel_id=1, source_target_pairs={{0,1},{1,0},{2,3},{3,2},{4,5},{5,4},{6,7},{7,6},{8,9},{9,8},{10,11... | collective-permute-start | bytes 38408 | tf_op jit(solution)/shard_map/ppermute | solution.py:60
  28.8 1.2 %collective-permute-done.10.refs_3_ = bf16[80,80]{1,0:T(8,128)(2,1)S(1)} collective-permute-done((bf16[80,80]{1,0:T(8,128)(2,1)S(1)}, bf16[80,80]{1,0:T(8,128)(2,1)S(1)}, u32[]{:S(2)}, u32[]{:S(2)}) %collective-permute-start.10) | collective-permute-done | bytes 12832 | tf_op jit(solution)/shard_map/ppermute | solution.py:60
  30.0 1.5 %collective-permute-done.9.refs_2_ = bf16[80,80]{1,0:T(8,128)(2,1)S(1)} collective-permute-done((bf16[80,80]{1,0:T(8,128)(2,1)S(1)}, bf16[80,80]{1,0:T(8,128)(2,1)S(1)}, u32[]{:S(2)}, u32[]{:S(2)}) %collective-permute-start.9) | collective-permute-done | bytes 12832 | tf_op jit(solution)/shard_map/ppermute | solution.py:60
  31.9 2.4 %collective-permute-start.12 = (bf16[192,128]{1,0:T(8,128)(2,1)S(1)}, bf16[192,128]{1,0:T(8,128)(2,1)S(1)}, u32[]{:S(2)}, u32[]{:S(2)}) collective-permute-start(bf16[192,128]{1,0:T(8,128)(2,1)S(1)} %columns.3.own_ref), channel_id=1, source_target_pairs={{0,28},{4,8},{8,4},{12,16},{16,12},{20,24},{24,20},{28,0},{1,29},{... | collective-permute-start | bytes 147464 | tf_op jit(solution)/shard_map/ppermute | solution.py:69
  34.2 3.3 %near.3.near_ref = f32[72,80]{1,0:T(8,128)S(1)} custom-call(bf16[192,128]{1,0:T(8,128)(2,1)S(1)} %columns.3.own_ref, bf16[192,128]{1,0:T(8,128)(2,1)S(1)} %collective-permute-done.11.mate_ref, bf16[1344,256]{1,0:T(8,128)(2,1)S(1)} %get-tuple-element.22.pick_ref, f32[80,128]{1,0:T(8,128)S(1)} %get-tuple-element.23.shift_ref, ...), custom_call_target="tpu_custom_call" | custom-call | bytes 12582912 | tf_op jit(solution)/shard_map/near/pallas_call | solution.py:41
  37.9 1.5 %collective-permute-start.15 = (bf16[80,80]{1,0:T(8,128)(2,1)S(1)}, bf16[80,80]{1,0:T(8,128)(2,1)S(1)}, u32[]{:S(2)}, u32[]{:S(2)}) collective-permute-start(bf16[80,80]{1,0:T(8,128)(2,1)S(1)} %far.3.refs_0_), channel_id=1, source_target_pairs={{0,3},{1,2},{2,1},{3,0},{4,7},{5,6},{6,5},{7,4},{8,11},{9,10},{10,... | collective-permute-start | bytes 38408 | tf_op jit(solution)/shard_map/ppermute | solution.py:60
  39.4 0.9 %collective-permute-start.14 = (bf16[80,80]{1,0:T(8,128)(2,1)S(1)}, bf16[80,80]{1,0:T(8,128)(2,1)S(1)}, u32[]{:S(2)}, u32[]{:S(2)}) collective-permute-start(bf16[80,80]{1,0:T(8,128)(2,1)S(1)} %far.3.refs_0_), channel_id=1, source_target_pairs={{0,2},{1,3},{2,0},{3,1},{4,6},{5,7},{6,4},{7,5},{8,10},{9,11},{10,... | collective-permute-start | bytes 38408 | tf_op jit(solution)/shard_map/ppermute | solution.py:60
  40.3 2.0 %collective-permute-start.13 = (bf16[80,80]{1,0:T(8,128)(2,1)S(1)}, bf16[80,80]{1,0:T(8,128)(2,1)S(1)}, u32[]{:S(2)}, u32[]{:S(2)}) collective-permute-start(bf16[80,80]{1,0:T(8,128)(2,1)S(1)} %far.3.refs_0_), channel_id=1, source_target_pairs={{0,1},{1,0},{2,3},{3,2},{4,5},{5,4},{6,7},{7,6},{8,9},{9,8},{10,11... | collective-permute-start | bytes 38408 | tf_op jit(solution)/shard_map/ppermute | solution.py:60
  42.3 0.6 %nodes.1 = (bf16[192,1536]{1,0:T(8,128)(2,1)S(1)}, s32[12,128]{1,0:T(8,128)S(1)}, bf16[24,80,192]{2,1,0:T(8,128)(2,1)S(1)}) custom-call(s32[24,64]{1,0:T(8,128)S(1)} %copy-done.4, bf16[24,80,192]{2,1,0:T(8,128)(2,1)S(1)} %copy-done.3), custom_call_target="tpu_custom_call" | custom-call | bytes 3145728 | tf_op jit(solution)/shard_map/nodes/pallas_call | solution.py:41
  43.5 1.3 %collective-permute-done.14.refs_2_ = bf16[80,80]{1,0:T(8,128)(2,1)S(1)} collective-permute-done((bf16[80,80]{1,0:T(8,128)(2,1)S(1)}, bf16[80,80]{1,0:T(8,128)(2,1)S(1)}, u32[]{:S(2)}, u32[]{:S(2)}) %collective-permute-start.14) | collective-permute-done | bytes 12832 | tf_op jit(solution)/shard_map/ppermute | solution.py:60
  44.8 1.7 %gradient.1 = (f32[72,80]{1,0:T(8,128)}, f32[48,192]{1,0:T(8,128)S(1)}, bf16[48,192]{1,0:T(8,128)(2,1)S(1)}, bf16[48,192]{1,0:T(8,128)(2,1)S(1)}) custom-call(bf16[80,80]{1,0:T(8,128)(2,1)S(1)} %far.3.refs_0_, bf16[80,80]{1,0:T(8,128)(2,1)S(1)} %collective-permute-done.13.refs_1_, bf16[80,80]{1,0:T(8,128)(2,1)S(1)} %collective-permute-done.14.refs_2_, ...), custom_call_target="tpu_custom_call" | custom-call | tf_op jit(solution)/shard_map/gradient/pallas_call | solution.py:41
  46.6 1.7 %collective-permute-start.17 = (bf16[48,192]{1,0:T(8,128)(2,1)S(1)}, bf16[48,192]{1,0:T(8,128)(2,1)S(1)}, u32[]{:S(2)}, u32[]{:S(2)}) collective-permute-start(bf16[48,192]{1,0:T(8,128)(2,1)S(1)} %get-tuple-element.35), channel_id=1, source_target_pairs={{0,28},{4,8},{8,4},{12,16},{16,12},{20,24},{24,20},{28,0},{1,29},{... | collective-permute-start | bytes 55304 | tf_op jit(solution)/shard_map/ppermute | solution.py:69
  48.4 2.4 %collective-permute-done.17.far_ref = bf16[48,192]{1,0:T(8,128)(2,1)S(1)} collective-permute-done((bf16[48,192]{1,0:T(8,128)(2,1)S(1)}, bf16[48,192]{1,0:T(8,128)(2,1)S(1)}, u32[]{:S(2)}, u32[]{:S(2)}) %collective-permute-start.17) | collective-permute-done | bytes 18464 | tf_op jit(solution)/shard_map/ppermute | solution.py:69
  50.8 2.2 %collective-permute-start.18 = (bf16[16,192]{1,0:T(8,128)(2,1)S(1)}, bf16[16,192]{1,0:T(8,128)(2,1)S(1)}, u32[]{:S(2)}, u32[]{:S(2)}) collective-permute-start(bf16[16,192]{1,0:T(8,128)(2,1)S(1)} %get-tuple-element.37), channel_id=1, source_target_pairs={{0,3},{1,2},{2,1},{3,0},{4,7},{5,6},{6,5},{7,4},{8,11},{9,10},{10,... | collective-permute-start | bytes 18440 | tf_op jit(solution)/shard_map/ppermute | solution.py:562
  53.0 0.7 %collective-permute-start.19 = (bf16[16,192]{1,0:T(8,128)(2,1)S(1)}, bf16[16,192]{1,0:T(8,128)(2,1)S(1)}, u32[]{:S(2)}, u32[]{:S(2)}) collective-permute-start(bf16[16,192]{1,0:T(8,128)(2,1)S(1)} %get-tuple-element.38), channel_id=1, source_target_pairs={{0,2},{1,3},{2,0},{3,1},{4,6},{5,7},{6,4},{7,5},{8,10},{9,11},{10,... | collective-permute-start | bytes 18440 | tf_op jit(solution)/shard_map/ppermute | solution.py:562
  53.7 1.5 %collective-permute-start.20 = (bf16[16,192]{1,0:T(8,128)(2,1)S(1)}, bf16[16,192]{1,0:T(8,128)(2,1)S(1)}, u32[]{:S(2)}, u32[]{:S(2)}) collective-permute-start(bf16[16,192]{1,0:T(8,128)(2,1)S(1)} %get-tuple-element.39), channel_id=1, source_target_pairs={{0,1},{1,0},{2,3},{3,2},{4,5},{5,4},{6,7},{7,6},{8,9},{9,8},{10,11... | collective-permute-start | bytes 18440 | tf_op jit(solution)/shard_map/ppermute | solution.py:562
  55.2 1.1 %collective-permute-done.18 = bf16[16,192]{1,0:T(8,128)(2,1)S(1)} collective-permute-done((bf16[16,192]{1,0:T(8,128)(2,1)S(1)}, bf16[16,192]{1,0:T(8,128)(2,1)S(1)}, u32[]{:S(2)}, u32[]{:S(2)}) %collective-permute-start.18) | collective-permute-done | bytes 6176 | tf_op jit(solution)/shard_map/ppermute | solution.py:562
  56.3 1.3 %collective-permute-done.19 = bf16[16,192]{1,0:T(8,128)(2,1)S(1)} collective-permute-done((bf16[16,192]{1,0:T(8,128)(2,1)S(1)}, bf16[16,192]{1,0:T(8,128)(2,1)S(1)}, u32[]{:S(2)}, u32[]{:S(2)}) %collective-permute-start.19) | collective-permute-done | bytes 6176 | tf_op jit(solution)/shard_map/ppermute | solution.py:562
  57.6 0.6 %convert_add_fusion = f32[9,192]{1,0:T(8,128)} fusion(f32[9,192]{1,0:T(8,128)S(1)} %get-tuple-element.36, bf16[16,192]{1,0:T(8,128)(2,1)S(1)} %collective-permute-done.20, bf16[16,192]{1,0:T(8,128)(2,1)S(1)} %collective-permute-done.19, bf16[16,192]{1,0:T(8,128)(2,1)S(1)} %collective-permute-done.18), kind=kLoop, calls=%fused_computation | loop fusion | flops 10368 | bytes 24192 | tf_op jit(solution)/shard_map/add | solution.py:562
  (32 shorter events, 2.7 us)
Async XLA Ops:
  0.6 12.9 %copy-start = (bf16[24,7,80,320]{3,2,1,0:T(8,128)(2,1)S(1)}, bf16[24,7,80,320]{3,2,1,0:T(8,128)(2,1)}, u32[]{:S(2)}) copy-start(bf16[24,7,80,320]{3,2,1,0:T(8,128)(2,1)} %jac_ref.7) | copy-start | bytes 25804804
  0.6 7.6 %collective-permute-start.2 = (f32[72,80]{1,0:T(8,128)}, f32[72,80]{1,0:T(8,128)S(1)}, u32[]{:S(2)}, u32[]{:S(2)}) collective-permute-start(f32[72,80]{1,0:T(8,128)} %bitcast.11), channel_id=1, source_target_pairs={{0,3},{1,2},{2,1},{3,0},{4,7},{5,6},{6,5},{7,4},{8,11},{9,10},{10,... | collective-permute-start | bytes 69128 | tf_op jit(solution)/shard_map/ppermute | solution.py:60
  5.8 5.1 %collective-permute-start.1 = (f32[72,80]{1,0:T(8,128)}, f32[72,80]{1,0:T(8,128)S(1)}, u32[]{:S(2)}, u32[]{:S(2)}) collective-permute-start(f32[72,80]{1,0:T(8,128)} %bitcast.12), channel_id=1, source_target_pairs={{0,2},{1,3},{2,0},{3,1},{4,6},{5,7},{6,4},{7,5},{8,10},{9,11},{10,... | collective-permute-start | bytes 69128 | tf_op jit(solution)/shard_map/ppermute | solution.py:60
  5.8 5.1 %collective-permute-start = (f32[72,80]{1,0:T(8,128)}, f32[72,80]{1,0:T(8,128)S(1)}, u32[]{:S(2)}, u32[]{:S(2)}) collective-permute-start(f32[72,80]{1,0:T(8,128)} %bitcast.13), channel_id=1, source_target_pairs={{0,1},{1,0},{2,3},{3,2},{4,5},{5,4},{6,7},{7,6},{8,9},{9,8},{10,11... | collective-permute-start | bytes 69128 | tf_op jit(solution)/shard_map/ppermute | solution.py:60
  11.0 2.6 %collective-permute-start.3 = (bf16[192,128]{1,0:T(8,128)(2,1)S(1)}, bf16[192,128]{1,0:T(8,128)(2,1)S(1)}, u32[]{:S(2)}, u32[]{:S(2)}) collective-permute-start(bf16[192,128]{1,0:T(8,128)(2,1)S(1)} %columns.2.own_ref), channel_id=1, source_target_pairs={{0,4},{4,0},{8,12},{12,8},{16,20},{20,16},{24,28},{28,24},{1,5},{5... | collective-permute-start | bytes 147464 | tf_op jit(solution)/shard_map/ppermute | solution.py:64
  11.0 5.8 %collective-permute-start.4 = (bf16[192,128]{1,0:T(8,128)(2,1)S(1)}, bf16[192,128]{1,0:T(8,128)(2,1)S(1)}, u32[]{:S(2)}, u32[]{:S(2)}) collective-permute-start(bf16[192,128]{1,0:T(8,128)(2,1)S(1)} %columns.2.own_ref), channel_id=1, source_target_pairs={{0,28},{4,8},{8,4},{12,16},{16,12},{20,24},{24,20},{28,0},{1,29},{... | collective-permute-start | bytes 147464 | tf_op jit(solution)/shard_map/ppermute | solution.py:69
  13.6 10.1 %copy-start.1 = (bf16[24,80,320]{2,1,0:T(8,128)(2,1)S(1)}, bf16[24,80,320]{2,1,0:T(8,128)(2,1)}, u32[]{:S(2)}) copy-start(bf16[24,80,320]{2,1,0:T(8,128)(2,1)} %refs_4_.3) | copy-start | bytes 3686404
  17.2 5.7 %collective-permute-start.7 = (bf16[80,80]{1,0:T(8,128)(2,1)S(1)}, bf16[80,80]{1,0:T(8,128)(2,1)S(1)}, u32[]{:S(2)}, u32[]{:S(2)}) collective-permute-start(bf16[80,80]{1,0:T(8,128)(2,1)S(1)} %far.2.refs_0_), channel_id=1, source_target_pairs={{0,3},{1,2},{2,1},{3,0},{4,7},{5,6},{6,5},{7,4},{8,11},{9,10},{10,... | collective-permute-start | bytes 38408 | tf_op jit(solution)/shard_map/ppermute | solution.py:60
  18.8 4.7 %collective-permute-start.6 = (bf16[80,80]{1,0:T(8,128)(2,1)S(1)}, bf16[80,80]{1,0:T(8,128)(2,1)S(1)}, u32[]{:S(2)}, u32[]{:S(2)}) collective-permute-start(bf16[80,80]{1,0:T(8,128)(2,1)S(1)} %far.2.refs_0_), channel_id=1, source_target_pairs={{0,2},{1,3},{2,0},{3,1},{4,6},{5,7},{6,4},{7,5},{8,10},{9,11},{10,... | collective-permute-start | bytes 38408 | tf_op jit(solution)/shard_map/ppermute | solution.py:60
  19.4 4.3 %collective-permute-start.5 = (bf16[80,80]{1,0:T(8,128)(2,1)S(1)}, bf16[80,80]{1,0:T(8,128)(2,1)S(1)}, u32[]{:S(2)}, u32[]{:S(2)}) collective-permute-start(bf16[80,80]{1,0:T(8,128)(2,1)S(1)} %far.2.refs_0_), channel_id=1, source_target_pairs={{0,1},{1,0},{2,3},{3,2},{4,5},{5,4},{6,7},{7,6},{8,9},{9,8},{10,11... | collective-permute-start | bytes 38408 | tf_op jit(solution)/shard_map/ppermute | solution.py:60
  24.3 5.7 %collective-permute-start.10 = (bf16[80,80]{1,0:T(8,128)(2,1)S(1)}, bf16[80,80]{1,0:T(8,128)(2,1)S(1)}, u32[]{:S(2)}, u32[]{:S(2)}) collective-permute-start(bf16[80,80]{1,0:T(8,128)(2,1)S(1)} %get-tuple-element.27.refs_0_), channel_id=1, source_target_pairs={{0,3},{1,2},{2,1},{3,0},{4,7},{5,6},{6,5},{7,4},{8,11},{9,10},{10,... | collective-permute-start | bytes 38408 | tf_op jit(solution)/shard_map/ppermute | solution.py:60
  26.8 4.7 %collective-permute-start.9 = (bf16[80,80]{1,0:T(8,128)(2,1)S(1)}, bf16[80,80]{1,0:T(8,128)(2,1)S(1)}, u32[]{:S(2)}, u32[]{:S(2)}) collective-permute-start(bf16[80,80]{1,0:T(8,128)(2,1)S(1)} %get-tuple-element.27.refs_0_), channel_id=1, source_target_pairs={{0,2},{1,3},{2,0},{3,1},{4,6},{5,7},{6,4},{7,5},{8,10},{9,11},{10,... | collective-permute-start | bytes 38408 | tf_op jit(solution)/shard_map/ppermute | solution.py:60
  27.7 4.0 %collective-permute-start.8 = (bf16[80,80]{1,0:T(8,128)(2,1)S(1)}, bf16[80,80]{1,0:T(8,128)(2,1)S(1)}, u32[]{:S(2)}, u32[]{:S(2)}) collective-permute-start(bf16[80,80]{1,0:T(8,128)(2,1)S(1)} %get-tuple-element.27.refs_0_), channel_id=1, source_target_pairs={{0,1},{1,0},{2,3},{3,2},{4,5},{5,4},{6,7},{7,6},{8,9},{9,8},{10,11... | collective-permute-start | bytes 38408 | tf_op jit(solution)/shard_map/ppermute | solution.py:60
  31.8 2.4 %collective-permute-start.11 = (bf16[192,128]{1,0:T(8,128)(2,1)S(1)}, bf16[192,128]{1,0:T(8,128)(2,1)S(1)}, u32[]{:S(2)}, u32[]{:S(2)}) collective-permute-start(bf16[192,128]{1,0:T(8,128)(2,1)S(1)} %columns.3.own_ref), channel_id=1, source_target_pairs={{0,4},{4,0},{8,12},{12,8},{16,20},{20,16},{24,28},{28,24},{1,5},{5... | collective-permute-start | bytes 147464 | tf_op jit(solution)/shard_map/ppermute | solution.py:64
  31.9 5.7 %collective-permute-start.12 = (bf16[192,128]{1,0:T(8,128)(2,1)S(1)}, bf16[192,128]{1,0:T(8,128)(2,1)S(1)}, u32[]{:S(2)}, u32[]{:S(2)}) collective-permute-start(bf16[192,128]{1,0:T(8,128)(2,1)S(1)} %columns.3.own_ref), channel_id=1, source_target_pairs={{0,28},{4,8},{8,4},{12,16},{16,12},{20,24},{24,20},{28,0},{1,29},{... | collective-permute-start | bytes 147464 | tf_op jit(solution)/shard_map/ppermute | solution.py:69
  34.2 8.1 %copy-start.3 = (bf16[24,80,192]{2,1,0:T(8,128)(2,1)S(1)}, bf16[24,80,192]{2,1,0:T(8,128)(2,1)}, u32[]{:S(2)}) copy-start(bf16[24,80,192]{2,1,0:T(8,128)(2,1)} %shape_ref.1) | copy-start | bytes 2211844
  34.2 8.1 %copy-start.4 = (s32[24,64]{1,0:T(8,128)S(1)}, s32[24,64]{1,0:T(8,128)}, u32[]{:S(2)}) copy-start(s32[24,64]{1,0:T(8,128)} %ids_ref.1) | copy-start | bytes 18436
  34.2 10.6 %copy-start.2 = (bf16[24,80,320]{2,1,0:T(8,128)(2,1)S(1)}, bf16[24,80,320]{2,1,0:T(8,128)(2,1)}, u32[]{:S(2)}) copy-start(bf16[24,80,320]{2,1,0:T(8,128)(2,1)} %refs_4_.3) | copy-start | bytes 3686404
  37.9 5.6 %collective-permute-start.15 = (bf16[80,80]{1,0:T(8,128)(2,1)S(1)}, bf16[80,80]{1,0:T(8,128)(2,1)S(1)}, u32[]{:S(2)}, u32[]{:S(2)}) collective-permute-start(bf16[80,80]{1,0:T(8,128)(2,1)S(1)} %far.3.refs_0_), channel_id=1, source_target_pairs={{0,3},{1,2},{2,1},{3,0},{4,7},{5,6},{6,5},{7,4},{8,11},{9,10},{10,... | collective-permute-start | bytes 38408 | tf_op jit(solution)/shard_map/ppermute | solution.py:60
  39.4 5.4 %collective-permute-start.14 = (bf16[80,80]{1,0:T(8,128)(2,1)S(1)}, bf16[80,80]{1,0:T(8,128)(2,1)S(1)}, u32[]{:S(2)}, u32[]{:S(2)}) collective-permute-start(bf16[80,80]{1,0:T(8,128)(2,1)S(1)} %far.3.refs_0_), channel_id=1, source_target_pairs={{0,2},{1,3},{2,0},{3,1},{4,6},{5,7},{6,4},{7,5},{8,10},{9,11},{10,... | collective-permute-start | bytes 38408 | tf_op jit(solution)/shard_map/ppermute | solution.py:60
  40.3 4.5 %collective-permute-start.13 = (bf16[80,80]{1,0:T(8,128)(2,1)S(1)}, bf16[80,80]{1,0:T(8,128)(2,1)S(1)}, u32[]{:S(2)}, u32[]{:S(2)}) collective-permute-start(bf16[80,80]{1,0:T(8,128)(2,1)S(1)} %far.3.refs_0_), channel_id=1, source_target_pairs={{0,1},{1,0},{2,3},{3,2},{4,5},{5,4},{6,7},{7,6},{8,9},{9,8},{10,11... | collective-permute-start | bytes 38408 | tf_op jit(solution)/shard_map/ppermute | solution.py:60
  46.5 1.9 %collective-permute-start.16 = (bf16[48,192]{1,0:T(8,128)(2,1)S(1)}, bf16[48,192]{1,0:T(8,128)(2,1)S(1)}, u32[]{:S(2)}, u32[]{:S(2)}) collective-permute-start(bf16[48,192]{1,0:T(8,128)(2,1)S(1)} %get-tuple-element.34), channel_id=1, source_target_pairs={{0,4},{4,0},{8,12},{12,8},{16,20},{20,16},{24,28},{28,24},{1,5},{5... | collective-permute-start | bytes 55304 | tf_op jit(solution)/shard_map/ppermute | solution.py:64
  46.6 4.2 %collective-permute-start.17 = (bf16[48,192]{1,0:T(8,128)(2,1)S(1)}, bf16[48,192]{1,0:T(8,128)(2,1)S(1)}, u32[]{:S(2)}, u32[]{:S(2)}) collective-permute-start(bf16[48,192]{1,0:T(8,128)(2,1)S(1)} %get-tuple-element.35), channel_id=1, source_target_pairs={{0,28},{4,8},{8,4},{12,16},{16,12},{20,24},{24,20},{28,0},{1,29},{... | collective-permute-start | bytes 55304 | tf_op jit(solution)/shard_map/ppermute | solution.py:69
  50.8 5.5 %collective-permute-start.18 = (bf16[16,192]{1,0:T(8,128)(2,1)S(1)}, bf16[16,192]{1,0:T(8,128)(2,1)S(1)}, u32[]{:S(2)}, u32[]{:S(2)}) collective-permute-start(bf16[16,192]{1,0:T(8,128)(2,1)S(1)} %get-tuple-element.37), channel_id=1, source_target_pairs={{0,3},{1,2},{2,1},{3,0},{4,7},{5,6},{6,5},{7,4},{8,11},{9,10},{10,... | collective-permute-start | bytes 18440 | tf_op jit(solution)/shard_map/ppermute | solution.py:562
  53.0 4.5 %collective-permute-start.19 = (bf16[16,192]{1,0:T(8,128)(2,1)S(1)}, bf16[16,192]{1,0:T(8,128)(2,1)S(1)}, u32[]{:S(2)}, u32[]{:S(2)}) collective-permute-start(bf16[16,192]{1,0:T(8,128)(2,1)S(1)} %get-tuple-element.38), channel_id=1, source_target_pairs={{0,2},{1,3},{2,0},{3,1},{4,6},{5,7},{6,4},{7,5},{8,10},{9,11},{10,... | collective-permute-start | bytes 18440 | tf_op jit(solution)/shard_map/ppermute | solution.py:562
  53.7 3.9 %collective-permute-start.20 = (bf16[16,192]{1,0:T(8,128)(2,1)S(1)}, bf16[16,192]{1,0:T(8,128)(2,1)S(1)}, u32[]{:S(2)}, u32[]{:S(2)}) collective-permute-start(bf16[16,192]{1,0:T(8,128)(2,1)S(1)} %get-tuple-element.39), channel_id=1, source_target_pairs={{0,1},{1,0},{2,3},{3,2},{4,5},{5,4},{6,7},{7,6},{8,9},{9,8},{10,11... | collective-permute-start | bytes 18440 | tf_op jit(solution)/shard_map/ppermute | solution.py:562

commit v5 on v4

--- a/solution.py
+++ b/solution.py
@@ -13,6 +13,7 @@
 FULL = jnp.float32
 LANES = 128
 PICK = 8
+QUAD = 4
 NT = (((1,), (1,)), ((), ()))
 VMEM = pl.BlockSpec(memory_space=pltpu.VMEM)
 SMEM = pl.BlockSpec(memory_space=pltpu.SMEM)
@@ -225,7 +226,7 @@
     out_ref[...] = rounded(jnp.concatenate(parts, axis=0), out_ref.shape[0])
 
 
-def unpacked(ref, rows, full):
+def unpacked(ref, rows, full, last_tile=lambda tile: tile):
     block = ref[...].astype(FULL)
     whole, cut = full // LANES, cut_of(rows, full)
     tiles = [block[i * rows : (i + 1) * rows] for i in range(whole)]
@@ -235,13 +236,13 @@
             low = iota(last.shape, 1) < LANES // 2
             lower = pltpu.roll(jnp.where(low, 0.0, last), LANES // 2, 1)
             last = jnp.concatenate([jnp.where(low, last, 0.0), lower[: rows - cut]], axis=0)
-        tiles.append(last)
+        tiles.append(last_tile(last))
     return rounded(jnp.concatenate(tiles, axis=1), round_up(rows, 16))
 
 
 def near_kernel(own_ref, mate_ref, pick_ref, shift_ref, adj_ref, rhs_ref, jac_ref, _, out_ref, image):
     rows, full = adj_ref.shape[0], jac_ref.shape[3]
-    products([unpacked(own_ref, rows, full), unpacked(mate_ref, rows, full)], pick_ref, jac_ref, image)
+    products([unpacked(ref, rows, full, twice) for ref in (own_ref, mate_ref)], pick_ref, jac_ref, image)
     out_ref[...] = without(shift_ref, adj_ref, rhs_ref, image)
 
 
@@ -251,7 +252,7 @@
 
 
 def products(parts, pick_ref, jac_ref, image):
-    elements, slots, width, _ = jac_ref.shape
+    elements, slots, width, full = jac_ref.shape
     rows_part, stride = parts[0].shape
     short = pick_ref.shape[1] - len(parts) * rows_part
     if short:
@@ -259,43 +260,62 @@
     stacked = jnp.concatenate(parts, axis=0)
     picked = jnp.dot(pick_ref[...], stacked, preferred_element_type=FULL).astype(HALF)
     image[...] = jnp.zeros(image.shape, FULL)
+    deep = full // (2 * LANES) * (2 * LANES)
+    low = iota((2 * PICK, LANES), 1) < LANES // 2
     for pair in range(elements // 2):
         starts = [k * elements * PICK + pair * 2 * PICK for k in range(slots)]
-        left = jnp.concatenate([picked[start : start + 2 * PICK] for start in starts], axis=1)
+        lefts = [picked[start : start + 2 * PICK] for start in starts]
+        tails = [left[:, deep:] for left in lefts]
+        tails = [jnp.where(low, *tails[k : k + 2]) if k + 1 < slots else tails[k] for k in range(0, slots, 2)]
+        left = jnp.concatenate([left[:, :deep] for left in lefts] + tails, axis=1)
         for side in range(2):
             e = 2 * pair + side
-            blocks = jnp.concatenate([widened(jac_ref[e, k], stride) for k in range(slots)], axis=1)
+            ends = [widened(jac_ref[e, k][:, deep:], LANES) for k in range(slots)]
+            for k in range(1, slots, 2):
+                ends[k - 1] = ends[k - 1] + pltpu.roll(ends[k], LANES // 2, 1)
+            blocks = jnp.concatenate([jac_ref[e, k][:, :deep] for k in range(slots)] + ends[::2], axis=1)
             product = lax.dot_general(left, blocks, NT, preferred_element_type=FULL)
             first = side * PICK
             image[pl.ds(e, 3, stride=elements), :width] = product[first : first + 3]
 
 
-def pair_products(lefts, blocks):
+def twice(tail):
+    return tail + pltpu.roll(tail, LANES // 2, 1)
+
+
+def quad_products(lefts, blocks):
     full = blocks[0].shape[1]
     deep = full // (2 * LANES) * (2 * LANES)
-    lower = iota((2 * PICK, LANES), 0) >= PICK
-    mine = [jnp.logical_not(lower), lower]
-    rest = [jnp.where(mine[i], lefts[i][:, deep : deep + LANES], 0.0).astype(HALF) for i in range(2)]
-    blocks_rest = [widened(block[:, deep:], LANES) for block in blocks]
+    shape = (4 * QUAD, LANES)
+    low = iota(shape, 1) < LANES // 2
+    mine = []
+    for i in range(4):
+        place = iota(shape, 0) - i * QUAD
+        mine.append(jnp.logical_and(jnp.logical_and(place >= 0, place < QUAD), low if i % 2 == 0 else jnp.logical_not(low)))
+    tails = [left[:, deep : deep + LANES] for left in lefts]
+    left = [jnp.where(mine[i], tails[i], jnp.where(mine[i + 1], tails[i + 1], 0.0).astype(HALF)) for i in (0, 2)]
+    low = iota((blocks[0].shape[0], LANES), 1) < LANES // 2
+    ends = [widened(block[:, deep:], LANES) for block in blocks]
+    right = [jnp.where(low, ends[i], pltpu.roll(ends[i + 1], LANES // 2, 1)) for i in (0, 2)]
     shared = lax.dot_general(
-        jnp.concatenate(rest, axis=1), jnp.concatenate(blocks_rest, axis=1), NT, preferred_element_type=FULL
+        jnp.concatenate(left, axis=1), jnp.concatenate(right, axis=1), NT, preferred_element_type=FULL
     )
     products = []
     for i, (left, block) in enumerate(zip(lefts, blocks)):
         product = lax.dot_general(left[:, :deep], block[:, :deep], NT, preferred_element_type=FULL)
-        half = slice(i * PICK, (i + 1) * PICK)
-        products.append(product[half] + shared[half])
+        part = slice(i * QUAD, (i + 1) * QUAD)
+        products.append(product[part] + shared[part])
     return products
 
 
 def far_kernel(near_ref, far_ref, jac_ref, list_ref, count_ref, _shapes, _ids, out_ref, spread, sums, image):
     elements, slots, width, _ = jac_ref.shape
-    far = unpacked(far_ref, near_ref.shape[0], jac_ref.shape[3])
+    far = unpacked(far_ref, near_ref.shape[0], jac_ref.shape[3], twice)
     rows, stride = far.shape
     deep = spread.shape[1]
     shape = (elements, deep, rows)
     element, row, lane = [iota(shape, dim).reshape(elements * deep, rows) for dim in range(3)]
-    row = row - jnp.where(row >= PICK, PICK, 0)
+    row = lax.bitwise_and(row, QUAD - 1)
     pick = hit(jnp.where(row < 3, row * elements + element, -1) == lane).astype(HALF)
     taken = jnp.dot(pick, far, preferred_element_type=FULL).astype(HALF)
     spread[:elements] = taken.reshape(elements, deep, stride)
@@ -304,16 +324,16 @@
 
     @pl.loop(0, count_ref[0])
     def _(step):
-        for i in range(0, GROUP, 2):
+        for i in range(0, GROUP, 4):
             owners, lefts, blocks = [], [], []
-            for side in range(2):
+            for side in range(4):
                 word = list_ref[step * GROUP + i + side]
                 block = lax.shift_right_logical(word, 5)
                 owners.append(lax.div(block, slots))
                 lefts.append(spread[lax.bitwise_and(word, 31)])
                 blocks.append(jac_ref[owners[side], block - owners[side] * slots])
-            for e, product in zip(owners, pair_products(lefts, blocks)):
-                sums[e, :, :width] += product
+            for e, product in zip(owners, quad_products(lefts, blocks)):
+                sums[e, :QUAD, :width] += product
 
     for e in range(elements):
         image[pl.ds(e, 3, stride=elements), :] = sums[e, :3, :]
@@ -333,17 +353,18 @@
     elements = rows // 3
     stride = round_up(inv_ref.shape[2], LANES)
     resid = put_columns([ref[...] for ref in resid_refs], distances(), stride)
+    resid[-1] = twice(resid[-1])
     resid = jnp.concatenate(resid, axis=1).astype(HALF)
-    shape = (elements, PICK, resid.shape[0])
-    deep = elements * PICK
+    shape = (elements, QUAD, resid.shape[0])
+    deep = elements * QUAD
     element, row, lane = [iota(shape, dim).reshape(deep, -1) for dim in range(3)]
     pick = hit(jnp.where(row < 3, row * elements + element, -1) == lane).astype(HALF)
     resid = jnp.dot(pick, resid, preferred_element_type=FULL).astype(HALF)
     update[...] = jnp.zeros(update.shape, FULL)
-    for pair in range(elements // 2):
-        left = resid[pair * 2 * PICK : (pair + 1) * 2 * PICK]
-        for side, product in enumerate(pair_products([left, left], [inv_ref[2 * pair], inv_ref[2 * pair + 1]])):
-            update[pl.ds(2 * pair + side, 3, stride=elements), :width] = product[:3]
+    for first in range(0, elements, 4):
+        left = resid[first * QUAD : (first + 4) * QUAD]
+        for i, product in enumerate(quad_products([left] * 4, [inv_ref[first + i] for i in range(4)])):
+            update[pl.ds(first + i, 3, stride=elements), :width] = product[:3]
     short = jnp.zeros((update.shape[0] - rows, width), FULL)
     return jnp.concatenate([adj_ref[...] + update[:rows, :width], short], axis=0)
 

time: 58.2 us -> 57.2 us (0.983)
  Pallas kernels: 12.3 us -> 11.5 us
  waiting for transfers between devices: 14.1 us -> 13.4 us
    pallas_call x11, Pallas kernels: 12.3 us -> 11.5 us  [call(): pl.pallas_call(kernel, in_specs=specs, out_specs=[SMEM if getattr(out, 'm...]
  transfers between devices with their start and end apart: 21 -> 21, of which waited for: 12 -> 14; matrix products, arithmetic and copies ran while one was open for 0% -> 0% of each run, Pallas kernels for 15% -> 14%
where the time goes in v5:
time: 57.2 us; the launch traced here: 57 us
  starting transfers between devices  30.8 us (54%)
  waiting for transfers between devices  13.4 us (23%)
  Pallas kernels  11.5 us (20%)
  between operations  0.78 us (1%)
  other arithmetic  0.61 us (1%)
    ppermute x12, starting transfers between devices, over_blk(): lax.ppermute(block, 'blk', [(i, i ^ k) for i in range(count)])  19.1 us
    pallas_call x11, Pallas kernels, call(): pl.pallas_call(kernel, in_specs=specs, out_specs=[SMEM if getattr(out, 'm...  11.5 us
    ppermute x12, waiting for transfers between devices, over_blk(): lax.ppermute(block, 'blk', [(i, i ^ k) for i in range(count)])  8.79 us
    ppermute x3, starting transfers between devices, to_far(): lax.ppermute(block, 'dom', [(i, ((i + 1 ^ 1) - 1) % count) for i in range...  7.08 us
    ppermute x3, starting transfers between devices, local(): lax.ppermute(pieces[k], 'blk', [(i, i ^ k) for i in range(count)])[:9]  4.45 us
    ppermute x3, waiting for transfers between devices, local(): lax.ppermute(pieces[k], 'blk', [(i, i ^ k) for i in range(count)])[:9]  2.61 us
    ppermute x3, waiting for transfers between devices, to_far(): lax.ppermute(block, 'dom', [(i, ((i + 1 ^ 1) - 1) % count) for i in range...  1.97 us
  transfers between devices with their start and end apart: 21, of which 14 were waited for; matrix products, arithmetic and copies ran while one was open for 0% of the time, Pallas kernels for 14%

profile of v5, /device:TPU:0, one launch (start us, length us, event | category | flops | bytes accessed | tf_op | source)
XLA Modules:
  0.0 57.0 jit_solution(4803803246066020693)
XLA Ops:
  0.6 5.1 %collective-permute-start.2 = (f32[72,80]{1,0:T(8,128)}, f32[72,80]{1,0:T(8,128)S(1)}, u32[]{:S(2)}, u32[]{:S(2)}) collective-permute-start(f32[72,80]{1,0:T(8,128)} %bitcast.11), channel_id=1, source_target_pairs={{0,3},{1,2},{2,1},{3,0},{4,7},{5,6},{6,5},{7,4},{8,11},{9,10},{10,... | collective-permute-start | bytes 69128 | tf_op jit(solution)/shard_map/ppermute | solution.py:61
  5.8 0.6 %collective-permute-start = (f32[72,80]{1,0:T(8,128)}, f32[72,80]{1,0:T(8,128)S(1)}, u32[]{:S(2)}, u32[]{:S(2)}) collective-permute-start(f32[72,80]{1,0:T(8,128)} %bitcast.13), channel_id=1, source_target_pairs={{0,1},{1,0},{2,3},{3,2},{4,5},{5,4},{6,7},{7,6},{8,9},{9,8},{10,11... | collective-permute-start | bytes 69128 | tf_op jit(solution)/shard_map/ppermute | solution.py:61
  6.4 1.8 %slots.1 = (bf16[1344,256]{1,0:T(8,128)(2,1)S(1)}, f32[80,128]{1,0:T(8,128)S(1)}, s32[256]{0:T(256)S(4)}, s32[1]{0:T(128)S(4)}, f32[72,80]{1,0:T(8,128)S(1)}, /*index=5*/f32[72,80]{1,0:T(8,128)S(1)}) custom-call(s32[6,24]{1,0:T(8,128)} %bitcast.15, f32[24]{0:T(128)} %shift_hbm.1, f32[72,80]{1,0:T(8,128)} %bitcast.14, f32[72,80]{1,0:T(8,128)} %bitcast.10, ...), custom_call_target="tpu_custom_call" | custom-call | bytes 16777216 | tf_op jit(solution)/shard_map/slots/pallas_call | solution.py:42
  8.2 2.6 %collective-permute-done.1.refs_2_ = f32[72,80]{1,0:T(8,128)S(1)} collective-permute-done((f32[72,80]{1,0:T(8,128)}, f32[72,80]{1,0:T(8,128)S(1)}, u32[]{:S(2)}, u32[]{:S(2)}) %collective-permute-start.1) | collective-permute-done | bytes 23072 | tf_op jit(solution)/shard_map/ppermute | solution.py:61
  11.0 2.5 %collective-permute-start.4 = (bf16[192,128]{1,0:T(8,128)(2,1)S(1)}, bf16[192,128]{1,0:T(8,128)(2,1)S(1)}, u32[]{:S(2)}, u32[]{:S(2)}) collective-permute-start(bf16[192,128]{1,0:T(8,128)(2,1)S(1)} %columns.2.own_ref), channel_id=1, source_target_pairs={{0,28},{4,8},{8,4},{12,16},{16,12},{20,24},{24,20},{28,0},{1,29},{... | collective-permute-start | bytes 147464 | tf_op jit(solution)/shard_map/ppermute | solution.py:70
  13.6 2.8 %near.2.near_ref = f32[72,80]{1,0:T(8,128)S(1)} custom-call(bf16[192,128]{1,0:T(8,128)(2,1)S(1)} %columns.2.own_ref, bf16[192,128]{1,0:T(8,128)(2,1)S(1)} %collective-permute-done.3.mate_ref, bf16[1344,256]{1,0:T(8,128)(2,1)S(1)} %get-tuple-element.22.pick_ref, f32[80,128]{1,0:T(8,128)S(1)} %get-tuple-element.23.shift_ref, ...), custom_call_target="tpu_custom_call" | custom-call | bytes 12582912 | tf_op jit(solution)/shard_map/near/pallas_call | solution.py:42
  16.8 1.6 %collective-permute-start.7 = (bf16[80,80]{1,0:T(8,128)(2,1)S(1)}, bf16[80,80]{1,0:T(8,128)(2,1)S(1)}, u32[]{:S(2)}, u32[]{:S(2)}) collective-permute-start(bf16[80,80]{1,0:T(8,128)(2,1)S(1)} %far.2.refs_0_), channel_id=1, source_target_pairs={{0,3},{1,2},{2,1},{3,0},{4,7},{5,6},{6,5},{7,4},{8,11},{9,10},{10,... | collective-permute-start | bytes 38408 | tf_op jit(solution)/shard_map/ppermute | solution.py:61
  18.4 0.6 %collective-permute-start.6 = (bf16[80,80]{1,0:T(8,128)(2,1)S(1)}, bf16[80,80]{1,0:T(8,128)(2,1)S(1)}, u32[]{:S(2)}, u32[]{:S(2)}) collective-permute-start(bf16[80,80]{1,0:T(8,128)(2,1)S(1)} %far.2.refs_0_), channel_id=1, source_target_pairs={{0,2},{1,3},{2,0},{3,1},{4,6},{5,7},{6,4},{7,5},{8,10},{9,11},{10,... | collective-permute-start | bytes 38408 | tf_op jit(solution)/shard_map/ppermute | solution.py:61
  19.0 2.3 %collective-permute-start.5 = (bf16[80,80]{1,0:T(8,128)(2,1)S(1)}, bf16[80,80]{1,0:T(8,128)(2,1)S(1)}, u32[]{:S(2)}, u32[]{:S(2)}) collective-permute-start(bf16[80,80]{1,0:T(8,128)(2,1)S(1)} %far.2.refs_0_), channel_id=1, source_target_pairs={{0,1},{1,0},{2,3},{3,2},{4,5},{5,4},{6,7},{7,6},{8,9},{9,8},{10,11... | collective-permute-start | bytes 38408 | tf_op jit(solution)/shard_map/ppermute | solution.py:61
  21.3 1.4 %collective-permute-done.7.refs_3_ = bf16[80,80]{1,0:T(8,128)(2,1)S(1)} collective-permute-done((bf16[80,80]{1,0:T(8,128)(2,1)S(1)}, bf16[80,80]{1,0:T(8,128)(2,1)S(1)}, u32[]{:S(2)}, u32[]{:S(2)}) %collective-permute-start.7) | collective-permute-done | bytes 12832 | tf_op jit(solution)/shard_map/ppermute | solution.py:61
  23.3 0.7 %update.1 = (f32[72,80]{1,0:T(8,128)S(1)}, bf16[80,80]{1,0:T(8,128)(2,1)S(1)}) custom-call(bf16[80,80]{1,0:T(8,128)(2,1)S(1)} %far.2.refs_0_, bf16[80,80]{1,0:T(8,128)(2,1)S(1)} %collective-permute-done.5.refs_1_, bf16[80,80]{1,0:T(8,128)(2,1)S(1)} %collective-permute-done.6.refs_2_, bf16[80,80]{1,0:T(8,128)(2,1)S(1)} %collective-permute-done.7.refs_3_, ...), custom_call_target="tpu_custom_call" | custom-call | bytes 8388608 | tf_op jit(solution)/shard_map/update/pallas_call | solution.py:42
  24.0 2.4 %collective-permute-start.10 = (bf16[80,80]{1,0:T(8,128)(2,1)S(1)}, bf16[80,80]{1,0:T(8,128)(2,1)S(1)}, u32[]{:S(2)}, u32[]{:S(2)}) collective-permute-start(bf16[80,80]{1,0:T(8,128)(2,1)S(1)} %get-tuple-element.27.refs_0_), channel_id=1, source_target_pairs={{0,3},{1,2},{2,1},{3,0},{4,7},{5,6},{6,5},{7,4},{8,11},{9,10},{10,... | collective-permute-start | bytes 38408 | tf_op jit(solution)/shard_map/ppermute | solution.py:61
  26.4 0.9 %collective-permute-start.9 = (bf16[80,80]{1,0:T(8,128)(2,1)S(1)}, bf16[80,80]{1,0:T(8,128)(2,1)S(1)}, u32[]{:S(2)}, u32[]{:S(2)}) collective-permute-start(bf16[80,80]{1,0:T(8,128)(2,1)S(1)} %get-tuple-element.27.refs_0_), channel_id=1, source_target_pairs={{0,2},{1,3},{2,0},{3,1},{4,6},{5,7},{6,4},{7,5},{8,10},{9,11},{10,... | collective-permute-start | bytes 38408 | tf_op jit(solution)/shard_map/ppermute | solution.py:61
  27.3 1.1 %collective-permute-start.8 = (bf16[80,80]{1,0:T(8,128)(2,1)S(1)}, bf16[80,80]{1,0:T(8,128)(2,1)S(1)}, u32[]{:S(2)}, u32[]{:S(2)}) collective-permute-start(bf16[80,80]{1,0:T(8,128)(2,1)S(1)} %get-tuple-element.27.refs_0_), channel_id=1, source_target_pairs={{0,1},{1,0},{2,3},{3,2},{4,5},{5,4},{6,7},{7,6},{8,9},{9,8},{10,11... | collective-permute-start | bytes 38408 | tf_op jit(solution)/shard_map/ppermute | solution.py:61
  28.4 1.3 %collective-permute-done.10.refs_3_ = bf16[80,80]{1,0:T(8,128)(2,1)S(1)} collective-permute-done((bf16[80,80]{1,0:T(8,128)(2,1)S(1)}, bf16[80,80]{1,0:T(8,128)(2,1)S(1)}, u32[]{:S(2)}, u32[]{:S(2)}) %collective-permute-start.10) | collective-permute-done | bytes 12832 | tf_op jit(solution)/shard_map/ppermute | solution.py:61
  29.8 1.4 %collective-permute-done.9.refs_2_ = bf16[80,80]{1,0:T(8,128)(2,1)S(1)} collective-permute-done((bf16[80,80]{1,0:T(8,128)(2,1)S(1)}, bf16[80,80]{1,0:T(8,128)(2,1)S(1)}, u32[]{:S(2)}, u32[]{:S(2)}) %collective-permute-start.9) | collective-permute-done | bytes 12832 | tf_op jit(solution)/shard_map/ppermute | solution.py:61
  31.5 2.3 %collective-permute-start.12 = (bf16[192,128]{1,0:T(8,128)(2,1)S(1)}, bf16[192,128]{1,0:T(8,128)(2,1)S(1)}, u32[]{:S(2)}, u32[]{:S(2)}) collective-permute-start(bf16[192,128]{1,0:T(8,128)(2,1)S(1)} %columns.3.own_ref), channel_id=1, source_target_pairs={{0,28},{4,8},{8,4},{12,16},{16,12},{20,24},{24,20},{28,0},{1,29},{... | collective-permute-start | bytes 147464 | tf_op jit(solution)/shard_map/ppermute | solution.py:70
  33.8 2.8 %near.3.near_ref = f32[72,80]{1,0:T(8,128)S(1)} custom-call(bf16[192,128]{1,0:T(8,128)(2,1)S(1)} %columns.3.own_ref, bf16[192,128]{1,0:T(8,128)(2,1)S(1)} %collective-permute-done.11.mate_ref, bf16[1344,256]{1,0:T(8,128)(2,1)S(1)} %get-tuple-element.22.pick_ref, f32[80,128]{1,0:T(8,128)S(1)} %get-tuple-element.23.shift_ref, ...), custom_call_target="tpu_custom_call" | custom-call | bytes 12582912 | tf_op jit(solution)/shard_map/near/pallas_call | solution.py:42
  37.1 1.5 %collective-permute-start.15 = (bf16[80,80]{1,0:T(8,128)(2,1)S(1)}, bf16[80,80]{1,0:T(8,128)(2,1)S(1)}, u32[]{:S(2)}, u32[]{:S(2)}) collective-permute-start(bf16[80,80]{1,0:T(8,128)(2,1)S(1)} %far.3.refs_0_), channel_id=1, source_target_pairs={{0,3},{1,2},{2,1},{3,0},{4,7},{5,6},{6,5},{7,4},{8,11},{9,10},{10,... | collective-permute-start | bytes 38408 | tf_op jit(solution)/shard_map/ppermute | solution.py:61
  38.6 0.9 %collective-permute-start.14 = (bf16[80,80]{1,0:T(8,128)(2,1)S(1)}, bf16[80,80]{1,0:T(8,128)(2,1)S(1)}, u32[]{:S(2)}, u32[]{:S(2)}) collective-permute-start(bf16[80,80]{1,0:T(8,128)(2,1)S(1)} %far.3.refs_0_), channel_id=1, source_target_pairs={{0,2},{1,3},{2,0},{3,1},{4,6},{5,7},{6,4},{7,5},{8,10},{9,11},{10,... | collective-permute-start | bytes 38408 | tf_op jit(solution)/shard_map/ppermute | solution.py:61
  39.5 2.0 %collective-permute-start.13 = (bf16[80,80]{1,0:T(8,128)(2,1)S(1)}, bf16[80,80]{1,0:T(8,128)(2,1)S(1)}, u32[]{:S(2)}, u32[]{:S(2)}) collective-permute-start(bf16[80,80]{1,0:T(8,128)(2,1)S(1)} %far.3.refs_0_), channel_id=1, source_target_pairs={{0,1},{1,0},{2,3},{3,2},{4,5},{5,4},{6,7},{7,6},{8,9},{9,8},{10,11... | collective-permute-start | bytes 38408 | tf_op jit(solution)/shard_map/ppermute | solution.py:61
  41.5 0.7 %nodes.1 = (bf16[192,1536]{1,0:T(8,128)(2,1)S(1)}, s32[12,128]{1,0:T(8,128)S(1)}, bf16[24,80,192]{2,1,0:T(8,128)(2,1)S(1)}) custom-call(s32[24,64]{1,0:T(8,128)S(1)} %copy-done.4, bf16[24,80,192]{2,1,0:T(8,128)(2,1)S(1)} %copy-done.3), custom_call_target="tpu_custom_call" | custom-call | bytes 3145728 | tf_op jit(solution)/shard_map/nodes/pallas_call | solution.py:42
  42.2 0.6 %collective-permute-done.15.refs_3_ = bf16[80,80]{1,0:T(8,128)(2,1)S(1)} collective-permute-done((bf16[80,80]{1,0:T(8,128)(2,1)S(1)}, bf16[80,80]{1,0:T(8,128)(2,1)S(1)}, u32[]{:S(2)}, u32[]{:S(2)}) %collective-permute-start.15) | collective-permute-done | bytes 12832 | tf_op jit(solution)/shard_map/ppermute | solution.py:61
  43.5 1.6 %gradient.1 = (f32[72,80]{1,0:T(8,128)}, f32[48,192]{1,0:T(8,128)S(1)}, bf16[48,192]{1,0:T(8,128)(2,1)S(1)}, bf16[48,192]{1,0:T(8,128)(2,1)S(1)}) custom-call(bf16[80,80]{1,0:T(8,128)(2,1)S(1)} %far.3.refs_0_, bf16[80,80]{1,0:T(8,128)(2,1)S(1)} %collective-permute-done.13.refs_1_, bf16[80,80]{1,0:T(8,128)(2,1)S(1)} %collective-permute-done.14.refs_2_, ...), custom_call_target="tpu_custom_call" | custom-call | tf_op jit(solution)/shard_map/gradient/pallas_call | solution.py:42
  45.1 2.3 %collective-permute-start.17 = (bf16[48,192]{1,0:T(8,128)(2,1)S(1)}, bf16[48,192]{1,0:T(8,128)(2,1)S(1)}, u32[]{:S(2)}, u32[]{:S(2)}) collective-permute-start(bf16[48,192]{1,0:T(8,128)(2,1)S(1)} %get-tuple-element.35), channel_id=1, source_target_pairs={{0,28},{4,8},{8,4},{12,16},{16,12},{20,24},{24,20},{28,0},{1,29},{... | collective-permute-start | bytes 55304 | tf_op jit(solution)/shard_map/ppermute | solution.py:70
  47.4 1.9 %collective-permute-done.17.far_ref = bf16[48,192]{1,0:T(8,128)(2,1)S(1)} collective-permute-done((bf16[48,192]{1,0:T(8,128)(2,1)S(1)}, bf16[48,192]{1,0:T(8,128)(2,1)S(1)}, u32[]{:S(2)}, u32[]{:S(2)}) %collective-permute-start.17) | collective-permute-done | bytes 18464 | tf_op jit(solution)/shard_map/ppermute | solution.py:70
  49.4 2.4 %collective-permute-start.18 = (bf16[16,192]{1,0:T(8,128)(2,1)S(1)}, bf16[16,192]{1,0:T(8,128)(2,1)S(1)}, u32[]{:S(2)}, u32[]{:S(2)}) collective-permute-start(bf16[16,192]{1,0:T(8,128)(2,1)S(1)} %get-tuple-element.37), channel_id=1, source_target_pairs={{0,3},{1,2},{2,1},{3,0},{4,7},{5,6},{6,5},{7,4},{8,11},{9,10},{10,... | collective-permute-start | bytes 18440 | tf_op jit(solution)/shard_map/ppermute | solution.py:583
  51.8 0.9 %collective-permute-start.19 = (bf16[16,192]{1,0:T(8,128)(2,1)S(1)}, bf16[16,192]{1,0:T(8,128)(2,1)S(1)}, u32[]{:S(2)}, u32[]{:S(2)}) collective-permute-start(bf16[16,192]{1,0:T(8,128)(2,1)S(1)} %get-tuple-element.38), channel_id=1, source_target_pairs={{0,2},{1,3},{2,0},{3,1},{4,6},{5,7},{6,4},{7,5},{8,10},{9,11},{10,... | collective-permute-start | bytes 18440 | tf_op jit(solution)/shard_map/ppermute | solution.py:583
  52.7 1.1 %collective-permute-start.20 = (bf16[16,192]{1,0:T(8,128)(2,1)S(1)}, bf16[16,192]{1,0:T(8,128)(2,1)S(1)}, u32[]{:S(2)}, u32[]{:S(2)}) collective-permute-start(bf16[16,192]{1,0:T(8,128)(2,1)S(1)} %get-tuple-element.39), channel_id=1, source_target_pairs={{0,1},{1,0},{2,3},{3,2},{4,5},{5,4},{6,7},{7,6},{8,9},{9,8},{10,11... | collective-permute-start | bytes 18440 | tf_op jit(solution)/shard_map/ppermute | solution.py:583
  53.8 1.1 %collective-permute-done.18 = bf16[16,192]{1,0:T(8,128)(2,1)S(1)} collective-permute-done((bf16[16,192]{1,0:T(8,128)(2,1)S(1)}, bf16[16,192]{1,0:T(8,128)(2,1)S(1)}, u32[]{:S(2)}, u32[]{:S(2)}) %collective-permute-start.18) | collective-permute-done | bytes 6176 | tf_op jit(solution)/shard_map/ppermute | solution.py:583
  54.9 1.5 %collective-permute-done.19 = bf16[16,192]{1,0:T(8,128)(2,1)S(1)} collective-permute-done((bf16[16,192]{1,0:T(8,128)(2,1)S(1)}, bf16[16,192]{1,0:T(8,128)(2,1)S(1)}, u32[]{:S(2)}, u32[]{:S(2)}) %collective-permute-start.19) | collective-permute-done | bytes 6176 | tf_op jit(solution)/shard_map/ppermute | solution.py:583
  56.4 0.6 %convert_add_fusion = f32[9,192]{1,0:T(8,128)} fusion(f32[9,192]{1,0:T(8,128)S(1)} %get-tuple-element.36, bf16[16,192]{1,0:T(8,128)(2,1)S(1)} %collective-permute-done.20, bf16[16,192]{1,0:T(8,128)(2,1)S(1)} %collective-permute-done.19, bf16[16,192]{1,0:T(8,128)(2,1)S(1)} %collective-permute-done.18), kind=kLoop, calls=%fused_computation | loop fusion | flops 10368 | bytes 24192 | tf_op jit(solution)/shard_map/add | solution.py:583
  (32 shorter events, 3.0 us)
Async XLA Ops:
  0.6 12.9 %copy-start = (bf16[24,7,80,320]{3,2,1,0:T(8,128)(2,1)S(1)}, bf16[24,7,80,320]{3,2,1,0:T(8,128)(2,1)}, u32[]{:S(2)}) copy-start(bf16[24,7,80,320]{3,2,1,0:T(8,128)(2,1)} %jac_ref.7) | copy-start | bytes 25804804
  0.6 7.6 %collective-permute-start.2 = (f32[72,80]{1,0:T(8,128)}, f32[72,80]{1,0:T(8,128)S(1)}, u32[]{:S(2)}, u32[]{:S(2)}) collective-permute-start(f32[72,80]{1,0:T(8,128)} %bitcast.11), channel_id=1, source_target_pairs={{0,3},{1,2},{2,1},{3,0},{4,7},{5,6},{6,5},{7,4},{8,11},{9,10},{10,... | collective-permute-start | bytes 69128 | tf_op jit(solution)/shard_map/ppermute | solution.py:61
  5.8 5.1 %collective-permute-start.1 = (f32[72,80]{1,0:T(8,128)}, f32[72,80]{1,0:T(8,128)S(1)}, u32[]{:S(2)}, u32[]{:S(2)}) collective-permute-start(f32[72,80]{1,0:T(8,128)} %bitcast.12), channel_id=1, source_target_pairs={{0,2},{1,3},{2,0},{3,1},{4,6},{5,7},{6,4},{7,5},{8,10},{9,11},{10,... | collective-permute-start | bytes 69128 | tf_op jit(solution)/shard_map/ppermute | solution.py:61
  5.8 5.1 %collective-permute-start = (f32[72,80]{1,0:T(8,128)}, f32[72,80]{1,0:T(8,128)S(1)}, u32[]{:S(2)}, u32[]{:S(2)}) collective-permute-start(f32[72,80]{1,0:T(8,128)} %bitcast.13), channel_id=1, source_target_pairs={{0,1},{1,0},{2,3},{3,2},{4,5},{5,4},{6,7},{7,6},{8,9},{9,8},{10,11... | collective-permute-start | bytes 69128 | tf_op jit(solution)/shard_map/ppermute | solution.py:61
  11.0 2.6 %collective-permute-start.3 = (bf16[192,128]{1,0:T(8,128)(2,1)S(1)}, bf16[192,128]{1,0:T(8,128)(2,1)S(1)}, u32[]{:S(2)}, u32[]{:S(2)}) collective-permute-start(bf16[192,128]{1,0:T(8,128)(2,1)S(1)} %columns.2.own_ref), channel_id=1, source_target_pairs={{0,4},{4,0},{8,12},{12,8},{16,20},{20,16},{24,28},{28,24},{1,5},{5... | collective-permute-start | bytes 147464 | tf_op jit(solution)/shard_map/ppermute | solution.py:65
  11.0 5.4 %collective-permute-start.4 = (bf16[192,128]{1,0:T(8,128)(2,1)S(1)}, bf16[192,128]{1,0:T(8,128)(2,1)S(1)}, u32[]{:S(2)}, u32[]{:S(2)}) collective-permute-start(bf16[192,128]{1,0:T(8,128)(2,1)S(1)} %columns.2.own_ref), channel_id=1, source_target_pairs={{0,28},{4,8},{8,4},{12,16},{16,12},{20,24},{24,20},{28,0},{1,29},{... | collective-permute-start | bytes 147464 | tf_op jit(solution)/shard_map/ppermute | solution.py:70
  13.6 9.7 %copy-start.1 = (bf16[24,80,320]{2,1,0:T(8,128)(2,1)S(1)}, bf16[24,80,320]{2,1,0:T(8,128)(2,1)}, u32[]{:S(2)}) copy-start(bf16[24,80,320]{2,1,0:T(8,128)(2,1)} %refs_4_.3) | copy-start | bytes 3686404
  16.8 5.8 %collective-permute-start.7 = (bf16[80,80]{1,0:T(8,128)(2,1)S(1)}, bf16[80,80]{1,0:T(8,128)(2,1)S(1)}, u32[]{:S(2)}, u32[]{:S(2)}) collective-permute-start(bf16[80,80]{1,0:T(8,128)(2,1)S(1)} %far.2.refs_0_), channel_id=1, source_target_pairs={{0,3},{1,2},{2,1},{3,0},{4,7},{5,6},{6,5},{7,4},{8,11},{9,10},{10,... | collective-permute-start | bytes 38408 | tf_op jit(solution)/shard_map/ppermute | solution.py:61
  18.4 4.7 %collective-permute-start.6 = (bf16[80,80]{1,0:T(8,128)(2,1)S(1)}, bf16[80,80]{1,0:T(8,128)(2,1)S(1)}, u32[]{:S(2)}, u32[]{:S(2)}) collective-permute-start(bf16[80,80]{1,0:T(8,128)(2,1)S(1)} %far.2.refs_0_), channel_id=1, source_target_pairs={{0,2},{1,3},{2,0},{3,1},{4,6},{5,7},{6,4},{7,5},{8,10},{9,11},{10,... | collective-permute-start | bytes 38408 | tf_op jit(solution)/shard_map/ppermute | solution.py:61
  19.0 4.3 %collective-permute-start.5 = (bf16[80,80]{1,0:T(8,128)(2,1)S(1)}, bf16[80,80]{1,0:T(8,128)(2,1)S(1)}, u32[]{:S(2)}, u32[]{:S(2)}) collective-permute-start(bf16[80,80]{1,0:T(8,128)(2,1)S(1)} %far.2.refs_0_), channel_id=1, source_target_pairs={{0,1},{1,0},{2,3},{3,2},{4,5},{5,4},{6,7},{7,6},{8,9},{9,8},{10,11... | collective-permute-start | bytes 38408 | tf_op jit(solution)/shard_map/ppermute | solution.py:61
  24.0 5.8 %collective-permute-start.10 = (bf16[80,80]{1,0:T(8,128)(2,1)S(1)}, bf16[80,80]{1,0:T(8,128)(2,1)S(1)}, u32[]{:S(2)}, u32[]{:S(2)}) collective-permute-start(bf16[80,80]{1,0:T(8,128)(2,1)S(1)} %get-tuple-element.27.refs_0_), channel_id=1, source_target_pairs={{0,3},{1,2},{2,1},{3,0},{4,7},{5,6},{6,5},{7,4},{8,11},{9,10},{10,... | collective-permute-start | bytes 38408 | tf_op jit(solution)/shard_map/ppermute | solution.py:61
  26.4 4.7 %collective-permute-start.9 = (bf16[80,80]{1,0:T(8,128)(2,1)S(1)}, bf16[80,80]{1,0:T(8,128)(2,1)S(1)}, u32[]{:S(2)}, u32[]{:S(2)}) collective-permute-start(bf16[80,80]{1,0:T(8,128)(2,1)S(1)} %get-tuple-element.27.refs_0_), channel_id=1, source_target_pairs={{0,2},{1,3},{2,0},{3,1},{4,6},{5,7},{6,4},{7,5},{8,10},{9,11},{10,... | collective-permute-start | bytes 38408 | tf_op jit(solution)/shard_map/ppermute | solution.py:61
  27.3 4.0 %collective-permute-start.8 = (bf16[80,80]{1,0:T(8,128)(2,1)S(1)}, bf16[80,80]{1,0:T(8,128)(2,1)S(1)}, u32[]{:S(2)}, u32[]{:S(2)}) collective-permute-start(bf16[80,80]{1,0:T(8,128)(2,1)S(1)} %get-tuple-element.27.refs_0_), channel_id=1, source_target_pairs={{0,1},{1,0},{2,3},{3,2},{4,5},{5,4},{6,7},{7,6},{8,9},{9,8},{10,11... | collective-permute-start | bytes 38408 | tf_op jit(solution)/shard_map/ppermute | solution.py:61
  31.5 2.3 %collective-permute-start.11 = (bf16[192,128]{1,0:T(8,128)(2,1)S(1)}, bf16[192,128]{1,0:T(8,128)(2,1)S(1)}, u32[]{:S(2)}, u32[]{:S(2)}) collective-permute-start(bf16[192,128]{1,0:T(8,128)(2,1)S(1)} %columns.3.own_ref), channel_id=1, source_target_pairs={{0,4},{4,0},{8,12},{12,8},{16,20},{20,16},{24,28},{28,24},{1,5},{5... | collective-permute-start | bytes 147464 | tf_op jit(solution)/shard_map/ppermute | solution.py:65
  31.5 5.1 %collective-permute-start.12 = (bf16[192,128]{1,0:T(8,128)(2,1)S(1)}, bf16[192,128]{1,0:T(8,128)(2,1)S(1)}, u32[]{:S(2)}, u32[]{:S(2)}) collective-permute-start(bf16[192,128]{1,0:T(8,128)(2,1)S(1)} %columns.3.own_ref), channel_id=1, source_target_pairs={{0,28},{4,8},{8,4},{12,16},{16,12},{20,24},{24,20},{28,0},{1,29},{... | collective-permute-start | bytes 147464 | tf_op jit(solution)/shard_map/ppermute | solution.py:70
  33.8 7.7 %copy-start.3 = (bf16[24,80,192]{2,1,0:T(8,128)(2,1)S(1)}, bf16[24,80,192]{2,1,0:T(8,128)(2,1)}, u32[]{:S(2)}) copy-start(bf16[24,80,192]{2,1,0:T(8,128)(2,1)} %shape_ref.1) | copy-start | bytes 2211844
  33.8 7.7 %copy-start.4 = (s32[24,64]{1,0:T(8,128)S(1)}, s32[24,64]{1,0:T(8,128)}, u32[]{:S(2)}) copy-start(s32[24,64]{1,0:T(8,128)} %ids_ref.1) | copy-start | bytes 18436
  33.8 9.7 %copy-start.2 = (bf16[24,80,320]{2,1,0:T(8,128)(2,1)S(1)}, bf16[24,80,320]{2,1,0:T(8,128)(2,1)}, u32[]{:S(2)}) copy-start(bf16[24,80,320]{2,1,0:T(8,128)(2,1)} %refs_4_.3) | copy-start | bytes 3686404
  37.1 5.7 %collective-permute-start.15 = (bf16[80,80]{1,0:T(8,128)(2,1)S(1)}, bf16[80,80]{1,0:T(8,128)(2,1)S(1)}, u32[]{:S(2)}, u32[]{:S(2)}) collective-permute-start(bf16[80,80]{1,0:T(8,128)(2,1)S(1)} %far.3.refs_0_), channel_id=1, source_target_pairs={{0,3},{1,2},{2,1},{3,0},{4,7},{5,6},{6,5},{7,4},{8,11},{9,10},{10,... | collective-permute-start | bytes 38408 | tf_op jit(solution)/shard_map/ppermute | solution.py:61
  38.6 4.7 %collective-permute-start.14 = (bf16[80,80]{1,0:T(8,128)(2,1)S(1)}, bf16[80,80]{1,0:T(8,128)(2,1)S(1)}, u32[]{:S(2)}, u32[]{:S(2)}) collective-permute-start(bf16[80,80]{1,0:T(8,128)(2,1)S(1)} %far.3.refs_0_), channel_id=1, source_target_pairs={{0,2},{1,3},{2,0},{3,1},{4,6},{5,7},{6,4},{7,5},{8,10},{9,11},{10,... | collective-permute-start | bytes 38408 | tf_op jit(solution)/shard_map/ppermute | solution.py:61
  39.5 4.0 %collective-permute-start.13 = (bf16[80,80]{1,0:T(8,128)(2,1)S(1)}, bf16[80,80]{1,0:T(8,128)(2,1)S(1)}, u32[]{:S(2)}, u32[]{:S(2)}) collective-permute-start(bf16[80,80]{1,0:T(8,128)(2,1)S(1)} %far.3.refs_0_), channel_id=1, source_target_pairs={{0,1},{1,0},{2,3},{3,2},{4,5},{5,4},{6,7},{7,6},{8,9},{9,8},{10,11... | collective-permute-start | bytes 38408 | tf_op jit(solution)/shard_map/ppermute | solution.py:61
  45.1 2.3 %collective-permute-start.16 = (bf16[48,192]{1,0:T(8,128)(2,1)S(1)}, bf16[48,192]{1,0:T(8,128)(2,1)S(1)}, u32[]{:S(2)}, u32[]{:S(2)}) collective-permute-start(bf16[48,192]{1,0:T(8,128)(2,1)S(1)} %get-tuple-element.34), channel_id=1, source_target_pairs={{0,4},{4,0},{8,12},{12,8},{16,20},{20,16},{24,28},{28,24},{1,5},{5... | collective-permute-start | bytes 55304 | tf_op jit(solution)/shard_map/ppermute | solution.py:65
  45.1 4.2 %collective-permute-start.17 = (bf16[48,192]{1,0:T(8,128)(2,1)S(1)}, bf16[48,192]{1,0:T(8,128)(2,1)S(1)}, u32[]{:S(2)}, u32[]{:S(2)}) collective-permute-start(bf16[48,192]{1,0:T(8,128)(2,1)S(1)} %get-tuple-element.35), channel_id=1, source_target_pairs={{0,28},{4,8},{8,4},{12,16},{16,12},{20,24},{24,20},{28,0},{1,29},{... | collective-permute-start | bytes 55304 | tf_op jit(solution)/shard_map/ppermute | solution.py:70
  49.4 5.5 %collective-permute-start.18 = (bf16[16,192]{1,0:T(8,128)(2,1)S(1)}, bf16[16,192]{1,0:T(8,128)(2,1)S(1)}, u32[]{:S(2)}, u32[]{:S(2)}) collective-permute-start(bf16[16,192]{1,0:T(8,128)(2,1)S(1)} %get-tuple-element.37), channel_id=1, source_target_pairs={{0,3},{1,2},{2,1},{3,0},{4,7},{5,6},{6,5},{7,4},{8,11},{9,10},{10,... | collective-permute-start | bytes 18440 | tf_op jit(solution)/shard_map/ppermute | solution.py:583
  51.8 4.6 %collective-permute-start.19 = (bf16[16,192]{1,0:T(8,128)(2,1)S(1)}, bf16[16,192]{1,0:T(8,128)(2,1)S(1)}, u32[]{:S(2)}, u32[]{:S(2)}) collective-permute-start(bf16[16,192]{1,0:T(8,128)(2,1)S(1)} %get-tuple-element.38), channel_id=1, source_target_pairs={{0,2},{1,3},{2,0},{3,1},{4,6},{5,7},{6,4},{7,5},{8,10},{9,11},{10,... | collective-permute-start | bytes 18440 | tf_op jit(solution)/shard_map/ppermute | solution.py:583
  52.7 3.7 %collective-permute-start.20 = (bf16[16,192]{1,0:T(8,128)(2,1)S(1)}, bf16[16,192]{1,0:T(8,128)(2,1)S(1)}, u32[]{:S(2)}, u32[]{:S(2)}) collective-permute-start(bf16[16,192]{1,0:T(8,128)(2,1)S(1)} %get-tuple-element.39), channel_id=1, source_target_pairs={{0,1},{1,0},{2,3},{3,2},{4,5},{5,4},{6,7},{7,6},{8,9},{9,8},{10,11... | collective-permute-start | bytes 18440 | tf_op jit(solution)/shard_map/ppermute | solution.py:583

commit v6 on v5

--- a/solution.py
+++ b/solution.py
@@ -12,7 +12,6 @@
 HALF = jnp.bfloat16
 FULL = jnp.float32
 LANES = 128
-PICK = 8
 QUAD = 4
 NT = (((1,), (1,)), ((), ()))
 VMEM = pl.BlockSpec(memory_space=pltpu.VMEM)
@@ -108,12 +107,12 @@
     rows_part = round_up(3 * elements, 16)
     part, inside = window(nb_ref[...], elements)
     bases = jnp.concatenate([iota((1, elements), 1), part * rows_part + inside], axis=0).astype(FULL)
-    deep = elements * PICK
+    deep = elements * QUAD
     shape = (deep, elements)
-    behind = iota(shape, 0) - PICK * iota(shape, 1)
-    owner = hit(jnp.logical_and(behind >= 0, behind < PICK)).astype(HALF)
+    behind = iota(shape, 0) - QUAD * iota(shape, 1)
+    owner = hit(jnp.logical_and(behind >= 0, behind < QUAD)).astype(HALF)
     columns = lax.dot_general(owner, bases.astype(HALF), NT, preferred_element_type=FULL)
-    shape = (elements, PICK, pick_out.shape[1])
+    shape = (elements, QUAD, pick_out.shape[1])
     row, lane = iota(shape, 1).reshape(deep, -1), iota(shape, 2).reshape(deep, -1)
     offset = jnp.where(row < 3, lane - elements * row, -1).astype(FULL)
     for k in range(faces + 1):
@@ -261,22 +260,21 @@
     picked = jnp.dot(pick_ref[...], stacked, preferred_element_type=FULL).astype(HALF)
     image[...] = jnp.zeros(image.shape, FULL)
     deep = full // (2 * LANES) * (2 * LANES)
-    low = iota((2 * PICK, LANES), 1) < LANES // 2
-    for pair in range(elements // 2):
-        starts = [k * elements * PICK + pair * 2 * PICK for k in range(slots)]
-        lefts = [picked[start : start + 2 * PICK] for start in starts]
+    low = iota((4 * QUAD, LANES), 1) < LANES // 2
+    for first in range(0, elements, 4):
+        starts = [(k * elements + first) * QUAD for k in range(slots)]
+        lefts = [picked[start : start + 4 * QUAD] for start in starts]
         tails = [left[:, deep:] for left in lefts]
         tails = [jnp.where(low, *tails[k : k + 2]) if k + 1 < slots else tails[k] for k in range(0, slots, 2)]
         left = jnp.concatenate([left[:, :deep] for left in lefts] + tails, axis=1)
-        for side in range(2):
-            e = 2 * pair + side
+        for i in range(4):
+            e = first + i
             ends = [widened(jac_ref[e, k][:, deep:], LANES) for k in range(slots)]
             for k in range(1, slots, 2):
                 ends[k - 1] = ends[k - 1] + pltpu.roll(ends[k], LANES // 2, 1)
             blocks = jnp.concatenate([jac_ref[e, k][:, :deep] for k in range(slots)] + ends[::2], axis=1)
             product = lax.dot_general(left, blocks, NT, preferred_element_type=FULL)
-            first = side * PICK
-            image[pl.ds(e, 3, stride=elements), :width] = product[first : first + 3]
+            image[pl.ds(e, 3, stride=elements), :width] = product[i * QUAD : i * QUAD + 3]
 
 
 def twice(tail):
@@ -488,7 +486,7 @@
         [in_hbm(neighbours.T), in_hbm(pseudo_shift), in_hbm(adj_hbm), in_hbm(rhs), in_hbm(jac_blocks)],
         [HBM] * 5,
         [
-            jax.ShapeDtypeStruct((slots * elements * PICK, stacked), HALF),
+            jax.ShapeDtypeStruct((slots * elements * QUAD, stacked), HALF),
             jax.ShapeDtypeStruct((tall, LANES), FULL),
             pltpu.SMEM((round_up(elements * (slots - 1) + GROUP, LANES),), jnp.int32),
             pltpu.SMEM((1,), jnp.int32),
@@ -526,7 +524,7 @@
         near_inputs = [own, mate, pick, shift, adj, rhs]
         far_scratch = [
             pltpu.VMEM((elements + 8, 16, stride), HALF),
-            pltpu.VMEM((elements, PICK, LANES), FULL),
+            pltpu.VMEM((elements, 8, LANES), FULL),
             image,
         ]
         (near,) = call(

time: 57.2 us -> 56.9 us (level)
  no operation moved by 1% of the time
where the time goes in v6:
time: 56.9 us; the launch traced here: 56.7 us
  starting transfers between devices  30.9 us (54%)
  waiting for transfers between devices  13.3 us (23%)
  Pallas kernels  11.1 us (20%)
  between operations  0.78 us (1%)
  other arithmetic  0.61 us (1%)
    ppermute x12, starting transfers between devices, over_blk(): lax.ppermute(block, 'blk', [(i, i ^ k) for i in range(count)])  19.1 us
    pallas_call x11, Pallas kernels, call(): pl.pallas_call(kernel, in_specs=specs, out_specs=[SMEM if getattr(out, 'm...  11.1 us
    ppermute x12, waiting for transfers between devices, over_blk(): lax.ppermute(block, 'blk', [(i, i ^ k) for i in range(count)])  8.79 us
    ppermute x3, starting transfers between devices, to_far(): lax.ppermute(block, 'dom', [(i, ((i + 1 ^ 1) - 1) % count) for i in range...  7.19 us
    ppermute x3, starting transfers between devices, local(): lax.ppermute(pieces[k], 'blk', [(i, i ^ k) for i in range(count)])[:9]  4.45 us
    ppermute x3, waiting for transfers between devices, local(): lax.ppermute(pieces[k], 'blk', [(i, i ^ k) for i in range(count)])[:9]  2.61 us
    ppermute x3, waiting for transfers between devices, to_far(): lax.ppermute(block, 'dom', [(i, ((i + 1 ^ 1) - 1) % count) for i in range...  1.91 us
  transfers between devices with their start and end apart: 21, of which 14 were waited for; matrix products, arithmetic and copies ran while one was open for 0% of the time, Pallas kernels for 14%

profile of v6, /device:TPU:0, one launch (start us, length us, event | category | flops | bytes accessed | tf_op | source)
XLA Modules:
  0.0 56.7 jit_solution(1571015849586400863)
XLA Ops:
  0.6 5.1 %collective-permute-start.2 = (f32[72,80]{1,0:T(8,128)}, f32[72,80]{1,0:T(8,128)S(1)}, u32[]{:S(2)}, u32[]{:S(2)}) collective-permute-start(f32[72,80]{1,0:T(8,128)} %bitcast.11), channel_id=1, source_target_pairs={{0,3},{1,2},{2,1},{3,0},{4,7},{5,6},{6,5},{7,4},{8,11},{9,10},{10,... | collective-permute-start | bytes 69128 | tf_op jit(solution)/shard_map/ppermute | solution.py:60
  5.8 0.6 %collective-permute-start = (f32[72,80]{1,0:T(8,128)}, f32[72,80]{1,0:T(8,128)S(1)}, u32[]{:S(2)}, u32[]{:S(2)}) collective-permute-start(f32[72,80]{1,0:T(8,128)} %bitcast.13), channel_id=1, source_target_pairs={{0,1},{1,0},{2,3},{3,2},{4,5},{5,4},{6,7},{7,6},{8,9},{9,8},{10,11... | collective-permute-start | bytes 69128 | tf_op jit(solution)/shard_map/ppermute | solution.py:60
  6.4 1.8 %slots.1 = (bf16[672,256]{1,0:T(8,128)(2,1)S(1)}, f32[80,128]{1,0:T(8,128)S(1)}, s32[256]{0:T(256)S(4)}, s32[1]{0:T(128)S(4)}, f32[72,80]{1,0:T(8,128)S(1)}, /*index=5*/f32[72,80]{1,0:T(8,128)S(1)}) custom-call(s32[6,24]{1,0:T(8,128)} %bitcast.15, f32[24]{0:T(128)} %shift_hbm.1, f32[72,80]{1,0:T(8,128)} %bitcast.14, f32[72,80]{1,0:T(8,128)} %bitcast.10, ...), custom_call_target="tpu_custom_call" | custom-call | bytes 16777216 | tf_op jit(solution)/shard_map/slots/pallas_call | solution.py:41
  8.2 2.6 %collective-permute-done.1.refs_2_ = f32[72,80]{1,0:T(8,128)S(1)} collective-permute-done((f32[72,80]{1,0:T(8,128)}, f32[72,80]{1,0:T(8,128)S(1)}, u32[]{:S(2)}, u32[]{:S(2)}) %collective-permute-start.1) | collective-permute-done | bytes 23072 | tf_op jit(solution)/shard_map/ppermute | solution.py:60
  11.0 2.5 %collective-permute-start.4 = (bf16[192,128]{1,0:T(8,128)(2,1)S(1)}, bf16[192,128]{1,0:T(8,128)(2,1)S(1)}, u32[]{:S(2)}, u32[]{:S(2)}) collective-permute-start(bf16[192,128]{1,0:T(8,128)(2,1)S(1)} %columns.2.own_ref), channel_id=1, source_target_pairs={{0,28},{4,8},{8,4},{12,16},{16,12},{20,24},{24,20},{28,0},{1,29},{... | collective-permute-start | bytes 147464 | tf_op jit(solution)/shard_map/ppermute | solution.py:69
  13.6 2.6 %near.2.near_ref = f32[72,80]{1,0:T(8,128)S(1)} custom-call(bf16[192,128]{1,0:T(8,128)(2,1)S(1)} %columns.2.own_ref, bf16[192,128]{1,0:T(8,128)(2,1)S(1)} %collective-permute-done.3.mate_ref, bf16[672,256]{1,0:T(8,128)(2,1)S(1)} %get-tuple-element.22.pick_ref, f32[80,128]{1,0:T(8,128)S(1)} %get-tuple-element.23.shift_ref, ...), custom_call_target="tpu_custom_call" | custom-call | bytes 12582912 | tf_op jit(solution)/shard_map/near/pallas_call | solution.py:41
  16.7 1.6 %collective-permute-start.7 = (bf16[80,80]{1,0:T(8,128)(2,1)S(1)}, bf16[80,80]{1,0:T(8,128)(2,1)S(1)}, u32[]{:S(2)}, u32[]{:S(2)}) collective-permute-start(bf16[80,80]{1,0:T(8,128)(2,1)S(1)} %far.2.refs_0_), channel_id=1, source_target_pairs={{0,3},{1,2},{2,1},{3,0},{4,7},{5,6},{6,5},{7,4},{8,11},{9,10},{10,... | collective-permute-start | bytes 38408 | tf_op jit(solution)/shard_map/ppermute | solution.py:60
  18.2 0.6 %collective-permute-start.6 = (bf16[80,80]{1,0:T(8,128)(2,1)S(1)}, bf16[80,80]{1,0:T(8,128)(2,1)S(1)}, u32[]{:S(2)}, u32[]{:S(2)}) collective-permute-start(bf16[80,80]{1,0:T(8,128)(2,1)S(1)} %far.2.refs_0_), channel_id=1, source_target_pairs={{0,2},{1,3},{2,0},{3,1},{4,6},{5,7},{6,4},{7,5},{8,10},{9,11},{10,... | collective-permute-start | bytes 38408 | tf_op jit(solution)/shard_map/ppermute | solution.py:60
  18.8 2.3 %collective-permute-start.5 = (bf16[80,80]{1,0:T(8,128)(2,1)S(1)}, bf16[80,80]{1,0:T(8,128)(2,1)S(1)}, u32[]{:S(2)}, u32[]{:S(2)}) collective-permute-start(bf16[80,80]{1,0:T(8,128)(2,1)S(1)} %far.2.refs_0_), channel_id=1, source_target_pairs={{0,1},{1,0},{2,3},{3,2},{4,5},{5,4},{6,7},{7,6},{8,9},{9,8},{10,11... | collective-permute-start | bytes 38408 | tf_op jit(solution)/shard_map/ppermute | solution.py:60
  21.1 1.3 %collective-permute-done.7.refs_3_ = bf16[80,80]{1,0:T(8,128)(2,1)S(1)} collective-permute-done((bf16[80,80]{1,0:T(8,128)(2,1)S(1)}, bf16[80,80]{1,0:T(8,128)(2,1)S(1)}, u32[]{:S(2)}, u32[]{:S(2)}) %collective-permute-start.7) | collective-permute-done | bytes 12832 | tf_op jit(solution)/shard_map/ppermute | solution.py:60
  23.1 0.7 %update.1 = (f32[72,80]{1,0:T(8,128)S(1)}, bf16[80,80]{1,0:T(8,128)(2,1)S(1)}) custom-call(bf16[80,80]{1,0:T(8,128)(2,1)S(1)} %far.2.refs_0_, bf16[80,80]{1,0:T(8,128)(2,1)S(1)} %collective-permute-done.5.refs_1_, bf16[80,80]{1,0:T(8,128)(2,1)S(1)} %collective-permute-done.6.refs_2_, bf16[80,80]{1,0:T(8,128)(2,1)S(1)} %collective-permute-done.7.refs_3_, ...), custom_call_target="tpu_custom_call" | custom-call | bytes 8388608 | tf_op jit(solution)/shard_map/update/pallas_call | solution.py:41
  23.8 2.4 %collective-permute-start.10 = (bf16[80,80]{1,0:T(8,128)(2,1)S(1)}, bf16[80,80]{1,0:T(8,128)(2,1)S(1)}, u32[]{:S(2)}, u32[]{:S(2)}) collective-permute-start(bf16[80,80]{1,0:T(8,128)(2,1)S(1)} %get-tuple-element.27.refs_0_), channel_id=1, source_target_pairs={{0,3},{1,2},{2,1},{3,0},{4,7},{5,6},{6,5},{7,4},{8,11},{9,10},{10,... | collective-permute-start | bytes 38408 | tf_op jit(solution)/shard_map/ppermute | solution.py:60
  26.2 0.9 %collective-permute-start.9 = (bf16[80,80]{1,0:T(8,128)(2,1)S(1)}, bf16[80,80]{1,0:T(8,128)(2,1)S(1)}, u32[]{:S(2)}, u32[]{:S(2)}) collective-permute-start(bf16[80,80]{1,0:T(8,128)(2,1)S(1)} %get-tuple-element.27.refs_0_), channel_id=1, source_target_pairs={{0,2},{1,3},{2,0},{3,1},{4,6},{5,7},{6,4},{7,5},{8,10},{9,11},{10,... | collective-permute-start | bytes 38408 | tf_op jit(solution)/shard_map/ppermute | solution.py:60
  27.1 1.1 %collective-permute-start.8 = (bf16[80,80]{1,0:T(8,128)(2,1)S(1)}, bf16[80,80]{1,0:T(8,128)(2,1)S(1)}, u32[]{:S(2)}, u32[]{:S(2)}) collective-permute-start(bf16[80,80]{1,0:T(8,128)(2,1)S(1)} %get-tuple-element.27.refs_0_), channel_id=1, source_target_pairs={{0,1},{1,0},{2,3},{3,2},{4,5},{5,4},{6,7},{7,6},{8,9},{9,8},{10,11... | collective-permute-start | bytes 38408 | tf_op jit(solution)/shard_map/ppermute | solution.py:60
  28.3 1.3 %collective-permute-done.10.refs_3_ = bf16[80,80]{1,0:T(8,128)(2,1)S(1)} collective-permute-done((bf16[80,80]{1,0:T(8,128)(2,1)S(1)}, bf16[80,80]{1,0:T(8,128)(2,1)S(1)}, u32[]{:S(2)}, u32[]{:S(2)}) %collective-permute-start.10) | collective-permute-done | bytes 12832 | tf_op jit(solution)/shard_map/ppermute | solution.py:60
  29.5 1.4 %collective-permute-done.9.refs_2_ = bf16[80,80]{1,0:T(8,128)(2,1)S(1)} collective-permute-done((bf16[80,80]{1,0:T(8,128)(2,1)S(1)}, bf16[80,80]{1,0:T(8,128)(2,1)S(1)}, u32[]{:S(2)}, u32[]{:S(2)}) %collective-permute-start.9) | collective-permute-done | bytes 12832 | tf_op jit(solution)/shard_map/ppermute | solution.py:60
  31.3 2.3 %collective-permute-start.12 = (bf16[192,128]{1,0:T(8,128)(2,1)S(1)}, bf16[192,128]{1,0:T(8,128)(2,1)S(1)}, u32[]{:S(2)}, u32[]{:S(2)}) collective-permute-start(bf16[192,128]{1,0:T(8,128)(2,1)S(1)} %columns.3.own_ref), channel_id=1, source_target_pairs={{0,28},{4,8},{8,4},{12,16},{16,12},{20,24},{24,20},{28,0},{1,29},{... | collective-permute-start | bytes 147464 | tf_op jit(solution)/shard_map/ppermute | solution.py:69
  33.6 2.6 %near.3.near_ref = f32[72,80]{1,0:T(8,128)S(1)} custom-call(bf16[192,128]{1,0:T(8,128)(2,1)S(1)} %columns.3.own_ref, bf16[192,128]{1,0:T(8,128)(2,1)S(1)} %collective-permute-done.11.mate_ref, bf16[672,256]{1,0:T(8,128)(2,1)S(1)} %get-tuple-element.22.pick_ref, f32[80,128]{1,0:T(8,128)S(1)} %get-tuple-element.23.shift_ref, ...), custom_call_target="tpu_custom_call" | custom-call | bytes 12582912 | tf_op jit(solution)/shard_map/near/pallas_call | solution.py:41
  36.7 1.5 %collective-permute-start.15 = (bf16[80,80]{1,0:T(8,128)(2,1)S(1)}, bf16[80,80]{1,0:T(8,128)(2,1)S(1)}, u32[]{:S(2)}, u32[]{:S(2)}) collective-permute-start(bf16[80,80]{1,0:T(8,128)(2,1)S(1)} %far.3.refs_0_), channel_id=1, source_target_pairs={{0,3},{1,2},{2,1},{3,0},{4,7},{5,6},{6,5},{7,4},{8,11},{9,10},{10,... | collective-permute-start | bytes 38408 | tf_op jit(solution)/shard_map/ppermute | solution.py:60
  38.2 0.9 %collective-permute-start.14 = (bf16[80,80]{1,0:T(8,128)(2,1)S(1)}, bf16[80,80]{1,0:T(8,128)(2,1)S(1)}, u32[]{:S(2)}, u32[]{:S(2)}) collective-permute-start(bf16[80,80]{1,0:T(8,128)(2,1)S(1)} %far.3.refs_0_), channel_id=1, source_target_pairs={{0,2},{1,3},{2,0},{3,1},{4,6},{5,7},{6,4},{7,5},{8,10},{9,11},{10,... | collective-permute-start | bytes 38408 | tf_op jit(solution)/shard_map/ppermute | solution.py:60
  39.1 2.0 %collective-permute-start.13 = (bf16[80,80]{1,0:T(8,128)(2,1)S(1)}, bf16[80,80]{1,0:T(8,128)(2,1)S(1)}, u32[]{:S(2)}, u32[]{:S(2)}) collective-permute-start(bf16[80,80]{1,0:T(8,128)(2,1)S(1)} %far.3.refs_0_), channel_id=1, source_target_pairs={{0,1},{1,0},{2,3},{3,2},{4,5},{5,4},{6,7},{7,6},{8,9},{9,8},{10,11... | collective-permute-start | bytes 38408 | tf_op jit(solution)/shard_map/ppermute | solution.py:60
  41.2 0.7 %nodes.1 = (bf16[192,1536]{1,0:T(8,128)(2,1)S(1)}, s32[12,128]{1,0:T(8,128)S(1)}, bf16[24,80,192]{2,1,0:T(8,128)(2,1)S(1)}) custom-call(s32[24,64]{1,0:T(8,128)S(1)} %copy-done.4, bf16[24,80,192]{2,1,0:T(8,128)(2,1)S(1)} %copy-done.3), custom_call_target="tpu_custom_call" | custom-call | bytes 3145728 | tf_op jit(solution)/shard_map/nodes/pallas_call | solution.py:41
  41.8 0.7 %collective-permute-done.15.refs_3_ = bf16[80,80]{1,0:T(8,128)(2,1)S(1)} collective-permute-done((bf16[80,80]{1,0:T(8,128)(2,1)S(1)}, bf16[80,80]{1,0:T(8,128)(2,1)S(1)}, u32[]{:S(2)}, u32[]{:S(2)}) %collective-permute-start.15) | collective-permute-done | bytes 12832 | tf_op jit(solution)/shard_map/ppermute | solution.py:60
  43.1 1.6 %gradient.1 = (f32[72,80]{1,0:T(8,128)}, f32[48,192]{1,0:T(8,128)S(1)}, bf16[48,192]{1,0:T(8,128)(2,1)S(1)}, bf16[48,192]{1,0:T(8,128)(2,1)S(1)}) custom-call(bf16[80,80]{1,0:T(8,128)(2,1)S(1)} %far.3.refs_0_, bf16[80,80]{1,0:T(8,128)(2,1)S(1)} %collective-permute-done.13.refs_1_, bf16[80,80]{1,0:T(8,128)(2,1)S(1)} %collective-permute-done.14.refs_2_, ...), custom_call_target="tpu_custom_call" | custom-call | tf_op jit(solution)/shard_map/gradient/pallas_call | solution.py:41
  44.8 2.4 %collective-permute-start.17 = (bf16[48,192]{1,0:T(8,128)(2,1)S(1)}, bf16[48,192]{1,0:T(8,128)(2,1)S(1)}, u32[]{:S(2)}, u32[]{:S(2)}) collective-permute-start(bf16[48,192]{1,0:T(8,128)(2,1)S(1)} %get-tuple-element.35), channel_id=1, source_target_pairs={{0,28},{4,8},{8,4},{12,16},{16,12},{20,24},{24,20},{28,0},{1,29},{... | collective-permute-start | bytes 55304 | tf_op jit(solution)/shard_map/ppermute | solution.py:69
  47.2 1.8 %collective-permute-done.17.far_ref = bf16[48,192]{1,0:T(8,128)(2,1)S(1)} collective-permute-done((bf16[48,192]{1,0:T(8,128)(2,1)S(1)}, bf16[48,192]{1,0:T(8,128)(2,1)S(1)}, u32[]{:S(2)}, u32[]{:S(2)}) %collective-permute-start.17) | collective-permute-done | bytes 18464 | tf_op jit(solution)/shard_map/ppermute | solution.py:69
  49.0 2.4 %collective-permute-start.18 = (bf16[16,192]{1,0:T(8,128)(2,1)S(1)}, bf16[16,192]{1,0:T(8,128)(2,1)S(1)}, u32[]{:S(2)}, u32[]{:S(2)}) collective-permute-start(bf16[16,192]{1,0:T(8,128)(2,1)S(1)} %get-tuple-element.37), channel_id=1, source_target_pairs={{0,3},{1,2},{2,1},{3,0},{4,7},{5,6},{6,5},{7,4},{8,11},{9,10},{10,... | collective-permute-start | bytes 18440 | tf_op jit(solution)/shard_map/ppermute | solution.py:581
  51.5 0.9 %collective-permute-start.19 = (bf16[16,192]{1,0:T(8,128)(2,1)S(1)}, bf16[16,192]{1,0:T(8,128)(2,1)S(1)}, u32[]{:S(2)}, u32[]{:S(2)}) collective-permute-start(bf16[16,192]{1,0:T(8,128)(2,1)S(1)} %get-tuple-element.38), channel_id=1, source_target_pairs={{0,2},{1,3},{2,0},{3,1},{4,6},{5,7},{6,4},{7,5},{8,10},{9,11},{10,... | collective-permute-start | bytes 18440 | tf_op jit(solution)/shard_map/ppermute | solution.py:581
  52.4 1.1 %collective-permute-start.20 = (bf16[16,192]{1,0:T(8,128)(2,1)S(1)}, bf16[16,192]{1,0:T(8,128)(2,1)S(1)}, u32[]{:S(2)}, u32[]{:S(2)}) collective-permute-start(bf16[16,192]{1,0:T(8,128)(2,1)S(1)} %get-tuple-element.39), channel_id=1, source_target_pairs={{0,1},{1,0},{2,3},{3,2},{4,5},{5,4},{6,7},{7,6},{8,9},{9,8},{10,11... | collective-permute-start | bytes 18440 | tf_op jit(solution)/shard_map/ppermute | solution.py:581
  53.5 1.1 %collective-permute-done.18 = bf16[16,192]{1,0:T(8,128)(2,1)S(1)} collective-permute-done((bf16[16,192]{1,0:T(8,128)(2,1)S(1)}, bf16[16,192]{1,0:T(8,128)(2,1)S(1)}, u32[]{:S(2)}, u32[]{:S(2)}) %collective-permute-start.18) | collective-permute-done | bytes 6176 | tf_op jit(solution)/shard_map/ppermute | solution.py:581
  54.5 1.5 %collective-permute-done.19 = bf16[16,192]{1,0:T(8,128)(2,1)S(1)} collective-permute-done((bf16[16,192]{1,0:T(8,128)(2,1)S(1)}, bf16[16,192]{1,0:T(8,128)(2,1)S(1)}, u32[]{:S(2)}, u32[]{:S(2)}) %collective-permute-start.19) | collective-permute-done | bytes 6176 | tf_op jit(solution)/shard_map/ppermute | solution.py:581
  56.1 0.6 %convert_add_fusion = f32[9,192]{1,0:T(8,128)} fusion(f32[9,192]{1,0:T(8,128)S(1)} %get-tuple-element.36, bf16[16,192]{1,0:T(8,128)(2,1)S(1)} %collective-permute-done.20, bf16[16,192]{1,0:T(8,128)(2,1)S(1)} %collective-permute-done.19, bf16[16,192]{1,0:T(8,128)(2,1)S(1)} %collective-permute-done.18), kind=kLoop, calls=%fused_computation | loop fusion | flops 10368 | bytes 24192 | tf_op jit(solution)/shard_map/add | solution.py:581
  (32 shorter events, 2.9 us)
Async XLA Ops:
  0.6 12.9 %copy-start = (bf16[24,7,80,320]{3,2,1,0:T(8,128)(2,1)S(1)}, bf16[24,7,80,320]{3,2,1,0:T(8,128)(2,1)}, u32[]{:S(2)}) copy-start(bf16[24,7,80,320]{3,2,1,0:T(8,128)(2,1)} %jac_ref.7) | copy-start | bytes 25804804
  0.6 7.6 %collective-permute-start.2 = (f32[72,80]{1,0:T(8,128)}, f32[72,80]{1,0:T(8,128)S(1)}, u32[]{:S(2)}, u32[]{:S(2)}) collective-permute-start(f32[72,80]{1,0:T(8,128)} %bitcast.11), channel_id=1, source_target_pairs={{0,3},{1,2},{2,1},{3,0},{4,7},{5,6},{6,5},{7,4},{8,11},{9,10},{10,... | collective-permute-start | bytes 69128 | tf_op jit(solution)/shard_map/ppermute | solution.py:60
  5.8 5.1 %collective-permute-start.1 = (f32[72,80]{1,0:T(8,128)}, f32[72,80]{1,0:T(8,128)S(1)}, u32[]{:S(2)}, u32[]{:S(2)}) collective-permute-start(f32[72,80]{1,0:T(8,128)} %bitcast.12), channel_id=1, source_target_pairs={{0,2},{1,3},{2,0},{3,1},{4,6},{5,7},{6,4},{7,5},{8,10},{9,11},{10,... | collective-permute-start | bytes 69128 | tf_op jit(solution)/shard_map/ppermute | solution.py:60
  5.8 5.1 %collective-permute-start = (f32[72,80]{1,0:T(8,128)}, f32[72,80]{1,0:T(8,128)S(1)}, u32[]{:S(2)}, u32[]{:S(2)}) collective-permute-start(f32[72,80]{1,0:T(8,128)} %bitcast.13), channel_id=1, source_target_pairs={{0,1},{1,0},{2,3},{3,2},{4,5},{5,4},{6,7},{7,6},{8,9},{9,8},{10,11... | collective-permute-start | bytes 69128 | tf_op jit(solution)/shard_map/ppermute | solution.py:60
  11.0 2.6 %collective-permute-start.3 = (bf16[192,128]{1,0:T(8,128)(2,1)S(1)}, bf16[192,128]{1,0:T(8,128)(2,1)S(1)}, u32[]{:S(2)}, u32[]{:S(2)}) collective-permute-start(bf16[192,128]{1,0:T(8,128)(2,1)S(1)} %columns.2.own_ref), channel_id=1, source_target_pairs={{0,4},{4,0},{8,12},{12,8},{16,20},{20,16},{24,28},{28,24},{1,5},{5... | collective-permute-start | bytes 147464 | tf_op jit(solution)/shard_map/ppermute | solution.py:64
  11.0 5.2 %collective-permute-start.4 = (bf16[192,128]{1,0:T(8,128)(2,1)S(1)}, bf16[192,128]{1,0:T(8,128)(2,1)S(1)}, u32[]{:S(2)}, u32[]{:S(2)}) collective-permute-start(bf16[192,128]{1,0:T(8,128)(2,1)S(1)} %columns.2.own_ref), channel_id=1, source_target_pairs={{0,28},{4,8},{8,4},{12,16},{16,12},{20,24},{24,20},{28,0},{1,29},{... | collective-permute-start | bytes 147464 | tf_op jit(solution)/shard_map/ppermute | solution.py:69
  13.6 9.5 %copy-start.1 = (bf16[24,80,320]{2,1,0:T(8,128)(2,1)S(1)}, bf16[24,80,320]{2,1,0:T(8,128)(2,1)}, u32[]{:S(2)}) copy-start(bf16[24,80,320]{2,1,0:T(8,128)(2,1)} %refs_4_.3) | copy-start | bytes 3686404
  16.7 5.8 %collective-permute-start.7 = (bf16[80,80]{1,0:T(8,128)(2,1)S(1)}, bf16[80,80]{1,0:T(8,128)(2,1)S(1)}, u32[]{:S(2)}, u32[]{:S(2)}) collective-permute-start(bf16[80,80]{1,0:T(8,128)(2,1)S(1)} %far.2.refs_0_), channel_id=1, source_target_pairs={{0,3},{1,2},{2,1},{3,0},{4,7},{5,6},{6,5},{7,4},{8,11},{9,10},{10,... | collective-permute-start | bytes 38408 | tf_op jit(solution)/shard_map/ppermute | solution.py:60
  18.2 4.7 %collective-permute-start.6 = (bf16[80,80]{1,0:T(8,128)(2,1)S(1)}, bf16[80,80]{1,0:T(8,128)(2,1)S(1)}, u32[]{:S(2)}, u32[]{:S(2)}) collective-permute-start(bf16[80,80]{1,0:T(8,128)(2,1)S(1)} %far.2.refs_0_), channel_id=1, source_target_pairs={{0,2},{1,3},{2,0},{3,1},{4,6},{5,7},{6,4},{7,5},{8,10},{9,11},{10,... | collective-permute-start | bytes 38408 | tf_op jit(solution)/shard_map/ppermute | solution.py:60
  18.8 4.3 %collective-permute-start.5 = (bf16[80,80]{1,0:T(8,128)(2,1)S(1)}, bf16[80,80]{1,0:T(8,128)(2,1)S(1)}, u32[]{:S(2)}, u32[]{:S(2)}) collective-permute-start(bf16[80,80]{1,0:T(8,128)(2,1)S(1)} %far.2.refs_0_), channel_id=1, source_target_pairs={{0,1},{1,0},{2,3},{3,2},{4,5},{5,4},{6,7},{7,6},{8,9},{9,8},{10,11... | collective-permute-start | bytes 38408 | tf_op jit(solution)/shard_map/ppermute | solution.py:60
  23.8 5.7 %collective-permute-start.10 = (bf16[80,80]{1,0:T(8,128)(2,1)S(1)}, bf16[80,80]{1,0:T(8,128)(2,1)S(1)}, u32[]{:S(2)}, u32[]{:S(2)}) collective-permute-start(bf16[80,80]{1,0:T(8,128)(2,1)S(1)} %get-tuple-element.27.refs_0_), channel_id=1, source_target_pairs={{0,3},{1,2},{2,1},{3,0},{4,7},{5,6},{6,5},{7,4},{8,11},{9,10},{10,... | collective-permute-start | bytes 38408 | tf_op jit(solution)/shard_map/ppermute | solution.py:60
  26.2 4.7 %collective-permute-start.9 = (bf16[80,80]{1,0:T(8,128)(2,1)S(1)}, bf16[80,80]{1,0:T(8,128)(2,1)S(1)}, u32[]{:S(2)}, u32[]{:S(2)}) collective-permute-start(bf16[80,80]{1,0:T(8,128)(2,1)S(1)} %get-tuple-element.27.refs_0_), channel_id=1, source_target_pairs={{0,2},{1,3},{2,0},{3,1},{4,6},{5,7},{6,4},{7,5},{8,10},{9,11},{10,... | collective-permute-start | bytes 38408 | tf_op jit(solution)/shard_map/ppermute | solution.py:60
  27.1 4.0 %collective-permute-start.8 = (bf16[80,80]{1,0:T(8,128)(2,1)S(1)}, bf16[80,80]{1,0:T(8,128)(2,1)S(1)}, u32[]{:S(2)}, u32[]{:S(2)}) collective-permute-start(bf16[80,80]{1,0:T(8,128)(2,1)S(1)} %get-tuple-element.27.refs_0_), channel_id=1, source_target_pairs={{0,1},{1,0},{2,3},{3,2},{4,5},{5,4},{6,7},{7,6},{8,9},{9,8},{10,11... | collective-permute-start | bytes 38408 | tf_op jit(solution)/shard_map/ppermute | solution.py:60
  31.3 2.3 %collective-permute-start.11 = (bf16[192,128]{1,0:T(8,128)(2,1)S(1)}, bf16[192,128]{1,0:T(8,128)(2,1)S(1)}, u32[]{:S(2)}, u32[]{:S(2)}) collective-permute-start(bf16[192,128]{1,0:T(8,128)(2,1)S(1)} %columns.3.own_ref), channel_id=1, source_target_pairs={{0,4},{4,0},{8,12},{12,8},{16,20},{20,16},{24,28},{28,24},{1,5},{5... | collective-permute-start | bytes 147464 | tf_op jit(solution)/shard_map/ppermute | solution.py:64
  31.3 5.0 %collective-permute-start.12 = (bf16[192,128]{1,0:T(8,128)(2,1)S(1)}, bf16[192,128]{1,0:T(8,128)(2,1)S(1)}, u32[]{:S(2)}, u32[]{:S(2)}) collective-permute-start(bf16[192,128]{1,0:T(8,128)(2,1)S(1)} %columns.3.own_ref), channel_id=1, source_target_pairs={{0,28},{4,8},{8,4},{12,16},{16,12},{20,24},{24,20},{28,0},{1,29},{... | collective-permute-start | bytes 147464 | tf_op jit(solution)/shard_map/ppermute | solution.py:69
  33.6 7.6 %copy-start.3 = (bf16[24,80,192]{2,1,0:T(8,128)(2,1)S(1)}, bf16[24,80,192]{2,1,0:T(8,128)(2,1)}, u32[]{:S(2)}) copy-start(bf16[24,80,192]{2,1,0:T(8,128)(2,1)} %shape_ref.1) | copy-start | bytes 2211844
  33.6 7.6 %copy-start.4 = (s32[24,64]{1,0:T(8,128)S(1)}, s32[24,64]{1,0:T(8,128)}, u32[]{:S(2)}) copy-start(s32[24,64]{1,0:T(8,128)} %ids_ref.1) | copy-start | bytes 18436
  33.6 9.5 %copy-start.2 = (bf16[24,80,320]{2,1,0:T(8,128)(2,1)S(1)}, bf16[24,80,320]{2,1,0:T(8,128)(2,1)}, u32[]{:S(2)}) copy-start(bf16[24,80,320]{2,1,0:T(8,128)(2,1)} %refs_4_.3) | copy-start | bytes 3686404
  36.7 5.8 %collective-permute-start.15 = (bf16[80,80]{1,0:T(8,128)(2,1)S(1)}, bf16[80,80]{1,0:T(8,128)(2,1)S(1)}, u32[]{:S(2)}, u32[]{:S(2)}) collective-permute-start(bf16[80,80]{1,0:T(8,128)(2,1)S(1)} %far.3.refs_0_), channel_id=1, source_target_pairs={{0,3},{1,2},{2,1},{3,0},{4,7},{5,6},{6,5},{7,4},{8,11},{9,10},{10,... | collective-permute-start | bytes 38408 | tf_op jit(solution)/shard_map/ppermute | solution.py:60
  38.2 4.7 %collective-permute-start.14 = (bf16[80,80]{1,0:T(8,128)(2,1)S(1)}, bf16[80,80]{1,0:T(8,128)(2,1)S(1)}, u32[]{:S(2)}, u32[]{:S(2)}) collective-permute-start(bf16[80,80]{1,0:T(8,128)(2,1)S(1)} %far.3.refs_0_), channel_id=1, source_target_pairs={{0,2},{1,3},{2,0},{3,1},{4,6},{5,7},{6,4},{7,5},{8,10},{9,11},{10,... | collective-permute-start | bytes 38408 | tf_op jit(solution)/shard_map/ppermute | solution.py:60
  39.1 4.0 %collective-permute-start.13 = (bf16[80,80]{1,0:T(8,128)(2,1)S(1)}, bf16[80,80]{1,0:T(8,128)(2,1)S(1)}, u32[]{:S(2)}, u32[]{:S(2)}) collective-permute-start(bf16[80,80]{1,0:T(8,128)(2,1)S(1)} %far.3.refs_0_), channel_id=1, source_target_pairs={{0,1},{1,0},{2,3},{3,2},{4,5},{5,4},{6,7},{7,6},{8,9},{9,8},{10,11... | collective-permute-start | bytes 38408 | tf_op jit(solution)/shard_map/ppermute | solution.py:60
  44.7 2.4 %collective-permute-start.16 = (bf16[48,192]{1,0:T(8,128)(2,1)S(1)}, bf16[48,192]{1,0:T(8,128)(2,1)S(1)}, u32[]{:S(2)}, u32[]{:S(2)}) collective-permute-start(bf16[48,192]{1,0:T(8,128)(2,1)S(1)} %get-tuple-element.34), channel_id=1, source_target_pairs={{0,4},{4,0},{8,12},{12,8},{16,20},{20,16},{24,28},{28,24},{1,5},{5... | collective-permute-start | bytes 55304 | tf_op jit(solution)/shard_map/ppermute | solution.py:64
  44.8 4.2 %collective-permute-start.17 = (bf16[48,192]{1,0:T(8,128)(2,1)S(1)}, bf16[48,192]{1,0:T(8,128)(2,1)S(1)}, u32[]{:S(2)}, u32[]{:S(2)}) collective-permute-start(bf16[48,192]{1,0:T(8,128)(2,1)S(1)} %get-tuple-element.35), channel_id=1, source_target_pairs={{0,28},{4,8},{8,4},{12,16},{16,12},{20,24},{24,20},{28,0},{1,29},{... | collective-permute-start | bytes 55304 | tf_op jit(solution)/shard_map/ppermute | solution.py:69
  49.0 5.5 %collective-permute-start.18 = (bf16[16,192]{1,0:T(8,128)(2,1)S(1)}, bf16[16,192]{1,0:T(8,128)(2,1)S(1)}, u32[]{:S(2)}, u32[]{:S(2)}) collective-permute-start(bf16[16,192]{1,0:T(8,128)(2,1)S(1)} %get-tuple-element.37), channel_id=1, source_target_pairs={{0,3},{1,2},{2,1},{3,0},{4,7},{5,6},{6,5},{7,4},{8,11},{9,10},{10,... | collective-permute-start | bytes 18440 | tf_op jit(solution)/shard_map/ppermute | solution.py:581
  51.5 4.6 %collective-permute-start.19 = (bf16[16,192]{1,0:T(8,128)(2,1)S(1)}, bf16[16,192]{1,0:T(8,128)(2,1)S(1)}, u32[]{:S(2)}, u32[]{:S(2)}) collective-permute-start(bf16[16,192]{1,0:T(8,128)(2,1)S(1)} %get-tuple-element.38), channel_id=1, source_target_pairs={{0,2},{1,3},{2,0},{3,1},{4,6},{5,7},{6,4},{7,5},{8,10},{9,11},{10,... | collective-permute-start | bytes 18440 | tf_op jit(solution)/shard_map/ppermute | solution.py:581
  52.4 3.7 %collective-permute-start.20 = (bf16[16,192]{1,0:T(8,128)(2,1)S(1)}, bf16[16,192]{1,0:T(8,128)(2,1)S(1)}, u32[]{:S(2)}, u32[]{:S(2)}) collective-permute-start(bf16[16,192]{1,0:T(8,128)(2,1)S(1)} %get-tuple-element.39), channel_id=1, source_target_pairs={{0,1},{1,0},{2,3},{3,2},{4,5},{5,4},{6,7},{7,6},{8,9},{9,8},{10,11... | collective-permute-start | bytes 18440 | tf_op jit(solution)/shard_map/ppermute | solution.py:581

commit v7 on v6

--- a/solution.py
+++ b/solution.py
@@ -383,8 +383,7 @@
     blks = lax.axis_size("blk")
     resid_refs = refs[:blks]
     inv_ref, adj_ref, shape_ref, low_ref, target_ref, adj_out = refs[blks : blks + 6]
-    part_outs = refs[blks + 6 : blks + 9]
-    sorted_ref, left_ref, sums_ref, update = refs[blks + 9 :]
+    mate_out, far_out, sorted_ref, left_ref, sums_ref, update = refs[blks + 6 :]
     adj = updated(resid_refs, inv_ref, adj_ref, update)
     adj_out[...] = adj[: adj_out.shape[0]]
     half = adj.astype(HALF)
@@ -422,29 +421,51 @@
     top, rest = split(jnp.concatenate(value, axis=1))
     sorted_ref[:tall] = top.astype(FULL)
     sorted_ref[tall:] = rest.astype(FULL)
-    deep = 16
+    node_sums(sorted_ref, low_ref, target_ref, left_ref, sums_ref, blks)
+    put_sums(mate_out, sums_ref, 0)
+    put_sums(far_out, sums_ref, blks)
+
+
+def own_sums_kernel(sorted_ref, low_ref, target_ref, out_ref, left_ref, sums_ref):
+    node_sums(sorted_ref, low_ref, target_ref, left_ref, sums_ref, 0)
+    put_sums(out_ref, sums_ref, 0)
+
+
+def node_sums(sorted_ref, low_ref, target_ref, left_ref, sums_ref, first):
+    deep = left_ref.shape[0] // 18
+    tall = sorted_ref.shape[0] // 2
+    pairs = target_ref.shape[0]
     for pair in range(pairs):
         lanes = slice(pair * LANES, (pair + 1) * LANES)
-        mine = iota((deep, LANES), 0) == target_ref[pair : pair + 1, :]
+        mine = iota((deep, LANES), 0) + first == target_ref[pair : pair + 1, :]
+        groups = []
         for part in range(2):
             for j in range(3):
+                at = part * tall + 2 * (j * pairs + pair)
                 for c in range(3):
-                    at = part * tall + j * elements + 2 * pair
-                    lanes_of_axis = slice(c * LANES, (c + 1) * LANES)
-                    values = sorted_ref[at : at + 1, lanes_of_axis] + sorted_ref[at + 1 : at + 2, lanes_of_axis]
-                    start = (part * 9 + j * 3 + c) * deep
-                    left_ref[start : start + deep, lanes] = jnp.where(mine, values, 0.0).astype(HALF)
+                    axis = slice(c * LANES, (c + 1) * LANES)
+                    values = sorted_ref[at : at + 1, axis] + sorted_ref[at + 1 : at + 2, axis]
+                    groups.append(jnp.where(mine, values, 0.0))
+        for i in range(0, 18, 2):
+            both = jnp.concatenate(groups[i : i + 2], axis=0)
+            left_ref[i * deep : (i + 2) * deep, lanes] = both.astype(HALF)
     sums = lax.dot_general(left_ref[...], low_ref[...], NT, preferred_element_type=FULL)
     span = low_ref.shape[0]
     sums = -(sums[: 9 * deep] + sums[9 * deep :])
-    tiles = [(tile, tile * LANES, min(span, (tile + 1) * LANES)) for tile in range(sums_ref.shape[0])]
-    for tile, start, stop in tiles:
-        sums_ref[tile, :, : stop - start] = sums[:, start:stop]
-    for part, out_ref in enumerate(part_outs):
-        for tile, start, stop in tiles:
-            found = [sums_ref[tile, pl.ds(part * blks + k, 9, stride=deep), :][:, : stop - start] for k in range(blks)]
-            found = jnp.concatenate(found + [jnp.zeros((out_ref.shape[0] - 9 * blks, stop - start), FULL)], axis=0)
-            out_ref[:, start:stop] = found.astype(out_ref.dtype)
+    for tile in range(sums_ref.shape[0]):
+        part = sums[:, tile * LANES : min(span, (tile + 1) * LANES)]
+        sums_ref[tile, :, : part.shape[1]] = part
+
+
+def put_sums(out_ref, sums_ref, first):
+    blks = lax.axis_size("blk")
+    deep = sums_ref.shape[1] // 9
+    rows, span = out_ref.shape
+    for tile in range(sums_ref.shape[0]):
+        start, stop = tile * LANES, min(span, (tile + 1) * LANES)
+        found = [sums_ref[tile, pl.ds(first + k, 9, stride=deep), :][:, : stop - start] for k in range(blks)]
+        found = jnp.concatenate(found + [jnp.zeros((rows - 9 * blks, stop - start), FULL)], axis=0)
+        out_ref[:, start:stop] = found.astype(out_ref.dtype)
 
 
 def combine_kernel(own_ref, mate_ref, far_ref, *piece_outs):
@@ -557,18 +578,21 @@
                 moved=8 * MIB,
             )
     deep = round_up(9 * blks, 16)
-    adj, own, mate, far = call(
+    part_shapes = [jax.ShapeDtypeStruct((deep, span), kind) for kind in (FULL, HALF)]
+    sums_scratch = [
+        pltpu.VMEM((18 * 2 * blks, entries), HALF),
+        pltpu.VMEM((-(-span // LANES), 9 * 2 * blks, LANES), FULL),
+    ]
+    adj, mate, far, by_axis = call(
         gradient_kernel,
         "gradient",
         resids + [block_inverse, adj, shapes, low, target],
         [VMEM] * (blks + 5),
-        [adj_shape] + [jax.ShapeDtypeStruct((deep, span), kind) for kind in (FULL, HALF, HALF)],
-        scratch=[
-            pltpu.VMEM((2 * tall, 3 * LANES), FULL),
-            pltpu.VMEM((2 * 9 * 16, entries), HALF),
-            pltpu.VMEM((-(-span // LANES), 9 * 16, LANES), FULL),
-            pltpu.VMEM((tall, LANES), FULL),
-        ],
+        [adj_shape, part_shapes[1], part_shapes[1], jax.ShapeDtypeStruct((2 * tall, 3 * LANES), FULL)],
+        scratch=sums_scratch + [pltpu.VMEM((tall, LANES), FULL)],
+    )
+    (own,) = call(
+        own_sums_kernel, "own_sums", [by_axis, low, target], [VMEM] * 3, part_shapes[:1], sums_scratch, moved=2 * MIB
     )
     far, mate = to_far(far), to_mate(mate)
     shapes = [jax.ShapeDtypeStruct((16, span), HALF)] * (blks - 1)

time: 56.9 us -> 56.8 us (level)
    pallas_call x11 -> x12, Pallas kernels: 11.1 us -> 11.4 us  [call(): pl.pallas_call(kernel, in_specs=specs, out_specs=[SMEM if getattr(out, 'm...]
where the time goes in v7:
time: 56.8 us; the launch traced here: 56.6 us
  starting transfers between devices  30.9 us (54%)
  waiting for transfers between devices  12.9 us (23%)
  Pallas kernels  11.4 us (20%)
  between operations  0.79 us (1%)
  other arithmetic  0.61 us (1%)
    ppermute x12, starting transfers between devices, over_blk(): lax.ppermute(block, 'blk', [(i, i ^ k) for i in range(count)])  19.1 us
    pallas_call x12, Pallas kernels, call(): pl.pallas_call(kernel, in_specs=specs, out_specs=[SMEM if getattr(out, 'm...  11.4 us
    ppermute x12, waiting for transfers between devices, over_blk(): lax.ppermute(block, 'blk', [(i, i ^ k) for i in range(count)])  8.79 us
    ppermute x3, starting transfers between devices, to_far(): lax.ppermute(block, 'dom', [(i, ((i + 1 ^ 1) - 1) % count) for i in range...  7.19 us
    ppermute x3, starting transfers between devices, local(): lax.ppermute(pieces[k], 'blk', [(i, i ^ k) for i in range(count)])[:9]  4.45 us
    ppermute x3, waiting for transfers between devices, local(): lax.ppermute(pieces[k], 'blk', [(i, i ^ k) for i in range(count)])[:9]  2.61 us
    ppermute x3, waiting for transfers between devices, to_far(): lax.ppermute(block, 'dom', [(i, ((i + 1 ^ 1) - 1) % count) for i in range...  1.5 us
  transfers between devices with their start and end apart: 21, of which 14 were waited for; matrix products, arithmetic and copies ran while one was open for 0% of the time, Pallas kernels for 14%

profile of v7, /device:TPU:0, one launch (start us, length us, event | category | flops | bytes accessed | tf_op | source)
XLA Modules:
  0.0 56.6 jit_solution(10839565549046603039)
XLA Ops:
  0.6 5.1 %collective-permute-start.2 = (f32[72,80]{1,0:T(8,128)}, f32[72,80]{1,0:T(8,128)S(1)}, u32[]{:S(2)}, u32[]{:S(2)}) collective-permute-start(f32[72,80]{1,0:T(8,128)} %bitcast.11), channel_id=1, source_target_pairs={{0,3},{1,2},{2,1},{3,0},{4,7},{5,6},{6,5},{7,4},{8,11},{9,10},{10,... | collective-permute-start | bytes 69128 | tf_op jit(solution)/shard_map/ppermute | solution.py:60
  5.8 0.6 %collective-permute-start = (f32[72,80]{1,0:T(8,128)}, f32[72,80]{1,0:T(8,128)S(1)}, u32[]{:S(2)}, u32[]{:S(2)}) collective-permute-start(f32[72,80]{1,0:T(8,128)} %bitcast.13), channel_id=1, source_target_pairs={{0,1},{1,0},{2,3},{3,2},{4,5},{5,4},{6,7},{7,6},{8,9},{9,8},{10,11... | collective-permute-start | bytes 69128 | tf_op jit(solution)/shard_map/ppermute | solution.py:60
  6.4 1.8 %slots.1 = (bf16[672,256]{1,0:T(8,128)(2,1)S(1)}, f32[80,128]{1,0:T(8,128)S(1)}, s32[256]{0:T(256)S(4)}, s32[1]{0:T(128)S(4)}, f32[72,80]{1,0:T(8,128)S(1)}, /*index=5*/f32[72,80]{1,0:T(8,128)S(1)}) custom-call(s32[6,24]{1,0:T(8,128)} %bitcast.15, f32[24]{0:T(128)} %shift_hbm.1, f32[72,80]{1,0:T(8,128)} %bitcast.14, f32[72,80]{1,0:T(8,128)} %bitcast.10, ...), custom_call_target="tpu_custom_call" | custom-call | bytes 16777216 | tf_op jit(solution)/shard_map/slots/pallas_call | solution.py:41
  8.2 2.6 %collective-permute-done.1.refs_2_ = f32[72,80]{1,0:T(8,128)S(1)} collective-permute-done((f32[72,80]{1,0:T(8,128)}, f32[72,80]{1,0:T(8,128)S(1)}, u32[]{:S(2)}, u32[]{:S(2)}) %collective-permute-start.1) | collective-permute-done | bytes 23072 | tf_op jit(solution)/shard_map/ppermute | solution.py:60
  11.0 2.5 %collective-permute-start.4 = (bf16[192,128]{1,0:T(8,128)(2,1)S(1)}, bf16[192,128]{1,0:T(8,128)(2,1)S(1)}, u32[]{:S(2)}, u32[]{:S(2)}) collective-permute-start(bf16[192,128]{1,0:T(8,128)(2,1)S(1)} %columns.2.own_ref), channel_id=1, source_target_pairs={{0,28},{4,8},{8,4},{12,16},{16,12},{20,24},{24,20},{28,0},{1,29},{... | collective-permute-start | bytes 147464 | tf_op jit(solution)/shard_map/ppermute | solution.py:69
  13.6 2.6 %near.2.near_ref = f32[72,80]{1,0:T(8,128)S(1)} custom-call(bf16[192,128]{1,0:T(8,128)(2,1)S(1)} %columns.2.own_ref, bf16[192,128]{1,0:T(8,128)(2,1)S(1)} %collective-permute-done.3.mate_ref, bf16[672,256]{1,0:T(8,128)(2,1)S(1)} %get-tuple-element.22.pick_ref, f32[80,128]{1,0:T(8,128)S(1)} %get-tuple-element.23.shift_ref, ...), custom_call_target="tpu_custom_call" | custom-call | bytes 12582912 | tf_op jit(solution)/shard_map/near/pallas_call | solution.py:41
  16.7 1.6 %collective-permute-start.7 = (bf16[80,80]{1,0:T(8,128)(2,1)S(1)}, bf16[80,80]{1,0:T(8,128)(2,1)S(1)}, u32[]{:S(2)}, u32[]{:S(2)}) collective-permute-start(bf16[80,80]{1,0:T(8,128)(2,1)S(1)} %far.2.refs_0_), channel_id=1, source_target_pairs={{0,3},{1,2},{2,1},{3,0},{4,7},{5,6},{6,5},{7,4},{8,11},{9,10},{10,... | collective-permute-start | bytes 38408 | tf_op jit(solution)/shard_map/ppermute | solution.py:60
  18.2 0.6 %collective-permute-start.6 = (bf16[80,80]{1,0:T(8,128)(2,1)S(1)}, bf16[80,80]{1,0:T(8,128)(2,1)S(1)}, u32[]{:S(2)}, u32[]{:S(2)}) collective-permute-start(bf16[80,80]{1,0:T(8,128)(2,1)S(1)} %far.2.refs_0_), channel_id=1, source_target_pairs={{0,2},{1,3},{2,0},{3,1},{4,6},{5,7},{6,4},{7,5},{8,10},{9,11},{10,... | collective-permute-start | bytes 38408 | tf_op jit(solution)/shard_map/ppermute | solution.py:60
  18.8 2.3 %collective-permute-start.5 = (bf16[80,80]{1,0:T(8,128)(2,1)S(1)}, bf16[80,80]{1,0:T(8,128)(2,1)S(1)}, u32[]{:S(2)}, u32[]{:S(2)}) collective-permute-start(bf16[80,80]{1,0:T(8,128)(2,1)S(1)} %far.2.refs_0_), channel_id=1, source_target_pairs={{0,1},{1,0},{2,3},{3,2},{4,5},{5,4},{6,7},{7,6},{8,9},{9,8},{10,11... | collective-permute-start | bytes 38408 | tf_op jit(solution)/shard_map/ppermute | solution.py:60
  21.1 1.3 %collective-permute-done.7.refs_3_ = bf16[80,80]{1,0:T(8,128)(2,1)S(1)} collective-permute-done((bf16[80,80]{1,0:T(8,128)(2,1)S(1)}, bf16[80,80]{1,0:T(8,128)(2,1)S(1)}, u32[]{:S(2)}, u32[]{:S(2)}) %collective-permute-start.7) | collective-permute-done | bytes 12832 | tf_op jit(solution)/shard_map/ppermute | solution.py:60
  23.1 0.7 %update.1 = (f32[72,80]{1,0:T(8,128)S(1)}, bf16[80,80]{1,0:T(8,128)(2,1)S(1)}) custom-call(bf16[80,80]{1,0:T(8,128)(2,1)S(1)} %far.2.refs_0_, bf16[80,80]{1,0:T(8,128)(2,1)S(1)} %collective-permute-done.5.refs_1_, bf16[80,80]{1,0:T(8,128)(2,1)S(1)} %collective-permute-done.6.refs_2_, bf16[80,80]{1,0:T(8,128)(2,1)S(1)} %collective-permute-done.7.refs_3_, ...), custom_call_target="tpu_custom_call" | custom-call | bytes 8388608 | tf_op jit(solution)/shard_map/update/pallas_call | solution.py:41
  23.8 2.4 %collective-permute-start.10 = (bf16[80,80]{1,0:T(8,128)(2,1)S(1)}, bf16[80,80]{1,0:T(8,128)(2,1)S(1)}, u32[]{:S(2)}, u32[]{:S(2)}) collective-permute-start(bf16[80,80]{1,0:T(8,128)(2,1)S(1)} %get-tuple-element.27.refs_0_), channel_id=1, source_target_pairs={{0,3},{1,2},{2,1},{3,0},{4,7},{5,6},{6,5},{7,4},{8,11},{9,10},{10,... | collective-permute-start | bytes 38408 | tf_op jit(solution)/shard_map/ppermute | solution.py:60
  26.2 0.9 %collective-permute-start.9 = (bf16[80,80]{1,0:T(8,128)(2,1)S(1)}, bf16[80,80]{1,0:T(8,128)(2,1)S(1)}, u32[]{:S(2)}, u32[]{:S(2)}) collective-permute-start(bf16[80,80]{1,0:T(8,128)(2,1)S(1)} %get-tuple-element.27.refs_0_), channel_id=1, source_target_pairs={{0,2},{1,3},{2,0},{3,1},{4,6},{5,7},{6,4},{7,5},{8,10},{9,11},{10,... | collective-permute-start | bytes 38408 | tf_op jit(solution)/shard_map/ppermute | solution.py:60
  27.1 1.1 %collective-permute-start.8 = (bf16[80,80]{1,0:T(8,128)(2,1)S(1)}, bf16[80,80]{1,0:T(8,128)(2,1)S(1)}, u32[]{:S(2)}, u32[]{:S(2)}) collective-permute-start(bf16[80,80]{1,0:T(8,128)(2,1)S(1)} %get-tuple-element.27.refs_0_), channel_id=1, source_target_pairs={{0,1},{1,0},{2,3},{3,2},{4,5},{5,4},{6,7},{7,6},{8,9},{9,8},{10,11... | collective-permute-start | bytes 38408 | tf_op jit(solution)/shard_map/ppermute | solution.py:60
  28.3 1.3 %collective-permute-done.10.refs_3_ = bf16[80,80]{1,0:T(8,128)(2,1)S(1)} collective-permute-done((bf16[80,80]{1,0:T(8,128)(2,1)S(1)}, bf16[80,80]{1,0:T(8,128)(2,1)S(1)}, u32[]{:S(2)}, u32[]{:S(2)}) %collective-permute-start.10) | collective-permute-done | bytes 12832 | tf_op jit(solution)/shard_map/ppermute | solution.py:60
  29.5 1.4 %collective-permute-done.9.refs_2_ = bf16[80,80]{1,0:T(8,128)(2,1)S(1)} collective-permute-done((bf16[80,80]{1,0:T(8,128)(2,1)S(1)}, bf16[80,80]{1,0:T(8,128)(2,1)S(1)}, u32[]{:S(2)}, u32[]{:S(2)}) %collective-permute-start.9) | collective-permute-done | bytes 12832 | tf_op jit(solution)/shard_map/ppermute | solution.py:60
  31.3 2.3 %collective-permute-start.12 = (bf16[192,128]{1,0:T(8,128)(2,1)S(1)}, bf16[192,128]{1,0:T(8,128)(2,1)S(1)}, u32[]{:S(2)}, u32[]{:S(2)}) collective-permute-start(bf16[192,128]{1,0:T(8,128)(2,1)S(1)} %columns.3.own_ref), channel_id=1, source_target_pairs={{0,28},{4,8},{8,4},{12,16},{16,12},{20,24},{24,20},{28,0},{1,29},{... | collective-permute-start | bytes 147464 | tf_op jit(solution)/shard_map/ppermute | solution.py:69
  33.6 2.6 %near.3.near_ref = f32[72,80]{1,0:T(8,128)S(1)} custom-call(bf16[192,128]{1,0:T(8,128)(2,1)S(1)} %columns.3.own_ref, bf16[192,128]{1,0:T(8,128)(2,1)S(1)} %collective-permute-done.11.mate_ref, bf16[672,256]{1,0:T(8,128)(2,1)S(1)} %get-tuple-element.22.pick_ref, f32[80,128]{1,0:T(8,128)S(1)} %get-tuple-element.23.shift_ref, ...), custom_call_target="tpu_custom_call" | custom-call | bytes 12582912 | tf_op jit(solution)/shard_map/near/pallas_call | solution.py:41
  36.7 1.5 %collective-permute-start.15 = (bf16[80,80]{1,0:T(8,128)(2,1)S(1)}, bf16[80,80]{1,0:T(8,128)(2,1)S(1)}, u32[]{:S(2)}, u32[]{:S(2)}) collective-permute-start(bf16[80,80]{1,0:T(8,128)(2,1)S(1)} %far.3.refs_0_), channel_id=1, source_target_pairs={{0,3},{1,2},{2,1},{3,0},{4,7},{5,6},{6,5},{7,4},{8,11},{9,10},{10,... | collective-permute-start | bytes 38408 | tf_op jit(solution)/shard_map/ppermute | solution.py:60
  38.2 0.9 %collective-permute-start.14 = (bf16[80,80]{1,0:T(8,128)(2,1)S(1)}, bf16[80,80]{1,0:T(8,128)(2,1)S(1)}, u32[]{:S(2)}, u32[]{:S(2)}) collective-permute-start(bf16[80,80]{1,0:T(8,128)(2,1)S(1)} %far.3.refs_0_), channel_id=1, source_target_pairs={{0,2},{1,3},{2,0},{3,1},{4,6},{5,7},{6,4},{7,5},{8,10},{9,11},{10,... | collective-permute-start | bytes 38408 | tf_op jit(solution)/shard_map/ppermute | solution.py:60
  39.1 2.0 %collective-permute-start.13 = (bf16[80,80]{1,0:T(8,128)(2,1)S(1)}, bf16[80,80]{1,0:T(8,128)(2,1)S(1)}, u32[]{:S(2)}, u32[]{:S(2)}) collective-permute-start(bf16[80,80]{1,0:T(8,128)(2,1)S(1)} %far.3.refs_0_), channel_id=1, source_target_pairs={{0,1},{1,0},{2,3},{3,2},{4,5},{5,4},{6,7},{7,6},{8,9},{9,8},{10,11... | collective-permute-start | bytes 38408 | tf_op jit(solution)/shard_map/ppermute | solution.py:60
  41.2 0.7 %nodes.1 = (bf16[192,1536]{1,0:T(8,128)(2,1)S(1)}, s32[12,128]{1,0:T(8,128)S(1)}, bf16[24,80,192]{2,1,0:T(8,128)(2,1)S(1)}) custom-call(s32[24,64]{1,0:T(8,128)S(1)} %copy-done.4, bf16[24,80,192]{2,1,0:T(8,128)(2,1)S(1)} %copy-done.3), custom_call_target="tpu_custom_call" | custom-call | bytes 3145728 | tf_op jit(solution)/shard_map/nodes/pallas_call | solution.py:41
  41.8 0.7 %collective-permute-done.15.refs_3_ = bf16[80,80]{1,0:T(8,128)(2,1)S(1)} collective-permute-done((bf16[80,80]{1,0:T(8,128)(2,1)S(1)}, bf16[80,80]{1,0:T(8,128)(2,1)S(1)}, u32[]{:S(2)}, u32[]{:S(2)}) %collective-permute-start.15) | collective-permute-done | bytes 12832 | tf_op jit(solution)/shard_map/ppermute | solution.py:60
  43.1 1.5 %gradient.1 = (f32[72,80]{1,0:T(8,128)}, bf16[48,192]{1,0:T(8,128)(2,1)S(1)}, bf16[48,192]{1,0:T(8,128)(2,1)S(1)}, f32[160,384]{1,0:T(8,128)S(1)}) custom-call(bf16[80,80]{1,0:T(8,128)(2,1)S(1)} %far.3.refs_0_, bf16[80,80]{1,0:T(8,128)(2,1)S(1)} %collective-permute-done.13.refs_1_, bf16[80,80]{1,0:T(8,128)(2,1)S(1)} %collective-permute-done.14.refs_2_, ...), custom_call_target="tpu_custom_call" | custom-call | tf_op jit(solution)/shard_map/gradient/pallas_call | solution.py:41
  44.7 2.4 %collective-permute-start.17 = (bf16[48,192]{1,0:T(8,128)(2,1)S(1)}, bf16[48,192]{1,0:T(8,128)(2,1)S(1)}, u32[]{:S(2)}, u32[]{:S(2)}) collective-permute-start(bf16[48,192]{1,0:T(8,128)(2,1)S(1)} %get-tuple-element.35), channel_id=1, source_target_pairs={{0,28},{4,8},{8,4},{12,16},{16,12},{20,24},{24,20},{28,0},{1,29},{... | collective-permute-start | bytes 55304 | tf_op jit(solution)/shard_map/ppermute | solution.py:69
  47.5 1.4 %collective-permute-done.17.far_ref = bf16[48,192]{1,0:T(8,128)(2,1)S(1)} collective-permute-done((bf16[48,192]{1,0:T(8,128)(2,1)S(1)}, bf16[48,192]{1,0:T(8,128)(2,1)S(1)}, u32[]{:S(2)}, u32[]{:S(2)}) %collective-permute-start.17) | collective-permute-done | bytes 18464 | tf_op jit(solution)/shard_map/ppermute | solution.py:69
  48.9 2.4 %collective-permute-start.18 = (bf16[16,192]{1,0:T(8,128)(2,1)S(1)}, bf16[16,192]{1,0:T(8,128)(2,1)S(1)}, u32[]{:S(2)}, u32[]{:S(2)}) collective-permute-start(bf16[16,192]{1,0:T(8,128)(2,1)S(1)} %get-tuple-element.37), channel_id=1, source_target_pairs={{0,3},{1,2},{2,1},{3,0},{4,7},{5,6},{6,5},{7,4},{8,11},{9,10},{10,... | collective-permute-start | bytes 18440 | tf_op jit(solution)/shard_map/ppermute | solution.py:605
  51.3 0.9 %collective-permute-start.19 = (bf16[16,192]{1,0:T(8,128)(2,1)S(1)}, bf16[16,192]{1,0:T(8,128)(2,1)S(1)}, u32[]{:S(2)}, u32[]{:S(2)}) collective-permute-start(bf16[16,192]{1,0:T(8,128)(2,1)S(1)} %get-tuple-element.38), channel_id=1, source_target_pairs={{0,2},{1,3},{2,0},{3,1},{4,6},{5,7},{6,4},{7,5},{8,10},{9,11},{10,... | collective-permute-start | bytes 18440 | tf_op jit(solution)/shard_map/ppermute | solution.py:605
  52.3 1.1 %collective-permute-start.20 = (bf16[16,192]{1,0:T(8,128)(2,1)S(1)}, bf16[16,192]{1,0:T(8,128)(2,1)S(1)}, u32[]{:S(2)}, u32[]{:S(2)}) collective-permute-start(bf16[16,192]{1,0:T(8,128)(2,1)S(1)} %get-tuple-element.39), channel_id=1, source_target_pairs={{0,1},{1,0},{2,3},{3,2},{4,5},{5,4},{6,7},{7,6},{8,9},{9,8},{10,11... | collective-permute-start | bytes 18440 | tf_op jit(solution)/shard_map/ppermute | solution.py:605
  53.4 1.1 %collective-permute-done.18 = bf16[16,192]{1,0:T(8,128)(2,1)S(1)} collective-permute-done((bf16[16,192]{1,0:T(8,128)(2,1)S(1)}, bf16[16,192]{1,0:T(8,128)(2,1)S(1)}, u32[]{:S(2)}, u32[]{:S(2)}) %collective-permute-start.18) | collective-permute-done | bytes 6176 | tf_op jit(solution)/shard_map/ppermute | solution.py:605
  54.4 1.5 %collective-permute-done.19 = bf16[16,192]{1,0:T(8,128)(2,1)S(1)} collective-permute-done((bf16[16,192]{1,0:T(8,128)(2,1)S(1)}, bf16[16,192]{1,0:T(8,128)(2,1)S(1)}, u32[]{:S(2)}, u32[]{:S(2)}) %collective-permute-start.19) | collective-permute-done | bytes 6176 | tf_op jit(solution)/shard_map/ppermute | solution.py:605
  56.0 0.6 %convert_add_fusion = f32[9,192]{1,0:T(8,128)} fusion(f32[9,192]{1,0:T(8,128)S(1)} %get-tuple-element.36, bf16[16,192]{1,0:T(8,128)(2,1)S(1)} %collective-permute-done.20, bf16[16,192]{1,0:T(8,128)(2,1)S(1)} %collective-permute-done.19, bf16[16,192]{1,0:T(8,128)(2,1)S(1)} %collective-permute-done.18), kind=kLoop, calls=%fused_computation | loop fusion | flops 10368 | bytes 24192 | tf_op jit(solution)/shard_map/add | solution.py:605
  (33 shorter events, 3.3 us)
Async XLA Ops:
  0.6 12.9 %copy-start = (bf16[24,7,80,320]{3,2,1,0:T(8,128)(2,1)S(1)}, bf16[24,7,80,320]{3,2,1,0:T(8,128)(2,1)}, u32[]{:S(2)}) copy-start(bf16[24,7,80,320]{3,2,1,0:T(8,128)(2,1)} %jac_ref.7) | copy-start | bytes 25804804
  0.6 7.6 %collective-permute-start.2 = (f32[72,80]{1,0:T(8,128)}, f32[72,80]{1,0:T(8,128)S(1)}, u32[]{:S(2)}, u32[]{:S(2)}) collective-permute-start(f32[72,80]{1,0:T(8,128)} %bitcast.11), channel_id=1, source_target_pairs={{0,3},{1,2},{2,1},{3,0},{4,7},{5,6},{6,5},{7,4},{8,11},{9,10},{10,... | collective-permute-start | bytes 69128 | tf_op jit(solution)/shard_map/ppermute | solution.py:60
  5.8 5.1 %collective-permute-start.1 = (f32[72,80]{1,0:T(8,128)}, f32[72,80]{1,0:T(8,128)S(1)}, u32[]{:S(2)}, u32[]{:S(2)}) collective-permute-start(f32[72,80]{1,0:T(8,128)} %bitcast.12), channel_id=1, source_target_pairs={{0,2},{1,3},{2,0},{3,1},{4,6},{5,7},{6,4},{7,5},{8,10},{9,11},{10,... | collective-permute-start | bytes 69128 | tf_op jit(solution)/shard_map/ppermute | solution.py:60
  5.8 5.1 %collective-permute-start = (f32[72,80]{1,0:T(8,128)}, f32[72,80]{1,0:T(8,128)S(1)}, u32[]{:S(2)}, u32[]{:S(2)}) collective-permute-start(f32[72,80]{1,0:T(8,128)} %bitcast.13), channel_id=1, source_target_pairs={{0,1},{1,0},{2,3},{3,2},{4,5},{5,4},{6,7},{7,6},{8,9},{9,8},{10,11... | collective-permute-start | bytes 69128 | tf_op jit(solution)/shard_map/ppermute | solution.py:60
  11.0 2.6 %collective-permute-start.3 = (bf16[192,128]{1,0:T(8,128)(2,1)S(1)}, bf16[192,128]{1,0:T(8,128)(2,1)S(1)}, u32[]{:S(2)}, u32[]{:S(2)}) collective-permute-start(bf16[192,128]{1,0:T(8,128)(2,1)S(1)} %columns.2.own_ref), channel_id=1, source_target_pairs={{0,4},{4,0},{8,12},{12,8},{16,20},{20,16},{24,28},{28,24},{1,5},{5... | collective-permute-start | bytes 147464 | tf_op jit(solution)/shard_map/ppermute | solution.py:64
  11.0 5.2 %collective-permute-start.4 = (bf16[192,128]{1,0:T(8,128)(2,1)S(1)}, bf16[192,128]{1,0:T(8,128)(2,1)S(1)}, u32[]{:S(2)}, u32[]{:S(2)}) collective-permute-start(bf16[192,128]{1,0:T(8,128)(2,1)S(1)} %columns.2.own_ref), channel_id=1, source_target_pairs={{0,28},{4,8},{8,4},{12,16},{16,12},{20,24},{24,20},{28,0},{1,29},{... | collective-permute-start | bytes 147464 | tf_op jit(solution)/shard_map/ppermute | solution.py:69
  13.6 9.5 %copy-start.1 = (bf16[24,80,320]{2,1,0:T(8,128)(2,1)S(1)}, bf16[24,80,320]{2,1,0:T(8,128)(2,1)}, u32[]{:S(2)}) copy-start(bf16[24,80,320]{2,1,0:T(8,128)(2,1)} %refs_4_.3) | copy-start | bytes 3686404
  16.7 5.8 %collective-permute-start.7 = (bf16[80,80]{1,0:T(8,128)(2,1)S(1)}, bf16[80,80]{1,0:T(8,128)(2,1)S(1)}, u32[]{:S(2)}, u32[]{:S(2)}) collective-permute-start(bf16[80,80]{1,0:T(8,128)(2,1)S(1)} %far.2.refs_0_), channel_id=1, source_target_pairs={{0,3},{1,2},{2,1},{3,0},{4,7},{5,6},{6,5},{7,4},{8,11},{9,10},{10,... | collective-permute-start | bytes 38408 | tf_op jit(solution)/shard_map/ppermute | solution.py:60
  18.2 4.7 %collective-permute-start.6 = (bf16[80,80]{1,0:T(8,128)(2,1)S(1)}, bf16[80,80]{1,0:T(8,128)(2,1)S(1)}, u32[]{:S(2)}, u32[]{:S(2)}) collective-permute-start(bf16[80,80]{1,0:T(8,128)(2,1)S(1)} %far.2.refs_0_), channel_id=1, source_target_pairs={{0,2},{1,3},{2,0},{3,1},{4,6},{5,7},{6,4},{7,5},{8,10},{9,11},{10,... | collective-permute-start | bytes 38408 | tf_op jit(solution)/shard_map/ppermute | solution.py:60
  18.8 4.3 %collective-permute-start.5 = (bf16[80,80]{1,0:T(8,128)(2,1)S(1)}, bf16[80,80]{1,0:T(8,128)(2,1)S(1)}, u32[]{:S(2)}, u32[]{:S(2)}) collective-permute-start(bf16[80,80]{1,0:T(8,128)(2,1)S(1)} %far.2.refs_0_), channel_id=1, source_target_pairs={{0,1},{1,0},{2,3},{3,2},{4,5},{5,4},{6,7},{7,6},{8,9},{9,8},{10,11... | collective-permute-start | bytes 38408 | tf_op jit(solution)/shard_map/ppermute | solution.py:60
  23.8 5.7 %collective-permute-start.10 = (bf16[80,80]{1,0:T(8,128)(2,1)S(1)}, bf16[80,80]{1,0:T(8,128)(2,1)S(1)}, u32[]{:S(2)}, u32[]{:S(2)}) collective-permute-start(bf16[80,80]{1,0:T(8,128)(2,1)S(1)} %get-tuple-element.27.refs_0_), channel_id=1, source_target_pairs={{0,3},{1,2},{2,1},{3,0},{4,7},{5,6},{6,5},{7,4},{8,11},{9,10},{10,... | collective-permute-start | bytes 38408 | tf_op jit(solution)/shard_map/ppermute | solution.py:60
  26.2 4.7 %collective-permute-start.9 = (bf16[80,80]{1,0:T(8,128)(2,1)S(1)}, bf16[80,80]{1,0:T(8,128)(2,1)S(1)}, u32[]{:S(2)}, u32[]{:S(2)}) collective-permute-start(bf16[80,80]{1,0:T(8,128)(2,1)S(1)} %get-tuple-element.27.refs_0_), channel_id=1, source_target_pairs={{0,2},{1,3},{2,0},{3,1},{4,6},{5,7},{6,4},{7,5},{8,10},{9,11},{10,... | collective-permute-start | bytes 38408 | tf_op jit(solution)/shard_map/ppermute | solution.py:60
  27.1 4.0 %collective-permute-start.8 = (bf16[80,80]{1,0:T(8,128)(2,1)S(1)}, bf16[80,80]{1,0:T(8,128)(2,1)S(1)}, u32[]{:S(2)}, u32[]{:S(2)}) collective-permute-start(bf16[80,80]{1,0:T(8,128)(2,1)S(1)} %get-tuple-element.27.refs_0_), channel_id=1, source_target_pairs={{0,1},{1,0},{2,3},{3,2},{4,5},{5,4},{6,7},{7,6},{8,9},{9,8},{10,11... | collective-permute-start | bytes 38408 | tf_op jit(solution)/shard_map/ppermute | solution.py:60
  31.3 2.3 %collective-permute-start.11 = (bf16[192,128]{1,0:T(8,128)(2,1)S(1)}, bf16[192,128]{1,0:T(8,128)(2,1)S(1)}, u32[]{:S(2)}, u32[]{:S(2)}) collective-permute-start(bf16[192,128]{1,0:T(8,128)(2,1)S(1)} %columns.3.own_ref), channel_id=1, source_target_pairs={{0,4},{4,0},{8,12},{12,8},{16,20},{20,16},{24,28},{28,24},{1,5},{5... | collective-permute-start | bytes 147464 | tf_op jit(solution)/shard_map/ppermute | solution.py:64
  31.3 5.0 %collective-permute-start.12 = (bf16[192,128]{1,0:T(8,128)(2,1)S(1)}, bf16[192,128]{1,0:T(8,128)(2,1)S(1)}, u32[]{:S(2)}, u32[]{:S(2)}) collective-permute-start(bf16[192,128]{1,0:T(8,128)(2,1)S(1)} %columns.3.own_ref), channel_id=1, source_target_pairs={{0,28},{4,8},{8,4},{12,16},{16,12},{20,24},{24,20},{28,0},{1,29},{... | collective-permute-start | bytes 147464 | tf_op jit(solution)/shard_map/ppermute | solution.py:69
  33.6 7.6 %copy-start.3 = (bf16[24,80,192]{2,1,0:T(8,128)(2,1)S(1)}, bf16[24,80,192]{2,1,0:T(8,128)(2,1)}, u32[]{:S(2)}) copy-start(bf16[24,80,192]{2,1,0:T(8,128)(2,1)} %shape_ref.1) | copy-start | bytes 2211844
  33.6 7.6 %copy-start.4 = (s32[24,64]{1,0:T(8,128)S(1)}, s32[24,64]{1,0:T(8,128)}, u32[]{:S(2)}) copy-start(s32[24,64]{1,0:T(8,128)} %ids_ref.1) | copy-start | bytes 18436
  33.6 9.5 %copy-start.2 = (bf16[24,80,320]{2,1,0:T(8,128)(2,1)S(1)}, bf16[24,80,320]{2,1,0:T(8,128)(2,1)}, u32[]{:S(2)}) copy-start(bf16[24,80,320]{2,1,0:T(8,128)(2,1)} %refs_4_.3) | copy-start | bytes 3686404
  36.7 5.8 %collective-permute-start.15 = (bf16[80,80]{1,0:T(8,128)(2,1)S(1)}, bf16[80,80]{1,0:T(8,128)(2,1)S(1)}, u32[]{:S(2)}, u32[]{:S(2)}) collective-permute-start(bf16[80,80]{1,0:T(8,128)(2,1)S(1)} %far.3.refs_0_), channel_id=1, source_target_pairs={{0,3},{1,2},{2,1},{3,0},{4,7},{5,6},{6,5},{7,4},{8,11},{9,10},{10,... | collective-permute-start | bytes 38408 | tf_op jit(solution)/shard_map/ppermute | solution.py:60
  38.2 4.7 %collective-permute-start.14 = (bf16[80,80]{1,0:T(8,128)(2,1)S(1)}, bf16[80,80]{1,0:T(8,128)(2,1)S(1)}, u32[]{:S(2)}, u32[]{:S(2)}) collective-permute-start(bf16[80,80]{1,0:T(8,128)(2,1)S(1)} %far.3.refs_0_), channel_id=1, source_target_pairs={{0,2},{1,3},{2,0},{3,1},{4,6},{5,7},{6,4},{7,5},{8,10},{9,11},{10,... | collective-permute-start | bytes 38408 | tf_op jit(solution)/shard_map/ppermute | solution.py:60
  39.1 4.0 %collective-permute-start.13 = (bf16[80,80]{1,0:T(8,128)(2,1)S(1)}, bf16[80,80]{1,0:T(8,128)(2,1)S(1)}, u32[]{:S(2)}, u32[]{:S(2)}) collective-permute-start(bf16[80,80]{1,0:T(8,128)(2,1)S(1)} %far.3.refs_0_), channel_id=1, source_target_pairs={{0,1},{1,0},{2,3},{3,2},{4,5},{5,4},{6,7},{7,6},{8,9},{9,8},{10,11... | collective-permute-start | bytes 38408 | tf_op jit(solution)/shard_map/ppermute | solution.py:60
  44.6 2.9 %collective-permute-start.16 = (bf16[48,192]{1,0:T(8,128)(2,1)S(1)}, bf16[48,192]{1,0:T(8,128)(2,1)S(1)}, u32[]{:S(2)}, u32[]{:S(2)}) collective-permute-start(bf16[48,192]{1,0:T(8,128)(2,1)S(1)} %get-tuple-element.34), channel_id=1, source_target_pairs={{0,4},{4,0},{8,12},{12,8},{16,20},{20,16},{24,28},{28,24},{1,5},{5... | collective-permute-start | bytes 55304 | tf_op jit(solution)/shard_map/ppermute | solution.py:64
  44.7 4.2 %collective-permute-start.17 = (bf16[48,192]{1,0:T(8,128)(2,1)S(1)}, bf16[48,192]{1,0:T(8,128)(2,1)S(1)}, u32[]{:S(2)}, u32[]{:S(2)}) collective-permute-start(bf16[48,192]{1,0:T(8,128)(2,1)S(1)} %get-tuple-element.35), channel_id=1, source_target_pairs={{0,28},{4,8},{8,4},{12,16},{16,12},{20,24},{24,20},{28,0},{1,29},{... | collective-permute-start | bytes 55304 | tf_op jit(solution)/shard_map/ppermute | solution.py:69
  48.9 5.5 %collective-permute-start.18 = (bf16[16,192]{1,0:T(8,128)(2,1)S(1)}, bf16[16,192]{1,0:T(8,128)(2,1)S(1)}, u32[]{:S(2)}, u32[]{:S(2)}) collective-permute-start(bf16[16,192]{1,0:T(8,128)(2,1)S(1)} %get-tuple-element.37), channel_id=1, source_target_pairs={{0,3},{1,2},{2,1},{3,0},{4,7},{5,6},{6,5},{7,4},{8,11},{9,10},{10,... | collective-permute-start | bytes 18440 | tf_op jit(solution)/shard_map/ppermute | solution.py:605
  51.3 4.6 %collective-permute-start.19 = (bf16[16,192]{1,0:T(8,128)(2,1)S(1)}, bf16[16,192]{1,0:T(8,128)(2,1)S(1)}, u32[]{:S(2)}, u32[]{:S(2)}) collective-permute-start(bf16[16,192]{1,0:T(8,128)(2,1)S(1)} %get-tuple-element.38), channel_id=1, source_target_pairs={{0,2},{1,3},{2,0},{3,1},{4,6},{5,7},{6,4},{7,5},{8,10},{9,11},{10,... | collective-permute-start | bytes 18440 | tf_op jit(solution)/shard_map/ppermute | solution.py:605
  52.3 3.7 %collective-permute-start.20 = (bf16[16,192]{1,0:T(8,128)(2,1)S(1)}, bf16[16,192]{1,0:T(8,128)(2,1)S(1)}, u32[]{:S(2)}, u32[]{:S(2)}) collective-permute-start(bf16[16,192]{1,0:T(8,128)(2,1)S(1)} %get-tuple-element.39), channel_id=1, source_target_pairs={{0,1},{1,0},{2,3},{3,2},{4,5},{5,4},{6,7},{7,6},{8,9},{9,8},{10,11... | collective-permute-start | bytes 18440 | tf_op jit(solution)/shard_map/ppermute | solution.py:605

commit v8 on v7

--- a/solution.py
+++ b/solution.py
@@ -1,4 +1,5 @@
 import functools
+import math
 
 import jax
 import jax.numpy as jnp
@@ -391,24 +392,16 @@
     pairs = elements // 2
     tall, width = half.shape
     coords = shape_ref.shape[2]
-    depth = 3 if elements % 3 == 0 and 3 * width <= 256 else 1
+    period = math.lcm(width, LANES) // width
+    if elements % period:
+        period = elements
     block = widened(half.astype(FULL), LANES)
-    left = jnp.concatenate(laid([block] * depth, width, round_up(depth * width, LANES)), axis=1)[:, : depth * width]
-    shape = left.shape
-    owner = element_of_row(shape, elements)
-    group = jnp.zeros(shape, jnp.int32)
-    for step in range(1, elements // depth):
-        group = group + jnp.where(owner >= step * depth, 1, 0)
-    first = (owner - group * depth) * width
-    behind = iota(shape, 1) - first
+    tiles = laid([block] * period, width, round_up(period * width, LANES))
+    left = jnp.concatenate(tiles * (elements // period), axis=1)[:, : elements * width]
+    behind = iota(left.shape, 1) - width * element_of_row(left.shape, elements)
     left = jnp.where(jnp.logical_and(behind >= 0, behind < width), left, 0.0).astype(HALF)
-    shape = (tall, coords)
-    owner = element_of_row(shape, elements)
-    total = jnp.zeros(shape, FULL)
-    for start in range(0, elements, depth):
-        partials = jnp.concatenate([shape_ref[start + step] for step in range(depth)], axis=0)
-        product = jnp.dot(left, partials, preferred_element_type=FULL)
-        total = jnp.where(owner >= start, product, total)
+    total = jnp.dot(left, shape_ref[...].reshape(elements * width, coords), preferred_element_type=FULL)
+    owner = element_of_row(total.shape, elements)
     low = iota((tall, LANES), 1) < LANES // 2
     odd = lax.bitwise_and(owner[:, :LANES], 1) == 1
     values = [total[:, :LANES], widened(total[:, LANES:], LANES)]

time: 56.8 us -> 57.2 us (level)
  Pallas kernels: 11.4 us -> 12 us
    pallas_call x12, Pallas kernels: 11.4 us -> 12 us  [call(): pl.pallas_call(kernel, in_specs=specs, out_specs=[SMEM if getattr(out, 'm...]
where the time goes in v8:
time: 57.2 us; the launch traced here: 57 us
  starting transfers between devices  30.8 us (54%)
  waiting for transfers between devices  12.8 us (22%)
  Pallas kernels  12 us (21%)
  between operations  0.77 us (1%)
  other arithmetic  0.61 us (1%)
    ppermute x12, starting transfers between devices, over_blk(): lax.ppermute(block, 'blk', [(i, i ^ k) for i in range(count)])  19.1 us
    pallas_call x12, Pallas kernels, call(): pl.pallas_call(kernel, in_specs=specs, out_specs=[SMEM if getattr(out, 'm...  12 us
    ppermute x12, waiting for transfers between devices, over_blk(): lax.ppermute(block, 'blk', [(i, i ^ k) for i in range(count)])  8.79 us
    ppermute x3, starting transfers between devices, to_far(): lax.ppermute(block, 'dom', [(i, ((i + 1 ^ 1) - 1) % count) for i in range...  7.19 us
    ppermute x3, starting transfers between devices, local(): lax.ppermute(pieces[k], 'blk', [(i, i ^ k) for i in range(count)])[:9]  4.45 us
    ppermute x3, waiting for transfers between devices, local(): lax.ppermute(pieces[k], 'blk', [(i, i ^ k) for i in range(count)])[:9]  2.61 us
    ppermute x3, waiting for transfers between devices, to_far(): lax.ppermute(block, 'dom', [(i, ((i + 1 ^ 1) - 1) % count) for i in range...  1.43 us
  transfers between devices with their start and end apart: 21, of which 14 were waited for; matrix products, arithmetic and copies ran while one was open for 0% of the time, Pallas kernels for 14%

profile of v8, /device:TPU:0, one launch (start us, length us, event | category | flops | bytes accessed | tf_op | source)
XLA Modules:
  0.0 57.0 jit_solution(6232376682538740135)
XLA Ops:
  0.6 5.1 %collective-permute-start.2 = (f32[72,80]{1,0:T(8,128)}, f32[72,80]{1,0:T(8,128)S(1)}, u32[]{:S(2)}, u32[]{:S(2)}) collective-permute-start(f32[72,80]{1,0:T(8,128)} %bitcast.11), channel_id=1, source_target_pairs={{0,3},{1,2},{2,1},{3,0},{4,7},{5,6},{6,5},{7,4},{8,11},{9,10},{10,... | collective-permute-start | bytes 69128 | tf_op jit(solution)/shard_map/ppermute | solution.py:61
  5.8 0.6 %collective-permute-start = (f32[72,80]{1,0:T(8,128)}, f32[72,80]{1,0:T(8,128)S(1)}, u32[]{:S(2)}, u32[]{:S(2)}) collective-permute-start(f32[72,80]{1,0:T(8,128)} %bitcast.13), channel_id=1, source_target_pairs={{0,1},{1,0},{2,3},{3,2},{4,5},{5,4},{6,7},{7,6},{8,9},{9,8},{10,11... | collective-permute-start | bytes 69128 | tf_op jit(solution)/shard_map/ppermute | solution.py:61
  6.4 1.8 %slots.1 = (bf16[672,256]{1,0:T(8,128)(2,1)S(1)}, f32[80,128]{1,0:T(8,128)S(1)}, s32[256]{0:T(256)S(4)}, s32[1]{0:T(128)S(4)}, f32[72,80]{1,0:T(8,128)S(1)}, /*index=5*/f32[72,80]{1,0:T(8,128)S(1)}) custom-call(s32[6,24]{1,0:T(8,128)} %bitcast.15, f32[24]{0:T(128)} %shift_hbm.1, f32[72,80]{1,0:T(8,128)} %bitcast.14, f32[72,80]{1,0:T(8,128)} %bitcast.10, ...), custom_call_target="tpu_custom_call" | custom-call | bytes 16777216 | tf_op jit(solution)/shard_map/slots/pallas_call | solution.py:42
  8.2 2.6 %collective-permute-done.1.refs_2_ = f32[72,80]{1,0:T(8,128)S(1)} collective-permute-done((f32[72,80]{1,0:T(8,128)}, f32[72,80]{1,0:T(8,128)S(1)}, u32[]{:S(2)}, u32[]{:S(2)}) %collective-permute-start.1) | collective-permute-done | bytes 23072 | tf_op jit(solution)/shard_map/ppermute | solution.py:61
  11.0 2.5 %collective-permute-start.4 = (bf16[192,128]{1,0:T(8,128)(2,1)S(1)}, bf16[192,128]{1,0:T(8,128)(2,1)S(1)}, u32[]{:S(2)}, u32[]{:S(2)}) collective-permute-start(bf16[192,128]{1,0:T(8,128)(2,1)S(1)} %columns.2.own_ref), channel_id=1, source_target_pairs={{0,28},{4,8},{8,4},{12,16},{16,12},{20,24},{24,20},{28,0},{1,29},{... | collective-permute-start | bytes 147464 | tf_op jit(solution)/shard_map/ppermute | solution.py:70
  13.6 2.6 %near.2.near_ref = f32[72,80]{1,0:T(8,128)S(1)} custom-call(bf16[192,128]{1,0:T(8,128)(2,1)S(1)} %columns.2.own_ref, bf16[192,128]{1,0:T(8,128)(2,1)S(1)} %collective-permute-done.3.mate_ref, bf16[672,256]{1,0:T(8,128)(2,1)S(1)} %get-tuple-element.22.pick_ref, f32[80,128]{1,0:T(8,128)S(1)} %get-tuple-element.23.shift_ref, ...), custom_call_target="tpu_custom_call" | custom-call | bytes 12582912 | tf_op jit(solution)/shard_map/near/pallas_call | solution.py:42
  16.7 1.6 %collective-permute-start.7 = (bf16[80,80]{1,0:T(8,128)(2,1)S(1)}, bf16[80,80]{1,0:T(8,128)(2,1)S(1)}, u32[]{:S(2)}, u32[]{:S(2)}) collective-permute-start(bf16[80,80]{1,0:T(8,128)(2,1)S(1)} %far.2.refs_0_), channel_id=1, source_target_pairs={{0,3},{1,2},{2,1},{3,0},{4,7},{5,6},{6,5},{7,4},{8,11},{9,10},{10,... | collective-permute-start | bytes 38408 | tf_op jit(solution)/shard_map/ppermute | solution.py:61
  18.2 0.6 %collective-permute-start.6 = (bf16[80,80]{1,0:T(8,128)(2,1)S(1)}, bf16[80,80]{1,0:T(8,128)(2,1)S(1)}, u32[]{:S(2)}, u32[]{:S(2)}) collective-permute-start(bf16[80,80]{1,0:T(8,128)(2,1)S(1)} %far.2.refs_0_), channel_id=1, source_target_pairs={{0,2},{1,3},{2,0},{3,1},{4,6},{5,7},{6,4},{7,5},{8,10},{9,11},{10,... | collective-permute-start | bytes 38408 | tf_op jit(solution)/shard_map/ppermute | solution.py:61
  18.8 2.3 %collective-permute-start.5 = (bf16[80,80]{1,0:T(8,128)(2,1)S(1)}, bf16[80,80]{1,0:T(8,128)(2,1)S(1)}, u32[]{:S(2)}, u32[]{:S(2)}) collective-permute-start(bf16[80,80]{1,0:T(8,128)(2,1)S(1)} %far.2.refs_0_), channel_id=1, source_target_pairs={{0,1},{1,0},{2,3},{3,2},{4,5},{5,4},{6,7},{7,6},{8,9},{9,8},{10,11... | collective-permute-start | bytes 38408 | tf_op jit(solution)/shard_map/ppermute | solution.py:61
  21.1 1.3 %collective-permute-done.7.refs_3_ = bf16[80,80]{1,0:T(8,128)(2,1)S(1)} collective-permute-done((bf16[80,80]{1,0:T(8,128)(2,1)S(1)}, bf16[80,80]{1,0:T(8,128)(2,1)S(1)}, u32[]{:S(2)}, u32[]{:S(2)}) %collective-permute-start.7) | collective-permute-done | bytes 12832 | tf_op jit(solution)/shard_map/ppermute | solution.py:61
  23.1 0.7 %update.1 = (f32[72,80]{1,0:T(8,128)S(1)}, bf16[80,80]{1,0:T(8,128)(2,1)S(1)}) custom-call(bf16[80,80]{1,0:T(8,128)(2,1)S(1)} %far.2.refs_0_, bf16[80,80]{1,0:T(8,128)(2,1)S(1)} %collective-permute-done.5.refs_1_, bf16[80,80]{1,0:T(8,128)(2,1)S(1)} %collective-permute-done.6.refs_2_, bf16[80,80]{1,0:T(8,128)(2,1)S(1)} %collective-permute-done.7.refs_3_, ...), custom_call_target="tpu_custom_call" | custom-call | bytes 8388608 | tf_op jit(solution)/shard_map/update/pallas_call | solution.py:42
  23.8 2.4 %collective-permute-start.10 = (bf16[80,80]{1,0:T(8,128)(2,1)S(1)}, bf16[80,80]{1,0:T(8,128)(2,1)S(1)}, u32[]{:S(2)}, u32[]{:S(2)}) collective-permute-start(bf16[80,80]{1,0:T(8,128)(2,1)S(1)} %get-tuple-element.27.refs_0_), channel_id=1, source_target_pairs={{0,3},{1,2},{2,1},{3,0},{4,7},{5,6},{6,5},{7,4},{8,11},{9,10},{10,... | collective-permute-start | bytes 38408 | tf_op jit(solution)/shard_map/ppermute | solution.py:61
  26.2 0.9 %collective-permute-start.9 = (bf16[80,80]{1,0:T(8,128)(2,1)S(1)}, bf16[80,80]{1,0:T(8,128)(2,1)S(1)}, u32[]{:S(2)}, u32[]{:S(2)}) collective-permute-start(bf16[80,80]{1,0:T(8,128)(2,1)S(1)} %get-tuple-element.27.refs_0_), channel_id=1, source_target_pairs={{0,2},{1,3},{2,0},{3,1},{4,6},{5,7},{6,4},{7,5},{8,10},{9,11},{10,... | collective-permute-start | bytes 38408 | tf_op jit(solution)/shard_map/ppermute | solution.py:61
  27.1 1.1 %collective-permute-start.8 = (bf16[80,80]{1,0:T(8,128)(2,1)S(1)}, bf16[80,80]{1,0:T(8,128)(2,1)S(1)}, u32[]{:S(2)}, u32[]{:S(2)}) collective-permute-start(bf16[80,80]{1,0:T(8,128)(2,1)S(1)} %get-tuple-element.27.refs_0_), channel_id=1, source_target_pairs={{0,1},{1,0},{2,3},{3,2},{4,5},{5,4},{6,7},{7,6},{8,9},{9,8},{10,11... | collective-permute-start | bytes 38408 | tf_op jit(solution)/shard_map/ppermute | solution.py:61
  28.3 1.3 %collective-permute-done.10.refs_3_ = bf16[80,80]{1,0:T(8,128)(2,1)S(1)} collective-permute-done((bf16[80,80]{1,0:T(8,128)(2,1)S(1)}, bf16[80,80]{1,0:T(8,128)(2,1)S(1)}, u32[]{:S(2)}, u32[]{:S(2)}) %collective-permute-start.10) | collective-permute-done | bytes 12832 | tf_op jit(solution)/shard_map/ppermute | solution.py:61
  29.5 1.4 %collective-permute-done.9.refs_2_ = bf16[80,80]{1,0:T(8,128)(2,1)S(1)} collective-permute-done((bf16[80,80]{1,0:T(8,128)(2,1)S(1)}, bf16[80,80]{1,0:T(8,128)(2,1)S(1)}, u32[]{:S(2)}, u32[]{:S(2)}) %collective-permute-start.9) | collective-permute-done | bytes 12832 | tf_op jit(solution)/shard_map/ppermute | solution.py:61
  31.3 2.3 %collective-permute-start.12 = (bf16[192,128]{1,0:T(8,128)(2,1)S(1)}, bf16[192,128]{1,0:T(8,128)(2,1)S(1)}, u32[]{:S(2)}, u32[]{:S(2)}) collective-permute-start(bf16[192,128]{1,0:T(8,128)(2,1)S(1)} %columns.3.own_ref), channel_id=1, source_target_pairs={{0,28},{4,8},{8,4},{12,16},{16,12},{20,24},{24,20},{28,0},{1,29},{... | collective-permute-start | bytes 147464 | tf_op jit(solution)/shard_map/ppermute | solution.py:70
  33.6 2.6 %near.3.near_ref = f32[72,80]{1,0:T(8,128)S(1)} custom-call(bf16[192,128]{1,0:T(8,128)(2,1)S(1)} %columns.3.own_ref, bf16[192,128]{1,0:T(8,128)(2,1)S(1)} %collective-permute-done.11.mate_ref, bf16[672,256]{1,0:T(8,128)(2,1)S(1)} %get-tuple-element.22.pick_ref, f32[80,128]{1,0:T(8,128)S(1)} %get-tuple-element.23.shift_ref, ...), custom_call_target="tpu_custom_call" | custom-call | bytes 12582912 | tf_op jit(solution)/shard_map/near/pallas_call | solution.py:42
  36.7 1.5 %collective-permute-start.15 = (bf16[80,80]{1,0:T(8,128)(2,1)S(1)}, bf16[80,80]{1,0:T(8,128)(2,1)S(1)}, u32[]{:S(2)}, u32[]{:S(2)}) collective-permute-start(bf16[80,80]{1,0:T(8,128)(2,1)S(1)} %far.3.refs_0_), channel_id=1, source_target_pairs={{0,3},{1,2},{2,1},{3,0},{4,7},{5,6},{6,5},{7,4},{8,11},{9,10},{10,... | collective-permute-start | bytes 38408 | tf_op jit(solution)/shard_map/ppermute | solution.py:61
  38.2 0.9 %collective-permute-start.14 = (bf16[80,80]{1,0:T(8,128)(2,1)S(1)}, bf16[80,80]{1,0:T(8,128)(2,1)S(1)}, u32[]{:S(2)}, u32[]{:S(2)}) collective-permute-start(bf16[80,80]{1,0:T(8,128)(2,1)S(1)} %far.3.refs_0_), channel_id=1, source_target_pairs={{0,2},{1,3},{2,0},{3,1},{4,6},{5,7},{6,4},{7,5},{8,10},{9,11},{10,... | collective-permute-start | bytes 38408 | tf_op jit(solution)/shard_map/ppermute | solution.py:61
  39.1 2.0 %collective-permute-start.13 = (bf16[80,80]{1,0:T(8,128)(2,1)S(1)}, bf16[80,80]{1,0:T(8,128)(2,1)S(1)}, u32[]{:S(2)}, u32[]{:S(2)}) collective-permute-start(bf16[80,80]{1,0:T(8,128)(2,1)S(1)} %far.3.refs_0_), channel_id=1, source_target_pairs={{0,1},{1,0},{2,3},{3,2},{4,5},{5,4},{6,7},{7,6},{8,9},{9,8},{10,11... | collective-permute-start | bytes 38408 | tf_op jit(solution)/shard_map/ppermute | solution.py:61
  41.2 0.6 %nodes.1 = (bf16[192,1536]{1,0:T(8,128)(2,1)S(1)}, s32[12,128]{1,0:T(8,128)S(1)}, bf16[24,80,192]{2,1,0:T(8,128)(2,1)S(1)}) custom-call(s32[24,64]{1,0:T(8,128)S(1)} %copy-done.4, bf16[24,80,192]{2,1,0:T(8,128)(2,1)S(1)} %copy-done.3), custom_call_target="tpu_custom_call" | custom-call | bytes 3145728 | tf_op jit(solution)/shard_map/nodes/pallas_call | solution.py:42
  41.8 0.7 %collective-permute-done.15.refs_3_ = bf16[80,80]{1,0:T(8,128)(2,1)S(1)} collective-permute-done((bf16[80,80]{1,0:T(8,128)(2,1)S(1)}, bf16[80,80]{1,0:T(8,128)(2,1)S(1)}, u32[]{:S(2)}, u32[]{:S(2)}) %collective-permute-start.15) | collective-permute-done | bytes 12832 | tf_op jit(solution)/shard_map/ppermute | solution.py:61
  43.1 2.1 %gradient.1 = (f32[72,80]{1,0:T(8,128)}, bf16[48,192]{1,0:T(8,128)(2,1)S(1)}, bf16[48,192]{1,0:T(8,128)(2,1)S(1)}, f32[160,384]{1,0:T(8,128)S(1)}) custom-call(bf16[80,80]{1,0:T(8,128)(2,1)S(1)} %far.3.refs_0_, bf16[80,80]{1,0:T(8,128)(2,1)S(1)} %collective-permute-done.13.refs_1_, bf16[80,80]{1,0:T(8,128)(2,1)S(1)} %collective-permute-done.14.refs_2_, ...), custom_call_target="tpu_custom_call" | custom-call | tf_op jit(solution)/shard_map/gradient/pallas_call | solution.py:42
  45.2 2.4 %collective-permute-start.17 = (bf16[48,192]{1,0:T(8,128)(2,1)S(1)}, bf16[48,192]{1,0:T(8,128)(2,1)S(1)}, u32[]{:S(2)}, u32[]{:S(2)}) collective-permute-start(bf16[48,192]{1,0:T(8,128)(2,1)S(1)} %get-tuple-element.35), channel_id=1, source_target_pairs={{0,28},{4,8},{8,4},{12,16},{16,12},{20,24},{24,20},{28,0},{1,29},{... | collective-permute-start | bytes 55304 | tf_op jit(solution)/shard_map/ppermute | solution.py:70
  48.0 1.4 %collective-permute-done.17.far_ref = bf16[48,192]{1,0:T(8,128)(2,1)S(1)} collective-permute-done((bf16[48,192]{1,0:T(8,128)(2,1)S(1)}, bf16[48,192]{1,0:T(8,128)(2,1)S(1)}, u32[]{:S(2)}, u32[]{:S(2)}) %collective-permute-start.17) | collective-permute-done | bytes 18464 | tf_op jit(solution)/shard_map/ppermute | solution.py:70
  49.4 2.4 %collective-permute-start.18 = (bf16[16,192]{1,0:T(8,128)(2,1)S(1)}, bf16[16,192]{1,0:T(8,128)(2,1)S(1)}, u32[]{:S(2)}, u32[]{:S(2)}) collective-permute-start(bf16[16,192]{1,0:T(8,128)(2,1)S(1)} %get-tuple-element.37), channel_id=1, source_target_pairs={{0,3},{1,2},{2,1},{3,0},{4,7},{5,6},{6,5},{7,4},{8,11},{9,10},{10,... | collective-permute-start | bytes 18440 | tf_op jit(solution)/shard_map/ppermute | solution.py:598
  51.8 0.9 %collective-permute-start.19 = (bf16[16,192]{1,0:T(8,128)(2,1)S(1)}, bf16[16,192]{1,0:T(8,128)(2,1)S(1)}, u32[]{:S(2)}, u32[]{:S(2)}) collective-permute-start(bf16[16,192]{1,0:T(8,128)(2,1)S(1)} %get-tuple-element.38), channel_id=1, source_target_pairs={{0,2},{1,3},{2,0},{3,1},{4,6},{5,7},{6,4},{7,5},{8,10},{9,11},{10,... | collective-permute-start | bytes 18440 | tf_op jit(solution)/shard_map/ppermute | solution.py:598
  52.7 1.1 %collective-permute-start.20 = (bf16[16,192]{1,0:T(8,128)(2,1)S(1)}, bf16[16,192]{1,0:T(8,128)(2,1)S(1)}, u32[]{:S(2)}, u32[]{:S(2)}) collective-permute-start(bf16[16,192]{1,0:T(8,128)(2,1)S(1)} %get-tuple-element.39), channel_id=1, source_target_pairs={{0,1},{1,0},{2,3},{3,2},{4,5},{5,4},{6,7},{7,6},{8,9},{9,8},{10,11... | collective-permute-start | bytes 18440 | tf_op jit(solution)/shard_map/ppermute | solution.py:598
  53.8 1.1 %collective-permute-done.18 = bf16[16,192]{1,0:T(8,128)(2,1)S(1)} collective-permute-done((bf16[16,192]{1,0:T(8,128)(2,1)S(1)}, bf16[16,192]{1,0:T(8,128)(2,1)S(1)}, u32[]{:S(2)}, u32[]{:S(2)}) %collective-permute-start.18) | collective-permute-done | bytes 6176 | tf_op jit(solution)/shard_map/ppermute | solution.py:598
  54.9 1.5 %collective-permute-done.19 = bf16[16,192]{1,0:T(8,128)(2,1)S(1)} collective-permute-done((bf16[16,192]{1,0:T(8,128)(2,1)S(1)}, bf16[16,192]{1,0:T(8,128)(2,1)S(1)}, u32[]{:S(2)}, u32[]{:S(2)}) %collective-permute-start.19) | collective-permute-done | bytes 6176 | tf_op jit(solution)/shard_map/ppermute | solution.py:598
  56.4 0.6 %convert_add_fusion = f32[9,192]{1,0:T(8,128)} fusion(f32[9,192]{1,0:T(8,128)S(1)} %get-tuple-element.36, bf16[16,192]{1,0:T(8,128)(2,1)S(1)} %collective-permute-done.20, bf16[16,192]{1,0:T(8,128)(2,1)S(1)} %collective-permute-done.19, bf16[16,192]{1,0:T(8,128)(2,1)S(1)} %collective-permute-done.18), kind=kLoop, calls=%fused_computation | loop fusion | flops 10368 | bytes 24192 | tf_op jit(solution)/shard_map/add | solution.py:598
  (33 shorter events, 3.3 us)
Async XLA Ops:
  0.6 12.9 %copy-start = (bf16[24,7,80,320]{3,2,1,0:T(8,128)(2,1)S(1)}, bf16[24,7,80,320]{3,2,1,0:T(8,128)(2,1)}, u32[]{:S(2)}) copy-start(bf16[24,7,80,320]{3,2,1,0:T(8,128)(2,1)} %jac_ref.7) | copy-start | bytes 25804804
  0.6 7.6 %collective-permute-start.2 = (f32[72,80]{1,0:T(8,128)}, f32[72,80]{1,0:T(8,128)S(1)}, u32[]{:S(2)}, u32[]{:S(2)}) collective-permute-start(f32[72,80]{1,0:T(8,128)} %bitcast.11), channel_id=1, source_target_pairs={{0,3},{1,2},{2,1},{3,0},{4,7},{5,6},{6,5},{7,4},{8,11},{9,10},{10,... | collective-permute-start | bytes 69128 | tf_op jit(solution)/shard_map/ppermute | solution.py:61
  5.8 5.1 %collective-permute-start.1 = (f32[72,80]{1,0:T(8,128)}, f32[72,80]{1,0:T(8,128)S(1)}, u32[]{:S(2)}, u32[]{:S(2)}) collective-permute-start(f32[72,80]{1,0:T(8,128)} %bitcast.12), channel_id=1, source_target_pairs={{0,2},{1,3},{2,0},{3,1},{4,6},{5,7},{6,4},{7,5},{8,10},{9,11},{10,... | collective-permute-start | bytes 69128 | tf_op jit(solution)/shard_map/ppermute | solution.py:61
  5.8 5.1 %collective-permute-start = (f32[72,80]{1,0:T(8,128)}, f32[72,80]{1,0:T(8,128)S(1)}, u32[]{:S(2)}, u32[]{:S(2)}) collective-permute-start(f32[72,80]{1,0:T(8,128)} %bitcast.13), channel_id=1, source_target_pairs={{0,1},{1,0},{2,3},{3,2},{4,5},{5,4},{6,7},{7,6},{8,9},{9,8},{10,11... | collective-permute-start | bytes 69128 | tf_op jit(solution)/shard_map/ppermute | solution.py:61
  11.0 2.6 %collective-permute-start.3 = (bf16[192,128]{1,0:T(8,128)(2,1)S(1)}, bf16[192,128]{1,0:T(8,128)(2,1)S(1)}, u32[]{:S(2)}, u32[]{:S(2)}) collective-permute-start(bf16[192,128]{1,0:T(8,128)(2,1)S(1)} %columns.2.own_ref), channel_id=1, source_target_pairs={{0,4},{4,0},{8,12},{12,8},{16,20},{20,16},{24,28},{28,24},{1,5},{5... | collective-permute-start | bytes 147464 | tf_op jit(solution)/shard_map/ppermute | solution.py:65
  11.0 5.2 %collective-permute-start.4 = (bf16[192,128]{1,0:T(8,128)(2,1)S(1)}, bf16[192,128]{1,0:T(8,128)(2,1)S(1)}, u32[]{:S(2)}, u32[]{:S(2)}) collective-permute-start(bf16[192,128]{1,0:T(8,128)(2,1)S(1)} %columns.2.own_ref), channel_id=1, source_target_pairs={{0,28},{4,8},{8,4},{12,16},{16,12},{20,24},{24,20},{28,0},{1,29},{... | collective-permute-start | bytes 147464 | tf_op jit(solution)/shard_map/ppermute | solution.py:70
  13.6 9.5 %copy-start.1 = (bf16[24,80,320]{2,1,0:T(8,128)(2,1)S(1)}, bf16[24,80,320]{2,1,0:T(8,128)(2,1)}, u32[]{:S(2)}) copy-start(bf16[24,80,320]{2,1,0:T(8,128)(2,1)} %refs_4_.3) | copy-start | bytes 3686404
  16.7 5.8 %collective-permute-start.7 = (bf16[80,80]{1,0:T(8,128)(2,1)S(1)}, bf16[80,80]{1,0:T(8,128)(2,1)S(1)}, u32[]{:S(2)}, u32[]{:S(2)}) collective-permute-start(bf16[80,80]{1,0:T(8,128)(2,1)S(1)} %far.2.refs_0_), channel_id=1, source_target_pairs={{0,3},{1,2},{2,1},{3,0},{4,7},{5,6},{6,5},{7,4},{8,11},{9,10},{10,... | collective-permute-start | bytes 38408 | tf_op jit(solution)/shard_map/ppermute | solution.py:61
  18.2 4.7 %collective-permute-start.6 = (bf16[80,80]{1,0:T(8,128)(2,1)S(1)}, bf16[80,80]{1,0:T(8,128)(2,1)S(1)}, u32[]{:S(2)}, u32[]{:S(2)}) collective-permute-start(bf16[80,80]{1,0:T(8,128)(2,1)S(1)} %far.2.refs_0_), channel_id=1, source_target_pairs={{0,2},{1,3},{2,0},{3,1},{4,6},{5,7},{6,4},{7,5},{8,10},{9,11},{10,... | collective-permute-start | bytes 38408 | tf_op jit(solution)/shard_map/ppermute | solution.py:61
  18.8 4.3 %collective-permute-start.5 = (bf16[80,80]{1,0:T(8,128)(2,1)S(1)}, bf16[80,80]{1,0:T(8,128)(2,1)S(1)}, u32[]{:S(2)}, u32[]{:S(2)}) collective-permute-start(bf16[80,80]{1,0:T(8,128)(2,1)S(1)} %far.2.refs_0_), channel_id=1, source_target_pairs={{0,1},{1,0},{2,3},{3,2},{4,5},{5,4},{6,7},{7,6},{8,9},{9,8},{10,11... | collective-permute-start | bytes 38408 | tf_op jit(solution)/shard_map/ppermute | solution.py:61
  23.8 5.7 %collective-permute-start.10 = (bf16[80,80]{1,0:T(8,128)(2,1)S(1)}, bf16[80,80]{1,0:T(8,128)(2,1)S(1)}, u32[]{:S(2)}, u32[]{:S(2)}) collective-permute-start(bf16[80,80]{1,0:T(8,128)(2,1)S(1)} %get-tuple-element.27.refs_0_), channel_id=1, source_target_pairs={{0,3},{1,2},{2,1},{3,0},{4,7},{5,6},{6,5},{7,4},{8,11},{9,10},{10,... | collective-permute-start | bytes 38408 | tf_op jit(solution)/shard_map/ppermute | solution.py:61
  26.2 4.7 %collective-permute-start.9 = (bf16[80,80]{1,0:T(8,128)(2,1)S(1)}, bf16[80,80]{1,0:T(8,128)(2,1)S(1)}, u32[]{:S(2)}, u32[]{:S(2)}) collective-permute-start(bf16[80,80]{1,0:T(8,128)(2,1)S(1)} %get-tuple-element.27.refs_0_), channel_id=1, source_target_pairs={{0,2},{1,3},{2,0},{3,1},{4,6},{5,7},{6,4},{7,5},{8,10},{9,11},{10,... | collective-permute-start | bytes 38408 | tf_op jit(solution)/shard_map/ppermute | solution.py:61
  27.1 4.0 %collective-permute-start.8 = (bf16[80,80]{1,0:T(8,128)(2,1)S(1)}, bf16[80,80]{1,0:T(8,128)(2,1)S(1)}, u32[]{:S(2)}, u32[]{:S(2)}) collective-permute-start(bf16[80,80]{1,0:T(8,128)(2,1)S(1)} %get-tuple-element.27.refs_0_), channel_id=1, source_target_pairs={{0,1},{1,0},{2,3},{3,2},{4,5},{5,4},{6,7},{7,6},{8,9},{9,8},{10,11... | collective-permute-start | bytes 38408 | tf_op jit(solution)/shard_map/ppermute | solution.py:61
  31.3 2.3 %collective-permute-start.11 = (bf16[192,128]{1,0:T(8,128)(2,1)S(1)}, bf16[192,128]{1,0:T(8,128)(2,1)S(1)}, u32[]{:S(2)}, u32[]{:S(2)}) collective-permute-start(bf16[192,128]{1,0:T(8,128)(2,1)S(1)} %columns.3.own_ref), channel_id=1, source_target_pairs={{0,4},{4,0},{8,12},{12,8},{16,20},{20,16},{24,28},{28,24},{1,5},{5... | collective-permute-start | bytes 147464 | tf_op jit(solution)/shard_map/ppermute | solution.py:65
  31.3 5.0 %collective-permute-start.12 = (bf16[192,128]{1,0:T(8,128)(2,1)S(1)}, bf16[192,128]{1,0:T(8,128)(2,1)S(1)}, u32[]{:S(2)}, u32[]{:S(2)}) collective-permute-start(bf16[192,128]{1,0:T(8,128)(2,1)S(1)} %columns.3.own_ref), channel_id=1, source_target_pairs={{0,28},{4,8},{8,4},{12,16},{16,12},{20,24},{24,20},{28,0},{1,29},{... | collective-permute-start | bytes 147464 | tf_op jit(solution)/shard_map/ppermute | solution.py:70
  33.6 7.6 %copy-start.3 = (bf16[24,80,192]{2,1,0:T(8,128)(2,1)S(1)}, bf16[24,80,192]{2,1,0:T(8,128)(2,1)}, u32[]{:S(2)}) copy-start(bf16[24,80,192]{2,1,0:T(8,128)(2,1)} %shape_ref.1) | copy-start | bytes 2211844
  33.6 7.6 %copy-start.4 = (s32[24,64]{1,0:T(8,128)S(1)}, s32[24,64]{1,0:T(8,128)}, u32[]{:S(2)}) copy-start(s32[24,64]{1,0:T(8,128)} %ids_ref.1) | copy-start | bytes 18436
  33.6 9.5 %copy-start.2 = (bf16[24,80,320]{2,1,0:T(8,128)(2,1)S(1)}, bf16[24,80,320]{2,1,0:T(8,128)(2,1)}, u32[]{:S(2)}) copy-start(bf16[24,80,320]{2,1,0:T(8,128)(2,1)} %refs_4_.3) | copy-start | bytes 3686404
  36.7 5.8 %collective-permute-start.15 = (bf16[80,80]{1,0:T(8,128)(2,1)S(1)}, bf16[80,80]{1,0:T(8,128)(2,1)S(1)}, u32[]{:S(2)}, u32[]{:S(2)}) collective-permute-start(bf16[80,80]{1,0:T(8,128)(2,1)S(1)} %far.3.refs_0_), channel_id=1, source_target_pairs={{0,3},{1,2},{2,1},{3,0},{4,7},{5,6},{6,5},{7,4},{8,11},{9,10},{10,... | collective-permute-start | bytes 38408 | tf_op jit(solution)/shard_map/ppermute | solution.py:61
  38.2 4.7 %collective-permute-start.14 = (bf16[80,80]{1,0:T(8,128)(2,1)S(1)}, bf16[80,80]{1,0:T(8,128)(2,1)S(1)}, u32[]{:S(2)}, u32[]{:S(2)}) collective-permute-start(bf16[80,80]{1,0:T(8,128)(2,1)S(1)} %far.3.refs_0_), channel_id=1, source_target_pairs={{0,2},{1,3},{2,0},{3,1},{4,6},{5,7},{6,4},{7,5},{8,10},{9,11},{10,... | collective-permute-start | bytes 38408 | tf_op jit(solution)/shard_map/ppermute | solution.py:61
  39.1 4.0 %collective-permute-start.13 = (bf16[80,80]{1,0:T(8,128)(2,1)S(1)}, bf16[80,80]{1,0:T(8,128)(2,1)S(1)}, u32[]{:S(2)}, u32[]{:S(2)}) collective-permute-start(bf16[80,80]{1,0:T(8,128)(2,1)S(1)} %far.3.refs_0_), channel_id=1, source_target_pairs={{0,1},{1,0},{2,3},{3,2},{4,5},{5,4},{6,7},{7,6},{8,9},{9,8},{10,11... | collective-permute-start | bytes 38408 | tf_op jit(solution)/shard_map/ppermute | solution.py:61
  45.2 2.8 %collective-permute-start.16 = (bf16[48,192]{1,0:T(8,128)(2,1)S(1)}, bf16[48,192]{1,0:T(8,128)(2,1)S(1)}, u32[]{:S(2)}, u32[]{:S(2)}) collective-permute-start(bf16[48,192]{1,0:T(8,128)(2,1)S(1)} %get-tuple-element.34), channel_id=1, source_target_pairs={{0,4},{4,0},{8,12},{12,8},{16,20},{20,16},{24,28},{28,24},{1,5},{5... | collective-permute-start | bytes 55304 | tf_op jit(solution)/shard_map/ppermute | solution.py:65
  45.2 4.2 %collective-permute-start.17 = (bf16[48,192]{1,0:T(8,128)(2,1)S(1)}, bf16[48,192]{1,0:T(8,128)(2,1)S(1)}, u32[]{:S(2)}, u32[]{:S(2)}) collective-permute-start(bf16[48,192]{1,0:T(8,128)(2,1)S(1)} %get-tuple-element.35), channel_id=1, source_target_pairs={{0,28},{4,8},{8,4},{12,16},{16,12},{20,24},{24,20},{28,0},{1,29},{... | collective-permute-start | bytes 55304 | tf_op jit(solution)/shard_map/ppermute | solution.py:70
  49.4 5.5 %collective-permute-start.18 = (bf16[16,192]{1,0:T(8,128)(2,1)S(1)}, bf16[16,192]{1,0:T(8,128)(2,1)S(1)}, u32[]{:S(2)}, u32[]{:S(2)}) collective-permute-start(bf16[16,192]{1,0:T(8,128)(2,1)S(1)} %get-tuple-element.37), channel_id=1, source_target_pairs={{0,3},{1,2},{2,1},{3,0},{4,7},{5,6},{6,5},{7,4},{8,11},{9,10},{10,... | collective-permute-start | bytes 18440 | tf_op jit(solution)/shard_map/ppermute | solution.py:598
  51.8 4.6 %collective-permute-start.19 = (bf16[16,192]{1,0:T(8,128)(2,1)S(1)}, bf16[16,192]{1,0:T(8,128)(2,1)S(1)}, u32[]{:S(2)}, u32[]{:S(2)}) collective-permute-start(bf16[16,192]{1,0:T(8,128)(2,1)S(1)} %get-tuple-element.38), channel_id=1, source_target_pairs={{0,2},{1,3},{2,0},{3,1},{4,6},{5,7},{6,4},{7,5},{8,10},{9,11},{10,... | collective-permute-start | bytes 18440 | tf_op jit(solution)/shard_map/ppermute | solution.py:598
  52.7 3.7 %collective-permute-start.20 = (bf16[16,192]{1,0:T(8,128)(2,1)S(1)}, bf16[16,192]{1,0:T(8,128)(2,1)S(1)}, u32[]{:S(2)}, u32[]{:S(2)}) collective-permute-start(bf16[16,192]{1,0:T(8,128)(2,1)S(1)} %get-tuple-element.39), channel_id=1, source_target_pairs={{0,1},{1,0},{2,3},{3,2},{4,5},{5,4},{6,7},{7,6},{8,9},{9,8},{10,11... | collective-permute-start | bytes 18440 | tf_op jit(solution)/shard_map/ppermute | solution.py:598

commit v9 on v7

--- a/solution.py
+++ b/solution.py
@@ -17,7 +17,7 @@
 VMEM = pl.BlockSpec(memory_space=pltpu.VMEM)
 SMEM = pl.BlockSpec(memory_space=pltpu.SMEM)
 HBM = pl.BlockSpec(memory_space=pltpu.HBM)
-GROUP = 60
+GROUP = 64
 MIB = 1024 * 1024
 
 

time: 56.8 us -> 56.8 us (level)
  no operation moved by 1% of the time
where the time goes in v9:
time: 56.8 us; the launch traced here: 56.7 us
  starting transfers between devices  31 us (55%)
  waiting for transfers between devices  12.8 us (23%)
  Pallas kernels  11.4 us (20%)
  between operations  0.79 us (1%)
  other arithmetic  0.61 us (1%)
    ppermute x12, starting transfers between devices, over_blk(): lax.ppermute(block, 'blk', [(i, i ^ k) for i in range(count)])  19.1 us
    pallas_call x12, Pallas kernels, call(): pl.pallas_call(kernel, in_specs=specs, out_specs=[SMEM if getattr(out, 'm...  11.4 us
    ppermute x12, waiting for transfers between devices, over_blk(): lax.ppermute(block, 'blk', [(i, i ^ k) for i in range(count)])  8.78 us
    ppermute x3, starting transfers between devices, to_far(): lax.ppermute(block, 'dom', [(i, ((i + 1 ^ 1) - 1) % count) for i in range...  7.32 us
    ppermute x3, starting transfers between devices, local(): lax.ppermute(pieces[k], 'blk', [(i, i ^ k) for i in range(count)])[:9]  4.45 us
    ppermute x3, waiting for transfers between devices, local(): lax.ppermute(pieces[k], 'blk', [(i, i ^ k) for i in range(count)])[:9]  2.61 us
    ppermute x3, waiting for transfers between devices, to_far(): lax.ppermute(block, 'dom', [(i, ((i + 1 ^ 1) - 1) % count) for i in range...  1.43 us
  transfers between devices with their start and end apart: 21, of which 14 were waited for; matrix products, arithmetic and copies ran while one was open for 0% of the time, Pallas kernels for 14%

profile of v9, /device:TPU:0, one launch (start us, length us, event | category | flops | bytes accessed | tf_op | source)
XLA Modules:
  0.0 56.7 jit_solution(17022246844365608377)
XLA Ops:
  0.6 5.1 %collective-permute-start.2 = (f32[72,80]{1,0:T(8,128)}, f32[72,80]{1,0:T(8,128)S(1)}, u32[]{:S(2)}, u32[]{:S(2)}) collective-permute-start(f32[72,80]{1,0:T(8,128)} %bitcast.11), channel_id=1, source_target_pairs={{0,3},{1,2},{2,1},{3,0},{4,7},{5,6},{6,5},{7,4},{8,11},{9,10},{10,... | collective-permute-start | bytes 69128 | tf_op jit(solution)/shard_map/ppermute | solution.py:60
  5.8 0.6 %collective-permute-start = (f32[72,80]{1,0:T(8,128)}, f32[72,80]{1,0:T(8,128)S(1)}, u32[]{:S(2)}, u32[]{:S(2)}) collective-permute-start(f32[72,80]{1,0:T(8,128)} %bitcast.13), channel_id=1, source_target_pairs={{0,1},{1,0},{2,3},{3,2},{4,5},{5,4},{6,7},{7,6},{8,9},{9,8},{10,11... | collective-permute-start | bytes 69128 | tf_op jit(solution)/shard_map/ppermute | solution.py:60
  6.4 1.8 %slots.1 = (bf16[672,256]{1,0:T(8,128)(2,1)S(1)}, f32[80,128]{1,0:T(8,128)S(1)}, s32[256]{0:T(256)S(4)}, s32[1]{0:T(128)S(4)}, f32[72,80]{1,0:T(8,128)S(1)}, /*index=5*/f32[72,80]{1,0:T(8,128)S(1)}) custom-call(s32[6,24]{1,0:T(8,128)} %bitcast.15, f32[24]{0:T(128)} %shift_hbm.1, f32[72,80]{1,0:T(8,128)} %bitcast.14, f32[72,80]{1,0:T(8,128)} %bitcast.10, ...), custom_call_target="tpu_custom_call" | custom-call | bytes 16777216 | tf_op jit(solution)/shard_map/slots/pallas_call | solution.py:41
  8.2 2.6 %collective-permute-done.1.refs_2_ = f32[72,80]{1,0:T(8,128)S(1)} collective-permute-done((f32[72,80]{1,0:T(8,128)}, f32[72,80]{1,0:T(8,128)S(1)}, u32[]{:S(2)}, u32[]{:S(2)}) %collective-permute-start.1) | collective-permute-done | bytes 23072 | tf_op jit(solution)/shard_map/ppermute | solution.py:60
  11.0 2.5 %collective-permute-start.4 = (bf16[192,128]{1,0:T(8,128)(2,1)S(1)}, bf16[192,128]{1,0:T(8,128)(2,1)S(1)}, u32[]{:S(2)}, u32[]{:S(2)}) collective-permute-start(bf16[192,128]{1,0:T(8,128)(2,1)S(1)} %columns.2.own_ref), channel_id=1, source_target_pairs={{0,28},{4,8},{8,4},{12,16},{16,12},{20,24},{24,20},{28,0},{1,29},{... | collective-permute-start | bytes 147464 | tf_op jit(solution)/shard_map/ppermute | solution.py:69
  13.6 2.6 %near.2.near_ref = f32[72,80]{1,0:T(8,128)S(1)} custom-call(bf16[192,128]{1,0:T(8,128)(2,1)S(1)} %columns.2.own_ref, bf16[192,128]{1,0:T(8,128)(2,1)S(1)} %collective-permute-done.3.mate_ref, bf16[672,256]{1,0:T(8,128)(2,1)S(1)} %get-tuple-element.22.pick_ref, f32[80,128]{1,0:T(8,128)S(1)} %get-tuple-element.23.shift_ref, ...), custom_call_target="tpu_custom_call" | custom-call | bytes 12582912 | tf_op jit(solution)/shard_map/near/pallas_call | solution.py:41
  16.7 1.6 %collective-permute-start.7 = (bf16[80,80]{1,0:T(8,128)(2,1)S(1)}, bf16[80,80]{1,0:T(8,128)(2,1)S(1)}, u32[]{:S(2)}, u32[]{:S(2)}) collective-permute-start(bf16[80,80]{1,0:T(8,128)(2,1)S(1)} %far.2.refs_0_), channel_id=1, source_target_pairs={{0,3},{1,2},{2,1},{3,0},{4,7},{5,6},{6,5},{7,4},{8,11},{9,10},{10,... | collective-permute-start | bytes 38408 | tf_op jit(solution)/shard_map/ppermute | solution.py:60
  18.2 0.6 %collective-permute-start.6 = (bf16[80,80]{1,0:T(8,128)(2,1)S(1)}, bf16[80,80]{1,0:T(8,128)(2,1)S(1)}, u32[]{:S(2)}, u32[]{:S(2)}) collective-permute-start(bf16[80,80]{1,0:T(8,128)(2,1)S(1)} %far.2.refs_0_), channel_id=1, source_target_pairs={{0,2},{1,3},{2,0},{3,1},{4,6},{5,7},{6,4},{7,5},{8,10},{9,11},{10,... | collective-permute-start | bytes 38408 | tf_op jit(solution)/shard_map/ppermute | solution.py:60
  18.8 2.3 %collective-permute-start.5 = (bf16[80,80]{1,0:T(8,128)(2,1)S(1)}, bf16[80,80]{1,0:T(8,128)(2,1)S(1)}, u32[]{:S(2)}, u32[]{:S(2)}) collective-permute-start(bf16[80,80]{1,0:T(8,128)(2,1)S(1)} %far.2.refs_0_), channel_id=1, source_target_pairs={{0,1},{1,0},{2,3},{3,2},{4,5},{5,4},{6,7},{7,6},{8,9},{9,8},{10,11... | collective-permute-start | bytes 38408 | tf_op jit(solution)/shard_map/ppermute | solution.py:60
  21.1 1.2 %collective-permute-done.7.refs_3_ = bf16[80,80]{1,0:T(8,128)(2,1)S(1)} collective-permute-done((bf16[80,80]{1,0:T(8,128)(2,1)S(1)}, bf16[80,80]{1,0:T(8,128)(2,1)S(1)}, u32[]{:S(2)}, u32[]{:S(2)}) %collective-permute-start.7) | collective-permute-done | bytes 12832 | tf_op jit(solution)/shard_map/ppermute | solution.py:60
  23.1 0.7 %update.1 = (f32[72,80]{1,0:T(8,128)S(1)}, bf16[80,80]{1,0:T(8,128)(2,1)S(1)}) custom-call(bf16[80,80]{1,0:T(8,128)(2,1)S(1)} %far.2.refs_0_, bf16[80,80]{1,0:T(8,128)(2,1)S(1)} %collective-permute-done.5.refs_1_, bf16[80,80]{1,0:T(8,128)(2,1)S(1)} %collective-permute-done.6.refs_2_, bf16[80,80]{1,0:T(8,128)(2,1)S(1)} %collective-permute-done.7.refs_3_, ...), custom_call_target="tpu_custom_call" | custom-call | bytes 8388608 | tf_op jit(solution)/shard_map/update/pallas_call | solution.py:41
  23.8 2.4 %collective-permute-start.10 = (bf16[80,80]{1,0:T(8,128)(2,1)S(1)}, bf16[80,80]{1,0:T(8,128)(2,1)S(1)}, u32[]{:S(2)}, u32[]{:S(2)}) collective-permute-start(bf16[80,80]{1,0:T(8,128)(2,1)S(1)} %get-tuple-element.27.refs_0_), channel_id=1, source_target_pairs={{0,3},{1,2},{2,1},{3,0},{4,7},{5,6},{6,5},{7,4},{8,11},{9,10},{10,... | collective-permute-start | bytes 38408 | tf_op jit(solution)/shard_map/ppermute | solution.py:60
  26.2 0.9 %collective-permute-start.9 = (bf16[80,80]{1,0:T(8,128)(2,1)S(1)}, bf16[80,80]{1,0:T(8,128)(2,1)S(1)}, u32[]{:S(2)}, u32[]{:S(2)}) collective-permute-start(bf16[80,80]{1,0:T(8,128)(2,1)S(1)} %get-tuple-element.27.refs_0_), channel_id=1, source_target_pairs={{0,2},{1,3},{2,0},{3,1},{4,6},{5,7},{6,4},{7,5},{8,10},{9,11},{10,... | collective-permute-start | bytes 38408 | tf_op jit(solution)/shard_map/ppermute | solution.py:60
  27.1 1.1 %collective-permute-start.8 = (bf16[80,80]{1,0:T(8,128)(2,1)S(1)}, bf16[80,80]{1,0:T(8,128)(2,1)S(1)}, u32[]{:S(2)}, u32[]{:S(2)}) collective-permute-start(bf16[80,80]{1,0:T(8,128)(2,1)S(1)} %get-tuple-element.27.refs_0_), channel_id=1, source_target_pairs={{0,1},{1,0},{2,3},{3,2},{4,5},{5,4},{6,7},{7,6},{8,9},{9,8},{10,11... | collective-permute-start | bytes 38408 | tf_op jit(solution)/shard_map/ppermute | solution.py:60
  28.3 1.2 %collective-permute-done.10.refs_3_ = bf16[80,80]{1,0:T(8,128)(2,1)S(1)} collective-permute-done((bf16[80,80]{1,0:T(8,128)(2,1)S(1)}, bf16[80,80]{1,0:T(8,128)(2,1)S(1)}, u32[]{:S(2)}, u32[]{:S(2)}) %collective-permute-start.10) | collective-permute-done | bytes 12832 | tf_op jit(solution)/shard_map/ppermute | solution.py:60
  29.5 1.5 %collective-permute-done.9.refs_2_ = bf16[80,80]{1,0:T(8,128)(2,1)S(1)} collective-permute-done((bf16[80,80]{1,0:T(8,128)(2,1)S(1)}, bf16[80,80]{1,0:T(8,128)(2,1)S(1)}, u32[]{:S(2)}, u32[]{:S(2)}) %collective-permute-start.9) | collective-permute-done | bytes 12832 | tf_op jit(solution)/shard_map/ppermute | solution.py:60
  31.3 2.3 %collective-permute-start.12 = (bf16[192,128]{1,0:T(8,128)(2,1)S(1)}, bf16[192,128]{1,0:T(8,128)(2,1)S(1)}, u32[]{:S(2)}, u32[]{:S(2)}) collective-permute-start(bf16[192,128]{1,0:T(8,128)(2,1)S(1)} %columns.3.own_ref), channel_id=1, source_target_pairs={{0,28},{4,8},{8,4},{12,16},{16,12},{20,24},{24,20},{28,0},{1,29},{... | collective-permute-start | bytes 147464 | tf_op jit(solution)/shard_map/ppermute | solution.py:69
  33.7 2.6 %near.3.near_ref = f32[72,80]{1,0:T(8,128)S(1)} custom-call(bf16[192,128]{1,0:T(8,128)(2,1)S(1)} %columns.3.own_ref, bf16[192,128]{1,0:T(8,128)(2,1)S(1)} %collective-permute-done.11.mate_ref, bf16[672,256]{1,0:T(8,128)(2,1)S(1)} %get-tuple-element.22.pick_ref, f32[80,128]{1,0:T(8,128)S(1)} %get-tuple-element.23.shift_ref, ...), custom_call_target="tpu_custom_call" | custom-call | bytes 12582912 | tf_op jit(solution)/shard_map/near/pallas_call | solution.py:41
  36.8 1.5 %collective-permute-start.15 = (bf16[80,80]{1,0:T(8,128)(2,1)S(1)}, bf16[80,80]{1,0:T(8,128)(2,1)S(1)}, u32[]{:S(2)}, u32[]{:S(2)}) collective-permute-start(bf16[80,80]{1,0:T(8,128)(2,1)S(1)} %far.3.refs_0_), channel_id=1, source_target_pairs={{0,3},{1,2},{2,1},{3,0},{4,7},{5,6},{6,5},{7,4},{8,11},{9,10},{10,... | collective-permute-start | bytes 38408 | tf_op jit(solution)/shard_map/ppermute | solution.py:60
  38.3 0.9 %collective-permute-start.14 = (bf16[80,80]{1,0:T(8,128)(2,1)S(1)}, bf16[80,80]{1,0:T(8,128)(2,1)S(1)}, u32[]{:S(2)}, u32[]{:S(2)}) collective-permute-start(bf16[80,80]{1,0:T(8,128)(2,1)S(1)} %far.3.refs_0_), channel_id=1, source_target_pairs={{0,2},{1,3},{2,0},{3,1},{4,6},{5,7},{6,4},{7,5},{8,10},{9,11},{10,... | collective-permute-start | bytes 38408 | tf_op jit(solution)/shard_map/ppermute | solution.py:60
  39.2 2.0 %collective-permute-start.13 = (bf16[80,80]{1,0:T(8,128)(2,1)S(1)}, bf16[80,80]{1,0:T(8,128)(2,1)S(1)}, u32[]{:S(2)}, u32[]{:S(2)}) collective-permute-start(bf16[80,80]{1,0:T(8,128)(2,1)S(1)} %far.3.refs_0_), channel_id=1, source_target_pairs={{0,1},{1,0},{2,3},{3,2},{4,5},{5,4},{6,7},{7,6},{8,9},{9,8},{10,11... | collective-permute-start | bytes 38408 | tf_op jit(solution)/shard_map/ppermute | solution.py:60
  41.2 0.7 %nodes.1 = (bf16[192,1536]{1,0:T(8,128)(2,1)S(1)}, s32[12,128]{1,0:T(8,128)S(1)}, bf16[24,80,192]{2,1,0:T(8,128)(2,1)S(1)}) custom-call(s32[24,64]{1,0:T(8,128)S(1)} %copy-done.4, bf16[24,80,192]{2,1,0:T(8,128)(2,1)S(1)} %copy-done.3), custom_call_target="tpu_custom_call" | custom-call | bytes 3145728 | tf_op jit(solution)/shard_map/nodes/pallas_call | solution.py:41
  41.9 0.7 %collective-permute-done.15.refs_3_ = bf16[80,80]{1,0:T(8,128)(2,1)S(1)} collective-permute-done((bf16[80,80]{1,0:T(8,128)(2,1)S(1)}, bf16[80,80]{1,0:T(8,128)(2,1)S(1)}, u32[]{:S(2)}, u32[]{:S(2)}) %collective-permute-start.15) | collective-permute-done | bytes 12832 | tf_op jit(solution)/shard_map/ppermute | solution.py:60
  43.2 1.5 %gradient.1 = (f32[72,80]{1,0:T(8,128)}, bf16[48,192]{1,0:T(8,128)(2,1)S(1)}, bf16[48,192]{1,0:T(8,128)(2,1)S(1)}, f32[160,384]{1,0:T(8,128)S(1)}) custom-call(bf16[80,80]{1,0:T(8,128)(2,1)S(1)} %far.3.refs_0_, bf16[80,80]{1,0:T(8,128)(2,1)S(1)} %collective-permute-done.13.refs_1_, bf16[80,80]{1,0:T(8,128)(2,1)S(1)} %collective-permute-done.14.refs_2_, ...), custom_call_target="tpu_custom_call" | custom-call | tf_op jit(solution)/shard_map/gradient/pallas_call | solution.py:41
  44.7 2.4 %collective-permute-start.17 = (bf16[48,192]{1,0:T(8,128)(2,1)S(1)}, bf16[48,192]{1,0:T(8,128)(2,1)S(1)}, u32[]{:S(2)}, u32[]{:S(2)}) collective-permute-start(bf16[48,192]{1,0:T(8,128)(2,1)S(1)} %get-tuple-element.35), channel_id=1, source_target_pairs={{0,28},{4,8},{8,4},{12,16},{16,12},{20,24},{24,20},{28,0},{1,29},{... | collective-permute-start | bytes 55304 | tf_op jit(solution)/shard_map/ppermute | solution.py:69
  47.6 1.4 %collective-permute-done.17.far_ref = bf16[48,192]{1,0:T(8,128)(2,1)S(1)} collective-permute-done((bf16[48,192]{1,0:T(8,128)(2,1)S(1)}, bf16[48,192]{1,0:T(8,128)(2,1)S(1)}, u32[]{:S(2)}, u32[]{:S(2)}) %collective-permute-start.17) | collective-permute-done | bytes 18464 | tf_op jit(solution)/shard_map/ppermute | solution.py:69
  49.0 2.4 %collective-permute-start.18 = (bf16[16,192]{1,0:T(8,128)(2,1)S(1)}, bf16[16,192]{1,0:T(8,128)(2,1)S(1)}, u32[]{:S(2)}, u32[]{:S(2)}) collective-permute-start(bf16[16,192]{1,0:T(8,128)(2,1)S(1)} %get-tuple-element.37), channel_id=1, source_target_pairs={{0,3},{1,2},{2,1},{3,0},{4,7},{5,6},{6,5},{7,4},{8,11},{9,10},{10,... | collective-permute-start | bytes 18440 | tf_op jit(solution)/shard_map/ppermute | solution.py:605
  51.4 0.9 %collective-permute-start.19 = (bf16[16,192]{1,0:T(8,128)(2,1)S(1)}, bf16[16,192]{1,0:T(8,128)(2,1)S(1)}, u32[]{:S(2)}, u32[]{:S(2)}) collective-permute-start(bf16[16,192]{1,0:T(8,128)(2,1)S(1)} %get-tuple-element.38), channel_id=1, source_target_pairs={{0,2},{1,3},{2,0},{3,1},{4,6},{5,7},{6,4},{7,5},{8,10},{9,11},{10,... | collective-permute-start | bytes 18440 | tf_op jit(solution)/shard_map/ppermute | solution.py:605
  52.3 1.1 %collective-permute-start.20 = (bf16[16,192]{1,0:T(8,128)(2,1)S(1)}, bf16[16,192]{1,0:T(8,128)(2,1)S(1)}, u32[]{:S(2)}, u32[]{:S(2)}) collective-permute-start(bf16[16,192]{1,0:T(8,128)(2,1)S(1)} %get-tuple-element.39), channel_id=1, source_target_pairs={{0,1},{1,0},{2,3},{3,2},{4,5},{5,4},{6,7},{7,6},{8,9},{9,8},{10,11... | collective-permute-start | bytes 18440 | tf_op jit(solution)/shard_map/ppermute | solution.py:605
  53.4 1.1 %collective-permute-done.18 = bf16[16,192]{1,0:T(8,128)(2,1)S(1)} collective-permute-done((bf16[16,192]{1,0:T(8,128)(2,1)S(1)}, bf16[16,192]{1,0:T(8,128)(2,1)S(1)}, u32[]{:S(2)}, u32[]{:S(2)}) %collective-permute-start.18) | collective-permute-done | bytes 6176 | tf_op jit(solution)/shard_map/ppermute | solution.py:605
  54.5 1.5 %collective-permute-done.19 = bf16[16,192]{1,0:T(8,128)(2,1)S(1)} collective-permute-done((bf16[16,192]{1,0:T(8,128)(2,1)S(1)}, bf16[16,192]{1,0:T(8,128)(2,1)S(1)}, u32[]{:S(2)}, u32[]{:S(2)}) %collective-permute-start.19) | collective-permute-done | bytes 6176 | tf_op jit(solution)/shard_map/ppermute | solution.py:605
  56.0 0.6 %convert_add_fusion = f32[9,192]{1,0:T(8,128)} fusion(f32[9,192]{1,0:T(8,128)S(1)} %get-tuple-element.36, bf16[16,192]{1,0:T(8,128)(2,1)S(1)} %collective-permute-done.20, bf16[16,192]{1,0:T(8,128)(2,1)S(1)} %collective-permute-done.19, bf16[16,192]{1,0:T(8,128)(2,1)S(1)} %collective-permute-done.18), kind=kLoop, calls=%fused_computation | loop fusion | flops 10368 | bytes 24192 | tf_op jit(solution)/shard_map/add | solution.py:605
  (33 shorter events, 3.4 us)
Async XLA Ops:
  0.6 12.9 %copy-start = (bf16[24,7,80,320]{3,2,1,0:T(8,128)(2,1)S(1)}, bf16[24,7,80,320]{3,2,1,0:T(8,128)(2,1)}, u32[]{:S(2)}) copy-start(bf16[24,7,80,320]{3,2,1,0:T(8,128)(2,1)} %jac_ref.7) | copy-start | bytes 25804804
  0.6 7.6 %collective-permute-start.2 = (f32[72,80]{1,0:T(8,128)}, f32[72,80]{1,0:T(8,128)S(1)}, u32[]{:S(2)}, u32[]{:S(2)}) collective-permute-start(f32[72,80]{1,0:T(8,128)} %bitcast.11), channel_id=1, source_target_pairs={{0,3},{1,2},{2,1},{3,0},{4,7},{5,6},{6,5},{7,4},{8,11},{9,10},{10,... | collective-permute-start | bytes 69128 | tf_op jit(solution)/shard_map/ppermute | solution.py:60
  5.8 5.1 %collective-permute-start.1 = (f32[72,80]{1,0:T(8,128)}, f32[72,80]{1,0:T(8,128)S(1)}, u32[]{:S(2)}, u32[]{:S(2)}) collective-permute-start(f32[72,80]{1,0:T(8,128)} %bitcast.12), channel_id=1, source_target_pairs={{0,2},{1,3},{2,0},{3,1},{4,6},{5,7},{6,4},{7,5},{8,10},{9,11},{10,... | collective-permute-start | bytes 69128 | tf_op jit(solution)/shard_map/ppermute | solution.py:60
  5.8 5.1 %collective-permute-start = (f32[72,80]{1,0:T(8,128)}, f32[72,80]{1,0:T(8,128)S(1)}, u32[]{:S(2)}, u32[]{:S(2)}) collective-permute-start(f32[72,80]{1,0:T(8,128)} %bitcast.13), channel_id=1, source_target_pairs={{0,1},{1,0},{2,3},{3,2},{4,5},{5,4},{6,7},{7,6},{8,9},{9,8},{10,11... | collective-permute-start | bytes 69128 | tf_op jit(solution)/shard_map/ppermute | solution.py:60
  11.0 2.6 %collective-permute-start.3 = (bf16[192,128]{1,0:T(8,128)(2,1)S(1)}, bf16[192,128]{1,0:T(8,128)(2,1)S(1)}, u32[]{:S(2)}, u32[]{:S(2)}) collective-permute-start(bf16[192,128]{1,0:T(8,128)(2,1)S(1)} %columns.2.own_ref), channel_id=1, source_target_pairs={{0,4},{4,0},{8,12},{12,8},{16,20},{20,16},{24,28},{28,24},{1,5},{5... | collective-permute-start | bytes 147464 | tf_op jit(solution)/shard_map/ppermute | solution.py:64
  11.0 5.2 %collective-permute-start.4 = (bf16[192,128]{1,0:T(8,128)(2,1)S(1)}, bf16[192,128]{1,0:T(8,128)(2,1)S(1)}, u32[]{:S(2)}, u32[]{:S(2)}) collective-permute-start(bf16[192,128]{1,0:T(8,128)(2,1)S(1)} %columns.2.own_ref), channel_id=1, source_target_pairs={{0,28},{4,8},{8,4},{12,16},{16,12},{20,24},{24,20},{28,0},{1,29},{... | collective-permute-start | bytes 147464 | tf_op jit(solution)/shard_map/ppermute | solution.py:69
  13.6 9.5 %copy-start.1 = (bf16[24,80,320]{2,1,0:T(8,128)(2,1)S(1)}, bf16[24,80,320]{2,1,0:T(8,128)(2,1)}, u32[]{:S(2)}) copy-start(bf16[24,80,320]{2,1,0:T(8,128)(2,1)} %refs_4_.3) | copy-start | bytes 3686404
  16.7 5.7 %collective-permute-start.7 = (bf16[80,80]{1,0:T(8,128)(2,1)S(1)}, bf16[80,80]{1,0:T(8,128)(2,1)S(1)}, u32[]{:S(2)}, u32[]{:S(2)}) collective-permute-start(bf16[80,80]{1,0:T(8,128)(2,1)S(1)} %far.2.refs_0_), channel_id=1, source_target_pairs={{0,3},{1,2},{2,1},{3,0},{4,7},{5,6},{6,5},{7,4},{8,11},{9,10},{10,... | collective-permute-start | bytes 38408 | tf_op jit(solution)/shard_map/ppermute | solution.py:60
  18.2 4.7 %collective-permute-start.6 = (bf16[80,80]{1,0:T(8,128)(2,1)S(1)}, bf16[80,80]{1,0:T(8,128)(2,1)S(1)}, u32[]{:S(2)}, u32[]{:S(2)}) collective-permute-start(bf16[80,80]{1,0:T(8,128)(2,1)S(1)} %far.2.refs_0_), channel_id=1, source_target_pairs={{0,2},{1,3},{2,0},{3,1},{4,6},{5,7},{6,4},{7,5},{8,10},{9,11},{10,... | collective-permute-start | bytes 38408 | tf_op jit(solution)/shard_map/ppermute | solution.py:60
  18.8 4.3 %collective-permute-start.5 = (bf16[80,80]{1,0:T(8,128)(2,1)S(1)}, bf16[80,80]{1,0:T(8,128)(2,1)S(1)}, u32[]{:S(2)}, u32[]{:S(2)}) collective-permute-start(bf16[80,80]{1,0:T(8,128)(2,1)S(1)} %far.2.refs_0_), channel_id=1, source_target_pairs={{0,1},{1,0},{2,3},{3,2},{4,5},{5,4},{6,7},{7,6},{8,9},{9,8},{10,11... | collective-permute-start | bytes 38408 | tf_op jit(solution)/shard_map/ppermute | solution.py:60
  23.8 5.7 %collective-permute-start.10 = (bf16[80,80]{1,0:T(8,128)(2,1)S(1)}, bf16[80,80]{1,0:T(8,128)(2,1)S(1)}, u32[]{:S(2)}, u32[]{:S(2)}) collective-permute-start(bf16[80,80]{1,0:T(8,128)(2,1)S(1)} %get-tuple-element.27.refs_0_), channel_id=1, source_target_pairs={{0,3},{1,2},{2,1},{3,0},{4,7},{5,6},{6,5},{7,4},{8,11},{9,10},{10,... | collective-permute-start | bytes 38408 | tf_op jit(solution)/shard_map/ppermute | solution.py:60
  26.2 4.7 %collective-permute-start.9 = (bf16[80,80]{1,0:T(8,128)(2,1)S(1)}, bf16[80,80]{1,0:T(8,128)(2,1)S(1)}, u32[]{:S(2)}, u32[]{:S(2)}) collective-permute-start(bf16[80,80]{1,0:T(8,128)(2,1)S(1)} %get-tuple-element.27.refs_0_), channel_id=1, source_target_pairs={{0,2},{1,3},{2,0},{3,1},{4,6},{5,7},{6,4},{7,5},{8,10},{9,11},{10,... | collective-permute-start | bytes 38408 | tf_op jit(solution)/shard_map/ppermute | solution.py:60
  27.1 4.0 %collective-permute-start.8 = (bf16[80,80]{1,0:T(8,128)(2,1)S(1)}, bf16[80,80]{1,0:T(8,128)(2,1)S(1)}, u32[]{:S(2)}, u32[]{:S(2)}) collective-permute-start(bf16[80,80]{1,0:T(8,128)(2,1)S(1)} %get-tuple-element.27.refs_0_), channel_id=1, source_target_pairs={{0,1},{1,0},{2,3},{3,2},{4,5},{5,4},{6,7},{7,6},{8,9},{9,8},{10,11... | collective-permute-start | bytes 38408 | tf_op jit(solution)/shard_map/ppermute | solution.py:60
  31.3 2.4 %collective-permute-start.11 = (bf16[192,128]{1,0:T(8,128)(2,1)S(1)}, bf16[192,128]{1,0:T(8,128)(2,1)S(1)}, u32[]{:S(2)}, u32[]{:S(2)}) collective-permute-start(bf16[192,128]{1,0:T(8,128)(2,1)S(1)} %columns.3.own_ref), channel_id=1, source_target_pairs={{0,4},{4,0},{8,12},{12,8},{16,20},{20,16},{24,28},{28,24},{1,5},{5... | collective-permute-start | bytes 147464 | tf_op jit(solution)/shard_map/ppermute | solution.py:64
  31.3 5.0 %collective-permute-start.12 = (bf16[192,128]{1,0:T(8,128)(2,1)S(1)}, bf16[192,128]{1,0:T(8,128)(2,1)S(1)}, u32[]{:S(2)}, u32[]{:S(2)}) collective-permute-start(bf16[192,128]{1,0:T(8,128)(2,1)S(1)} %columns.3.own_ref), channel_id=1, source_target_pairs={{0,28},{4,8},{8,4},{12,16},{16,12},{20,24},{24,20},{28,0},{1,29},{... | collective-permute-start | bytes 147464 | tf_op jit(solution)/shard_map/ppermute | solution.py:69
  33.7 7.6 %copy-start.3 = (bf16[24,80,192]{2,1,0:T(8,128)(2,1)S(1)}, bf16[24,80,192]{2,1,0:T(8,128)(2,1)}, u32[]{:S(2)}) copy-start(bf16[24,80,192]{2,1,0:T(8,128)(2,1)} %shape_ref.1) | copy-start | bytes 2211844
  33.7 7.6 %copy-start.4 = (s32[24,64]{1,0:T(8,128)S(1)}, s32[24,64]{1,0:T(8,128)}, u32[]{:S(2)}) copy-start(s32[24,64]{1,0:T(8,128)} %ids_ref.1) | copy-start | bytes 18436
  33.7 9.5 %copy-start.2 = (bf16[24,80,320]{2,1,0:T(8,128)(2,1)S(1)}, bf16[24,80,320]{2,1,0:T(8,128)(2,1)}, u32[]{:S(2)}) copy-start(bf16[24,80,320]{2,1,0:T(8,128)(2,1)} %refs_4_.3) | copy-start | bytes 3686404
  36.8 5.8 %collective-permute-start.15 = (bf16[80,80]{1,0:T(8,128)(2,1)S(1)}, bf16[80,80]{1,0:T(8,128)(2,1)S(1)}, u32[]{:S(2)}, u32[]{:S(2)}) collective-permute-start(bf16[80,80]{1,0:T(8,128)(2,1)S(1)} %far.3.refs_0_), channel_id=1, source_target_pairs={{0,3},{1,2},{2,1},{3,0},{4,7},{5,6},{6,5},{7,4},{8,11},{9,10},{10,... | collective-permute-start | bytes 38408 | tf_op jit(solution)/shard_map/ppermute | solution.py:60
  38.3 4.7 %collective-permute-start.14 = (bf16[80,80]{1,0:T(8,128)(2,1)S(1)}, bf16[80,80]{1,0:T(8,128)(2,1)S(1)}, u32[]{:S(2)}, u32[]{:S(2)}) collective-permute-start(bf16[80,80]{1,0:T(8,128)(2,1)S(1)} %far.3.refs_0_), channel_id=1, source_target_pairs={{0,2},{1,3},{2,0},{3,1},{4,6},{5,7},{6,4},{7,5},{8,10},{9,11},{10,... | collective-permute-start | bytes 38408 | tf_op jit(solution)/shard_map/ppermute | solution.py:60
  39.2 4.0 %collective-permute-start.13 = (bf16[80,80]{1,0:T(8,128)(2,1)S(1)}, bf16[80,80]{1,0:T(8,128)(2,1)S(1)}, u32[]{:S(2)}, u32[]{:S(2)}) collective-permute-start(bf16[80,80]{1,0:T(8,128)(2,1)S(1)} %far.3.refs_0_), channel_id=1, source_target_pairs={{0,1},{1,0},{2,3},{3,2},{4,5},{5,4},{6,7},{7,6},{8,9},{9,8},{10,11... | collective-permute-start | bytes 38408 | tf_op jit(solution)/shard_map/ppermute | solution.py:60
  44.7 2.9 %collective-permute-start.16 = (bf16[48,192]{1,0:T(8,128)(2,1)S(1)}, bf16[48,192]{1,0:T(8,128)(2,1)S(1)}, u32[]{:S(2)}, u32[]{:S(2)}) collective-permute-start(bf16[48,192]{1,0:T(8,128)(2,1)S(1)} %get-tuple-element.34), channel_id=1, source_target_pairs={{0,4},{4,0},{8,12},{12,8},{16,20},{20,16},{24,28},{28,24},{1,5},{5... | collective-permute-start | bytes 55304 | tf_op jit(solution)/shard_map/ppermute | solution.py:64
  44.7 4.2 %collective-permute-start.17 = (bf16[48,192]{1,0:T(8,128)(2,1)S(1)}, bf16[48,192]{1,0:T(8,128)(2,1)S(1)}, u32[]{:S(2)}, u32[]{:S(2)}) collective-permute-start(bf16[48,192]{1,0:T(8,128)(2,1)S(1)} %get-tuple-element.35), channel_id=1, source_target_pairs={{0,28},{4,8},{8,4},{12,16},{16,12},{20,24},{24,20},{28,0},{1,29},{... | collective-permute-start | bytes 55304 | tf_op jit(solution)/shard_map/ppermute | solution.py:69
  49.0 5.5 %collective-permute-start.18 = (bf16[16,192]{1,0:T(8,128)(2,1)S(1)}, bf16[16,192]{1,0:T(8,128)(2,1)S(1)}, u32[]{:S(2)}, u32[]{:S(2)}) collective-permute-start(bf16[16,192]{1,0:T(8,128)(2,1)S(1)} %get-tuple-element.37), channel_id=1, source_target_pairs={{0,3},{1,2},{2,1},{3,0},{4,7},{5,6},{6,5},{7,4},{8,11},{9,10},{10,... | collective-permute-start | bytes 18440 | tf_op jit(solution)/shard_map/ppermute | solution.py:605
  51.4 4.6 %collective-permute-start.19 = (bf16[16,192]{1,0:T(8,128)(2,1)S(1)}, bf16[16,192]{1,0:T(8,128)(2,1)S(1)}, u32[]{:S(2)}, u32[]{:S(2)}) collective-permute-start(bf16[16,192]{1,0:T(8,128)(2,1)S(1)} %get-tuple-element.38), channel_id=1, source_target_pairs={{0,2},{1,3},{2,0},{3,1},{4,6},{5,7},{6,4},{7,5},{8,10},{9,11},{10,... | collective-permute-start | bytes 18440 | tf_op jit(solution)/shard_map/ppermute | solution.py:605
  52.3 3.7 %collective-permute-start.20 = (bf16[16,192]{1,0:T(8,128)(2,1)S(1)}, bf16[16,192]{1,0:T(8,128)(2,1)S(1)}, u32[]{:S(2)}, u32[]{:S(2)}) collective-permute-start(bf16[16,192]{1,0:T(8,128)(2,1)S(1)} %get-tuple-element.39), channel_id=1, source_target_pairs={{0,1},{1,0},{2,3},{3,2},{4,5},{5,4},{6,7},{7,6},{8,9},{9,8},{10,11... | collective-permute-start | bytes 18440 | tf_op jit(solution)/shard_map/ppermute | solution.py:605
